TPU v7x, 32 devices: a whole 2x2x4 slice. The times are simulated.
32 devices in a mesh: groups: 2 (over y), ctx: 16 (over z, x, core).
Axes of the slice: x: 2, y: 2, z: 4, core: 2. Of those that a mesh axis runs over, the one named last changes fastest.
Arguments:
- queries: bfloat16 [8192, 4096], P(('groups', 'ctx')), parts along dimension 0, may hold values from -13 to 13
- all_key_states: bfloat16 [8192, 512], P(('groups', 'ctx')), parts along dimension 0, may hold values from -9.5 to 9.5
- all_value_states: bfloat16 [8192, 512], P(('groups', 'ctx')), parts along dimension 0, may hold values from -6 to 6
- selected: int32 [32, 2], P(('groups', 'ctx')), parts along dimension 0, may hold values from 0 to 14, as said below
Outputs:
- attended: bfloat16 [8192, 4096], P(('groups', 'ctx')), parts along dimension 0
There are 2 independent parts, one for each index of `groups`. A program takes and returns all parts, laid end to end along the dimension named above; each array names one. Nothing has to cross between parts.
Inputs may be any that keep to these rules, and one draw needn't show every extreme that they name: `selected`: for block i >= 2 the two entries of row i are different blocks below i; rows 0 and 1 hold 0 and 0; the last block's first entry is 14.
All inputs are finite; a program needn't handle non-finite values.
Results may differ from a plain program's by a relative error of at most 0.004.
Values may be sent and summed in bfloat16 or wider, within the bound.
No kernel may reach another device: no remote copies, remote signals or barrier semaphores. Data moves between devices by JAX's collectives and lax.ppermute only.
A program may use at most 64 MiB of HBM per device.

v0:
```python
import math

import jax
import jax.numpy as jnp
from jax import lax
from jax.sharding import PartitionSpec as P

QUERY_HEADS = 32
KEY_VALUE_HEADS = 4
HEAD_SIZE = 128


def attend(query_head_count, key_head_count, value_heads, allowed):
    score_scale = 1.0 / math.sqrt(query_head_count.shape[-1])

    def one_head(operands):
        query_part, key_part, value_part = operands
        scores = (
            jnp.einsum("trd,ud->tru", query_part, key_part, preferred_element_type=jnp.float32)
            * score_scale
        )
        scores = jnp.where(allowed[:, None, :], scores, jnp.float32(-1e30))
        row_max = jnp.max(scores, axis=2, keepdims=True)
        weights = jnp.exp(scores - row_max)
        row_sum = jnp.sum(weights, axis=2, keepdims=True)
        mixture = jnp.einsum(
            "tru,ud->trd",
            weights.astype(jnp.bfloat16),
            value_part,
            preferred_element_type=jnp.float32,
        )
        return (mixture / row_sum).astype(jnp.bfloat16)

    stacked = lax.map(
        one_head,
        (
            query_head_count.transpose(1, 0, 2, 3),
            key_head_count.transpose(1, 0, 2),
            value_heads.transpose(1, 0, 2),
        ),
    )
    return stacked.transpose(1, 0, 2, 3)


def local(queries, all_key_states, all_value_states, selected):
    devices = lax.axis_size("ctx")
    my_block = lax.axis_index("ctx")
    block_row_count, feature_width = all_key_states.shape
    piece_rows = block_row_count // devices
    key_split = all_key_states.reshape(devices, piece_rows, feature_width)
    value_split = all_value_states.reshape(devices, piece_rows, feature_width)
    requests = lax.all_gather(selected, "ctx", axis=0, tiled=True)
    held_keys, held_values = (
        lax.all_to_all(key_split, "ctx", split_axis=0, concat_axis=0, tiled=True),
        lax.all_to_all(value_split, "ctx", split_axis=0, concat_axis=0, tiled=True),
    )
    wanted = requests.T
    first_keys, first_values = (
        lax.all_to_all(
            jnp.take(held_keys, wanted[0], axis=0), "ctx", split_axis=0, concat_axis=0, tiled=True
        ),
        lax.all_to_all(
            jnp.take(held_values, wanted[0], axis=0), "ctx", split_axis=0, concat_axis=0, tiled=True
        ),
    )
    second_keys, second_values = (
        lax.all_to_all(
            jnp.take(held_keys, wanted[1], axis=0), "ctx", split_axis=0, concat_axis=0, tiled=True
        ),
        lax.all_to_all(
            jnp.take(held_values, wanted[1], axis=0), "ctx", split_axis=0, concat_axis=0, tiled=True
        ),
    )
    distant_keys = jnp.concatenate(
        [
            first_keys.reshape(block_row_count, feature_width),
            second_keys.reshape(block_row_count, feature_width),
        ],
        axis=0,
    )
    remote_values = jnp.concatenate(
        [
            first_values.reshape(block_row_count, feature_width),
            second_values.reshape(block_row_count, feature_width),
        ],
        axis=0,
    )
    first_block = selected[0, 0]
    second_block = selected[0, 1]
    first_valid = first_block < my_block
    second_valid = jnp.logical_and(second_block < my_block, second_block != first_block)
    row_ids = jnp.arange(block_row_count, dtype=jnp.int32)
    causal = row_ids[None, :] <= row_ids[:, None]
    allowed = jnp.concatenate(
        [
            causal,
            jnp.broadcast_to(first_valid, (block_row_count, block_row_count)),
            jnp.broadcast_to(second_valid, (block_row_count, block_row_count)),
        ],
        axis=1,
    )
    key_head_count = jnp.concatenate([all_key_states, distant_keys], axis=0).reshape(
        3 * block_row_count, KEY_VALUE_HEADS, HEAD_SIZE
    )
    value_heads = jnp.concatenate([all_value_states, remote_values], axis=0).reshape(
        3 * block_row_count, KEY_VALUE_HEADS, HEAD_SIZE
    )
    query_head_count = queries.reshape(
        block_row_count, KEY_VALUE_HEADS, QUERY_HEADS // KEY_VALUE_HEADS, HEAD_SIZE
    )
    attended = attend(query_head_count, key_head_count, value_heads, allowed)
    return attended.reshape(block_row_count, QUERY_HEADS * HEAD_SIZE)


def solution(mesh):
    placed = (
        P(("groups", "ctx"), None),
        P(("groups", "ctx"), None),
        P(("groups", "ctx"), None),
        P(("groups", "ctx"), None),
    )
    return jax.shard_map(
        local, mesh=mesh, in_specs=placed, out_specs=P(("groups", "ctx"), None), check_vma=False
    )
```

profile of v0, /device:TPU:5, one launch (start us, length us, event | category | flops | bytes accessed | tf_op | source)
XLA Modules:
  0.0 135.4 jit_solution(8048211730979571622)
XLA Ops:
  0.0 16.0 %all_to_all.30 = bf16[16,16,512]{2,1,0:T(8,128)(2,1)S(1)} all-to-all(bf16[16,16,512]{2,1,0:T(8,128)(2,1)} %bitcast.63), channel_id=1, replica_groups=mesh['groups'=2,'ctx'=16] {'ctx'}, dimensions={0} | all-to-all | bytes 524288 | tf_op jit(solution)/shard_map/all_to_all | solution.py:54
  16.0 4.0 %all-to-all-start.3 = ((bf16[16,16,512]{2,1,0:T(8,128)(2,1)}), bf16[16,16,512]{2,1,0:T(8,128)(2,1)S(1)}, u32[]{:S(2)}, u32[]{:S(2)}) async-start(bf16[16,16,512]{2,1,0:T(8,128)(2,1)} %bitcast.64), calls=%async_computation.3 | async-start | bytes 524288 | tf_op jit(solution)/shard_map/all_to_all | solution.py:55
  20.0 21.7 %all-gather = s32[16,1,2]{2,1,0:T(1,128)S(1)} all-gather(s32[1,1,2]{2,1,0:T(1,128)} %bitcast.65), channel_id=1, replica_groups=mesh['groups'=2,'ctx'=16] {'ctx'}, dimensions={0}, use_global_device_ids=true | all-gather | bytes 136 | tf_op jit(solution)/shard_map/all_gather | solution.py:52
  43.8 3.7 %all-to-all-start.1 = ((bf16[16,16,512]{2,1,0:T(8,128)(2,1)}), bf16[16,16,512]{2,1,0:T(8,128)(2,1)S(1)}, u32[]{:S(2)}, u32[]{:S(2)}) async-start(bf16[16,16,512]{2,1,0:T(8,128)(2,1)} %get-tuple-element.72), calls=%async_computation.1 | async-start | bytes 524288 | tf_op jit(solution)/shard_map/all_to_all | solution.py:59
  49.4 7.5 %all-to-all-done.1 = bf16[16,16,512]{2,1,0:T(8,128)(2,1)S(1)} async-done(((bf16[16,16,512]{2,1,0:T(8,128)(2,1)}), bf16[16,16,512]{2,1,0:T(8,128)(2,1)S(1)}, u32[]{:S(2)}, u32[]{:S(2)}) %all-to-all-start.1) | async-done | bytes 262176 | tf_op jit(solution)/shard_map/all_to_all | solution.py:59
  57.0 13.3 %all_to_all.31 = bf16[16,16,512]{2,1,0:T(8,128)(2,1)} all-to-all(bf16[16,16,512]{2,1,0:T(8,128)(2,1)S(1)} %get-tuple-element.74), channel_id=1, replica_groups=mesh['groups'=2,'ctx'=16] {'ctx'}, dimensions={0} | all-to-all | bytes 524288 | tf_op jit(solution)/shard_map/all_to_all | solution.py:67
  70.3 12.8 %all_to_all.32 = bf16[16,16,512]{2,1,0:T(8,128)(2,1)S(1)} all-to-all(bf16[16,16,512]{2,1,0:T(8,128)(2,1)S(1)} %get-tuple-element.71), channel_id=1, replica_groups=mesh['groups'=2,'ctx'=16] {'ctx'}, dimensions={0} | all-to-all | bytes 524288 | tf_op jit(solution)/shard_map/all_to_all | solution.py:62
  83.1 4.0 %all-to-all-start.5 = ((bf16[16,16,512]{2,1,0:T(8,128)(2,1)}), bf16[16,16,512]{2,1,0:T(8,128)(2,1)S(1)}, u32[]{:S(2)}, u32[]{:S(2)}) async-start(bf16[16,16,512]{2,1,0:T(8,128)(2,1)} %get-tuple-element.73), calls=%async_computation.5 | async-start | bytes 524288 | tf_op jit(solution)/shard_map/all_to_all | solution.py:70
  91.2 3.3 %copy.19 = bf16[256,4096]{0,1:T(8,128)(2,1)S(1)} copy(bf16[256,4096]{1,0:T(8,128)(2,1)} %param.8) | data formatting | bytes 4194304 | tf_op args[0]
  95.4 1.8 %copy.22 = bf16[256,4,128]{0,2,1:T(8,128)(2,1)} copy(bf16[256,4,128]{2,1,0:T(4,128)(2,1)} %concatenate.25) | data formatting | bytes 524288 | tf_op jit(solution)/shard_map/concatenate | solution.py:102
  101.0 2.3 %maximum_bitcast_fusion = (bf16[4,768,128]{1,2,0:T(8,128)(2,1)S(1)}, bf16[4,768,128]{1,2,0:T(8,128)(2,1)}) fusion(bf16[256,4,128]{0,2,1:T(8,128)(2,1)} %copy.23, bf16[256,4,128]{0,2,1:T(8,128)(2,1)} %copy.22, bf16[256,4,128]{0,2,1:T(8,128)(2,1)S(1)} %bitcast.61, bf16[256,4,128]{0,2,1:T(8,128)(2,1)} %copy.26, bf16[256,4,128]{0,2,1:T(8,128)(2,1)} %copy.25, ...), kind=kLoop, calls=%fused_computation.26 | loop fusion | flops 4718592 | bytes 3145728 | tf_op jit(solution)/shard_map/transpose | solution.py:38
  103.3 26.9 %while.10 = (s32[]{:T(128)}, bf16[4,256,8,128]{3,1,2,0:T(8,128)(2,1)}, pred[256,768]{1,0:T(8,128)(4,1)S(1)}, bf16[4,256,8,128]{1,3,2,0:T(8,128)(2,1)S(1)}, bf16[...) while((s32[]{:T(128)}, bf16[4,256,8,128]{3,1,2,0:T(8,128)(2,1)}, ...), condition=%wide.region_3.5_spmd, body=%wide.region_0.4_spmd.sunk | while | flops 823128064 | bytes 20949068 | solution.py:34
  104.6 1.7 %fusion.34 = f32[256,8]{0,1:T(8,128)S(1)} fusion(f32[256,8,768]{2,0,1:T(8,128)S(1)} %get-tuple-element.118, f32[256,8]{0,1:T(8,128)S(1)} %get-tuple-element.119, pred[256,768]{1,0:T(8,128)(4,1)S(1)} %get-tuple-element.136), kind=kLoop, calls=%fused_computation.7.clone.1 | loop fusion | flops 6289408 | bytes 6504448 | tf_op jit(solution)/shard_map/while/body/eval_jaxpr/reduce_sum | solution.py:25
  106.3 3.7 %fusion.35 = bf16[4,256,8,128]{3,1,2,0:T(8,128)(2,1)} fusion(bf16[4,256,8,128]{3,1,2,0:T(8,128)(2,1)} %get-tuple-element.128, s32[]{:T(128)} %get-tuple-element.127, f32[256,8,768]{2,0,1:T(8,128)S(1)} %get-tuple-element.118, f32[256,8]{0,1:T(8,128)S(1)} %get-tuple-element.119, pred[256,768]{1,0:T(8,128)(4,1)S(1)} %get-tuple-element.136, ...), kind=kOutput, calls=%fused_computation.13.clone.1 | convolution fusion | flops 409468928 | bytes 7226368 | tf_op jit(solution)/shard_map/while/body/eval_jaxpr/tru,ud->trd/dot_general | solution.py:26
  110.0 1.3 fusion.33
  111.3 1.7 %fusion.34 = f32[256,8]{0,1:T(8,128)S(1)} fusion(f32[256,8,768]{2,0,1:T(8,128)S(1)} %get-tuple-element.118, f32[256,8]{0,1:T(8,128)S(1)} %get-tuple-element.119, pred[256,768]{1,0:T(8,128)(4,1)S(1)} %get-tuple-element.136), kind=kLoop, calls=%fused_computation.7.clone.1 | loop fusion | flops 6289408 | bytes 6504448 | tf_op jit(solution)/shard_map/while/body/eval_jaxpr/reduce_sum | solution.py:25
  113.0 3.7 %fusion.35 = bf16[4,256,8,128]{3,1,2,0:T(8,128)(2,1)} fusion(bf16[4,256,8,128]{3,1,2,0:T(8,128)(2,1)} %get-tuple-element.128, s32[]{:T(128)} %get-tuple-element.127, f32[256,8,768]{2,0,1:T(8,128)S(1)} %get-tuple-element.118, f32[256,8]{0,1:T(8,128)S(1)} %get-tuple-element.119, pred[256,768]{1,0:T(8,128)(4,1)S(1)} %get-tuple-element.136, ...), kind=kOutput, calls=%fused_computation.13.clone.1 | convolution fusion | flops 409468928 | bytes 7226368 | tf_op jit(solution)/shard_map/while/body/eval_jaxpr/tru,ud->trd/dot_general | solution.py:26
  116.7 1.3 fusion.33
  118.1 1.7 %fusion.34 = f32[256,8]{0,1:T(8,128)S(1)} fusion(f32[256,8,768]{2,0,1:T(8,128)S(1)} %get-tuple-element.118, f32[256,8]{0,1:T(8,128)S(1)} %get-tuple-element.119, pred[256,768]{1,0:T(8,128)(4,1)S(1)} %get-tuple-element.136), kind=kLoop, calls=%fused_computation.7.clone.1 | loop fusion | flops 6289408 | bytes 6504448 | tf_op jit(solution)/shard_map/while/body/eval_jaxpr/reduce_sum | solution.py:25
  119.7 3.7 %fusion.35 = bf16[4,256,8,128]{3,1,2,0:T(8,128)(2,1)} fusion(bf16[4,256,8,128]{3,1,2,0:T(8,128)(2,1)} %get-tuple-element.128, s32[]{:T(128)} %get-tuple-element.127, f32[256,8,768]{2,0,1:T(8,128)S(1)} %get-tuple-element.118, f32[256,8]{0,1:T(8,128)S(1)} %get-tuple-element.119, pred[256,768]{1,0:T(8,128)(4,1)S(1)} %get-tuple-element.136, ...), kind=kOutput, calls=%fused_computation.13.clone.1 | convolution fusion | flops 409468928 | bytes 7226368 | tf_op jit(solution)/shard_map/while/body/eval_jaxpr/tru,ud->trd/dot_general | solution.py:26
  124.8 1.7 %fusion.34 = f32[256,8]{0,1:T(8,128)S(1)} fusion(f32[256,8,768]{2,0,1:T(8,128)S(1)} %get-tuple-element.118, f32[256,8]{0,1:T(8,128)S(1)} %get-tuple-element.119, pred[256,768]{1,0:T(8,128)(4,1)S(1)} %get-tuple-element.136), kind=kLoop, calls=%fused_computation.7.clone.1 | loop fusion | flops 6289408 | bytes 6504448 | tf_op jit(solution)/shard_map/while/body/eval_jaxpr/reduce_sum | solution.py:25
  126.5 3.7 %fusion.35 = bf16[4,256,8,128]{3,1,2,0:T(8,128)(2,1)} fusion(bf16[4,256,8,128]{3,1,2,0:T(8,128)(2,1)} %get-tuple-element.128, s32[]{:T(128)} %get-tuple-element.127, f32[256,8,768]{2,0,1:T(8,128)S(1)} %get-tuple-element.118, f32[256,8]{0,1:T(8,128)S(1)} %get-tuple-element.119, pred[256,768]{1,0:T(8,128)(4,1)S(1)} %get-tuple-element.136, ...), kind=kOutput, calls=%fused_computation.13.clone.1 | convolution fusion | flops 409468928 | bytes 7226368 | tf_op jit(solution)/shard_map/while/body/eval_jaxpr/tru,ud->trd/dot_general | solution.py:26
  130.2 2.9 %copy.30 = bf16[256,4,8,128]{3,2,1,0:T(8,128)(2,1)S(1)} copy(bf16[256,4,8,128]{3,0,2,1:T(8,128)(2,1)} %bitcast.22) | data formatting | bytes 4194304 | tf_op jit(solution)/shard_map/transpose | solution.py:42
  133.1 2.3 %copy.36 = bf16[32,8,32,128]{3,1,2,0:T(8,128)(2,1)} copy(bf16[32,8,32,128]{3,2,1,0:T(8,128)(2,1)S(1)} %bitcast.60) | data formatting | bytes 4194304
  (37 shorter events, 13.0 us)
Async XLA Ops:
  16.0 26.4 %all-to-all-start.3 = ((bf16[16,16,512]{2,1,0:T(8,128)(2,1)}), bf16[16,16,512]{2,1,0:T(8,128)(2,1)S(1)}, u32[]{:S(2)}, u32[]{:S(2)}) async-start(bf16[16,16,512]{2,1,0:T(8,128)(2,1)} %bitcast.64), calls=%async_computation.3 | async-start | bytes 524288 | tf_op jit(solution)/shard_map/all_to_all | solution.py:55
  43.8 43.3 %copy-start = (bf16[256,512]{1,0:T(8,128)(2,1)S(1)}, bf16[256,512]{1,0:T(8,128)(2,1)}, u32[]{:S(2)}) copy-start(bf16[256,512]{1,0:T(8,128)(2,1)} %param.9) | copy-start | bytes 786436
  43.8 13.2 %all-to-all-start.1 = ((bf16[16,16,512]{2,1,0:T(8,128)(2,1)}), bf16[16,16,512]{2,1,0:T(8,128)(2,1)S(1)}, u32[]{:S(2)}, u32[]{:S(2)}) async-start(bf16[16,16,512]{2,1,0:T(8,128)(2,1)} %get-tuple-element.72), calls=%async_computation.1 | async-start | bytes 524288 | tf_op jit(solution)/shard_map/all_to_all | solution.py:59
  47.5 39.8 %copy-start.1 = (bf16[256,512]{1,0:T(8,128)(2,1)S(1)}, bf16[256,512]{1,0:T(8,128)(2,1)}, u32[]{:S(2)}) copy-start(bf16[256,512]{1,0:T(8,128)(2,1)} %param.10) | copy-start | bytes 786436
  48.0 40.1 %copy-start.2 = (s32[1,2]{1,0:T(1,128)S(1)}, s32[1,2]{1,0:T(1,128)}, u32[]{:S(2)}) copy-start(s32[1,2]{1,0:T(1,128)} %param.11) | copy-start | bytes 28
  83.1 16.9 %all-to-all-start.5 = ((bf16[16,16,512]{2,1,0:T(8,128)(2,1)}), bf16[16,16,512]{2,1,0:T(8,128)(2,1)S(1)}, u32[]{:S(2)}, u32[]{:S(2)}) async-start(bf16[16,16,512]{2,1,0:T(8,128)(2,1)} %get-tuple-element.73), calls=%async_computation.5 | async-start | bytes 524288 | tf_op jit(solution)/shard_map/all_to_all | solution.py:70
where the time goes:
time: 137 us; the launch traced here: 135 us
  blocking collectives  63.9 us (47%)
  matrix products  20.1 us (15%)
  local copies, waits for them, and re-layouts  18.8 us (14%)
  starting transfers between devices  11.6 us (8%)
  other arithmetic  10.7 us (8%)
  waiting for transfers between devices  7.55 us (6%)
  between operations  2.63 us (2%)
    all_gather x1, blocking collectives, local(): requests = lax.all_gather(selected, 'ctx', axis=0, tiled=True)  21.7 us
    all_to_all x1, blocking collectives, local(): lax.all_to_all(key_split, 'ctx', split_axis=0, concat_axis=0, tiled=True)  16 us
    dot_general x4, matrix products, one_head(): jnp.einsum('tru,ud->trd', weights.astype(jnp.bfloat16), value_part, prefe...  14.8 us
    all_to_all x1, blocking collectives, local(): lax.all_to_all(jnp.take(held_keys, wanted[1], axis=0), 'ctx', split_axis=...  13.3 us
    all_to_all x1, blocking collectives, local(): lax.all_to_all(jnp.take(held_values, wanted[0], axis=0), 'ctx', split_axi...  12.8 us
    all_to_all x1, waiting for transfers between devices, local(): lax.all_to_all(jnp.take(held_keys, wanted[0], axis=0), 'ctx', split_axis=...  7.55 us
    reduce_sum x4, other arithmetic, one_head(): row_sum = jnp.sum(weights, axis=2, keepdims=True)  6.7 us
    unnamed x10, local copies, waits for them, and re-layouts  6.56 us
  transfers between devices with their start and end apart: 3, of which 1 were waited for; matrix products, arithmetic and copies ran while one was open for 10% of the time, Pallas kernels for 0%

commit v1 on v0

v1 whole, which is shorter than its diff:
```python
import functools
import math

import jax
import jax.numpy as jnp
from jax import lax
from jax.experimental import pallas as pl
from jax.experimental.pallas import tpu as pltpu
from jax.sharding import PartitionSpec as P

QUERY_HEADS = 32
KEY_VALUE_HEADS = 4
HEAD_SIZE = 128
GROUP = QUERY_HEADS // KEY_VALUE_HEADS
SLOTS = 2 * KEY_VALUE_HEADS
REQUEST_ROWS = 16
MIB = 1024 * 1024


def pack_kernel(selected_ref, key_ref, value_ref, out_ref):
    devices, piece_rows = out_ref.shape[0], key_ref.shape[0] // out_ref.shape[0]
    for slot in range(SLOTS):
        ref = key_ref if slot < KEY_VALUE_HEADS else value_ref
        head = slot % KEY_VALUE_HEADS
        part = ref[:, head * HEAD_SIZE : (head + 1) * HEAD_SIZE]
        out_ref[:, slot * piece_rows : (slot + 1) * piece_rows, :] = part.reshape(
            devices, piece_rows, HEAD_SIZE
        )
    lane = lax.broadcasted_iota(jnp.int32, (devices, REQUEST_ROWS, HEAD_SIZE), 2)
    request = jnp.where(lane == 0, selected_ref[0, 0], selected_ref[0, 1])
    out_ref[:, SLOTS * piece_rows :, :] = request.astype(jnp.float32).astype(jnp.bfloat16)


def pack(keys, values, selected, devices):
    rows = keys.shape[0]
    piece_rows = rows // devices
    shape = (devices, SLOTS * piece_rows + REQUEST_ROWS, HEAD_SIZE)
    if piece_rows % 16 == 0:
        return pl.pallas_call(
            pack_kernel,
            out_shape=jax.ShapeDtypeStruct(shape, jnp.bfloat16),
            in_specs=[
                pl.BlockSpec(memory_space=pltpu.SMEM),
                pl.BlockSpec(memory_space=pltpu.VMEM),
                pl.BlockSpec(memory_space=pltpu.VMEM),
            ],
            out_specs=pl.BlockSpec(memory_space=pltpu.VMEM),
            name="pack",
        )(selected, keys, values)
    both = jnp.concatenate([keys, values], axis=1)
    both = both.reshape(devices, piece_rows, SLOTS, HEAD_SIZE).transpose(0, 2, 1, 3)
    both = both.reshape(devices, SLOTS * piece_rows, HEAD_SIZE)
    lane = jnp.arange(HEAD_SIZE) == 0
    request = jnp.where(lane, selected[0, 0], selected[0, 1]).astype(jnp.bfloat16)
    request = jnp.broadcast_to(request, (devices, REQUEST_ROWS, HEAD_SIZE))
    return jnp.concatenate([both, request], axis=1)


def pick_kernel(wanted_ref, held_ref, out_ref):
    rows = out_ref.shape[2]

    @pl.loop(0, out_ref.shape[0])
    def _(device):
        for pick in range(2):
            out_ref[device, pick] = held_ref[wanted_ref[device, pick], :rows, :]


def pick_pieces(wanted, held):
    devices, rows = held.shape[0], held.shape[1] - REQUEST_ROWS
    return pl.pallas_call(
        pick_kernel,
        out_shape=jax.ShapeDtypeStruct((devices, 2, rows, HEAD_SIZE), jnp.bfloat16),
        in_specs=[
            pl.BlockSpec(memory_space=pltpu.SMEM),
            pl.BlockSpec(memory_space=pltpu.VMEM),
        ],
        out_specs=pl.BlockSpec(memory_space=pltpu.VMEM),
        compiler_params=pltpu.CompilerParams(vmem_limit_bytes=16 * MIB),
        name="pick_pieces",
    )(wanted, held)


NT = (((1,), (1,)), ((), ()))
NN = (((1,), (0,)), ((), ()))


def attention_kernel(
    flags_ref, query_ref, key_ref, value_ref, far_key_ref, far_value_ref, out_ref
):
    rows = query_ref.shape[0]
    half = rows // 2
    factor = math.log2(math.e) / math.sqrt(HEAD_SIZE)
    row = lax.broadcasted_iota(jnp.int32, (half, half), 0)
    column = lax.broadcasted_iota(jnp.int32, (half, half), 1)
    causal = column <= row

    def attend(picks):
        own_key, own_value = key_ref[...], value_ref[...]
        far = [
            (
                far_key_ref[:, pick, 0].reshape(rows, HEAD_SIZE),
                far_value_ref[:, pick, 0].reshape(rows, HEAD_SIZE),
            )
            for pick in picks
        ]
        for head in range(GROUP):
            lanes = slice(head * HEAD_SIZE, (head + 1) * HEAD_SIZE)
            for part in range(2):
                query = query_ref[part * half : (part + 1) * half, lanes]
                pieces = []
                for block in range(part + 1):
                    span = slice(block * half, (block + 1) * half)
                    scores = lax.dot_general(
                        query, own_key[span], NT, preferred_element_type=jnp.float32
                    )
                    if block == part:
                        scores = jnp.where(causal, scores, -1e30)
                    pieces.append((scores, own_value[span]))
                for far_key, far_value in far:
                    scores = lax.dot_general(
                        query, far_key, NT, preferred_element_type=jnp.float32
                    )
                    pieces.append((scores, far_value))
                row_max = functools.reduce(
                    jnp.maximum, [jnp.max(s, axis=1, keepdims=True) for s, _ in pieces]
                )
                shift = row_max * factor
                row_sum, mixture = 0.0, 0.0
                for scores, value in pieces:
                    weights = jnp.exp2(scores * factor - shift)
                    row_sum = row_sum + jnp.sum(weights, axis=1, keepdims=True)
                    mixture = mixture + lax.dot_general(
                        weights.astype(jnp.bfloat16), value, NN, preferred_element_type=jnp.float32
                    )
                out_ref[part * half : (part + 1) * half, lanes] = (
                    mixture / row_sum
                ).astype(out_ref.dtype)

    first, second = flags_ref[0], flags_ref[1]

    @pl.when(first + second == 2)
    def _():
        attend((0, 1))

    @pl.when(first + second == 1)
    def _():
        attend((second,))

    @pl.when(first + second == 0)
    def _():
        attend(())


def attention(flags, queries, keys, values, far):
    rows = queries.shape[0]
    holders, _, _, piece_rows, _ = far.shape
    width = GROUP * HEAD_SIZE
    far_shape = (holders, 2, 1, piece_rows, HEAD_SIZE)
    scores = QUERY_HEADS * rows * 3 * rows
    return pl.pallas_call(
        attention_kernel,
        out_shape=jax.ShapeDtypeStruct(queries.shape, jnp.bfloat16),
        grid=(KEY_VALUE_HEADS,),
        in_specs=[
            pl.BlockSpec(memory_space=pltpu.SMEM),
            pl.BlockSpec((rows, width), lambda g: (0, g)),
            pl.BlockSpec((rows, HEAD_SIZE), lambda g: (0, g)),
            pl.BlockSpec((rows, HEAD_SIZE), lambda g: (0, g)),
            pl.BlockSpec(far_shape, lambda g: (0, 0, g, 0, 0)),
            pl.BlockSpec(far_shape, lambda g: (0, 0, g + KEY_VALUE_HEADS, 0, 0)),
        ],
        out_specs=pl.BlockSpec((rows, width), lambda g: (0, g)),
        compiler_params=pltpu.CompilerParams(vmem_limit_bytes=40 * MIB),
        cost_estimate=pl.CostEstimate(
            flops=4 * scores * HEAD_SIZE, bytes_accessed=6 * MIB, transcendentals=scores
        ),
        name="attention",
    )(flags, queries, keys, values, far, far)


def local(queries, all_key_states, all_value_states, selected):
    devices = lax.axis_size("ctx")
    my_block = lax.axis_index("ctx")
    rows = all_key_states.shape[0]
    piece_rows = rows // devices
    packed = pack(all_key_states, all_value_states, selected, devices)
    held = lax.all_to_all(packed, "ctx", split_axis=0, concat_axis=0, tiled=True)
    wanted = held[:, SLOTS * piece_rows, :2].astype(jnp.int32)
    wanted = jnp.clip(wanted, 0, devices - 1)
    chosen = pick_pieces(wanted, held)
    far = lax.all_to_all(chosen, "ctx", split_axis=0, concat_axis=0, tiled=True)
    far = far.reshape(devices, 2, SLOTS, piece_rows, HEAD_SIZE)
    if piece_rows % 16 != 0:
        far = far.transpose(1, 2, 0, 3, 4).reshape(1, 2, SLOTS, rows, HEAD_SIZE)
    first, second = selected[0, 0], selected[0, 1]
    first_valid = first < my_block
    second_valid = jnp.logical_and(second < my_block, second != first)
    flags = jnp.stack([first_valid, second_valid]).astype(jnp.int32)
    return attention(flags, queries, all_key_states, all_value_states, far)


def solution(mesh):
    placed = P(("groups", "ctx"), None)
    return jax.shard_map(
        local, mesh=mesh, in_specs=(placed,) * 4, out_specs=placed, check_vma=False
    )
```

time: 137 us -> 81 us (0.59)
  the two profiles are of different devices: /device:TPU:5 before, /device:TPU:11 now
where the time goes in v1:
time: 81 us; the launch traced here: 80.6 us
  Pallas kernels  26.7 us (33%)
  blocking collectives  21.7 us (27%)
  waiting for transfers between devices  21.7 us (27%)
  starting transfers between devices  5.74 us (7%)
  between operations  2.52 us (3%)
  local copies, waits for them, and re-layouts  2.2 us (3%)
    pallas_call x1, Pallas kernels, attention(): pl.pallas_call(attention_kernel, out_shape=jax.ShapeDtypeStruct(queries.s...  22.9 us
    all_to_all x1, waiting for transfers between devices, local(): far = lax.all_to_all(chosen, 'ctx', split_axis=0, concat_axis=0, tiled=True)  21.7 us
    all_to_all x1, blocking collectives, local(): lax.all_to_all(packed, 'ctx', split_axis=0, concat_axis=0, tiled=True)  21.7 us
    all_to_all x1, starting transfers between devices, local(): far = lax.all_to_all(chosen, 'ctx', split_axis=0, concat_axis=0, tiled=True)  5.74 us
    pallas_call x1, Pallas kernels, pack(): pl.pallas_call(pack_kernel, out_shape=jax.ShapeDtypeStruct(shape, jnp.bfl...  1.95 us
    pallas_call x1, Pallas kernels, pick_pieces(): pl.pallas_call(pick_kernel, out_shape=jax.ShapeDtypeStruct((devices, 2, r...  1.8 us
  transfers between devices with their start and end apart: 1, of which 1 were waited for; matrix products, arithmetic and copies ran while one was open for 1% of the time, Pallas kernels for 0%

profile of v1, /device:TPU:11, one launch (start us, length us, event | category | flops | bytes accessed | tf_op | source)
XLA Modules:
  0.0 80.6 jit_solution(13277650391674770395)
XLA Ops:
  0.0 2.0 %pack.1 = bf16[16,144,128]{2,1,0:T(8,128)(2,1)} custom-call(s32[1,2]{1,0:T(1,128)} %selected_ref.1, bf16[256,512]{1,0:T(8,128)(2,1)} %key_ref.3, bf16[256,512]{1,0:T(8,128)(2,1)} %value_ref.3), custom_call_target="tpu_custom_call" | custom-call | tf_op jit(solution)/shard_map/pack/pallas_call | solution.py:39
  2.0 21.7 %all_to_all.10.held_ref = bf16[16,144,128]{2,1,0:T(8,128)(2,1)S(1)} all-to-all(bf16[16,144,128]{2,1,0:T(8,128)(2,1)} %pack.1), channel_id=1, replica_groups=mesh['groups'=2,'ctx'=16] {'ctx'}, dimensions={0} | all-to-all | bytes 1179648 | tf_op jit(solution)/shard_map/all_to_all | solution.py:187
  23.6 0.0 copy-start.3
  23.6 0.0 copy-start
  23.6 0.0 copy-start.1
  23.6 1.8 %pick_pieces.1 = bf16[16,2,128,128]{3,2,1,0:T(8,128)(2,1)} custom-call(s32[16,2]{1,0:T(8,128)S(1)} %bitcast.8, bf16[16,144,128]{2,1,0:T(8,128)(2,1)S(1)} %all_to_all.10.held_ref), custom_call_target="tpu_custom_call" | custom-call | tf_op jit(solution)/shard_map/pick_pieces/pallas_call | solution.py:70
  25.4 5.7 %all-to-all-start.1 = ((bf16[16,2,128,128]{3,2,1,0:T(8,128)(2,1)}), bf16[16,2,128,128]{3,2,1,0:T(8,128)(2,1)S(1)}, u32[]{:S(2)}, u32[]{:S(2)}) async-start(bf16[16,2,128,128]{3,2,1,0:T(8,128)(2,1)} %pick_pieces.1), calls=%async_computation.1 | async-start | bytes 2097152 | tf_op jit(solution)/shard_map/all_to_all | solution.py:191
  31.2 0.0 copy-done.3
  31.2 0.6 fusion.1
  34.3 0.1 add_convert_fusion.flags_ref
  34.4 21.7 %all-to-all-done.1 = bf16[16,2,128,128]{3,2,1,0:T(8,128)(2,1)S(1)} async-done(((bf16[16,2,128,128]{3,2,1,0:T(8,128)(2,1)}), bf16[16,2,128,128]{3,2,1,0:T(8,128)(2,1)S(1)}, u32[]{:S(2)}, u32[]{:S(2)}) %all-to-all-start.1) | async-done | bytes 1048608 | tf_op jit(solution)/shard_map/all_to_all | solution.py:191
  56.1 0.0 copy-done
  56.1 0.0 copy-done.1
  56.1 0.0 copy-start.2
  56.1 1.6 %copy-done.2 = bf16[256,4096]{1,0:T(8,128)(2,1)S(1)} copy-done((bf16[256,4096]{1,0:T(8,128)(2,1)S(1)}, bf16[256,4096]{1,0:T(8,128)(2,1)}, u32[]{:S(2)}) %copy-start.2) | copy-done | bytes 2097176
  57.7 22.9 %attention.1 = bf16[256,4096]{1,0:T(8,128)(2,1)} custom-call(s32[2]{0:T(128)S(1)} %add_convert_fusion.flags_ref, bf16[256,4096]{1,0:T(8,128)(2,1)S(1)} %copy-done.2, bf16[256,512]{1,0:T(8,128)(2,1)S(1)} %copy-done, bf16[256,512]{1,0:T(8,128)(2,1)S(1)} %copy-done.1, bf16[16,2,8,16,128]{4,3,2,1,0:T(8,128)(2,1)S(1)} %bitcast.6, ...), custom_call_target="tpu_custom_call" | custom-call | flops 3221225472 | bytes 6291456 | tf_op jit(solution)/shard_map/attention/pallas_call | solution.py:160
  (1 shorter events, 0.0 us)
Async XLA Ops:
  23.6 7.6 %copy-start.3 = (s32[1,2]{1,0:T(1,128)S(1)}, s32[1,2]{1,0:T(1,128)}, u32[]{:S(2)}) copy-start(s32[1,2]{1,0:T(1,128)} %selected_ref.1) | copy-start | bytes 28
  23.6 32.5 %copy-start = (bf16[256,512]{1,0:T(8,128)(2,1)S(1)}, bf16[256,512]{1,0:T(8,128)(2,1)}, u32[]{:S(2)}) copy-start(bf16[256,512]{1,0:T(8,128)(2,1)} %key_ref.3) | copy-start | bytes 786436
  23.6 32.5 %copy-start.1 = (bf16[256,512]{1,0:T(8,128)(2,1)S(1)}, bf16[256,512]{1,0:T(8,128)(2,1)}, u32[]{:S(2)}) copy-start(bf16[256,512]{1,0:T(8,128)(2,1)} %value_ref.3) | copy-start | bytes 786436
  25.4 30.6 %all-to-all-start.1 = ((bf16[16,2,128,128]{3,2,1,0:T(8,128)(2,1)}), bf16[16,2,128,128]{3,2,1,0:T(8,128)(2,1)S(1)}, u32[]{:S(2)}, u32[]{:S(2)}) async-start(bf16[16,2,128,128]{3,2,1,0:T(8,128)(2,1)} %pick_pieces.1), calls=%async_computation.1 | async-start | bytes 2097152 | tf_op jit(solution)/shard_map/all_to_all | solution.py:191
  56.1 1.6 %copy-start.2 = (bf16[256,4096]{1,0:T(8,128)(2,1)S(1)}, bf16[256,4096]{1,0:T(8,128)(2,1)}, u32[]{:S(2)}) copy-start(bf16[256,4096]{1,0:T(8,128)(2,1)} %query_ref.1) | copy-start | bytes 6291460

commit v2 on v1

--- a/solution.py
+++ b/solution.py
@@ -1,4 +1,3 @@
-import functools
 import math
 
 import jax
@@ -80,61 +79,62 @@
     )(wanted, held)
 
 
-NT = (((1,), (1,)), ((), ()))
-NN = (((1,), (0,)), ((), ()))
+HEADS_AT_ONCE = 2
 
 
 def attention_kernel(
     flags_ref, query_ref, key_ref, value_ref, far_key_ref, far_value_ref, out_ref
 ):
     rows = query_ref.shape[0]
-    half = rows // 2
     factor = math.log2(math.e) / math.sqrt(HEAD_SIZE)
-    row = lax.broadcasted_iota(jnp.int32, (half, half), 0)
-    column = lax.broadcasted_iota(jnp.int32, (half, half), 1)
+    row = lax.broadcasted_iota(jnp.int32, (rows, rows), 0)
+    column = lax.broadcasted_iota(jnp.int32, (rows, rows), 1)
     causal = column <= row
 
     def attend(picks):
-        own_key, own_value = key_ref[...], value_ref[...]
-        far = [
-            (
-                far_key_ref[:, pick, 0].reshape(rows, HEAD_SIZE),
-                far_value_ref[:, pick, 0].reshape(rows, HEAD_SIZE),
+        keys = [key_ref[...]] + [far_key_ref[:, p, 0].reshape(rows, HEAD_SIZE) for p in picks]
+        values = [value_ref[...]] + [far_value_ref[:, p, 0].reshape(rows, HEAD_SIZE) for p in picks]
+        keys_across = jnp.concatenate(keys, axis=0).T
+        value = jnp.concatenate(values, axis=0)
+        value = jnp.concatenate([value, jnp.ones_like(value)], axis=1)
+
+        def score(first):
+            query = jnp.concatenate(
+                [
+                    query_ref[:, h * HEAD_SIZE : (h + 1) * HEAD_SIZE]
+                    for h in range(first, first + HEADS_AT_ONCE)
+                ],
+                axis=0,
             )
-            for pick in picks
-        ]
-        for head in range(GROUP):
-            lanes = slice(head * HEAD_SIZE, (head + 1) * HEAD_SIZE)
-            for part in range(2):
-                query = query_ref[part * half : (part + 1) * half, lanes]
-                pieces = []
-                for block in range(part + 1):
-                    span = slice(block * half, (block + 1) * half)
-                    scores = lax.dot_general(
-                        query, own_key[span], NT, preferred_element_type=jnp.float32
-                    )
-                    if block == part:
-                        scores = jnp.where(causal, scores, -1e30)
-                    pieces.append((scores, own_value[span]))
-                for far_key, far_value in far:
-                    scores = lax.dot_general(
-                        query, far_key, NT, preferred_element_type=jnp.float32
-                    )
-                    pieces.append((scores, far_value))
-                row_max = functools.reduce(
-                    jnp.maximum, [jnp.max(s, axis=1, keepdims=True) for s, _ in pieces]
-                )
-                shift = row_max * factor
-                row_sum, mixture = 0.0, 0.0
-                for scores, value in pieces:
-                    weights = jnp.exp2(scores * factor - shift)
-                    row_sum = row_sum + jnp.sum(weights, axis=1, keepdims=True)
-                    mixture = mixture + lax.dot_general(
-                        weights.astype(jnp.bfloat16), value, NN, preferred_element_type=jnp.float32
-                    )
-                out_ref[part * half : (part + 1) * half, lanes] = (
-                    mixture / row_sum
-                ).astype(out_ref.dtype)
+            return jnp.dot(query, keys_across, preferred_element_type=jnp.float32)
+
+        def finish(first, scores):
+            weights = []
+            for h in range(HEADS_AT_ONCE):
+                part = scores[h * rows : (h + 1) * rows]
+                own = jnp.where(causal, part[:, :rows], -1e30)
+                part = jnp.concatenate([own, part[:, rows:]], axis=1) if picks else own
+                shift = jnp.max(part, axis=1, keepdims=True) * factor
+                weights.append(jnp.exp2(part * factor - shift).astype(jnp.bfloat16))
+            both = jnp.dot(
+                jnp.concatenate(weights, axis=0), value, preferred_element_type=jnp.float32
+            )
+            row_sum = both[:, HEAD_SIZE:]
+            inverse = pl.reciprocal(row_sum, approx=True)
+            inverse = inverse * (2.0 - row_sum * inverse)
+            mixture = (both[:, :HEAD_SIZE] * inverse).astype(out_ref.dtype)
+            for h in range(HEADS_AT_ONCE):
+                head = first + h
+                out_ref[:, head * HEAD_SIZE : (head + 1) * HEAD_SIZE] = mixture[
+                    h * rows : (h + 1) * rows
+                ]
+
+        scores = score(0)
+        for first in range(0, GROUP, HEADS_AT_ONCE):
+            later = first + HEADS_AT_ONCE
+            following = score(later) if later < GROUP else None
+            finish(first, scores)
+            scores = following
 
     first, second = flags_ref[0], flags_ref[1]
 
@@ -170,7 +170,7 @@
             pl.BlockSpec(far_shape, lambda g: (0, 0, g + KEY_VALUE_HEADS, 0, 0)),
         ],
         out_specs=pl.BlockSpec((rows, width), lambda g: (0, g)),
-        compiler_params=pltpu.CompilerParams(vmem_limit_bytes=40 * MIB),
+        compiler_params=pltpu.CompilerParams(vmem_limit_bytes=24 * MIB),
         cost_estimate=pl.CostEstimate(
             flops=4 * scores * HEAD_SIZE, bytes_accessed=6 * MIB, transcendentals=scores
         ),

time: 81 us -> 68.9 us (0.85)
  Pallas kernels: 26.7 us -> 14.6 us
    pallas_call x1, Pallas kernels: 22.9 us -> 10.8 us  [attention(): pl.pallas_call(attention_kernel, out_shape=jax.ShapeDtypeStruct(queries.s...]
where the time goes in v2:
time: 68.9 us; the launch traced here: 68.5 us
  blocking collectives  21.7 us (31%)
  waiting for transfers between devices  21.7 us (31%)
  Pallas kernels  14.6 us (21%)
  starting transfers between devices  5.74 us (8%)
  between operations  2.52 us (4%)
  local copies, waits for them, and re-layouts  2.2 us (3%)
    all_to_all x1, waiting for transfers between devices, local(): far = lax.all_to_all(chosen, 'ctx', split_axis=0, concat_axis=0, tiled=True)  21.7 us
    all_to_all x1, blocking collectives, local(): lax.all_to_all(packed, 'ctx', split_axis=0, concat_axis=0, tiled=True)  21.7 us
    pallas_call x1, Pallas kernels, attention(): pl.pallas_call(attention_kernel, out_shape=jax.ShapeDtypeStruct(queries.s...  10.8 us
    all_to_all x1, starting transfers between devices, local(): far = lax.all_to_all(chosen, 'ctx', split_axis=0, concat_axis=0, tiled=True)  5.74 us
    pallas_call x1, Pallas kernels, pack(): pl.pallas_call(pack_kernel, out_shape=jax.ShapeDtypeStruct(shape, jnp.bfl...  1.95 us
    pallas_call x1, Pallas kernels, pick_pieces(): pl.pallas_call(pick_kernel, out_shape=jax.ShapeDtypeStruct((devices, 2, r...  1.8 us
    unnamed x8, local copies, waits for them, and re-layouts  1.6 us
  transfers between devices with their start and end apart: 1, of which 1 were waited for; matrix products, arithmetic and copies ran while one was open for 1% of the time, Pallas kernels for 0%

profile of v2, /device:TPU:11, one launch (start us, length us, event | category | flops | bytes accessed | tf_op | source)
XLA Modules:
  0.0 68.5 jit_solution(5212233644835459293)
XLA Ops:
  0.0 2.0 %pack.1 = bf16[16,144,128]{2,1,0:T(8,128)(2,1)} custom-call(s32[1,2]{1,0:T(1,128)} %selected_ref.1, bf16[256,512]{1,0:T(8,128)(2,1)} %key_ref.3, bf16[256,512]{1,0:T(8,128)(2,1)} %value_ref.3), custom_call_target="tpu_custom_call" | custom-call | tf_op jit(solution)/shard_map/pack/pallas_call | solution.py:38
  2.0 21.7 %all_to_all.10.held_ref = bf16[16,144,128]{2,1,0:T(8,128)(2,1)S(1)} all-to-all(bf16[16,144,128]{2,1,0:T(8,128)(2,1)} %pack.1), channel_id=1, replica_groups=mesh['groups'=2,'ctx'=16] {'ctx'}, dimensions={0} | all-to-all | bytes 1179648 | tf_op jit(solution)/shard_map/all_to_all | solution.py:187
  23.6 0.0 copy-start.3
  23.6 0.0 copy-start
  23.6 0.0 copy-start.1
  23.6 1.8 %pick_pieces.1 = bf16[16,2,128,128]{3,2,1,0:T(8,128)(2,1)} custom-call(s32[16,2]{1,0:T(8,128)S(1)} %bitcast.8, bf16[16,144,128]{2,1,0:T(8,128)(2,1)S(1)} %all_to_all.10.held_ref), custom_call_target="tpu_custom_call" | custom-call | tf_op jit(solution)/shard_map/pick_pieces/pallas_call | solution.py:69
  25.4 5.7 %all-to-all-start.1 = ((bf16[16,2,128,128]{3,2,1,0:T(8,128)(2,1)}), bf16[16,2,128,128]{3,2,1,0:T(8,128)(2,1)S(1)}, u32[]{:S(2)}, u32[]{:S(2)}) async-start(bf16[16,2,128,128]{3,2,1,0:T(8,128)(2,1)} %pick_pieces.1), calls=%async_computation.1 | async-start | bytes 2097152 | tf_op jit(solution)/shard_map/all_to_all | solution.py:191
  31.2 0.0 copy-done.3
  31.2 0.6 fusion.1
  34.3 0.1 add_convert_fusion.flags_ref
  34.4 21.7 %all-to-all-done.1 = bf16[16,2,128,128]{3,2,1,0:T(8,128)(2,1)S(1)} async-done(((bf16[16,2,128,128]{3,2,1,0:T(8,128)(2,1)}), bf16[16,2,128,128]{3,2,1,0:T(8,128)(2,1)S(1)}, u32[]{:S(2)}, u32[]{:S(2)}) %all-to-all-start.1) | async-done | bytes 1048608 | tf_op jit(solution)/shard_map/all_to_all | solution.py:191
  56.1 0.0 copy-done
  56.1 0.0 copy-done.1
  56.1 0.0 copy-start.2
  56.1 1.6 %copy-done.2 = bf16[256,4096]{1,0:T(8,128)(2,1)S(1)} copy-done((bf16[256,4096]{1,0:T(8,128)(2,1)S(1)}, bf16[256,4096]{1,0:T(8,128)(2,1)}, u32[]{:S(2)}) %copy-start.2) | copy-done | bytes 2097176
  57.7 10.8 %attention.1 = bf16[256,4096]{1,0:T(8,128)(2,1)} custom-call(s32[2]{0:T(128)S(1)} %add_convert_fusion.flags_ref, bf16[256,4096]{1,0:T(8,128)(2,1)S(1)} %copy-done.2, bf16[256,512]{1,0:T(8,128)(2,1)S(1)} %copy-done, bf16[256,512]{1,0:T(8,128)(2,1)S(1)} %copy-done.1, bf16[16,2,8,16,128]{4,3,2,1,0:T(8,128)(2,1)S(1)} %bitcast.6, ...), custom_call_target="tpu_custom_call" | custom-call | flops 3221225472 | bytes 6291456 | tf_op jit(solution)/shard_map/attention/pallas_call | solution.py:160
  (1 shorter events, 0.0 us)
Async XLA Ops:
  23.6 7.6 %copy-start.3 = (s32[1,2]{1,0:T(1,128)S(1)}, s32[1,2]{1,0:T(1,128)}, u32[]{:S(2)}) copy-start(s32[1,2]{1,0:T(1,128)} %selected_ref.1) | copy-start | bytes 28
  23.6 32.5 %copy-start = (bf16[256,512]{1,0:T(8,128)(2,1)S(1)}, bf16[256,512]{1,0:T(8,128)(2,1)}, u32[]{:S(2)}) copy-start(bf16[256,512]{1,0:T(8,128)(2,1)} %key_ref.3) | copy-start | bytes 786436
  23.6 32.5 %copy-start.1 = (bf16[256,512]{1,0:T(8,128)(2,1)S(1)}, bf16[256,512]{1,0:T(8,128)(2,1)}, u32[]{:S(2)}) copy-start(bf16[256,512]{1,0:T(8,128)(2,1)} %value_ref.3) | copy-start | bytes 786436
  25.4 30.6 %all-to-all-start.1 = ((bf16[16,2,128,128]{3,2,1,0:T(8,128)(2,1)}), bf16[16,2,128,128]{3,2,1,0:T(8,128)(2,1)S(1)}, u32[]{:S(2)}, u32[]{:S(2)}) async-start(bf16[16,2,128,128]{3,2,1,0:T(8,128)(2,1)} %pick_pieces.1), calls=%async_computation.1 | async-start | bytes 2097152 | tf_op jit(solution)/shard_map/all_to_all | solution.py:191
  56.1 1.6 %copy-start.2 = (bf16[256,4096]{1,0:T(8,128)(2,1)S(1)}, bf16[256,4096]{1,0:T(8,128)(2,1)}, u32[]{:S(2)}) copy-start(bf16[256,4096]{1,0:T(8,128)(2,1)} %query_ref.1) | copy-start | bytes 6291460

commit v3 on v2

--- a/solution.py
+++ b/solution.py
@@ -55,45 +55,59 @@
     return jnp.concatenate([both, request], axis=1)
 
 
-def pick_kernel(wanted_ref, held_ref, out_ref):
-    rows = out_ref.shape[2]
-
-    @pl.loop(0, out_ref.shape[0])
-    def _(device):
+def partner(position, step):
+    return position ^ step
+
+
+def pick_kernel(place_ref, wanted_ref, held_ref, *out_refs):
+    rows = out_refs[0].shape[1]
+    for step, out_ref in enumerate(out_refs):
+        device = partner(place_ref[0], step)
         for pick in range(2):
-            out_ref[device, pick] = held_ref[wanted_ref[device, pick], :rows, :]
-
-
-def pick_pieces(wanted, held):
+            out_ref[pick] = held_ref[wanted_ref[device, pick], :rows, :]
+
+
+def pick_pieces(place, wanted, held):
     devices, rows = held.shape[0], held.shape[1] - REQUEST_ROWS
     return pl.pallas_call(
         pick_kernel,
-        out_shape=jax.ShapeDtypeStruct((devices, 2, rows, HEAD_SIZE), jnp.bfloat16),
+        out_shape=[jax.ShapeDtypeStruct((2, rows, HEAD_SIZE), jnp.bfloat16)] * devices,
         in_specs=[
+            pl.BlockSpec(memory_space=pltpu.SMEM),
             pl.BlockSpec(memory_space=pltpu.SMEM),
             pl.BlockSpec(memory_space=pltpu.VMEM),
         ],
-        out_specs=pl.BlockSpec(memory_space=pltpu.VMEM),
+        out_specs=[pl.BlockSpec(memory_space=pltpu.VMEM)] * devices,
         compiler_params=pltpu.CompilerParams(vmem_limit_bytes=16 * MIB),
         name="pick_pieces",
-    )(wanted, held)
+    )(place, wanted, held)
+
+
+def deliver(pieces):
+    devices = len(pieces)
+    moved = [None] * devices
+    moved[0] = pieces[0]
+    for step in reversed(range(1, devices)):
+        pairs = [(i, partner(i, step)) for i in range(devices)]
+        moved[step] = lax.ppermute(pieces[step], "ctx", pairs)
+    return moved
 
 
 HEADS_AT_ONCE = 2
 
 
-def attention_kernel(
-    flags_ref, query_ref, key_ref, value_ref, far_key_ref, far_value_ref, out_ref
-):
+def attention_kernel(flags_ref, query_ref, key_ref, value_ref, *refs):
     rows = query_ref.shape[0]
+    far_refs, out_ref = refs[:-1], refs[-1]
+    far_key_refs, far_value_refs = far_refs[: len(far_refs) // 2], far_refs[len(far_refs) // 2 :]
     factor = math.log2(math.e) / math.sqrt(HEAD_SIZE)
     row = lax.broadcasted_iota(jnp.int32, (rows, rows), 0)
     column = lax.broadcasted_iota(jnp.int32, (rows, rows), 1)
     causal = column <= row
 
     def attend(picks):
-        keys = [key_ref[...]] + [far_key_ref[:, p, 0].reshape(rows, HEAD_SIZE) for p in picks]
-        values = [value_ref[...]] + [far_value_ref[:, p, 0].reshape(rows, HEAD_SIZE) for p in picks]
+        keys = [key_ref[...]] + [ref[p, 0] for p in picks for ref in far_key_refs]
+        values = [value_ref[...]] + [ref[p, 0] for p in picks for ref in far_value_refs]
         keys_across = jnp.concatenate(keys, axis=0).T
         value = jnp.concatenate(values, axis=0)
         value = jnp.concatenate([value, jnp.ones_like(value)], axis=1)
@@ -153,9 +167,11 @@
 
 def attention(flags, queries, keys, values, far):
     rows = queries.shape[0]
-    holders, _, _, piece_rows, _ = far.shape
+    piece_rows = far[0].shape[2]
     width = GROUP * HEAD_SIZE
-    far_shape = (holders, 2, 1, piece_rows, HEAD_SIZE)
+    far_shape = (2, 1, piece_rows, HEAD_SIZE)
+    far_key = pl.BlockSpec(far_shape, lambda g: (0, g, 0, 0))
+    far_value = pl.BlockSpec(far_shape, lambda g: (0, g + KEY_VALUE_HEADS, 0, 0))
     scores = QUERY_HEADS * rows * 3 * rows
     return pl.pallas_call(
         attention_kernel,
@@ -166,8 +182,8 @@
             pl.BlockSpec((rows, width), lambda g: (0, g)),
             pl.BlockSpec((rows, HEAD_SIZE), lambda g: (0, g)),
             pl.BlockSpec((rows, HEAD_SIZE), lambda g: (0, g)),
-            pl.BlockSpec(far_shape, lambda g: (0, 0, g, 0, 0)),
-            pl.BlockSpec(far_shape, lambda g: (0, 0, g + KEY_VALUE_HEADS, 0, 0)),
+            *[far_key] * len(far),
+            *[far_value] * len(far),
         ],
         out_specs=pl.BlockSpec((rows, width), lambda g: (0, g)),
         compiler_params=pltpu.CompilerParams(vmem_limit_bytes=24 * MIB),
@@ -175,7 +191,7 @@
             flops=4 * scores * HEAD_SIZE, bytes_accessed=6 * MIB, transcendentals=scores
         ),
         name="attention",
-    )(flags, queries, keys, values, far, far)
+    )(flags, queries, keys, values, *far, *far)
 
 
 def local(queries, all_key_states, all_value_states, selected):
@@ -187,11 +203,11 @@
     held = lax.all_to_all(packed, "ctx", split_axis=0, concat_axis=0, tiled=True)
     wanted = held[:, SLOTS * piece_rows, :2].astype(jnp.int32)
     wanted = jnp.clip(wanted, 0, devices - 1)
-    chosen = pick_pieces(wanted, held)
-    far = lax.all_to_all(chosen, "ctx", split_axis=0, concat_axis=0, tiled=True)
-    far = far.reshape(devices, 2, SLOTS, piece_rows, HEAD_SIZE)
+    place = my_block.astype(jnp.int32)[None]
+    moved = deliver(pick_pieces(place, wanted, held))
+    far = [m.reshape(2, SLOTS, piece_rows, HEAD_SIZE) for m in moved]
     if piece_rows % 16 != 0:
-        far = far.transpose(1, 2, 0, 3, 4).reshape(1, 2, SLOTS, rows, HEAD_SIZE)
+        far = [jnp.concatenate(far, axis=2)]
     first, second = selected[0, 0], selected[0, 1]
     first_valid = first < my_block
     second_valid = jnp.logical_and(second < my_block, second != first)

time: 68.9 us -> 70.6 us (1.025)
  the two profiles are of different devices: /device:TPU:11 before, /device:TPU:9 now
where the time goes in v3:
time: 70.6 us; the launch traced here: 70.3 us
  waiting for transfers between devices  27.6 us (39%)
  starting transfers between devices  23.8 us (34%)
  Pallas kernels  15.2 us (22%)
  between operations  2.42 us (3%)
  local copies, waits for them, and re-layouts  1.18 us (2%)
    ppermute x15, starting transfers between devices, deliver(): moved[step] = lax.ppermute(pieces[step], 'ctx', pairs)  17.2 us
    all_to_all x1, waiting for transfers between devices, local(): lax.all_to_all(packed, 'ctx', split_axis=0, concat_axis=0, tiled=True)  15.5 us
    ppermute x15, waiting for transfers between devices, deliver(): moved[step] = lax.ppermute(pieces[step], 'ctx', pairs)  12.1 us
    pallas_call x1, Pallas kernels, attention(): pl.pallas_call(attention_kernel, out_shape=jax.ShapeDtypeStruct(queries.s...  11.7 us
    all_to_all x1, starting transfers between devices, local(): lax.all_to_all(packed, 'ctx', split_axis=0, concat_axis=0, tiled=True)  6.58 us
    pallas_call x1, Pallas kernels, pack(): pl.pallas_call(pack_kernel, out_shape=jax.ShapeDtypeStruct(shape, jnp.bfl...  2.1 us
    pallas_call x1, Pallas kernels, pick_pieces(): pl.pallas_call(pick_kernel, out_shape=[jax.ShapeDtypeStruct((2, rows, HEA...  1.42 us
  transfers between devices with their start and end apart: 16, of which 6 were waited for; matrix products, arithmetic and copies ran while one was open for 1% of the time, Pallas kernels for 0%

profile of v3, /device:TPU:9, one launch (start us, length us, event | category | flops | bytes accessed | tf_op | source)
XLA Modules:
  0.0 70.3 jit_solution(10033291738903419206)
XLA Ops:
  0.0 2.1 %pack.1 = bf16[16,144,128]{2,1,0:T(8,128)(2,1)} custom-call(s32[1,2]{1,0:T(1,128)} %selected_ref.1, bf16[256,512]{1,0:T(8,128)(2,1)} %key_ref.3, bf16[256,512]{1,0:T(8,128)(2,1)} %value_ref.3), custom_call_target="tpu_custom_call" | custom-call | tf_op jit(solution)/shard_map/pack/pallas_call | solution.py:38
  2.1 6.6 %all-to-all-start = ((bf16[16,144,128]{2,1,0:T(8,128)(2,1)}), bf16[16,144,128]{2,1,0:T(8,128)(2,1)S(1)}, u32[]{:S(2)}, u32[]{:S(2)}) async-start(bf16[16,144,128]{2,1,0:T(8,128)(2,1)} %pack.1), calls=%async_computation | async-start | bytes 1179648 | tf_op jit(solution)/shard_map/all_to_all | solution.py:203
  8.7 15.5 %all-to-all-done.held_ref = bf16[16,144,128]{2,1,0:T(8,128)(2,1)S(1)} async-done(((bf16[16,144,128]{2,1,0:T(8,128)(2,1)}), bf16[16,144,128]{2,1,0:T(8,128)(2,1)S(1)}, u32[]{:S(2)}, u32[]{:S(2)}) %all-to-all-start) | async-done | bytes 589856 | tf_op jit(solution)/shard_map/all_to_all | solution.py:203
  24.3 1.4 %pick_pieces.1 = (bf16[2,128,128]{2,1,0:T(8,128)(2,1)S(1)}, bf16[2,128,128]{2,1,0:T(8,128)(2,1)S(1)}, bf16[2,128,128]{2,1,0:T(8,128)(2,1)S(1)}, bf16[2,128,128]{...) custom-call(s32[1]{0:T(128)} %bitcast.4.place_ref, ...), custom_call_target="tpu_custom_call" | custom-call | tf_op jit(solution)/shard_map/pick_pieces/pallas_call | solution.py:72
  25.7 0.6 copy-done.3
  26.3 0.9 %collective-permute-start.1 = (bf16[2,128,128]{2,1,0:T(8,128)(2,1)S(1)}, bf16[2,128,128]{2,1,0:T(8,128)(2,1)S(1)}, u32[]{:S(2)}, u32[]{:S(2)}) collective-permute-start(bf16[2,128,128]{2,1,0:T(8,128)(2,1)S(1)} %get-tuple-element.23), channel_id=1, source_target_pairs={{0,2},{1,3},{2,0},{3,1},{4,6},{5,7},{6,4},{7,5},{8,10},{9,11},{10,... | collective-permute-start | bytes 196616 | tf_op jit(solution)/shard_map/ppermute | solution.py:92
  27.2 1.3 %collective-permute-start.2 = (bf16[2,128,128]{2,1,0:T(8,128)(2,1)S(1)}, bf16[2,128,128]{2,1,0:T(8,128)(2,1)S(1)}, u32[]{:S(2)}, u32[]{:S(2)}) collective-permute-start(bf16[2,128,128]{2,1,0:T(8,128)(2,1)S(1)} %get-tuple-element.24), channel_id=1, source_target_pairs={{0,3},{1,2},{2,1},{3,0},{4,7},{5,6},{6,5},{7,4},{8,11},{9,10},{10,... | collective-permute-start | bytes 196616 | tf_op jit(solution)/shard_map/ppermute | solution.py:92
  28.4 1.4 %collective-permute-start.4 = (bf16[2,128,128]{2,1,0:T(8,128)(2,1)S(1)}, bf16[2,128,128]{2,1,0:T(8,128)(2,1)S(1)}, u32[]{:S(2)}, u32[]{:S(2)}) collective-permute-start(bf16[2,128,128]{2,1,0:T(8,128)(2,1)S(1)} %get-tuple-element.26), channel_id=1, source_target_pairs={{0,5},{1,4},{2,7},{3,6},{4,1},{5,0},{6,3},{7,2},{8,13},{9,12},{10,... | collective-permute-start | bytes 196616 | tf_op jit(solution)/shard_map/ppermute | solution.py:92
  30.3 2.5 %collective-permute-start.6 = (bf16[2,128,128]{2,1,0:T(8,128)(2,1)}, bf16[2,128,128]{2,1,0:T(8,128)(2,1)S(1)}, u32[]{:S(2)}, u32[]{:S(2)}) collective-permute-start(bf16[2,128,128]{2,1,0:T(8,128)(2,1)} %get-tuple-element.28), channel_id=1, source_target_pairs={{0,7},{1,6},{2,5},{3,4},{4,3},{5,2},{6,1},{7,0},{8,15},{9,14},{10,... | collective-permute-start | bytes 196616 | tf_op jit(solution)/shard_map/ppermute | solution.py:92
  32.8 0.6 collective-permute-start.7
  33.5 1.6 %collective-permute-start.8 = (bf16[2,128,128]{2,1,0:T(8,128)(2,1)}, bf16[2,128,128]{2,1,0:T(8,128)(2,1)S(1)}, u32[]{:S(2)}, u32[]{:S(2)}) collective-permute-start(bf16[2,128,128]{2,1,0:T(8,128)(2,1)} %get-tuple-element.30), channel_id=1, source_target_pairs={{0,9},{1,8},{2,11},{3,10},{4,13},{5,12},{6,15},{7,14},{8,1},{9,0},... | collective-permute-start | bytes 196616 | tf_op jit(solution)/shard_map/ppermute | solution.py:92
  35.1 1.8 %collective-permute-start.9 = (bf16[2,128,128]{2,1,0:T(8,128)(2,1)}, bf16[2,128,128]{2,1,0:T(8,128)(2,1)}, u32[]{:S(2)}, u32[]{:S(2)}) collective-permute-start(bf16[2,128,128]{2,1,0:T(8,128)(2,1)} %get-tuple-element.31), channel_id=1, source_target_pairs={{0,10},{1,11},{2,8},{3,9},{4,14},{5,15},{6,12},{7,13},{8,2},{9,3},... | collective-permute-start | bytes 196616 | tf_op jit(solution)/shard_map/ppermute | solution.py:92
  36.9 0.6 fusion.1
  39.8 2.2 %collective-permute-start.10 = (bf16[2,128,128]{2,1,0:T(8,128)(2,1)}, bf16[2,128,128]{2,1,0:T(8,128)(2,1)S(1)}, u32[]{:S(2)}, u32[]{:S(2)}) collective-permute-start(bf16[2,128,128]{2,1,0:T(8,128)(2,1)} %copy-done.3), channel_id=1, source_target_pairs={{0,11},{1,10},{2,9},{3,8},{4,15},{5,14},{6,13},{7,12},{8,3},{9,2},... | collective-permute-start | bytes 196616 | tf_op jit(solution)/shard_map/ppermute | solution.py:92
  42.1 0.8 %collective-permute-start.11 = (bf16[2,128,128]{2,1,0:T(8,128)(2,1)S(1)}, bf16[2,128,128]{2,1,0:T(8,128)(2,1)S(1)}, u32[]{:S(2)}, u32[]{:S(2)}) collective-permute-start(bf16[2,128,128]{2,1,0:T(8,128)(2,1)S(1)} %get-tuple-element.33), channel_id=1, source_target_pairs={{0,12},{1,13},{2,14},{3,15},{4,8},{5,9},{6,10},{7,11},{8,4},{9,5},... | collective-permute-start | bytes 196616 | tf_op jit(solution)/shard_map/ppermute | solution.py:92
  42.9 0.5 collective-permute-start.12
  43.4 1.1 %collective-permute-start.13 = (bf16[2,128,128]{2,1,0:T(8,128)(2,1)S(1)}, bf16[2,128,128]{2,1,0:T(8,128)(2,1)S(1)}, u32[]{:S(2)}, u32[]{:S(2)}) collective-permute-start(bf16[2,128,128]{2,1,0:T(8,128)(2,1)S(1)} %get-tuple-element.35), channel_id=1, source_target_pairs={{0,14},{1,15},{2,12},{3,13},{4,10},{5,11},{6,8},{7,9},{8,6},{9,7},... | collective-permute-start | bytes 196616 | tf_op jit(solution)/shard_map/ppermute | solution.py:92
  44.5 2.0 %collective-permute-start.14 = (bf16[2,128,128]{2,1,0:T(8,128)(2,1)S(1)}, bf16[2,128,128]{2,1,0:T(8,128)(2,1)S(1)}, u32[]{:S(2)}, u32[]{:S(2)}) collective-permute-start(bf16[2,128,128]{2,1,0:T(8,128)(2,1)S(1)} %get-tuple-element.36), channel_id=1, source_target_pairs={{0,15},{1,14},{2,13},{3,12},{4,11},{5,10},{6,9},{7,8},{8,7},{9,6},... | collective-permute-start | bytes 196616 | tf_op jit(solution)/shard_map/ppermute | solution.py:92
  46.5 2.0 %collective-permute-done.10 = bf16[2,128,128]{2,1,0:T(8,128)(2,1)S(1)} collective-permute-done((bf16[2,128,128]{2,1,0:T(8,128)(2,1)}, bf16[2,128,128]{2,1,0:T(8,128)(2,1)S(1)}, u32[]{:S(2)}, u32[]{:S(2)}) %collective-permute-start.10) | collective-permute-done | bytes 65568 | tf_op jit(solution)/shard_map/ppermute | solution.py:92
  48.5 4.2 %collective-permute-done.11 = bf16[2,128,128]{2,1,0:T(8,128)(2,1)S(1)} collective-permute-done((bf16[2,128,128]{2,1,0:T(8,128)(2,1)S(1)}, bf16[2,128,128]{2,1,0:T(8,128)(2,1)S(1)}, u32[]{:S(2)}, u32[]{:S(2)}) %collective-permute-start.11) | collective-permute-done | bytes 65568 | tf_op jit(solution)/shard_map/ppermute | solution.py:92
  52.7 2.8 %collective-permute-done.12 = bf16[2,128,128]{2,1,0:T(8,128)(2,1)S(1)} collective-permute-done((bf16[2,128,128]{2,1,0:T(8,128)(2,1)S(1)}, bf16[2,128,128]{2,1,0:T(8,128)(2,1)S(1)}, u32[]{:S(2)}, u32[]{:S(2)}) %collective-permute-start.12) | collective-permute-done | bytes 65568 | tf_op jit(solution)/shard_map/ppermute | solution.py:92
  55.5 1.7 %collective-permute-done.13 = bf16[2,128,128]{2,1,0:T(8,128)(2,1)S(1)} collective-permute-done((bf16[2,128,128]{2,1,0:T(8,128)(2,1)S(1)}, bf16[2,128,128]{2,1,0:T(8,128)(2,1)S(1)}, u32[]{:S(2)}, u32[]{:S(2)}) %collective-permute-start.13) | collective-permute-done | bytes 65568 | tf_op jit(solution)/shard_map/ppermute | solution.py:92
  57.2 1.4 %collective-permute-done.14 = bf16[2,128,128]{2,1,0:T(8,128)(2,1)S(1)} collective-permute-done((bf16[2,128,128]{2,1,0:T(8,128)(2,1)S(1)}, bf16[2,128,128]{2,1,0:T(8,128)(2,1)S(1)}, u32[]{:S(2)}, u32[]{:S(2)}) %collective-permute-start.14) | collective-permute-done | bytes 65568 | tf_op jit(solution)/shard_map/ppermute | solution.py:92
  58.6 11.7 %attention.1 = bf16[256,4096]{1,0:T(8,128)(2,1)} custom-call(s32[2]{0:T(128)S(1)} %add_convert_fusion.flags_ref, bf16[256,4096]{1,0:T(8,128)(2,1)S(1)} %copy-done.2, bf16[256,512]{1,0:T(8,128)(2,1)S(1)} %copy-done, bf16[256,512]{1,0:T(8,128)(2,1)S(1)} %copy-done.1, bf16[2,8,16,128]{3,2,1,0:T(8,128)(2,1)S(1)} %bitcast.23, ...), custom_call_target="tpu_custom_call" | custom-call | flops 3221225472 | bytes 6291456 | tf_op jit(solution)/shard_map/attention/pallas_call | solution.py:176
  (24 shorter events, 0.7 us)
Async XLA Ops:
  0.0 36.9 %copy-start.4 = (s32[1,2]{1,0:T(1,128)S(1)}, s32[1,2]{1,0:T(1,128)}, u32[]{:S(2)}) copy-start(s32[1,2]{1,0:T(1,128)} %selected_ref.1) | copy-start | bytes 28
  0.0 58.6 %copy-start.1 = (bf16[256,512]{1,0:T(8,128)(2,1)S(1)}, bf16[256,512]{1,0:T(8,128)(2,1)}, u32[]{:S(2)}) copy-start(bf16[256,512]{1,0:T(8,128)(2,1)} %value_ref.3) | copy-start | bytes 786436
  0.0 58.6 %copy-start = (bf16[256,512]{1,0:T(8,128)(2,1)S(1)}, bf16[256,512]{1,0:T(8,128)(2,1)}, u32[]{:S(2)}) copy-start(bf16[256,512]{1,0:T(8,128)(2,1)} %key_ref.3) | copy-start | bytes 786436
  0.0 58.6 %copy-start.2 = (bf16[256,4096]{1,0:T(8,128)(2,1)S(1)}, bf16[256,4096]{1,0:T(8,128)(2,1)}, u32[]{:S(2)}) copy-start(bf16[256,4096]{1,0:T(8,128)(2,1)} %query_ref.1) | copy-start | bytes 6291460
  2.1 22.1 %all-to-all-start = ((bf16[16,144,128]{2,1,0:T(8,128)(2,1)}), bf16[16,144,128]{2,1,0:T(8,128)(2,1)S(1)}, u32[]{:S(2)}, u32[]{:S(2)}) async-start(bf16[16,144,128]{2,1,0:T(8,128)(2,1)} %pack.1), calls=%async_computation | async-start | bytes 1179648 | tf_op jit(solution)/shard_map/all_to_all | solution.py:203
  25.7 0.6 copy-start.3
  26.3 3.5 %collective-permute-start = (bf16[2,128,128]{2,1,0:T(8,128)(2,1)S(1)}, bf16[2,128,128]{2,1,0:T(8,128)(2,1)S(1)}, u32[]{:S(2)}, u32[]{:S(2)}) collective-permute-start(bf16[2,128,128]{2,1,0:T(8,128)(2,1)S(1)} %get-tuple-element.22), channel_id=1, source_target_pairs={{0,1},{1,0},{2,3},{3,2},{4,5},{5,4},{6,7},{7,6},{8,9},{9,8},{10,11... | collective-permute-start | bytes 196616 | tf_op jit(solution)/shard_map/ppermute | solution.py:92
  26.3 4.0 %collective-permute-start.1 = (bf16[2,128,128]{2,1,0:T(8,128)(2,1)S(1)}, bf16[2,128,128]{2,1,0:T(8,128)(2,1)S(1)}, u32[]{:S(2)}, u32[]{:S(2)}) collective-permute-start(bf16[2,128,128]{2,1,0:T(8,128)(2,1)S(1)} %get-tuple-element.23), channel_id=1, source_target_pairs={{0,2},{1,3},{2,0},{3,1},{4,6},{5,7},{6,4},{7,5},{8,10},{9,11},{10,... | collective-permute-start | bytes 196616 | tf_op jit(solution)/shard_map/ppermute | solution.py:92
  27.2 5.7 %collective-permute-start.2 = (bf16[2,128,128]{2,1,0:T(8,128)(2,1)S(1)}, bf16[2,128,128]{2,1,0:T(8,128)(2,1)S(1)}, u32[]{:S(2)}, u32[]{:S(2)}) collective-permute-start(bf16[2,128,128]{2,1,0:T(8,128)(2,1)S(1)} %get-tuple-element.24), channel_id=1, source_target_pairs={{0,3},{1,2},{2,1},{3,0},{4,7},{5,6},{6,5},{7,4},{8,11},{9,10},{10,... | collective-permute-start | bytes 196616 | tf_op jit(solution)/shard_map/ppermute | solution.py:92
  28.4 5.0 %collective-permute-start.3 = (bf16[2,128,128]{2,1,0:T(8,128)(2,1)S(1)}, bf16[2,128,128]{2,1,0:T(8,128)(2,1)S(1)}, u32[]{:S(2)}, u32[]{:S(2)}) collective-permute-start(bf16[2,128,128]{2,1,0:T(8,128)(2,1)S(1)} %get-tuple-element.25), channel_id=1, source_target_pairs={{0,4},{1,5},{2,6},{3,7},{4,0},{5,1},{6,2},{7,3},{8,12},{9,13},{10,... | collective-permute-start | bytes 196616 | tf_op jit(solution)/shard_map/ppermute | solution.py:92
  28.4 6.7 %collective-permute-start.4 = (bf16[2,128,128]{2,1,0:T(8,128)(2,1)S(1)}, bf16[2,128,128]{2,1,0:T(8,128)(2,1)S(1)}, u32[]{:S(2)}, u32[]{:S(2)}) collective-permute-start(bf16[2,128,128]{2,1,0:T(8,128)(2,1)S(1)} %get-tuple-element.26), channel_id=1, source_target_pairs={{0,5},{1,4},{2,7},{3,6},{4,1},{5,0},{6,3},{7,2},{8,13},{9,12},{10,... | collective-permute-start | bytes 196616 | tf_op jit(solution)/shard_map/ppermute | solution.py:92
  29.8 10.0 %collective-permute-start.5 = (bf16[2,128,128]{2,1,0:T(8,128)(2,1)}, bf16[2,128,128]{2,1,0:T(8,128)(2,1)S(1)}, u32[]{:S(2)}, u32[]{:S(2)}) collective-permute-start(bf16[2,128,128]{2,1,0:T(8,128)(2,1)} %get-tuple-element.27), channel_id=1, source_target_pairs={{0,6},{1,7},{2,4},{3,5},{4,2},{5,3},{6,0},{7,1},{8,14},{9,15},{10,... | collective-permute-start | bytes 196616 | tf_op jit(solution)/shard_map/ppermute | solution.py:92
  30.3 11.7 %collective-permute-start.6 = (bf16[2,128,128]{2,1,0:T(8,128)(2,1)}, bf16[2,128,128]{2,1,0:T(8,128)(2,1)S(1)}, u32[]{:S(2)}, u32[]{:S(2)}) collective-permute-start(bf16[2,128,128]{2,1,0:T(8,128)(2,1)} %get-tuple-element.28), channel_id=1, source_target_pairs={{0,7},{1,6},{2,5},{3,4},{4,3},{5,2},{6,1},{7,0},{8,15},{9,14},{10,... | collective-permute-start | bytes 196616 | tf_op jit(solution)/shard_map/ppermute | solution.py:92
  32.8 10.0 %collective-permute-start.7 = (bf16[2,128,128]{2,1,0:T(8,128)(2,1)}, bf16[2,128,128]{2,1,0:T(8,128)(2,1)S(1)}, u32[]{:S(2)}, u32[]{:S(2)}) collective-permute-start(bf16[2,128,128]{2,1,0:T(8,128)(2,1)} %get-tuple-element.29), channel_id=1, source_target_pairs={{0,8},{1,9},{2,10},{3,11},{4,12},{5,13},{6,14},{7,15},{8,0},{9,1},... | collective-permute-start | bytes 196616 | tf_op jit(solution)/shard_map/ppermute | solution.py:92
  33.5 9.9 %collective-permute-start.8 = (bf16[2,128,128]{2,1,0:T(8,128)(2,1)}, bf16[2,128,128]{2,1,0:T(8,128)(2,1)S(1)}, u32[]{:S(2)}, u32[]{:S(2)}) collective-permute-start(bf16[2,128,128]{2,1,0:T(8,128)(2,1)} %get-tuple-element.30), channel_id=1, source_target_pairs={{0,9},{1,8},{2,11},{3,10},{4,13},{5,12},{6,15},{7,14},{8,1},{9,0},... | collective-permute-start | bytes 196616 | tf_op jit(solution)/shard_map/ppermute | solution.py:92
  35.1 9.4 %collective-permute-start.9 = (bf16[2,128,128]{2,1,0:T(8,128)(2,1)}, bf16[2,128,128]{2,1,0:T(8,128)(2,1)}, u32[]{:S(2)}, u32[]{:S(2)}) collective-permute-start(bf16[2,128,128]{2,1,0:T(8,128)(2,1)} %get-tuple-element.31), channel_id=1, source_target_pairs={{0,10},{1,11},{2,8},{3,9},{4,14},{5,15},{6,12},{7,13},{8,2},{9,3},... | collective-permute-start | bytes 196616 | tf_op jit(solution)/shard_map/ppermute | solution.py:92
  39.8 8.7 %collective-permute-start.10 = (bf16[2,128,128]{2,1,0:T(8,128)(2,1)}, bf16[2,128,128]{2,1,0:T(8,128)(2,1)S(1)}, u32[]{:S(2)}, u32[]{:S(2)}) collective-permute-start(bf16[2,128,128]{2,1,0:T(8,128)(2,1)} %copy-done.3), channel_id=1, source_target_pairs={{0,11},{1,10},{2,9},{3,8},{4,15},{5,14},{6,13},{7,12},{8,3},{9,2},... | collective-permute-start | bytes 196616 | tf_op jit(solution)/shard_map/ppermute | solution.py:92
  42.1 10.7 %collective-permute-start.11 = (bf16[2,128,128]{2,1,0:T(8,128)(2,1)S(1)}, bf16[2,128,128]{2,1,0:T(8,128)(2,1)S(1)}, u32[]{:S(2)}, u32[]{:S(2)}) collective-permute-start(bf16[2,128,128]{2,1,0:T(8,128)(2,1)S(1)} %get-tuple-element.33), channel_id=1, source_target_pairs={{0,12},{1,13},{2,14},{3,15},{4,8},{5,9},{6,10},{7,11},{8,4},{9,5},... | collective-permute-start | bytes 196616 | tf_op jit(solution)/shard_map/ppermute | solution.py:92
  42.9 12.7 %collective-permute-start.12 = (bf16[2,128,128]{2,1,0:T(8,128)(2,1)S(1)}, bf16[2,128,128]{2,1,0:T(8,128)(2,1)S(1)}, u32[]{:S(2)}, u32[]{:S(2)}) collective-permute-start(bf16[2,128,128]{2,1,0:T(8,128)(2,1)S(1)} %get-tuple-element.34), channel_id=1, source_target_pairs={{0,13},{1,12},{2,15},{3,14},{4,9},{5,8},{6,11},{7,10},{8,5},{9,4},... | collective-permute-start | bytes 196616 | tf_op jit(solution)/shard_map/ppermute | solution.py:92
  43.4 13.8 %collective-permute-start.13 = (bf16[2,128,128]{2,1,0:T(8,128)(2,1)S(1)}, bf16[2,128,128]{2,1,0:T(8,128)(2,1)S(1)}, u32[]{:S(2)}, u32[]{:S(2)}) collective-permute-start(bf16[2,128,128]{2,1,0:T(8,128)(2,1)S(1)} %get-tuple-element.35), channel_id=1, source_target_pairs={{0,14},{1,15},{2,12},{3,13},{4,10},{5,11},{6,8},{7,9},{8,6},{9,7},... | collective-permute-start | bytes 196616 | tf_op jit(solution)/shard_map/ppermute | solution.py:92
  44.5 14.1 %collective-permute-start.14 = (bf16[2,128,128]{2,1,0:T(8,128)(2,1)S(1)}, bf16[2,128,128]{2,1,0:T(8,128)(2,1)S(1)}, u32[]{:S(2)}, u32[]{:S(2)}) collective-permute-start(bf16[2,128,128]{2,1,0:T(8,128)(2,1)S(1)} %get-tuple-element.36), channel_id=1, source_target_pairs={{0,15},{1,14},{2,13},{3,12},{4,11},{5,10},{6,9},{7,8},{8,7},{9,6},... | collective-permute-start | bytes 196616 | tf_op jit(solution)/shard_map/ppermute | solution.py:92

commit v4 on v2

v4 whole, which is shorter than its diff:
```python
import math

import jax
import jax.numpy as jnp
from jax import lax
from jax.experimental import pallas as pl
from jax.experimental.pallas import tpu as pltpu
from jax.sharding import PartitionSpec as P

QUERY_HEADS = 32
KEY_VALUE_HEADS = 4
HEAD_SIZE = 128
GROUP = QUERY_HEADS // KEY_VALUE_HEADS
SLOTS = 2 * KEY_VALUE_HEADS
REQUEST_ROWS = 16
MIB = 1024 * 1024


def pack_kernel(selected_ref, key_ref, value_ref, out_ref):
    devices, piece_rows = out_ref.shape[0], key_ref.shape[0] // out_ref.shape[0]
    for slot in range(SLOTS):
        ref = key_ref if slot < KEY_VALUE_HEADS else value_ref
        head = slot % KEY_VALUE_HEADS
        part = ref[:, head * HEAD_SIZE : (head + 1) * HEAD_SIZE]
        out_ref[:, slot * piece_rows : (slot + 1) * piece_rows, :] = part.reshape(
            devices, piece_rows, HEAD_SIZE
        )
    lane = lax.broadcasted_iota(jnp.int32, (devices, REQUEST_ROWS, HEAD_SIZE), 2)
    request = jnp.where(lane == 0, selected_ref[0, 0], selected_ref[0, 1])
    out_ref[:, SLOTS * piece_rows :, :] = request.astype(jnp.float32).astype(jnp.bfloat16)


def pack(keys, values, selected, devices):
    rows = keys.shape[0]
    piece_rows = rows // devices
    shape = (devices, SLOTS * piece_rows + REQUEST_ROWS, HEAD_SIZE)
    if piece_rows % 16 == 0:
        return pl.pallas_call(
            pack_kernel,
            out_shape=pltpu.VMEM(shape, jnp.bfloat16),
            in_specs=[
                pl.BlockSpec(memory_space=pltpu.SMEM),
                pl.BlockSpec(memory_space=pltpu.VMEM),
                pl.BlockSpec(memory_space=pltpu.VMEM),
            ],
            out_specs=pl.BlockSpec(memory_space=pltpu.VMEM),
            name="pack",
        )(selected, keys, values)
    both = jnp.concatenate([keys, values], axis=1)
    both = both.reshape(devices, piece_rows, SLOTS, HEAD_SIZE).transpose(0, 2, 1, 3)
    both = both.reshape(devices, SLOTS * piece_rows, HEAD_SIZE)
    lane = jnp.arange(HEAD_SIZE) == 0
    request = jnp.where(lane, selected[0, 0], selected[0, 1]).astype(jnp.bfloat16)
    request = jnp.broadcast_to(request, (devices, REQUEST_ROWS, HEAD_SIZE))
    return jnp.concatenate([both, request], axis=1)


def pick_kernel(wanted_ref, held_ref, out_ref):
    rows = out_ref.shape[2]

    @pl.loop(0, out_ref.shape[0])
    def _(device):
        for pick in range(2):
            out_ref[device, pick] = held_ref[wanted_ref[device, pick], :rows, :]


def pick_pieces(wanted, held):
    devices, rows = held.shape[0], held.shape[1] - REQUEST_ROWS
    return pl.pallas_call(
        pick_kernel,
        out_shape=pltpu.VMEM((devices, 2, rows, HEAD_SIZE), jnp.bfloat16),
        in_specs=[
            pl.BlockSpec(memory_space=pltpu.SMEM),
            pl.BlockSpec(memory_space=pltpu.VMEM),
        ],
        out_specs=pl.BlockSpec(memory_space=pltpu.VMEM),
        compiler_params=pltpu.CompilerParams(vmem_limit_bytes=16 * MIB),
        name="pick_pieces",
    )(wanted, held)


FACTOR = math.log2(math.e) / math.sqrt(HEAD_SIZE)
PAIR = 2
LARGE_SUM = 2.0**100


def head_lanes(head):
    return slice(head * HEAD_SIZE, (head + 1) * HEAD_SIZE)


def with_ones(value):
    return jnp.concatenate([value, jnp.ones_like(value)], axis=1)


def inverse_of(positive):
    return pl.reciprocal(positive, approx=True)


def dot(a, b):
    return jnp.dot(a, b, preferred_element_type=jnp.float32)


def stack_heads(wide):
    heads = wide.shape[1] // HEAD_SIZE
    return jnp.concatenate([wide[:, head_lanes(h)] for h in range(heads)], axis=0)


def own_kernel(query_ref, key_ref, value_ref, out_ref, level_ref):
    rows = query_ref.shape[0]
    row = lax.broadcasted_iota(jnp.int32, (rows, rows), 0)
    column = lax.broadcasted_iota(jnp.int32, (rows, rows), 1)
    causal = column <= row
    keys_across = key_ref[...].T
    value = with_ones(value_ref[...])

    def score(first):
        lanes = slice(first * HEAD_SIZE, (first + PAIR) * HEAD_SIZE)
        return dot(stack_heads(query_ref[:, lanes]), keys_across)

    def finish(first, scores):
        weights, shifts = [], []
        for h in range(PAIR):
            part = jnp.where(causal, scores[h * rows : (h + 1) * rows], -1e30)
            shift = jnp.max(part, axis=1, keepdims=True) * FACTOR
            shifts.append(shift)
            weights.append(jnp.exp2(part * FACTOR - shift).astype(jnp.bfloat16))
        both = dot(jnp.concatenate(weights, axis=0), value)
        for h in range(PAIR):
            part = both[h * rows : (h + 1) * rows]
            row_sum = part[:, HEAD_SIZE:]
            out_ref[:, head_lanes(first + h)] = part[:, :HEAD_SIZE] / row_sum
            level_ref[:, head_lanes(first + h)] = shifts[h] + jnp.log2(row_sum)

    scores = score(0)
    for first in range(0, GROUP, PAIR):
        following = score(first + PAIR) if first + PAIR < GROUP else None
        finish(first, scores)
        scores = following


def own_attention(queries, keys, values):
    rows = queries.shape[0]
    width = GROUP * HEAD_SIZE
    scores = QUERY_HEADS * rows * rows
    return pl.pallas_call(
        own_kernel,
        out_shape=[pltpu.VMEM(queries.shape, jnp.float32)] * 2,
        grid=(KEY_VALUE_HEADS,),
        in_specs=[
            pl.BlockSpec((rows, width), lambda g: (0, g)),
            pl.BlockSpec((rows, HEAD_SIZE), lambda g: (0, g)),
            pl.BlockSpec((rows, HEAD_SIZE), lambda g: (0, g)),
        ],
        out_specs=[pl.BlockSpec((rows, width), lambda g: (0, g))] * 2,
        compiler_params=pltpu.CompilerParams(vmem_limit_bytes=16 * MIB),
        cost_estimate=pl.CostEstimate(
            flops=4 * scores * HEAD_SIZE, bytes_accessed=11 * MIB, transcendentals=scores
        ),
        name="own_attention",
    )(queries, keys, values)


def far_kernel(
    selected_ref,
    query_ref,
    far_ref,
    own_ref,
    level_ref,
    out_ref,
    keys_ref,
    values_ref,
    scores_ref,
    other_scores_ref,
    staged,
    sems,
):
    rows = query_ref.shape[0]
    pair_width = PAIR * HEAD_SIZE
    step_width = 2 * pair_width
    steps = query_ref.shape[1] // step_width
    steps_of_group = steps // KEY_VALUE_HEADS

    def lanes(index, size):
        return pl.ds(pl.multiple_of(index * size, size), size)

    def send(step):
        out = out_ref.at[:, lanes(step, step_width)]
        return pltpu.make_async_copy(staged.at[step], out, sems.at[step])

    def finish_own(step):
        staged[step] = own_ref[:, lanes(step, step_width)].astype(staged.dtype)

    def attend(picks):
        count = len(picks) * rows

        def block(slot):
            blocks = [far_ref[:, p, slot].reshape(rows, HEAD_SIZE) for p in picks]
            return jnp.concatenate(blocks, axis=0)

        @pl.loop(0, KEY_VALUE_HEADS)
        def _(group):
            keys_ref[group, :, :count] = block(group).T
            values_ref[group, :count] = with_ones(block(group + KEY_VALUE_HEADS))

        def score(pair, group, buffer):
            query = stack_heads(query_ref[:, lanes(pair, pair_width)])
            buffer[:, :count] = dot(query, keys_ref[group, :, :count])

        def repeat(narrow):
            return jnp.concatenate([narrow] * (count // HEAD_SIZE), axis=1)

        def quick(pair, group, buffer, step, half, largest):
            level = level_ref[:, lanes(pair, pair_width)]
            own = own_ref[:, lanes(pair, pair_width)]
            weights = [
                jnp.exp2(
                    buffer[h * rows : (h + 1) * rows, :count] * FACTOR
                    - repeat(level[:, head_lanes(h)])
                ).astype(jnp.bfloat16)
                for h in range(PAIR)
            ]
            both = dot(jnp.concatenate(weights, axis=0), values_ref[group, :count])
            for h in range(PAIR):
                part = both[h * rows : (h + 1) * rows]
                row_sum = 1.0 + part[:, HEAD_SIZE:]
                largest = jnp.maximum(
                    largest, jnp.max(row_sum.reshape(rows // 8, 8, HEAD_SIZE), axis=0)
                )
                mixture = own[:, head_lanes(h)] + part[:, :HEAD_SIZE]
                staged[step, :, head_lanes(half * PAIR + h)] = (
                    mixture * inverse_of(row_sum)
                ).astype(staged.dtype)
            return largest

        def careful(pair, group, buffer, step, half):
            score(pair, group, buffer)
            level = level_ref[:, lanes(pair, pair_width)]
            own = own_ref[:, lanes(pair, pair_width)]
            for h in range(PAIR):
                part = buffer[h * rows : (h + 1) * rows, :count] * FACTOR
                mine = level[:, head_lanes(h)]
                shift = jnp.maximum(jnp.max(part, axis=1, keepdims=True), mine)
                weights = jnp.exp2(part - repeat(shift)).astype(jnp.bfloat16)
                both = dot(weights, values_ref[group, :count])
                share = jnp.exp2(mine - shift)
                mixture = own[:, head_lanes(h)] * share + both[:, :HEAD_SIZE]
                staged[step, :, head_lanes(half * PAIR + h)] = (
                    mixture * inverse_of(share + both[:, HEAD_SIZE:])
                ).astype(staged.dtype)

        def body(step, largest):
            group = step // steps_of_group
            following = jnp.minimum(step + 1, steps - 1)
            score(2 * step + 1, group, other_scores_ref)
            largest = quick(2 * step, group, scores_ref, step, 0, largest)
            score(2 * following, following // steps_of_group, scores_ref)
            largest = quick(2 * step + 1, group, other_scores_ref, step, 1, largest)
            send(step).start()
            return largest

        score(0, 0, scores_ref)
        largest = lax.fori_loop(0, steps, body, jnp.zeros((8, HEAD_SIZE), jnp.float32))

        @pl.when(jnp.max(largest) > LARGE_SUM)
        def _():
            @pl.loop(0, steps)
            def _(step):
                send(step).wait()
                for half in range(2):
                    careful(2 * step + half, step // steps_of_group, scores_ref, step, half)
                send(step).start()

    my_block = lax.axis_index("ctx")
    chosen = selected_ref[0, 0], selected_ref[0, 1]
    first = chosen[0] < my_block
    second = jnp.logical_and(chosen[1] < my_block, chosen[1] != chosen[0])
    valid = first.astype(jnp.int32) + second.astype(jnp.int32)

    @pl.when(valid == 2)
    def _():
        attend((0, 1))

    @pl.when(valid == 1)
    def _():
        attend((second.astype(jnp.int32),))

    @pl.when(valid == 0)
    def _():
        @pl.loop(0, steps)
        def _(step):
            finish_own(step)
            send(step).start()

    @pl.loop(0, steps)
    def _(step):
        send(step).wait()


def far_attention(selected, queries, own, level, far):
    rows = queries.shape[0]
    scores = QUERY_HEADS * rows * 2 * rows
    step_width = 2 * PAIR * HEAD_SIZE
    steps = queries.shape[1] // step_width
    own = pltpu.with_memory_space_constraint(own, pltpu.VMEM)
    level = pltpu.with_memory_space_constraint(level, pltpu.VMEM)
    return pl.pallas_call(
        far_kernel,
        out_shape=jax.ShapeDtypeStruct(queries.shape, jnp.bfloat16),
        in_specs=[
            pl.BlockSpec(memory_space=pltpu.SMEM),
            *[pl.BlockSpec(memory_space=pltpu.VMEM)] * 4,
        ],
        out_specs=pl.BlockSpec(memory_space=pl.ANY),
        scratch_shapes=[
            pltpu.VMEM((KEY_VALUE_HEADS, HEAD_SIZE, 2 * rows), jnp.bfloat16),
            pltpu.VMEM((KEY_VALUE_HEADS, 2 * rows, 2 * HEAD_SIZE), jnp.bfloat16),
            pltpu.VMEM((PAIR * rows, 2 * rows), jnp.float32),
            pltpu.VMEM((PAIR * rows, 2 * rows), jnp.float32),
            pltpu.VMEM((steps, rows, step_width), jnp.bfloat16),
            pltpu.SemaphoreType.DMA((steps,)),
        ],
        compiler_params=pltpu.CompilerParams(vmem_limit_bytes=24 * MIB),
        cost_estimate=pl.CostEstimate(
            flops=4 * scores * HEAD_SIZE, bytes_accessed=10 * MIB, transcendentals=scores
        ),
        name="far_attention",
    )(selected, queries, far, own, level)


def local(queries, all_key_states, all_value_states, selected):
    devices = lax.axis_size("ctx")
    rows = all_key_states.shape[0]
    piece_rows = rows // devices
    packed = pack(all_key_states, all_value_states, selected, devices)
    held = lax.all_to_all(packed, "ctx", split_axis=0, concat_axis=0, tiled=True)
    own, level = own_attention(queries, all_key_states, all_value_states)
    wanted = held[:, SLOTS * piece_rows, :2].astype(jnp.int32)
    wanted = jnp.clip(wanted, 0, devices - 1)
    chosen = pick_pieces(wanted, held)
    far = lax.all_to_all(chosen, "ctx", split_axis=0, concat_axis=0, tiled=True)
    far = far.reshape(devices, 2, SLOTS, piece_rows, HEAD_SIZE)
    if piece_rows % 16 != 0:
        far = far.transpose(1, 2, 0, 3, 4).reshape(1, 2, SLOTS, rows, HEAD_SIZE)
    return far_attention(selected, queries, own, level, far)


def solution(mesh):
    placed = P(("groups", "ctx"), None)
    return jax.shard_map(
        local, mesh=mesh, in_specs=(placed,) * 4, out_specs=placed, check_vma=False
    )
```

time: 68.9 us -> 77.7 us (1.13)
  Pallas kernels: 14.6 us -> 25.3 us
  local copies, waits for them, and re-layouts: 2.2 us -> 9.25 us
  waiting for transfers between devices: 21.7 us -> 15.4 us
  between operations: 2.52 us -> 0.06 us
    pallas_call x3 -> x4, Pallas kernels: 14.6 us -> 25.3 us  [the longest x1 17.7 us: far_attention(): pl.pallas_call(far_kernel, out_shape=jax.ShapeDtypeStruct(queries.shape,...]
    unnamed x8 -> x16, local copies, waits for them, and re-layouts: 1.6 us -> 9.25 us
    all_to_all x1, waiting for transfers between devices: 21.7 us -> 15.4 us  [local(): far = lax.all_to_all(chosen, 'ctx', split_axis=0, concat_axis=0, tiled=True)]
  transfers between devices with their start and end apart: 1 -> 1, of which waited for: 1 -> 1; matrix products, arithmetic and copies ran while one was open for 1% -> 0% of each run, Pallas kernels for 0% -> 6%
where the time goes in v4:
time: 77.7 us; the launch traced here: 77.3 us
  Pallas kernels  25.3 us (33%)
  blocking collectives  21.5 us (28%)
  waiting for transfers between devices  15.4 us (20%)
  local copies, waits for them, and re-layouts  9.25 us (12%)
  starting transfers between devices  5.74 us (7%)
    all_to_all x1, blocking collectives, local(): lax.all_to_all(packed, 'ctx', split_axis=0, concat_axis=0, tiled=True)  21.5 us
    pallas_call x1, Pallas kernels, far_attention(): pl.pallas_call(far_kernel, out_shape=jax.ShapeDtypeStruct(queries.shape,...  17.7 us
    all_to_all x1, waiting for transfers between devices, local(): far = lax.all_to_all(chosen, 'ctx', split_axis=0, concat_axis=0, tiled=True)  15.4 us
    unnamed x16, local copies, waits for them, and re-layouts  9.25 us
    all_to_all x1, starting transfers between devices, local(): far = lax.all_to_all(chosen, 'ctx', split_axis=0, concat_axis=0, tiled=True)  5.74 us
    pallas_call x1, Pallas kernels, own_attention(): pl.pallas_call(own_kernel, out_shape=[pltpu.VMEM(queries.shape, jnp.float...  4.55 us
    pallas_call x1, Pallas kernels, pick_pieces(): pl.pallas_call(pick_kernel, out_shape=pltpu.VMEM((devices, 2, rows, HEAD_...  1.8 us
  transfers between devices with their start and end apart: 1, of which 1 were waited for; matrix products, arithmetic and copies ran while one was open for 0% of the time, Pallas kernels for 6%

profile of v4, /device:TPU:11, one launch (start us, length us, event | category | flops | bytes accessed | tf_op | source)
XLA Modules:
  0.0 77.3 jit_solution(8362936539562389380)
XLA Ops:
  0.0 0.0 copy-start.5
  0.0 0.0 copy-start.4
  0.0 1.3 %pack.1 = bf16[16,144,128]{2,1,0:T(8,128)(2,1)S(1)} custom-call(s32[1,2]{1,0:T(1,128)} %selected_ref.3, bf16[256,512]{1,0:T(8,128)(2,1)} %key_ref.3, bf16[256,512]{1,0:T(8,128)(2,1)} %value_ref.3), custom_call_target="tpu_custom_call" | custom-call | tf_op jit(solution)/shard_map/pack/pallas_call | solution.py:38
  1.3 0.0 copy-start.7
  1.3 21.5 %all_to_all.10.held_ref = bf16[16,144,128]{2,1,0:T(8,128)(2,1)S(1)} all-to-all(bf16[16,144,128]{2,1,0:T(8,128)(2,1)S(1)} %pack.1), channel_id=1, replica_groups=mesh['groups'=2,'ctx'=16] {'ctx'}, dimensions={0} | all-to-all | bytes 1179648 | tf_op jit(solution)/shard_map/all_to_all | solution.py:335
  22.8 1.8 %pick_pieces.1 = bf16[16,2,128,128]{3,2,1,0:T(8,128)(2,1)} custom-call(s32[16,2]{1,0:T(8,128)S(1)} %bitcast.3, bf16[16,144,128]{2,1,0:T(8,128)(2,1)S(1)} %all_to_all.10.held_ref), custom_call_target="tpu_custom_call" | custom-call | tf_op jit(solution)/shard_map/pick_pieces/pallas_call | solution.py:69
  24.6 5.7 %all-to-all-start.1 = ((bf16[16,2,128,128]{3,2,1,0:T(8,128)(2,1)}), bf16[16,2,128,128]{3,2,1,0:T(8,128)(2,1)S(1)}, u32[]{:S(2)}, u32[]{:S(2)}) async-start(bf16[16,2,128,128]{3,2,1,0:T(8,128)(2,1)} %pick_pieces.1), calls=%async_computation.1 | async-start | bytes 2097152 | tf_op jit(solution)/shard_map/all_to_all | solution.py:340
  30.3 0.0 copy-done.5
  30.3 0.0 copy-done.4
  30.4 0.0 copy-start.6
  30.4 0.9 %copy-done.6 = bf16[256,512]{1,0:T(8,128)(2,1)S(1)} copy-done((bf16[256,512]{1,0:T(8,128)(2,1)S(1)}, bf16[256,512]{1,0:T(8,128)(2,1)}, u32[]{:S(2)}) %copy-start.6) | copy-done | bytes 262168
  31.3 4.5 %own_attention.1 = (f32[256,4096]{1,0:T(8,128)S(1)}, f32[256,4096]{1,0:T(8,128)S(1)}) custom-call(bf16[256,4096]{1,0:T(8,128)(2,1)S(1)} %copy-done.4, bf16[256,512]{1,0:T(8,128)(2,1)S(1)} %copy-done.5, bf16[256,512]{1,0:T(8,128)(2,1)S(1)} %copy-done.6), custom_call_target="tpu_custom_call" | custom-call | flops 1073741824 | bytes 11534336 | tf_op jit(solution)/shard_map/own_attention/pallas_call | solution.py:145
  35.9 0.0 copy-start
  35.9 1.9 %copy-done = f32[256,4096]{1,0:T(8,128)} copy-done((f32[256,4096]{1,0:T(8,128)}, f32[256,4096]{1,0:T(8,128)S(1)}, u32[]{:S(2)}) %copy-start) | copy-done | bytes 4194328
  37.8 0.0 copy-start.2
  37.8 2.0 %copy-done.2 = f32[256,4096]{1,0:T(8,128)} copy-done((f32[256,4096]{1,0:T(8,128)}, f32[256,4096]{1,0:T(8,128)S(1)}, u32[]{:S(2)}) %copy-start.2) | copy-done | bytes 4194328
  39.8 15.4 %all-to-all-done.1 = bf16[16,2,128,128]{3,2,1,0:T(8,128)(2,1)S(1)} async-done(((bf16[16,2,128,128]{3,2,1,0:T(8,128)(2,1)}), bf16[16,2,128,128]{3,2,1,0:T(8,128)(2,1)S(1)}, u32[]{:S(2)}, u32[]{:S(2)}) %all-to-all-start.1) | async-done | bytes 1048608 | tf_op jit(solution)/shard_map/all_to_all | solution.py:340
  55.2 0.0 copy-done.7
  55.2 0.0 copy-start.1
  55.2 2.2 %copy-done.1 = f32[256,4096]{1,0:T(8,128)S(1)} copy-done((f32[256,4096]{1,0:T(8,128)S(1)}, f32[256,4096]{1,0:T(8,128)}, u32[]{:S(2)}) %copy-start.1) | copy-done | bytes 4194328
  57.4 0.0 copy-start.3
  57.4 2.2 %copy-done.3 = f32[256,4096]{1,0:T(8,128)S(1)} copy-done((f32[256,4096]{1,0:T(8,128)S(1)}, f32[256,4096]{1,0:T(8,128)}, u32[]{:S(2)}) %copy-start.3) | copy-done | bytes 4194328
  59.6 17.7 %far_attention.1 = bf16[256,4096]{1,0:T(8,128)(2,1)} custom-call(s32[1,2]{1,0:T(1,128)S(1)} %copy-done.7, bf16[256,4096]{1,0:T(8,128)(2,1)S(1)} %copy-done.4, bf16[16,2,8,16,128]{4,3,2,1,0:T(8,128)(2,1)S(1)} %bitcast.2, f32[256,4096]{1,0:T(8,128)S(1)} %copy-done.1, f32[256,4096]{1,0:T(8,128)S(1)} %copy-done.3), custom_call_target="tpu_custom_call" | custom-call | flops 2147483648 | bytes 10485760 | tf_op jit(solution)/shard_map/far_attention/pallas_call | solution.py:306
  (1 shorter events, 0.0 us)
Async XLA Ops:
  0.0 30.3 %copy-start.5 = (bf16[256,512]{1,0:T(8,128)(2,1)S(1)}, bf16[256,512]{1,0:T(8,128)(2,1)}, u32[]{:S(2)}) copy-start(bf16[256,512]{1,0:T(8,128)(2,1)} %key_ref.3) | copy-start | bytes 786436
  0.0 30.3 %copy-start.4 = (bf16[256,4096]{1,0:T(8,128)(2,1)S(1)}, bf16[256,4096]{1,0:T(8,128)(2,1)}, u32[]{:S(2)}) copy-start(bf16[256,4096]{1,0:T(8,128)(2,1)} %query_ref.3) | copy-start | bytes 6291460
  1.3 53.9 %copy-start.7 = (s32[1,2]{1,0:T(1,128)S(1)}, s32[1,2]{1,0:T(1,128)}, u32[]{:S(2)}) copy-start(s32[1,2]{1,0:T(1,128)} %selected_ref.3) | copy-start | bytes 28
  24.6 30.6 %all-to-all-start.1 = ((bf16[16,2,128,128]{3,2,1,0:T(8,128)(2,1)}), bf16[16,2,128,128]{3,2,1,0:T(8,128)(2,1)S(1)}, u32[]{:S(2)}, u32[]{:S(2)}) async-start(bf16[16,2,128,128]{3,2,1,0:T(8,128)(2,1)} %pick_pieces.1), calls=%async_computation.1 | async-start | bytes 2097152 | tf_op jit(solution)/shard_map/all_to_all | solution.py:340
  30.4 1.0 %copy-start.6 = (bf16[256,512]{1,0:T(8,128)(2,1)S(1)}, bf16[256,512]{1,0:T(8,128)(2,1)}, u32[]{:S(2)}) copy-start(bf16[256,512]{1,0:T(8,128)(2,1)} %value_ref.3) | copy-start | bytes 786436
  35.9 1.9 %copy-start = (f32[256,4096]{1,0:T(8,128)}, f32[256,4096]{1,0:T(8,128)S(1)}, u32[]{:S(2)}) copy-start(f32[256,4096]{1,0:T(8,128)S(1)} %get-tuple-element.7.own_ref) | copy-start | bytes 12582916
  37.8 2.0 %copy-start.2 = (f32[256,4096]{1,0:T(8,128)}, f32[256,4096]{1,0:T(8,128)S(1)}, u32[]{:S(2)}) copy-start(f32[256,4096]{1,0:T(8,128)S(1)} %get-tuple-element.8.level_ref) | copy-start | bytes 12582916
  55.2 2.2 %copy-start.1 = (f32[256,4096]{1,0:T(8,128)S(1)}, f32[256,4096]{1,0:T(8,128)}, u32[]{:S(2)}) copy-start(f32[256,4096]{1,0:T(8,128)} %copy-done) | copy-start | bytes 12582916
  57.4 2.2 %copy-start.3 = (f32[256,4096]{1,0:T(8,128)S(1)}, f32[256,4096]{1,0:T(8,128)}, u32[]{:S(2)}) copy-start(f32[256,4096]{1,0:T(8,128)} %copy-done.2) | copy-start | bytes 12582916

commit v5 on v4

--- a/solution.py
+++ b/solution.py
@@ -1,3 +1,4 @@
+import functools
 import math
 
 import jax
@@ -13,31 +14,38 @@
 GROUP = QUERY_HEADS // KEY_VALUE_HEADS
 SLOTS = 2 * KEY_VALUE_HEADS
 REQUEST_ROWS = 16
+COPIES = 2
 MIB = 1024 * 1024
 
 
 def pack_kernel(selected_ref, key_ref, value_ref, out_ref):
-    devices, piece_rows = out_ref.shape[0], key_ref.shape[0] // out_ref.shape[0]
+    devices = out_ref.shape[0]
+    shares = devices // COPIES
+    piece_rows = key_ref.shape[0] // shares
     for slot in range(SLOTS):
         ref = key_ref if slot < KEY_VALUE_HEADS else value_ref
         head = slot % KEY_VALUE_HEADS
         part = ref[:, head * HEAD_SIZE : (head + 1) * HEAD_SIZE]
-        out_ref[:, slot * piece_rows : (slot + 1) * piece_rows, :] = part.reshape(
-            devices, piece_rows, HEAD_SIZE
-        )
+        part = part.reshape(shares, piece_rows, HEAD_SIZE)
+        for copy in range(COPIES):
+            out_ref[
+                copy * shares : (copy + 1) * shares,
+                slot * piece_rows : (slot + 1) * piece_rows,
+                :,
+            ] = part
     lane = lax.broadcasted_iota(jnp.int32, (devices, REQUEST_ROWS, HEAD_SIZE), 2)
     request = jnp.where(lane == 0, selected_ref[0, 0], selected_ref[0, 1])
     out_ref[:, SLOTS * piece_rows :, :] = request.astype(jnp.float32).astype(jnp.bfloat16)
 
 
 def pack(keys, values, selected, devices):
-    rows = keys.shape[0]
-    piece_rows = rows // devices
+    shares = devices // COPIES
+    piece_rows = keys.shape[0] // shares
     shape = (devices, SLOTS * piece_rows + REQUEST_ROWS, HEAD_SIZE)
     if piece_rows % 16 == 0:
         return pl.pallas_call(
             pack_kernel,
-            out_shape=pltpu.VMEM(shape, jnp.bfloat16),
+            out_shape=jax.ShapeDtypeStruct(shape, jnp.bfloat16),
             in_specs=[
                 pl.BlockSpec(memory_space=pltpu.SMEM),
                 pl.BlockSpec(memory_space=pltpu.VMEM),
@@ -47,36 +55,55 @@
             name="pack",
         )(selected, keys, values)
     both = jnp.concatenate([keys, values], axis=1)
-    both = both.reshape(devices, piece_rows, SLOTS, HEAD_SIZE).transpose(0, 2, 1, 3)
-    both = both.reshape(devices, SLOTS * piece_rows, HEAD_SIZE)
+    both = both.reshape(shares, piece_rows, SLOTS, HEAD_SIZE).transpose(0, 2, 1, 3)
+    both = both.reshape(shares, SLOTS * piece_rows, HEAD_SIZE)
     lane = jnp.arange(HEAD_SIZE) == 0
     request = jnp.where(lane, selected[0, 0], selected[0, 1]).astype(jnp.bfloat16)
-    request = jnp.broadcast_to(request, (devices, REQUEST_ROWS, HEAD_SIZE))
-    return jnp.concatenate([both, request], axis=1)
-
-
-def pick_kernel(wanted_ref, held_ref, out_ref):
-    rows = out_ref.shape[2]
-
-    @pl.loop(0, out_ref.shape[0])
-    def _(device):
+    request = jnp.broadcast_to(request, (shares, REQUEST_ROWS, HEAD_SIZE))
+    return jnp.concatenate([jnp.concatenate([both, request], axis=1)] * COPIES, axis=0)
+
+
+def partner(position, step):
+    return position ^ step
+
+
+def pick_kernel(wanted_ref, held_ref, *out_refs):
+    rows = out_refs[0].shape[1]
+    me = lax.axis_index("ctx")
+    for step, out_ref in enumerate(out_refs):
+        device = partner(me, step)
         for pick in range(2):
-            out_ref[device, pick] = held_ref[wanted_ref[device, pick], :rows, :]
+            out_ref[pick] = held_ref[wanted_ref[device, pick], :rows, :]
 
 
 def pick_pieces(wanted, held):
     devices, rows = held.shape[0], held.shape[1] - REQUEST_ROWS
+    shares = devices // COPIES
     return pl.pallas_call(
         pick_kernel,
-        out_shape=pltpu.VMEM((devices, 2, rows, HEAD_SIZE), jnp.bfloat16),
+        out_shape=[jax.ShapeDtypeStruct((2, rows, HEAD_SIZE), jnp.bfloat16)] * shares,
         in_specs=[
             pl.BlockSpec(memory_space=pltpu.SMEM),
             pl.BlockSpec(memory_space=pltpu.VMEM),
         ],
-        out_specs=pl.BlockSpec(memory_space=pltpu.VMEM),
+        out_specs=[pl.BlockSpec(memory_space=pltpu.VMEM)] * shares,
         compiler_params=pltpu.CompilerParams(vmem_limit_bytes=16 * MIB),
         name="pick_pieces",
     )(wanted, held)
+
+
+def delivery_order(shares):
+    half, quarter = shares // 2, shares // 4
+    apart = zip(range(half, half + quarter), range(quarter, half))
+    return [s for pair in apart for s in pair] + [*range(half + quarter, shares), *range(1, quarter)]
+
+
+def deliver(pieces, devices):
+    moved = [pieces[0]]
+    for step in delivery_order(len(pieces)):
+        pairs = [(i, partner(i, step)) for i in range(devices)]
+        moved.append(lax.ppermute(pieces[step], "ctx", pairs))
+    return moved
 
 
 FACTOR = math.log2(math.e) / math.sqrt(HEAD_SIZE)
@@ -144,7 +171,7 @@
     scores = QUERY_HEADS * rows * rows
     return pl.pallas_call(
         own_kernel,
-        out_shape=[pltpu.VMEM(queries.shape, jnp.float32)] * 2,
+        out_shape=[pltpu.HBM(queries.shape, jnp.float32)] * 2,
         grid=(KEY_VALUE_HEADS,),
         in_specs=[
             pl.BlockSpec((rows, width), lambda g: (0, g)),
@@ -160,20 +187,11 @@
     )(queries, keys, values)
 
 
-def far_kernel(
-    selected_ref,
-    query_ref,
-    far_ref,
-    own_ref,
-    level_ref,
-    out_ref,
-    keys_ref,
-    values_ref,
-    scores_ref,
-    other_scores_ref,
-    staged,
-    sems,
-):
+def far_kernel(selected_ref, query_ref, own_ref, level_ref, *refs, last):
+    if last:
+        *far_refs, out_ref, keys_ref, values_ref, scores_ref, other_scores_ref, staged, sems = refs
+    else:
+        *far_refs, out_ref, new_level_ref, keys_ref, values_ref, scores_ref, other_scores_ref = refs
     rows = query_ref.shape[0]
     pair_width = PAIR * HEAD_SIZE
     step_width = 2 * pair_width
@@ -187,15 +205,19 @@
         out = out_ref.at[:, lanes(step, step_width)]
         return pltpu.make_async_copy(staged.at[step], out, sems.at[step])
 
-    def finish_own(step):
-        staged[step] = own_ref[:, lanes(step, step_width)].astype(staged.dtype)
+    def store(step, head, mixture, row_sum, level):
+        result = mixture * inverse_of(row_sum)
+        if last:
+            staged[step, :, head_lanes(head)] = result.astype(staged.dtype)
+        else:
+            out_ref[:, lanes(2 * PAIR * step + head, HEAD_SIZE)] = result
+            new_level_ref[:, lanes(2 * PAIR * step + head, HEAD_SIZE)] = level + jnp.log2(row_sum)
 
     def attend(picks):
-        count = len(picks) * rows
+        count = len(picks) * sum(ref.shape[2] for ref in far_refs)
 
         def block(slot):
-            blocks = [far_ref[:, p, slot].reshape(rows, HEAD_SIZE) for p in picks]
-            return jnp.concatenate(blocks, axis=0)
+            return jnp.concatenate([ref[p, slot] for p in picks for ref in far_refs], axis=0)
 
         @pl.loop(0, KEY_VALUE_HEADS)
         def _(group):
@@ -227,9 +249,7 @@
                     largest, jnp.max(row_sum.reshape(rows // 8, 8, HEAD_SIZE), axis=0)
                 )
                 mixture = own[:, head_lanes(h)] + part[:, :HEAD_SIZE]
-                staged[step, :, head_lanes(half * PAIR + h)] = (
-                    mixture * inverse_of(row_sum)
-                ).astype(staged.dtype)
+                store(step, half * PAIR + h, mixture, row_sum, level[:, head_lanes(h)])
             return largest
 
         def careful(pair, group, buffer, step, half):
@@ -244,9 +264,7 @@
                 both = dot(weights, values_ref[group, :count])
                 share = jnp.exp2(mine - shift)
                 mixture = own[:, head_lanes(h)] * share + both[:, :HEAD_SIZE]
-                staged[step, :, head_lanes(half * PAIR + h)] = (
-                    mixture * inverse_of(share + both[:, HEAD_SIZE:])
-                ).astype(staged.dtype)
+                store(step, half * PAIR + h, mixture, share + both[:, HEAD_SIZE:], shift)
 
         def body(step, largest):
             group = step // steps_of_group
@@ -255,7 +273,8 @@
             largest = quick(2 * step, group, scores_ref, step, 0, largest)
             score(2 * following, following // steps_of_group, scores_ref)
             largest = quick(2 * step + 1, group, other_scores_ref, step, 1, largest)
-            send(step).start()
+            if last:
+                send(step).start()
             return largest
 
         score(0, 0, scores_ref)
@@ -265,10 +284,12 @@
         def _():
             @pl.loop(0, steps)
             def _(step):
-                send(step).wait()
+                if last:
+                    send(step).wait()
                 for half in range(2):
                     careful(2 * step + half, step // steps_of_group, scores_ref, step, half)
-                send(step).start()
+                if last:
+                    send(step).start()
 
     my_block = lax.axis_index("ctx")
     chosen = selected_ref[0, 0], selected_ref[0, 1]
@@ -288,60 +309,75 @@
     def _():
         @pl.loop(0, steps)
         def _(step):
-            finish_own(step)
-            send(step).start()
-
-    @pl.loop(0, steps)
-    def _(step):
-        send(step).wait()
-
-
-def far_attention(selected, queries, own, level, far):
+            wide = lanes(step, step_width)
+            if last:
+                staged[step] = own_ref[:, wide].astype(staged.dtype)
+                send(step).start()
+            else:
+                out_ref[:, wide] = own_ref[:, wide]
+                new_level_ref[:, wide] = level_ref[:, wide]
+
+    if last:
+
+        @pl.loop(0, steps)
+        def _(step):
+            send(step).wait()
+
+
+def far_attention(selected, queries, own, level, far, last):
     rows = queries.shape[0]
-    scores = QUERY_HEADS * rows * 2 * rows
+    keys = 2 * sum(piece.shape[2] for piece in far)
+    scores = QUERY_HEADS * rows * keys
     step_width = 2 * PAIR * HEAD_SIZE
     steps = queries.shape[1] // step_width
-    own = pltpu.with_memory_space_constraint(own, pltpu.VMEM)
-    level = pltpu.with_memory_space_constraint(level, pltpu.VMEM)
-    return pl.pallas_call(
-        far_kernel,
-        out_shape=jax.ShapeDtypeStruct(queries.shape, jnp.bfloat16),
-        in_specs=[
-            pl.BlockSpec(memory_space=pltpu.SMEM),
-            *[pl.BlockSpec(memory_space=pltpu.VMEM)] * 4,
-        ],
-        out_specs=pl.BlockSpec(memory_space=pl.ANY),
-        scratch_shapes=[
-            pltpu.VMEM((KEY_VALUE_HEADS, HEAD_SIZE, 2 * rows), jnp.bfloat16),
-            pltpu.VMEM((KEY_VALUE_HEADS, 2 * rows, 2 * HEAD_SIZE), jnp.bfloat16),
-            pltpu.VMEM((PAIR * rows, 2 * rows), jnp.float32),
-            pltpu.VMEM((PAIR * rows, 2 * rows), jnp.float32),
+    in_vmem = pl.BlockSpec(memory_space=pltpu.VMEM)
+    scratch = [
+        pltpu.VMEM((KEY_VALUE_HEADS, HEAD_SIZE, keys), jnp.bfloat16),
+        pltpu.VMEM((KEY_VALUE_HEADS, keys, 2 * HEAD_SIZE), jnp.bfloat16),
+        pltpu.VMEM((PAIR * rows, keys), jnp.float32),
+        pltpu.VMEM((PAIR * rows, keys), jnp.float32),
+    ]
+    if last:
+        out_shape = jax.ShapeDtypeStruct(queries.shape, jnp.bfloat16)
+        out_specs = pl.BlockSpec(memory_space=pl.ANY)
+        scratch += [
             pltpu.VMEM((steps, rows, step_width), jnp.bfloat16),
             pltpu.SemaphoreType.DMA((steps,)),
-        ],
-        compiler_params=pltpu.CompilerParams(vmem_limit_bytes=24 * MIB),
+        ]
+    else:
+        out_shape = [jax.ShapeDtypeStruct(queries.shape, jnp.float32)] * 2
+        out_specs = [in_vmem] * 2
+    return pl.pallas_call(
+        functools.partial(far_kernel, last=last),
+        out_shape=out_shape,
+        in_specs=[pl.BlockSpec(memory_space=pltpu.SMEM), *[in_vmem] * (3 + len(far))],
+        out_specs=out_specs,
+        scratch_shapes=scratch,
+        compiler_params=pltpu.CompilerParams(vmem_limit_bytes=28 * MIB),
         cost_estimate=pl.CostEstimate(
             flops=4 * scores * HEAD_SIZE, bytes_accessed=10 * MIB, transcendentals=scores
         ),
-        name="far_attention",
-    )(selected, queries, far, own, level)
+        name="late_attention" if last else "early_attention",
+    )(selected, queries, own, level, *far)
 
 
 def local(queries, all_key_states, all_value_states, selected):
     devices = lax.axis_size("ctx")
     rows = all_key_states.shape[0]
-    piece_rows = rows // devices
+    piece_rows = rows * COPIES // devices
     packed = pack(all_key_states, all_value_states, selected, devices)
     held = lax.all_to_all(packed, "ctx", split_axis=0, concat_axis=0, tiled=True)
     own, level = own_attention(queries, all_key_states, all_value_states)
+    held, own, level = lax.optimization_barrier((held, own, level))
     wanted = held[:, SLOTS * piece_rows, :2].astype(jnp.int32)
     wanted = jnp.clip(wanted, 0, devices - 1)
-    chosen = pick_pieces(wanted, held)
-    far = lax.all_to_all(chosen, "ctx", split_axis=0, concat_axis=0, tiled=True)
-    far = far.reshape(devices, 2, SLOTS, piece_rows, HEAD_SIZE)
+    moved = deliver(pick_pieces(wanted, held), devices)
+    far = [m.reshape(2, SLOTS, piece_rows, HEAD_SIZE) for m in moved]
+    early, late = far[: len(far) // 2], far[len(far) // 2 :]
     if piece_rows % 16 != 0:
-        far = far.transpose(1, 2, 0, 3, 4).reshape(1, 2, SLOTS, rows, HEAD_SIZE)
-    return far_attention(selected, queries, own, level, far)
+        early, late = [jnp.concatenate(early, axis=2)], [jnp.concatenate(late, axis=2)]
+    own, level = far_attention(selected, queries, own, level, early, last=False)
+    return far_attention(selected, queries, own, level, late, last=True)
 
 
 def solution(mesh):

time: 77.7 us -> 66.3 us (0.85)
  the two profiles are of different devices: /device:TPU:11 before, /device:TPU:5 now
where the time goes in v5:
time: 66.3 us; the launch traced here: 65.5 us
  Pallas kernels  25 us (38%)
  waiting for transfers between devices  17.8 us (27%)
  starting transfers between devices  17.3 us (26%)
  local copies, waits for them, and re-layouts  5.32 us (8%)
    all_to_all x1, waiting for transfers between devices, local(): lax.all_to_all(packed, 'ctx', split_axis=0, concat_axis=0, tiled=True)  17.8 us
    pallas_call x2, Pallas kernels, far_attention(): pl.pallas_call(functools.partial(far_kernel, last=last), out_shape=out_sh...  16.3 us
    ppermute x7, starting transfers between devices, deliver(): moved.append(lax.ppermute(pieces[step], 'ctx', pairs))  10.8 us
    all_to_all x1, starting transfers between devices, local(): lax.all_to_all(packed, 'ctx', split_axis=0, concat_axis=0, tiled=True)  6.49 us
    pallas_call x1, Pallas kernels, own_attention(): pl.pallas_call(own_kernel, out_shape=[pltpu.HBM(queries.shape, jnp.float3...  5.63 us
    unnamed x12, local copies, waits for them, and re-layouts  5.32 us
    pallas_call x1, Pallas kernels, pack(): pl.pallas_call(pack_kernel, out_shape=jax.ShapeDtypeStruct(shape, jnp.bfl...  2.32 us
  transfers between devices with their start and end apart: 8, of which 1 were waited for; matrix products, arithmetic and copies ran while one was open for 0% of the time, Pallas kernels for 26%

profile of v5, /device:TPU:5, one launch (start us, length us, event | category | flops | bytes accessed | tf_op | source)
XLA Modules:
  0.0 65.5 jit_solution(2431537508946253171)
XLA Ops:
  0.0 2.3 %pack.1 = bf16[16,272,128]{2,1,0:T(8,128)(2,1)} custom-call(s32[1,2]{1,0:T(1,128)} %selected_ref.5, bf16[256,512]{1,0:T(8,128)(2,1)} %key_ref.3, bf16[256,512]{1,0:T(8,128)(2,1)} %value_ref.3), custom_call_target="tpu_custom_call" | custom-call | tf_op jit(solution)/shard_map/pack/pallas_call | solution.py:46
  2.3 6.5 %all-to-all-start = ((bf16[16,272,128]{2,1,0:T(8,128)(2,1)}), bf16[16,272,128]{2,1,0:T(8,128)(2,1)S(1)}, u32[]{:S(2)}, u32[]{:S(2)}) async-start(bf16[16,272,128]{2,1,0:T(8,128)(2,1)} %pack.1), calls=%async_computation | async-start | bytes 2228224 | tf_op jit(solution)/shard_map/all_to_all | solution.py:369
  8.8 0.0 copy-start.4
  8.8 0.9 %copy-done.4 = bf16[256,512]{1,0:T(8,128)(2,1)S(1)} copy-done((bf16[256,512]{1,0:T(8,128)(2,1)S(1)}, bf16[256,512]{1,0:T(8,128)(2,1)}, u32[]{:S(2)}) %copy-start.4) | copy-done | bytes 262168
  9.8 5.6 %own_attention.1 = (f32[256,4096]{1,0:T(8,128)}, f32[256,4096]{1,0:T(8,128)}) custom-call(bf16[256,4096]{1,0:T(8,128)(2,1)S(1)} %copy-done, bf16[256,512]{1,0:T(8,128)(2,1)S(1)} %copy-done.3, bf16[256,512]{1,0:T(8,128)(2,1)S(1)} %copy-done.4), custom_call_target="tpu_custom_call" | custom-call | flops 1073741824 | bytes 11534336 | tf_op jit(solution)/shard_map/own_attention/pallas_call | solution.py:172
  15.4 17.8 %all-to-all-done.held_ref = bf16[16,272,128]{2,1,0:T(8,128)(2,1)S(1)} async-done(((bf16[16,272,128]{2,1,0:T(8,128)(2,1)}), bf16[16,272,128]{2,1,0:T(8,128)(2,1)S(1)}, u32[]{:S(2)}, u32[]{:S(2)}) %all-to-all-start) | async-done | bytes 1114144 | tf_op jit(solution)/shard_map/all_to_all | solution.py:369
  33.2 0.8 %pick_pieces.1 = (bf16[2,256,128]{2,1,0:T(8,128)(2,1)S(1)}, bf16[2,256,128]{2,1,0:T(8,128)(2,1)S(1)}, bf16[2,256,128]{2,1,0:T(8,128)(2,1)S(1)}, bf16[2,256,128]{...) custom-call(s32[16,2]{1,0:T(8,128)S(1)} %bitcast.17, ...), custom_call_target="tpu_custom_call" | custom-call | tf_op jit(solution)/shard_map/pick_pieces/pallas_call | solution.py:82
  33.9 3.3 %collective-permute-start = (bf16[2,256,128]{2,1,0:T(8,128)(2,1)S(1)}, bf16[2,256,128]{2,1,0:T(8,128)(2,1)S(1)}, u32[]{:S(2)}, u32[]{:S(2)}) collective-permute-start(bf16[2,256,128]{2,1,0:T(8,128)(2,1)S(1)} %get-tuple-element.26), channel_id=1, source_target_pairs={{0,4},{1,5},{2,6},{3,7},{4,0},{5,1},{6,2},{7,3},{8,12},{9,13},{10,... | collective-permute-start | bytes 393224 | tf_op jit(solution)/shard_map/ppermute | solution.py:105
  37.3 1.3 %collective-permute-start.1 = (bf16[2,256,128]{2,1,0:T(8,128)(2,1)S(1)}, bf16[2,256,128]{2,1,0:T(8,128)(2,1)S(1)}, u32[]{:S(2)}, u32[]{:S(2)}) collective-permute-start(bf16[2,256,128]{2,1,0:T(8,128)(2,1)S(1)} %get-tuple-element.27), channel_id=1, source_target_pairs={{0,2},{1,3},{2,0},{3,1},{4,6},{5,7},{6,4},{7,5},{8,10},{9,11},{10,... | collective-permute-start | bytes 393224 | tf_op jit(solution)/shard_map/ppermute | solution.py:105
  38.6 0.5 collective-permute-start.2
  39.0 0.1 collective-permute-start.3
  39.1 2.4 %collective-permute-start.4 = (bf16[2,256,128]{2,1,0:T(8,128)(2,1)S(1)}, bf16[2,256,128]{2,1,0:T(8,128)(2,1)S(1)}, u32[]{:S(2)}, u32[]{:S(2)}) collective-permute-start(bf16[2,256,128]{2,1,0:T(8,128)(2,1)S(1)} %get-tuple-element.32), channel_id=1, source_target_pairs={{0,6},{1,7},{2,4},{3,5},{4,2},{5,3},{6,0},{7,1},{8,14},{9,15},{10,... | collective-permute-start | bytes 393224 | tf_op jit(solution)/shard_map/ppermute | solution.py:105
  41.5 0.0 collective-permute-done
  41.5 3.2 %collective-permute-start.5 = (bf16[2,256,128]{2,1,0:T(8,128)(2,1)S(1)}, bf16[2,256,128]{2,1,0:T(8,128)(2,1)S(1)}, u32[]{:S(2)}, u32[]{:S(2)}) collective-permute-start(bf16[2,256,128]{2,1,0:T(8,128)(2,1)S(1)} %get-tuple-element.33), channel_id=1, source_target_pairs={{0,7},{1,6},{2,5},{3,4},{4,3},{5,2},{6,1},{7,0},{8,15},{9,14},{10,... | collective-permute-start | bytes 393224 | tf_op jit(solution)/shard_map/ppermute | solution.py:105
  44.7 0.0 collective-permute-done.1
  44.7 0.0 collective-permute-start.6
  44.7 0.0 collective-permute-done.2
  44.8 2.2 %copy-done.1 = f32[256,4096]{1,0:T(8,128)S(1)} copy-done((f32[256,4096]{1,0:T(8,128)S(1)}, f32[256,4096]{1,0:T(8,128)}, u32[]{:S(2)}) %copy-start.1) | copy-done | bytes 4194328
  46.9 2.2 %copy-done.2 = f32[256,4096]{1,0:T(8,128)S(1)} copy-done((f32[256,4096]{1,0:T(8,128)S(1)}, f32[256,4096]{1,0:T(8,128)}, u32[]{:S(2)}) %copy-start.2) | copy-done | bytes 4194328
  49.1 11.1 %early_attention.1 = (f32[256,4096]{1,0:T(8,128)S(1)}, f32[256,4096]{1,0:T(8,128)S(1)}) custom-call(s32[1,2]{1,0:T(1,128)S(1)} %copy-done.5, bf16[256,4096]{1,0:T(8,128)(2,1)S(1)} %copy-done, f32[256,4096]{1,0:T(8,128)S(1)} %copy-done.1, f32[256,4096]{1,0:T(8,128)S(1)} %copy-done.2, bf16[2,8,32,128]{3,2,1,0:T(8,128)(2,1)S(1)} %bitcast.9, ...), custom_call_target="tpu_custom_call" | custom-call | flops 1073741824 | bytes 10485760 | tf_op jit(solution)/shard_map/early_attention/pallas_call | solution.py:350
  60.3 0.0 collective-permute-done.3
  60.3 0.0 collective-permute-done.4
  60.3 0.0 collective-permute-done.5
  60.3 5.2 %late_attention.1 = bf16[256,4096]{1,0:T(8,128)(2,1)} custom-call(s32[1,2]{1,0:T(1,128)S(1)} %copy-done.5, bf16[256,4096]{1,0:T(8,128)(2,1)S(1)} %copy-done, f32[256,4096]{1,0:T(8,128)S(1)} %get-tuple-element.29.own_ref, f32[256,4096]{1,0:T(8,128)S(1)} %get-tuple-element.30.level_ref, bf16[2,8,32,128]{3,2,1,0:T(8,128)(2,1)S(1)} %bitcast.10, ...), custom_call_target="tpu_custom_call" | custom-call | flops 1073741824 | bytes 10485760 | tf_op jit(solution)/shard_map/late_attention/pallas_call | solution.py:350
  (10 shorter events, 0.0 us)
Async XLA Ops:
  0.0 8.8 %copy-start.3 = (bf16[256,512]{1,0:T(8,128)(2,1)S(1)}, bf16[256,512]{1,0:T(8,128)(2,1)}, u32[]{:S(2)}) copy-start(bf16[256,512]{1,0:T(8,128)(2,1)} %key_ref.3) | copy-start | bytes 786436
  0.0 8.8 %copy-start = (bf16[256,4096]{1,0:T(8,128)(2,1)S(1)}, bf16[256,4096]{1,0:T(8,128)(2,1)}, u32[]{:S(2)}) copy-start(bf16[256,4096]{1,0:T(8,128)(2,1)} %query_ref.5) | copy-start | bytes 6291460
  2.3 30.8 %all-to-all-start = ((bf16[16,272,128]{2,1,0:T(8,128)(2,1)}), bf16[16,272,128]{2,1,0:T(8,128)(2,1)S(1)}, u32[]{:S(2)}, u32[]{:S(2)}) async-start(bf16[16,272,128]{2,1,0:T(8,128)(2,1)} %pack.1), calls=%async_computation | async-start | bytes 2228224 | tf_op jit(solution)/shard_map/all_to_all | solution.py:369
  8.8 1.0 %copy-start.4 = (bf16[256,512]{1,0:T(8,128)(2,1)S(1)}, bf16[256,512]{1,0:T(8,128)(2,1)}, u32[]{:S(2)}) copy-start(bf16[256,512]{1,0:T(8,128)(2,1)} %value_ref.3) | copy-start | bytes 786436
  9.8 34.9 %copy-start.5 = (s32[1,2]{1,0:T(1,128)S(1)}, s32[1,2]{1,0:T(1,128)}, u32[]{:S(2)}) copy-start(s32[1,2]{1,0:T(1,128)} %selected_ref.5) | copy-start | bytes 28
  33.9 7.6 %collective-permute-start = (bf16[2,256,128]{2,1,0:T(8,128)(2,1)S(1)}, bf16[2,256,128]{2,1,0:T(8,128)(2,1)S(1)}, u32[]{:S(2)}, u32[]{:S(2)}) collective-permute-start(bf16[2,256,128]{2,1,0:T(8,128)(2,1)S(1)} %get-tuple-element.26), channel_id=1, source_target_pairs={{0,4},{1,5},{2,6},{3,7},{4,0},{5,1},{6,2},{7,3},{8,12},{9,13},{10,... | collective-permute-start | bytes 393224 | tf_op jit(solution)/shard_map/ppermute | solution.py:105
  37.3 7.4 %collective-permute-start.1 = (bf16[2,256,128]{2,1,0:T(8,128)(2,1)S(1)}, bf16[2,256,128]{2,1,0:T(8,128)(2,1)S(1)}, u32[]{:S(2)}, u32[]{:S(2)}) collective-permute-start(bf16[2,256,128]{2,1,0:T(8,128)(2,1)S(1)} %get-tuple-element.27), channel_id=1, source_target_pairs={{0,2},{1,3},{2,0},{3,1},{4,6},{5,7},{6,4},{7,5},{8,10},{9,11},{10,... | collective-permute-start | bytes 393224 | tf_op jit(solution)/shard_map/ppermute | solution.py:105
  38.6 6.1 %collective-permute-start.2 = (bf16[2,256,128]{2,1,0:T(8,128)(2,1)S(1)}, bf16[2,256,128]{2,1,0:T(8,128)(2,1)S(1)}, u32[]{:S(2)}, u32[]{:S(2)}) collective-permute-start(bf16[2,256,128]{2,1,0:T(8,128)(2,1)S(1)} %get-tuple-element.28), channel_id=1, source_target_pairs={{0,5},{1,4},{2,7},{3,6},{4,1},{5,0},{6,3},{7,2},{8,13},{9,12},{10,... | collective-permute-start | bytes 393224 | tf_op jit(solution)/shard_map/ppermute | solution.py:105
  39.0 21.2 %collective-permute-start.3 = (bf16[2,256,128]{2,1,0:T(8,128)(2,1)S(1)}, bf16[2,256,128]{2,1,0:T(8,128)(2,1)S(1)}, u32[]{:S(2)}, u32[]{:S(2)}) collective-permute-start(bf16[2,256,128]{2,1,0:T(8,128)(2,1)S(1)} %get-tuple-element.31), channel_id=1, source_target_pairs={{0,3},{1,2},{2,1},{3,0},{4,7},{5,6},{6,5},{7,4},{8,11},{9,10},{10,... | collective-permute-start | bytes 393224 | tf_op jit(solution)/shard_map/ppermute | solution.py:105
  39.1 21.2 %collective-permute-start.4 = (bf16[2,256,128]{2,1,0:T(8,128)(2,1)S(1)}, bf16[2,256,128]{2,1,0:T(8,128)(2,1)S(1)}, u32[]{:S(2)}, u32[]{:S(2)}) collective-permute-start(bf16[2,256,128]{2,1,0:T(8,128)(2,1)S(1)} %get-tuple-element.32), channel_id=1, source_target_pairs={{0,6},{1,7},{2,4},{3,5},{4,2},{5,3},{6,0},{7,1},{8,14},{9,15},{10,... | collective-permute-start | bytes 393224 | tf_op jit(solution)/shard_map/ppermute | solution.py:105
  41.5 18.8 %collective-permute-start.5 = (bf16[2,256,128]{2,1,0:T(8,128)(2,1)S(1)}, bf16[2,256,128]{2,1,0:T(8,128)(2,1)S(1)}, u32[]{:S(2)}, u32[]{:S(2)}) collective-permute-start(bf16[2,256,128]{2,1,0:T(8,128)(2,1)S(1)} %get-tuple-element.33), channel_id=1, source_target_pairs={{0,7},{1,6},{2,5},{3,4},{4,3},{5,2},{6,1},{7,0},{8,15},{9,14},{10,... | collective-permute-start | bytes 393224 | tf_op jit(solution)/shard_map/ppermute | solution.py:105
  44.7 15.6 %collective-permute-start.6 = (bf16[2,256,128]{2,1,0:T(8,128)(2,1)S(1)}, bf16[2,256,128]{2,1,0:T(8,128)(2,1)S(1)}, u32[]{:S(2)}, u32[]{:S(2)}) collective-permute-start(bf16[2,256,128]{2,1,0:T(8,128)(2,1)S(1)} %get-tuple-element.34), channel_id=1, source_target_pairs={{0,1},{1,0},{2,3},{3,2},{4,5},{5,4},{6,7},{7,6},{8,9},{9,8},{10,11... | collective-permute-start | bytes 393224 | tf_op jit(solution)/shard_map/ppermute | solution.py:105
  44.7 2.2 %copy-start.1 = (f32[256,4096]{1,0:T(8,128)S(1)}, f32[256,4096]{1,0:T(8,128)}, u32[]{:S(2)}) copy-start(f32[256,4096]{1,0:T(8,128)} %get-tuple-element.22.own_ref) | copy-start | bytes 12582916
  46.9 2.2 %copy-start.2 = (f32[256,4096]{1,0:T(8,128)S(1)}, f32[256,4096]{1,0:T(8,128)}, u32[]{:S(2)}) copy-start(f32[256,4096]{1,0:T(8,128)} %get-tuple-element.23.level_ref) | copy-start | bytes 12582916

commit v6 on v5

v6 whole, which is shorter than its diff:
```python
import functools
import math

import jax
import jax.numpy as jnp
from jax import lax
from jax.experimental import pallas as pl
from jax.experimental.pallas import tpu as pltpu
from jax.sharding import PartitionSpec as P

QUERY_HEADS = 32
KEY_VALUE_HEADS = 4
HEAD_SIZE = 128
GROUP = QUERY_HEADS // KEY_VALUE_HEADS
SLOTS = 2 * KEY_VALUE_HEADS
COPIES = 2
MIB = 1024 * 1024


def pack_kernel(key_ref, value_ref, out_ref):
    shares = out_ref.shape[0] // COPIES
    piece_rows = key_ref.shape[0] // shares
    for slot in range(SLOTS):
        ref = key_ref if slot < KEY_VALUE_HEADS else value_ref
        head = slot % KEY_VALUE_HEADS
        part = ref[:, head * HEAD_SIZE : (head + 1) * HEAD_SIZE]
        part = part.reshape(shares, piece_rows, HEAD_SIZE)
        for copy in range(COPIES):
            out_ref[
                copy * shares : (copy + 1) * shares,
                slot * piece_rows : (slot + 1) * piece_rows,
                :,
            ] = part


def pack(keys, values, devices):
    shares = devices // COPIES
    piece_rows = keys.shape[0] // shares
    if piece_rows % 16 == 0:
        return pl.pallas_call(
            pack_kernel,
            out_shape=jax.ShapeDtypeStruct(
                (devices, SLOTS * piece_rows, HEAD_SIZE), jnp.bfloat16
            ),
            in_specs=[pl.BlockSpec(memory_space=pltpu.VMEM)] * 2,
            out_specs=pl.BlockSpec(memory_space=pltpu.VMEM),
            name="pack",
        )(keys, values)
    both = jnp.concatenate([keys, values], axis=1)
    both = both.reshape(shares, piece_rows, SLOTS, HEAD_SIZE).transpose(0, 2, 1, 3)
    both = both.reshape(shares, SLOTS * piece_rows, HEAD_SIZE)
    return jnp.concatenate([both] * COPIES, axis=0)


def partner(position, step):
    return position ^ step


def swap(array, step, devices):
    return lax.ppermute(array, "ctx", [(i, partner(i, step)) for i in range(devices)])


def exchange_requests(selected, shares, devices):
    requests = selected
    step = 1
    while step < shares:
        requests = jnp.concatenate([requests, swap(requests, step, devices)], axis=0)
        step *= 2
    return requests


def pick_kernel(requests_ref, held_ref, *out_refs):
    for step, out_ref in enumerate(out_refs):
        for pick in range(2):
            out_ref[pick] = held_ref[requests_ref[step, pick]]


def pick_pieces(requests, held):
    devices, rows, _ = held.shape
    shares = devices // COPIES
    return pl.pallas_call(
        pick_kernel,
        out_shape=[jax.ShapeDtypeStruct((2, rows, HEAD_SIZE), jnp.bfloat16)] * shares,
        in_specs=[
            pl.BlockSpec(memory_space=pltpu.SMEM),
            pl.BlockSpec(memory_space=pltpu.VMEM),
        ],
        out_specs=[pl.BlockSpec(memory_space=pltpu.VMEM)] * shares,
        compiler_params=pltpu.CompilerParams(vmem_limit_bytes=16 * MIB),
        name="pick_pieces",
    )(requests, held)


def delivery_order(shares):
    half, quarter = shares // 2, shares // 4
    apart = zip(range(half, half + quarter), range(quarter, half))
    return [*range(1, quarter), *[s for pair in apart for s in pair], *range(half + quarter, shares)]


def deliver(pieces, devices):
    order = delivery_order(len(pieces))
    return [pieces[0]] + [swap(pieces[step], step, devices) for step in order]


FACTOR = math.log2(math.e) / math.sqrt(HEAD_SIZE)
PAIR = 2
LARGE_SUM = 2.0**100


def head_lanes(head):
    return slice(head * HEAD_SIZE, (head + 1) * HEAD_SIZE)


def with_ones(value):
    return jnp.concatenate([value, jnp.ones_like(value)], axis=1)


def inverse_of(positive):
    return pl.reciprocal(positive, approx=True)


def dot(a, b):
    return jnp.dot(a, b, preferred_element_type=jnp.float32)


def stack_heads(wide):
    heads = wide.shape[1] // HEAD_SIZE
    return jnp.concatenate([wide[:, head_lanes(h)] for h in range(heads)], axis=0)


def own_kernel(query_ref, key_ref, value_ref, out_ref, level_ref):
    rows = query_ref.shape[0]
    row = lax.broadcasted_iota(jnp.int32, (rows, rows), 0)
    column = lax.broadcasted_iota(jnp.int32, (rows, rows), 1)
    causal = column <= row
    keys_across = key_ref[...].T
    value = with_ones(value_ref[...])

    def score(first):
        lanes = slice(first * HEAD_SIZE, (first + PAIR) * HEAD_SIZE)
        return dot(stack_heads(query_ref[:, lanes]), keys_across)

    def finish(first, scores):
        weights, shifts = [], []
        for h in range(PAIR):
            part = jnp.where(causal, scores[h * rows : (h + 1) * rows], -1e30)
            shift = jnp.max(part, axis=1, keepdims=True) * FACTOR
            shifts.append(shift)
            weights.append(jnp.exp2(part * FACTOR - shift).astype(jnp.bfloat16))
        both = dot(jnp.concatenate(weights, axis=0), value)
        for h in range(PAIR):
            part = both[h * rows : (h + 1) * rows]
            row_sum = part[:, HEAD_SIZE:]
            out_ref[:, head_lanes(first + h)] = part[:, :HEAD_SIZE] / row_sum
            level_ref[:, head_lanes(first + h)] = shifts[h] + jnp.log2(row_sum)

    scores = score(0)
    for first in range(0, GROUP, PAIR):
        following = score(first + PAIR) if first + PAIR < GROUP else None
        finish(first, scores)
        scores = following


def own_attention(queries, keys, values):
    rows = queries.shape[0]
    width = GROUP * HEAD_SIZE
    scores = QUERY_HEADS * rows * rows
    return pl.pallas_call(
        own_kernel,
        out_shape=[pltpu.HBM(queries.shape, jnp.float32)] * 2,
        grid=(KEY_VALUE_HEADS,),
        in_specs=[
            pl.BlockSpec((rows, width), lambda g: (0, g)),
            pl.BlockSpec((rows, HEAD_SIZE), lambda g: (0, g)),
            pl.BlockSpec((rows, HEAD_SIZE), lambda g: (0, g)),
        ],
        out_specs=[pl.BlockSpec((rows, width), lambda g: (0, g))] * 2,
        compiler_params=pltpu.CompilerParams(vmem_limit_bytes=16 * MIB),
        cost_estimate=pl.CostEstimate(
            flops=4 * scores * HEAD_SIZE, bytes_accessed=11 * MIB, transcendentals=scores
        ),
        name="own_attention",
    )(queries, keys, values)


def far_kernel(selected_ref, query_ref, own_in, level_in, *refs, last):
    if last:
        *far_refs, out_ref, staged, sems = refs
        own_ref, level_ref = own_in, level_in
    else:
        *far_refs, out_ref, new_level_ref, own_ref, level_ref, sems = refs
    rows = query_ref.shape[0]
    width = GROUP * HEAD_SIZE

    def wide(group):
        start = group * width
        return pl.ds(start if isinstance(group, int) else pl.multiple_of(start, width), width)

    def fetch(group, which):
        source, target = ((own_in, own_ref), (level_in, level_ref))[which]
        lanes = wide(group)
        return pltpu.make_async_copy(
            source.at[:, lanes], target.at[:, lanes], sems.at[which, group]
        )

    def send(group):
        lanes = wide(group)
        return pltpu.make_async_copy(staged.at[:, lanes], out_ref.at[:, lanes], sems.at[group])

    if not last:
        for group in range(KEY_VALUE_HEADS):
            fetch(group, 1).start()
            fetch(group, 0).start()

    def head_of(group, head):
        start = (group * GROUP + head) * HEAD_SIZE
        fixed = isinstance(group, int)
        return pl.ds(start if fixed else pl.multiple_of(start, HEAD_SIZE), HEAD_SIZE)

    def store(lanes, mixture, row_sum, level):
        result = mixture * inverse_of(row_sum)
        if last:
            staged[:, lanes] = result.astype(staged.dtype)
        else:
            out_ref[:, lanes] = result
            new_level_ref[:, lanes] = level + jnp.log2(row_sum)

    def attend(picks):
        count = len(picks) * sum(ref.shape[2] for ref in far_refs)

        def block(slot):
            return jnp.concatenate([ref[p, slot] for p in picks for ref in far_refs], axis=0)

        def keys_and_values(group):
            return block(group).T, with_ones(block(group + KEY_VALUE_HEADS))

        def repeat(narrow):
            return jnp.concatenate([narrow] * (count // HEAD_SIZE), axis=1)

        def quick(group, head, scores, value, largest):
            lanes = head_of(group, head)
            level = level_ref[:, lanes]
            weights = jnp.exp2(scores * FACTOR - repeat(level)).astype(jnp.bfloat16)
            both = dot(weights, value)
            row_sum = 1.0 + both[:, HEAD_SIZE:]
            store(lanes, own_ref[:, lanes] + both[:, :HEAD_SIZE], row_sum, level)
            return jnp.maximum(
                largest, jnp.max(row_sum.reshape(rows // 8, 8, HEAD_SIZE), axis=0)
            )

        def careful(group, head, scores, value):
            lanes = head_of(group, head)
            part = scores * FACTOR
            level = level_ref[:, lanes]
            shift = jnp.maximum(jnp.max(part, axis=1, keepdims=True), level)
            weights = jnp.exp2(part - repeat(shift)).astype(jnp.bfloat16)
            both = dot(weights, value)
            share = jnp.exp2(level - shift)
            mixture = own_ref[:, lanes] * share + both[:, :HEAD_SIZE]
            store(lanes, mixture, share + both[:, HEAD_SIZE:], shift)

        def score(group, head, keys_across):
            return dot(query_ref[:, head_of(group, head)], keys_across)

        largest = jnp.zeros((8, HEAD_SIZE), jnp.float32)
        order = [(g, h) for g in range(KEY_VALUE_HEADS) for h in range(GROUP)]
        held = {0: keys_and_values(0)}
        scores = score(0, 0, held[0][0])
        for (group, head), later in zip(order, order[1:] + [None]):
            following = None
            if later is not None:
                if later[0] not in held:
                    held[later[0]] = keys_and_values(later[0])
                following = score(*later, held[later[0]][0])
            if head == 0 and not last:
                fetch(group, 1).wait()
                fetch(group, 0).wait()
            largest = quick(group, head, scores, held[group][1], largest)
            if head == GROUP - 1 and last:
                send(group).start()
            scores = following

        @pl.when(jnp.max(largest) > LARGE_SUM)
        def _():
            @pl.loop(0, KEY_VALUE_HEADS)
            def _(group):
                if last:
                    send(group).wait()
                keys_across, value = keys_and_values(group)
                for head in range(GROUP):
                    careful(group, head, score(group, head, keys_across), value)
                if last:
                    send(group).start()

    my_block = lax.axis_index("ctx")
    chosen = selected_ref[0, 0], selected_ref[0, 1]
    first = chosen[0] < my_block
    second = jnp.logical_and(chosen[1] < my_block, chosen[1] != chosen[0])
    valid = first.astype(jnp.int32) + second.astype(jnp.int32)

    @pl.when(valid == 2)
    def _():
        attend((0, 1))

    @pl.when(valid == 1)
    def _():
        attend((second.astype(jnp.int32),))

    @pl.when(valid == 0)
    def _():
        @pl.loop(0, KEY_VALUE_HEADS)
        def _(group):
            lanes = wide(group)
            if last:
                staged[:, lanes] = own_ref[:, lanes].astype(staged.dtype)
                send(group).start()
            else:
                fetch(group, 1).wait()
                fetch(group, 0).wait()
                out_ref[:, lanes] = own_ref[:, lanes]
                new_level_ref[:, lanes] = level_ref[:, lanes]

    if last:

        @pl.loop(0, KEY_VALUE_HEADS)
        def _(group):
            send(group).wait()


def far_attention(selected, queries, own, level, far, last):
    rows = queries.shape[0]
    scores = QUERY_HEADS * rows * 2 * sum(piece.shape[2] for piece in far)
    in_vmem = pl.BlockSpec(memory_space=pltpu.VMEM)
    anywhere = pl.BlockSpec(memory_space=pl.ANY)
    if last:
        earlier = in_vmem
        out_shape = jax.ShapeDtypeStruct(queries.shape, jnp.bfloat16)
        out_specs = anywhere
        scratch = [
            pltpu.VMEM(queries.shape, jnp.bfloat16),
            pltpu.SemaphoreType.DMA((KEY_VALUE_HEADS,)),
        ]
    else:
        earlier = anywhere
        own = pltpu.with_memory_space_constraint(own, pltpu.HBM)
        level = pltpu.with_memory_space_constraint(level, pltpu.HBM)
        out_shape = [jax.ShapeDtypeStruct(queries.shape, jnp.float32)] * 2
        out_specs = [in_vmem] * 2
        scratch = [
            pltpu.VMEM(queries.shape, jnp.float32),
            pltpu.VMEM(queries.shape, jnp.float32),
            pltpu.SemaphoreType.DMA((2, KEY_VALUE_HEADS)),
        ]
    return pl.pallas_call(
        functools.partial(far_kernel, last=last),
        out_shape=out_shape,
        in_specs=[
            pl.BlockSpec(memory_space=pltpu.SMEM),
            in_vmem,
            earlier,
            earlier,
            *[in_vmem] * len(far),
        ],
        out_specs=out_specs,
        scratch_shapes=scratch,
        compiler_params=pltpu.CompilerParams(vmem_limit_bytes=30 * MIB),
        cost_estimate=pl.CostEstimate(
            flops=4 * scores * HEAD_SIZE, bytes_accessed=10 * MIB, transcendentals=scores
        ),
        name="late_attention" if last else "early_attention",
    )(selected, queries, own, level, *far)


def local(queries, all_key_states, all_value_states, selected):
    devices = lax.axis_size("ctx")
    rows = all_key_states.shape[0]
    piece_rows = rows * COPIES // devices
    packed = pack(all_key_states, all_value_states, devices)
    packed, queries = lax.optimization_barrier((packed, queries))
    held = lax.all_to_all(packed, "ctx", split_axis=0, concat_axis=0, tiled=True)
    own, level = own_attention(queries, all_key_states, all_value_states)
    mine, own, level = lax.optimization_barrier((selected, own, level))
    requests = exchange_requests(mine, devices // COPIES, devices)
    requests = jnp.clip(requests, 0, devices - 1)
    moved = deliver(pick_pieces(requests, held), devices)
    far = [m.reshape(2, SLOTS, piece_rows, HEAD_SIZE) for m in moved]
    early, late = far[: len(far) // 2], far[len(far) // 2 :]
    if piece_rows % 16 != 0:
        early, late = [jnp.concatenate(early, axis=2)], [jnp.concatenate(late, axis=2)]
    own, level = far_attention(selected, queries, own, level, early, last=False)
    return far_attention(selected, queries, own, level, late, last=True)


def solution(mesh):
    placed = P(("groups", "ctx"), None)
    return jax.shard_map(
        local, mesh=mesh, in_specs=(placed,) * 4, out_specs=placed, check_vma=False
    )
```

time: 66.3 us -> 57.8 us (0.87)
  the two profiles are of different devices: /device:TPU:5 before, /device:TPU:7 now
where the time goes in v6:
time: 57.8 us; the launch traced here: 56.7 us
  Pallas kernels  22.6 us (39%)
  starting transfers between devices  17.1 us (30%)
  waiting for transfers between devices  12.9 us (22%)
  local copies, waits for them, and re-layouts  3.67 us (6%)
    pallas_call x2, Pallas kernels, far_attention(): pl.pallas_call(functools.partial(far_kernel, last=last), out_shape=out_sh...  14 us
    ppermute x10, starting transfers between devices, swap(): lax.ppermute(array, 'ctx', [(i, partner(i, step)) for i in range(devices)])  10.4 us
    ppermute x10, waiting for transfers between devices, swap(): lax.ppermute(array, 'ctx', [(i, partner(i, step)) for i in range(devices)])  6.87 us
    all_to_all x1, starting transfers between devices, local(): lax.all_to_all(packed, 'ctx', split_axis=0, concat_axis=0, tiled=True)  6.67 us
    all_to_all x1, waiting for transfers between devices, local(): lax.all_to_all(packed, 'ctx', split_axis=0, concat_axis=0, tiled=True)  5.99 us
    pallas_call x1, Pallas kernels, own_attention(): pl.pallas_call(own_kernel, out_shape=[pltpu.HBM(queries.shape, jnp.float3...  5.63 us
    unnamed x10, local copies, waits for them, and re-layouts  3.49 us
    pallas_call x1, Pallas kernels, pack(): pl.pallas_call(pack_kernel, out_shape=jax.ShapeDtypeStruct((devices, SLOT...  2.3 us
  transfers between devices with their start and end apart: 11, of which 5 were waited for; matrix products, arithmetic and copies ran while one was open for 1% of the time, Pallas kernels for 27%

profile of v6, /device:TPU:7, one launch (start us, length us, event | category | flops | bytes accessed | tf_op | source)
XLA Modules:
  0.0 56.7 jit_solution(6126027407842969250)
XLA Ops:
  0.0 2.3 %pack.1 = bf16[16,256,128]{2,1,0:T(8,128)(2,1)} custom-call(bf16[256,512]{1,0:T(8,128)(2,1)} %key_ref.3, bf16[256,512]{1,0:T(8,128)(2,1)} %value_ref.3), custom_call_target="tpu_custom_call" | custom-call | tf_op jit(solution)/shard_map/pack/pallas_call | solution.py:40
  2.3 6.7 %all-to-all-start = ((bf16[16,256,128]{2,1,0:T(8,128)(2,1)}), bf16[16,256,128]{2,1,0:T(8,128)(2,1)S(1)}, u32[]{:S(2)}, u32[]{:S(2)}) async-start(bf16[16,256,128]{2,1,0:T(8,128)(2,1)} %pack.1), calls=%async_computation | async-start | bytes 2097152 | tf_op jit(solution)/shard_map/all_to_all | solution.py:380
  9.0 1.6 %copy-done = bf16[256,4096]{1,0:T(8,128)(2,1)S(1)} copy-done((bf16[256,4096]{1,0:T(8,128)(2,1)S(1)}, bf16[256,4096]{1,0:T(8,128)(2,1)}, u32[]{:S(2)}) %copy-start) | copy-done | bytes 2097176
  10.6 0.9 %copy-done.2 = bf16[256,512]{1,0:T(8,128)(2,1)S(1)} copy-done((bf16[256,512]{1,0:T(8,128)(2,1)S(1)}, bf16[256,512]{1,0:T(8,128)(2,1)}, u32[]{:S(2)}) %copy-start.2) | copy-done | bytes 262168
  11.5 0.9 %copy-done.3 = bf16[256,512]{1,0:T(8,128)(2,1)S(1)} copy-done((bf16[256,512]{1,0:T(8,128)(2,1)S(1)}, bf16[256,512]{1,0:T(8,128)(2,1)}, u32[]{:S(2)}) %copy-start.3) | copy-done | bytes 262168
  12.5 5.6 %own_attention.1 = (f32[256,4096]{1,0:T(8,128)}, f32[256,4096]{1,0:T(8,128)}) custom-call(bf16[256,4096]{1,0:T(8,128)(2,1)S(1)} %copy-done, bf16[256,512]{1,0:T(8,128)(2,1)S(1)} %copy-done.2, bf16[256,512]{1,0:T(8,128)(2,1)S(1)} %copy-done.3), custom_call_target="tpu_custom_call" | custom-call | flops 1073741824 | bytes 11534336 | tf_op jit(solution)/shard_map/own_attention/pallas_call | solution.py:168
  18.1 0.1 copy.8
  18.2 0.4 collective-permute-start
  18.6 0.8 %collective-permute-done = s32[1,2]{0,1:T(2,128)S(1)} collective-permute-done((s32[1,2]{0,1:T(2,128)S(1)}, s32[1,2]{0,1:T(2,128)S(1)}, u32[]{:S(2)}, u32[]{:S(2)}) %collective-permute-start) | collective-permute-done | bytes 40 | tf_op jit(solution)/shard_map/ppermute | solution.py:60
  19.5 2.7 %collective-permute-done.1 = s32[2,2]{0,1:T(2,128)S(1)} collective-permute-done((s32[2,2]{0,1:T(2,128)S(1)}, s32[2,2]{0,1:T(2,128)S(1)}, u32[]{:S(2)}, u32[]{:S(2)}) %collective-permute-start.1) | collective-permute-done | bytes 48 | tf_op jit(solution)/shard_map/ppermute | solution.py:60
  22.3 0.9 %collective-permute-start.2 = (s32[4,2]{0,1:T(2,128)S(1)}, s32[4,2]{0,1:T(2,128)S(1)}, u32[]{:S(2)}, u32[]{:S(2)}) collective-permute-start(s32[4,2]{0,1:T(2,128)S(1)} %pad_add_fusion.1), channel_id=1, source_target_pairs={{0,4},{1,5},{2,6},{3,7},{4,0},{5,1},{6,2},{7,3},{8,12},{9,13},{10,... | collective-permute-start | bytes 104 | tf_op jit(solution)/shard_map/ppermute | solution.py:60
  23.1 3.1 %collective-permute-done.2 = s32[4,2]{0,1:T(2,128)S(1)} collective-permute-done((s32[4,2]{0,1:T(2,128)S(1)}, s32[4,2]{0,1:T(2,128)S(1)}, u32[]{:S(2)}, u32[]{:S(2)}) %collective-permute-start.2) | collective-permute-done | bytes 64 | tf_op jit(solution)/shard_map/ppermute | solution.py:60
  26.3 0.1 copy.9
  26.4 6.0 %all-to-all-done.held_ref = bf16[16,256,128]{2,1,0:T(8,128)(2,1)S(1)} async-done(((bf16[16,256,128]{2,1,0:T(8,128)(2,1)}), bf16[16,256,128]{2,1,0:T(8,128)(2,1)S(1)}, u32[]{:S(2)}, u32[]{:S(2)}) %all-to-all-start) | async-done | bytes 1048608 | tf_op jit(solution)/shard_map/all_to_all | solution.py:380
  32.4 0.7 %pick_pieces.1 = (bf16[2,256,128]{2,1,0:T(8,128)(2,1)S(1)}, bf16[2,256,128]{2,1,0:T(8,128)(2,1)S(1)}, bf16[2,256,128]{2,1,0:T(8,128)(2,1)S(1)}, bf16[2,256,128]{...) custom-call(s32[8,2]{1,0:T(8,128)S(1)} %broadcast_clamp_fusion.reque, ...), custom_call_target="tpu_custom_call" | custom-call | tf_op jit(solution)/shard_map/pick_pieces/pallas_call | solution.py:81
  33.2 2.8 %collective-permute-start.4 = (bf16[2,256,128]{2,1,0:T(8,128)(2,1)S(1)}, bf16[2,256,128]{2,1,0:T(8,128)(2,1)S(1)}, u32[]{:S(2)}, u32[]{:S(2)}) collective-permute-start(bf16[2,256,128]{2,1,0:T(8,128)(2,1)S(1)} %get-tuple-element.31), channel_id=1, source_target_pairs={{0,4},{1,5},{2,6},{3,7},{4,0},{5,1},{6,2},{7,3},{8,12},{9,13},{10,... | collective-permute-start | bytes 393224 | tf_op jit(solution)/shard_map/ppermute | solution.py:60
  36.0 0.1 collective-permute-start.5
  36.1 0.6 %collective-permute-start.6 = (bf16[2,256,128]{2,1,0:T(8,128)(2,1)S(1)}, bf16[2,256,128]{2,1,0:T(8,128)(2,1)S(1)}, u32[]{:S(2)}, u32[]{:S(2)}) collective-permute-start(bf16[2,256,128]{2,1,0:T(8,128)(2,1)S(1)} %get-tuple-element.35), channel_id=1, source_target_pairs={{0,5},{1,4},{2,7},{3,6},{4,1},{5,0},{6,3},{7,2},{8,13},{9,12},{10,... | collective-permute-start | bytes 393224 | tf_op jit(solution)/shard_map/ppermute | solution.py:60
  36.7 1.5 %collective-permute-start.7 = (bf16[2,256,128]{2,1,0:T(8,128)(2,1)S(1)}, bf16[2,256,128]{2,1,0:T(8,128)(2,1)S(1)}, u32[]{:S(2)}, u32[]{:S(2)}) collective-permute-start(bf16[2,256,128]{2,1,0:T(8,128)(2,1)S(1)} %get-tuple-element.36), channel_id=1, source_target_pairs={{0,3},{1,2},{2,1},{3,0},{4,7},{5,6},{6,5},{7,4},{8,11},{9,10},{10,... | collective-permute-start | bytes 393224 | tf_op jit(solution)/shard_map/ppermute | solution.py:60
  38.2 1.2 %collective-permute-start.8 = (bf16[2,256,128]{2,1,0:T(8,128)(2,1)S(1)}, bf16[2,256,128]{2,1,0:T(8,128)(2,1)S(1)}, u32[]{:S(2)}, u32[]{:S(2)}) collective-permute-start(bf16[2,256,128]{2,1,0:T(8,128)(2,1)S(1)} %get-tuple-element.37), channel_id=1, source_target_pairs={{0,6},{1,7},{2,4},{3,5},{4,2},{5,3},{6,0},{7,1},{8,14},{9,15},{10,... | collective-permute-start | bytes 393224 | tf_op jit(solution)/shard_map/ppermute | solution.py:60
  39.4 0.2 collective-permute-done.4
  39.6 2.9 %collective-permute-start.9 = (bf16[2,256,128]{2,1,0:T(8,128)(2,1)S(1)}, bf16[2,256,128]{2,1,0:T(8,128)(2,1)S(1)}, u32[]{:S(2)}, u32[]{:S(2)}) collective-permute-start(bf16[2,256,128]{2,1,0:T(8,128)(2,1)S(1)} %get-tuple-element.38), channel_id=1, source_target_pairs={{0,7},{1,6},{2,5},{3,4},{4,3},{5,2},{6,1},{7,0},{8,15},{9,14},{10,... | collective-permute-start | bytes 393224 | tf_op jit(solution)/shard_map/ppermute | solution.py:60
  42.5 9.8 %early_attention.1 = (f32[256,4096]{1,0:T(8,128)S(1)}, f32[256,4096]{1,0:T(8,128)S(1)}) custom-call(s32[1,2]{1,0:T(1,128)S(1)} %copy-done.4, bf16[256,4096]{1,0:T(8,128)(2,1)S(1)} %copy-done.1, f32[256,4096]{1,0:T(8,128)} %get-tuple-element.25.own_in, f32[256,4096]{1,0:T(8,128)} %get-tuple-element.26.level_in, bf16[2,8,32,128]{3,2,1,0:T(8,128)(2,1)S(1)} %bitcast.8, ...), custom_call_target="tpu_custom_call" | custom-call | flops 1073741824 | bytes 10485760 | tf_op jit(solution)/shard_map/early_attention/pallas_call | solution.py:354
  52.4 4.2 %late_attention.1 = bf16[256,4096]{1,0:T(8,128)(2,1)} custom-call(s32[1,2]{1,0:T(1,128)S(1)} %copy-done.4, bf16[256,4096]{1,0:T(8,128)(2,1)S(1)} %copy-done.1, f32[256,4096]{1,0:T(8,128)S(1)} %get-tuple-element.33.own_in, f32[256,4096]{1,0:T(8,128)S(1)} %get-tuple-element.34.level_in, bf16[2,8,32,128]{3,2,1,0:T(8,128)(2,1)S(1)} %bitcast.9, ...), custom_call_target="tpu_custom_call" | custom-call | flops 1073741824 | bytes 10485760 | tf_op jit(solution)/shard_map/late_attention/pallas_call | solution.py:354
  (19 shorter events, 0.4 us)
Async XLA Ops:
  0.0 42.5 %copy-start.1 = (bf16[256,4096]{1,0:T(8,128)(2,1)S(1)}, bf16[256,4096]{1,0:T(8,128)(2,1)}, u32[]{:S(2)}) copy-start(bf16[256,4096]{1,0:T(8,128)(2,1)} %query_ref.2) | copy-start | bytes 6291460
  0.0 18.1 %copy-start.4 = (s32[1,2]{1,0:T(1,128)S(1)}, s32[1,2]{1,0:T(1,128)}, u32[]{:S(2)}) copy-start(s32[1,2]{1,0:T(1,128)} %selected_ref.3) | copy-start | bytes 28
  2.3 30.1 %all-to-all-start = ((bf16[16,256,128]{2,1,0:T(8,128)(2,1)}), bf16[16,256,128]{2,1,0:T(8,128)(2,1)S(1)}, u32[]{:S(2)}, u32[]{:S(2)}) async-start(bf16[16,256,128]{2,1,0:T(8,128)(2,1)} %pack.1), calls=%async_computation | async-start | bytes 2097152 | tf_op jit(solution)/shard_map/all_to_all | solution.py:380
  9.0 1.6 %copy-start = (bf16[256,4096]{1,0:T(8,128)(2,1)S(1)}, bf16[256,4096]{1,0:T(8,128)(2,1)}, u32[]{:S(2)}) copy-start(bf16[256,4096]{1,0:T(8,128)(2,1)} %query_ref.2) | copy-start | bytes 6291460
  10.6 0.9 %copy-start.2 = (bf16[256,512]{1,0:T(8,128)(2,1)S(1)}, bf16[256,512]{1,0:T(8,128)(2,1)}, u32[]{:S(2)}) copy-start(bf16[256,512]{1,0:T(8,128)(2,1)} %key_ref.3) | copy-start | bytes 786436
  11.5 0.9 %copy-start.3 = (bf16[256,512]{1,0:T(8,128)(2,1)S(1)}, bf16[256,512]{1,0:T(8,128)(2,1)}, u32[]{:S(2)}) copy-start(bf16[256,512]{1,0:T(8,128)(2,1)} %value_ref.3) | copy-start | bytes 786436
  18.2 1.2 %collective-permute-start = (s32[1,2]{0,1:T(2,128)S(1)}, s32[1,2]{0,1:T(2,128)S(1)}, u32[]{:S(2)}, u32[]{:S(2)}) collective-permute-start(s32[1,2]{0,1:T(2,128)S(1)} %copy.8), channel_id=1, source_target_pairs={{0,1},{1,0},{2,3},{3,2},{4,5},{5,4},{6,7},{7,6},{8,9},{9,8},{10,11... | collective-permute-start | bytes 32 | tf_op jit(solution)/shard_map/ppermute | solution.py:60
  19.5 2.7 %collective-permute-start.1 = (s32[2,2]{0,1:T(2,128)S(1)}, s32[2,2]{0,1:T(2,128)S(1)}, u32[]{:S(2)}, u32[]{:S(2)}) collective-permute-start(s32[2,2]{0,1:T(2,128)S(1)} %pad_add_fusion), channel_id=1, source_target_pairs={{0,2},{1,3},{2,0},{3,1},{4,6},{5,7},{6,4},{7,5},{8,10},{9,11},{10,... | collective-permute-start | bytes 56 | tf_op jit(solution)/shard_map/ppermute | solution.py:60
  22.3 4.0 %collective-permute-start.2 = (s32[4,2]{0,1:T(2,128)S(1)}, s32[4,2]{0,1:T(2,128)S(1)}, u32[]{:S(2)}, u32[]{:S(2)}) collective-permute-start(s32[4,2]{0,1:T(2,128)S(1)} %pad_add_fusion.1), channel_id=1, source_target_pairs={{0,4},{1,5},{2,6},{3,7},{4,0},{5,1},{6,2},{7,3},{8,12},{9,13},{10,... | collective-permute-start | bytes 104 | tf_op jit(solution)/shard_map/ppermute | solution.py:60
  33.1 5.1 %collective-permute-start.3 = (bf16[2,256,128]{2,1,0:T(8,128)(2,1)S(1)}, bf16[2,256,128]{2,1,0:T(8,128)(2,1)S(1)}, u32[]{:S(2)}, u32[]{:S(2)}) collective-permute-start(bf16[2,256,128]{2,1,0:T(8,128)(2,1)S(1)} %get-tuple-element.30), channel_id=1, source_target_pairs={{0,1},{1,0},{2,3},{3,2},{4,5},{5,4},{6,7},{7,6},{8,9},{9,8},{10,11... | collective-permute-start | bytes 393224 | tf_op jit(solution)/shard_map/ppermute | solution.py:60
  33.2 6.5 %collective-permute-start.4 = (bf16[2,256,128]{2,1,0:T(8,128)(2,1)S(1)}, bf16[2,256,128]{2,1,0:T(8,128)(2,1)S(1)}, u32[]{:S(2)}, u32[]{:S(2)}) collective-permute-start(bf16[2,256,128]{2,1,0:T(8,128)(2,1)S(1)} %get-tuple-element.31), channel_id=1, source_target_pairs={{0,4},{1,5},{2,6},{3,7},{4,0},{5,1},{6,2},{7,3},{8,12},{9,13},{10,... | collective-permute-start | bytes 393224 | tf_op jit(solution)/shard_map/ppermute | solution.py:60
  36.0 6.5 %collective-permute-start.5 = (bf16[2,256,128]{2,1,0:T(8,128)(2,1)S(1)}, bf16[2,256,128]{2,1,0:T(8,128)(2,1)S(1)}, u32[]{:S(2)}, u32[]{:S(2)}) collective-permute-start(bf16[2,256,128]{2,1,0:T(8,128)(2,1)S(1)} %get-tuple-element.32), channel_id=1, source_target_pairs={{0,2},{1,3},{2,0},{3,1},{4,6},{5,7},{6,4},{7,5},{8,10},{9,11},{10,... | collective-permute-start | bytes 393224 | tf_op jit(solution)/shard_map/ppermute | solution.py:60
  36.1 16.2 %collective-permute-start.6 = (bf16[2,256,128]{2,1,0:T(8,128)(2,1)S(1)}, bf16[2,256,128]{2,1,0:T(8,128)(2,1)S(1)}, u32[]{:S(2)}, u32[]{:S(2)}) collective-permute-start(bf16[2,256,128]{2,1,0:T(8,128)(2,1)S(1)} %get-tuple-element.35), channel_id=1, source_target_pairs={{0,5},{1,4},{2,7},{3,6},{4,1},{5,0},{6,3},{7,2},{8,13},{9,12},{10,... | collective-permute-start | bytes 393224 | tf_op jit(solution)/shard_map/ppermute | solution.py:60
  36.7 15.6 %collective-permute-start.7 = (bf16[2,256,128]{2,1,0:T(8,128)(2,1)S(1)}, bf16[2,256,128]{2,1,0:T(8,128)(2,1)S(1)}, u32[]{:S(2)}, u32[]{:S(2)}) collective-permute-start(bf16[2,256,128]{2,1,0:T(8,128)(2,1)S(1)} %get-tuple-element.36), channel_id=1, source_target_pairs={{0,3},{1,2},{2,1},{3,0},{4,7},{5,6},{6,5},{7,4},{8,11},{9,10},{10,... | collective-permute-start | bytes 393224 | tf_op jit(solution)/shard_map/ppermute | solution.py:60
  38.2 14.1 %collective-permute-start.8 = (bf16[2,256,128]{2,1,0:T(8,128)(2,1)S(1)}, bf16[2,256,128]{2,1,0:T(8,128)(2,1)S(1)}, u32[]{:S(2)}, u32[]{:S(2)}) collective-permute-start(bf16[2,256,128]{2,1,0:T(8,128)(2,1)S(1)} %get-tuple-element.37), channel_id=1, source_target_pairs={{0,6},{1,7},{2,4},{3,5},{4,2},{5,3},{6,0},{7,1},{8,14},{9,15},{10,... | collective-permute-start | bytes 393224 | tf_op jit(solution)/shard_map/ppermute | solution.py:60
  39.6 12.7 %collective-permute-start.9 = (bf16[2,256,128]{2,1,0:T(8,128)(2,1)S(1)}, bf16[2,256,128]{2,1,0:T(8,128)(2,1)S(1)}, u32[]{:S(2)}, u32[]{:S(2)}) collective-permute-start(bf16[2,256,128]{2,1,0:T(8,128)(2,1)S(1)} %get-tuple-element.38), channel_id=1, source_target_pairs={{0,7},{1,6},{2,5},{3,4},{4,3},{5,2},{6,1},{7,0},{8,15},{9,14},{10,... | collective-permute-start | bytes 393224 | tf_op jit(solution)/shard_map/ppermute | solution.py:60

commit v7 on v6

--- a/solution.py
+++ b/solution.py
@@ -17,35 +17,58 @@
 MIB = 1024 * 1024
 
 
-def pack_kernel(key_ref, value_ref, out_ref):
-    shares = out_ref.shape[0] // COPIES
-    piece_rows = key_ref.shape[0] // shares
-    for slot in range(SLOTS):
+def pack_kernel(key_ref, value_ref, out_ref, staged, arrived, left):
+    shares, piece_rows, _ = key_ref.shape
+    half = KEY_VALUE_HEADS * piece_rows
+
+    def take(slot):
         ref = key_ref if slot < KEY_VALUE_HEADS else value_ref
         head = slot % KEY_VALUE_HEADS
-        part = ref[:, head * HEAD_SIZE : (head + 1) * HEAD_SIZE]
-        part = part.reshape(shares, piece_rows, HEAD_SIZE)
+        lanes = pl.ds(head * HEAD_SIZE, HEAD_SIZE)
+        rows = pl.ds(slot * piece_rows, piece_rows)
+        return pltpu.make_async_copy(
+            ref.at[:, :, lanes], staged.at[:, rows, :], arrived.at[slot]
+        )
+
+    def give(which, copy):
+        rows = pl.ds(which * half, half)
+        return pltpu.make_async_copy(
+            staged.at[:, rows, :],
+            out_ref.at[pl.ds(copy * shares, shares), rows, :],
+            left.at[which, copy],
+        )
+
+    for slot in range(SLOTS):
+        take(slot).start()
+    for which in range(2):
+        for head in range(KEY_VALUE_HEADS):
+            take(which * KEY_VALUE_HEADS + head).wait()
         for copy in range(COPIES):
-            out_ref[
-                copy * shares : (copy + 1) * shares,
-                slot * piece_rows : (slot + 1) * piece_rows,
-                :,
-            ] = part
+            give(which, copy).start()
+    for which in range(2):
+        for copy in range(COPIES):
+            give(which, copy).wait()
 
 
 def pack(keys, values, devices):
     shares = devices // COPIES
     piece_rows = keys.shape[0] // shares
     if piece_rows % 16 == 0:
+        split = (shares, piece_rows, keys.shape[1])
         return pl.pallas_call(
             pack_kernel,
             out_shape=jax.ShapeDtypeStruct(
                 (devices, SLOTS * piece_rows, HEAD_SIZE), jnp.bfloat16
             ),
-            in_specs=[pl.BlockSpec(memory_space=pltpu.VMEM)] * 2,
-            out_specs=pl.BlockSpec(memory_space=pltpu.VMEM),
+            in_specs=[pl.BlockSpec(memory_space=pl.ANY)] * 2,
+            out_specs=pl.BlockSpec(memory_space=pl.ANY),
+            scratch_shapes=[
+                pltpu.VMEM((shares, SLOTS * piece_rows, HEAD_SIZE), jnp.bfloat16),
+                pltpu.SemaphoreType.DMA((SLOTS,)),
+                pltpu.SemaphoreType.DMA((2, COPIES)),
+            ],
             name="pack",
-        )(keys, values)
+        )(keys.reshape(split), values.reshape(split))
     both = jnp.concatenate([keys, values], axis=1)
     both = both.reshape(shares, piece_rows, SLOTS, HEAD_SIZE).transpose(0, 2, 1, 3)
     both = both.reshape(shares, SLOTS * piece_rows, HEAD_SIZE)
@@ -133,6 +156,7 @@
     row = lax.broadcasted_iota(jnp.int32, (rows, rows), 0)
     column = lax.broadcasted_iota(jnp.int32, (rows, rows), 1)
     causal = column <= row
+    lane = lax.broadcasted_iota(jnp.int32, (rows, HEAD_SIZE), 1)
     keys_across = key_ref[...].T
     value = with_ones(value_ref[...])
 
@@ -152,8 +176,10 @@
             part = both[h * rows : (h + 1) * rows]
             row_sum = part[:, HEAD_SIZE:]
             out_ref[:, head_lanes(first + h)] = part[:, :HEAD_SIZE] / row_sum
-            level_ref[:, head_lanes(first + h)] = shifts[h] + jnp.log2(row_sum)
-
+            level = shifts[h] + jnp.log2(row_sum)
+            level_ref[...] = jnp.where(lane == first + h, level, level_ref[...])
+
+    level_ref[...] = jnp.zeros_like(level_ref)
     scores = score(0)
     for first in range(0, GROUP, PAIR):
         following = score(first + PAIR) if first + PAIR < GROUP else None
@@ -167,17 +193,23 @@
     scores = QUERY_HEADS * rows * rows
     return pl.pallas_call(
         own_kernel,
-        out_shape=[pltpu.HBM(queries.shape, jnp.float32)] * 2,
+        out_shape=[
+            pltpu.HBM(queries.shape, jnp.float32),
+            pltpu.HBM((rows, KEY_VALUE_HEADS * HEAD_SIZE), jnp.float32),
+        ],
         grid=(KEY_VALUE_HEADS,),
         in_specs=[
             pl.BlockSpec((rows, width), lambda g: (0, g)),
             pl.BlockSpec((rows, HEAD_SIZE), lambda g: (0, g)),
             pl.BlockSpec((rows, HEAD_SIZE), lambda g: (0, g)),
         ],
-        out_specs=[pl.BlockSpec((rows, width), lambda g: (0, g))] * 2,
+        out_specs=[
+            pl.BlockSpec((rows, width), lambda g: (0, g)),
+            pl.BlockSpec((rows, HEAD_SIZE), lambda g: (0, g)),
+        ],
         compiler_params=pltpu.CompilerParams(vmem_limit_bytes=16 * MIB),
         cost_estimate=pl.CostEstimate(
-            flops=4 * scores * HEAD_SIZE, bytes_accessed=11 * MIB, transcendentals=scores
+            flops=4 * scores * HEAD_SIZE, bytes_accessed=7 * MIB, transcendentals=scores
         ),
         name="own_attention",
     )(queries, keys, values)
@@ -196,9 +228,20 @@
         start = group * width
         return pl.ds(start if isinstance(group, int) else pl.multiple_of(start, width), width)
 
+    def narrow(group):
+        start = group * HEAD_SIZE
+        fixed = isinstance(group, int)
+        return pl.ds(start if fixed else pl.multiple_of(start, HEAD_SIZE), HEAD_SIZE)
+
+    def level_of(group, head):
+        if last:
+            return level_ref[:, head_of(group, head)]
+        one = level_ref[:, narrow(group)][:, head : head + 1]
+        return jnp.broadcast_to(one, (rows, HEAD_SIZE))
+
     def fetch(group, which):
         source, target = ((own_in, own_ref), (level_in, level_ref))[which]
-        lanes = wide(group)
+        lanes = wide(group) if which == 0 else narrow(group)
         return pltpu.make_async_copy(
             source.at[:, lanes], target.at[:, lanes], sems.at[which, group]
         )
@@ -239,7 +282,7 @@
 
         def quick(group, head, scores, value, largest):
             lanes = head_of(group, head)
-            level = level_ref[:, lanes]
+            level = level_of(group, head)
             weights = jnp.exp2(scores * FACTOR - repeat(level)).astype(jnp.bfloat16)
             both = dot(weights, value)
             row_sum = 1.0 + both[:, HEAD_SIZE:]
@@ -251,7 +294,7 @@
         def careful(group, head, scores, value):
             lanes = head_of(group, head)
             part = scores * FACTOR
-            level = level_ref[:, lanes]
+            level = level_of(group, head)
             shift = jnp.maximum(jnp.max(part, axis=1, keepdims=True), level)
             weights = jnp.exp2(part - repeat(shift)).astype(jnp.bfloat16)
             both = dot(weights, value)
@@ -318,7 +361,8 @@
                 fetch(group, 1).wait()
                 fetch(group, 0).wait()
                 out_ref[:, lanes] = own_ref[:, lanes]
-                new_level_ref[:, lanes] = level_ref[:, lanes]
+                for head in range(GROUP):
+                    new_level_ref[:, head_of(group, head)] = level_of(group, head)
 
     if last:
 
@@ -348,7 +392,7 @@
         out_specs = [in_vmem] * 2
         scratch = [
             pltpu.VMEM(queries.shape, jnp.float32),
-            pltpu.VMEM(queries.shape, jnp.float32),
+            pltpu.VMEM(level.shape, jnp.float32),
             pltpu.SemaphoreType.DMA((2, KEY_VALUE_HEADS)),
         ]
     return pl.pallas_call(

time: 57.8 us -> 60.7 us (1.050)
  the two profiles are of different devices: /device:TPU:7 before, /device:TPU:1 now
where the time goes in v7:
time: 60.7 us; the launch traced here: 60.4 us
  Pallas kernels  24 us (40%)
  starting transfers between devices  21.1 us (35%)
  waiting for transfers between devices  11.2 us (18%)
  local copies, waits for them, and re-layouts  3.67 us (6%)
    pallas_call x2, Pallas kernels, far_attention(): pl.pallas_call(functools.partial(far_kernel, last=last), out_shape=out_sh...  16.1 us
    ppermute x10, starting transfers between devices, swap(): lax.ppermute(array, 'ctx', [(i, partner(i, step)) for i in range(devices)])  13.7 us
    all_to_all x1, starting transfers between devices, local(): lax.all_to_all(packed, 'ctx', split_axis=0, concat_axis=0, tiled=True)  7.33 us
    ppermute x10, waiting for transfers between devices, swap(): lax.ppermute(array, 'ctx', [(i, partner(i, step)) for i in range(devices)])  5.88 us
    all_to_all x1, waiting for transfers between devices, local(): lax.all_to_all(packed, 'ctx', split_axis=0, concat_axis=0, tiled=True)  5.31 us
    pallas_call x1, Pallas kernels, own_attention(): pl.pallas_call(own_kernel, out_shape=[pltpu.HBM(queries.shape, jnp.float3...  5.13 us
    unnamed x10, local copies, waits for them, and re-layouts  3.49 us
    pallas_call x1, Pallas kernels, pack(): pl.pallas_call(pack_kernel, out_shape=jax.ShapeDtypeStruct((devices, SLOT...  2.16 us
  transfers between devices with their start and end apart: 11, of which 4 were waited for; matrix products, arithmetic and copies ran while one was open for 1% of the time, Pallas kernels for 28%

profile of v7, /device:TPU:1, one launch (start us, length us, event | category | flops | bytes accessed | tf_op | source)
XLA Modules:
  0.0 60.4 jit_solution(7682419125298577874)
XLA Ops:
  0.0 2.2 %pack.1 = bf16[16,256,128]{2,1,0:T(8,128)(2,1)} custom-call(bf16[8,32,512]{2,1,0:T(8,128)(2,1)} %bitcast.10, bf16[8,32,512]{2,1,0:T(8,128)(2,1)} %bitcast.11), custom_call_target="tpu_custom_call" | custom-call | tf_op jit(solution)/shard_map/pack/pallas_call | solution.py:58
  2.2 7.3 %all-to-all-start = ((bf16[16,256,128]{2,1,0:T(8,128)(2,1)}), bf16[16,256,128]{2,1,0:T(8,128)(2,1)S(1)}, u32[]{:S(2)}, u32[]{:S(2)}) async-start(bf16[16,256,128]{2,1,0:T(8,128)(2,1)} %pack.1), calls=%async_computation | async-start | bytes 2097152 | tf_op jit(solution)/shard_map/all_to_all | solution.py:424
  9.5 1.6 %copy-done = bf16[256,4096]{1,0:T(8,128)(2,1)S(1)} copy-done((bf16[256,4096]{1,0:T(8,128)(2,1)S(1)}, bf16[256,4096]{1,0:T(8,128)(2,1)}, u32[]{:S(2)}) %copy-start) | copy-done | bytes 2097176
  11.1 0.9 %copy-done.2 = bf16[256,512]{1,0:T(8,128)(2,1)S(1)} copy-done((bf16[256,512]{1,0:T(8,128)(2,1)S(1)}, bf16[256,512]{1,0:T(8,128)(2,1)}, u32[]{:S(2)}) %copy-start.2) | copy-done | bytes 262168
  12.0 0.9 %copy-done.3 = bf16[256,512]{1,0:T(8,128)(2,1)S(1)} copy-done((bf16[256,512]{1,0:T(8,128)(2,1)S(1)}, bf16[256,512]{1,0:T(8,128)(2,1)}, u32[]{:S(2)}) %copy-start.3) | copy-done | bytes 262168
  13.0 5.1 %own_attention.1 = (f32[256,4096]{1,0:T(8,128)}, f32[256,512]{1,0:T(8,128)}) custom-call(bf16[256,4096]{1,0:T(8,128)(2,1)S(1)} %copy-done, bf16[256,512]{1,0:T(8,128)(2,1)S(1)} %copy-done.2, bf16[256,512]{1,0:T(8,128)(2,1)S(1)} %copy-done.3), custom_call_target="tpu_custom_call" | custom-call | flops 1073741824 | bytes 7340032 | tf_op jit(solution)/shard_map/own_attention/pallas_call | solution.py:194
  18.1 0.1 copy.8
  18.2 0.1 collective-permute-start
  18.3 1.0 %collective-permute-done = s32[1,2]{0,1:T(2,128)S(1)} collective-permute-done((s32[1,2]{0,1:T(2,128)S(1)}, s32[1,2]{0,1:T(2,128)S(1)}, u32[]{:S(2)}, u32[]{:S(2)}) %collective-permute-start) | collective-permute-done | bytes 40 | tf_op jit(solution)/shard_map/ppermute | solution.py:83
  19.4 1.4 %collective-permute-start.1 = (s32[2,2]{0,1:T(2,128)S(1)}, s32[2,2]{0,1:T(2,128)S(1)}, u32[]{:S(2)}, u32[]{:S(2)}) collective-permute-start(s32[2,2]{0,1:T(2,128)S(1)} %pad_add_fusion), channel_id=1, source_target_pairs={{0,2},{1,3},{2,0},{3,1},{4,6},{5,7},{6,4},{7,5},{8,10},{9,11},{10,... | collective-permute-start | bytes 56 | tf_op jit(solution)/shard_map/ppermute | solution.py:83
  20.9 1.3 %collective-permute-done.1 = s32[2,2]{0,1:T(2,128)S(1)} collective-permute-done((s32[2,2]{0,1:T(2,128)S(1)}, s32[2,2]{0,1:T(2,128)S(1)}, u32[]{:S(2)}, u32[]{:S(2)}) %collective-permute-start.1) | collective-permute-done | bytes 48 | tf_op jit(solution)/shard_map/ppermute | solution.py:83
  22.2 1.4 %collective-permute-start.2 = (s32[4,2]{0,1:T(2,128)S(1)}, s32[4,2]{0,1:T(2,128)S(1)}, u32[]{:S(2)}, u32[]{:S(2)}) collective-permute-start(s32[4,2]{0,1:T(2,128)S(1)} %pad_add_fusion.1), channel_id=1, source_target_pairs={{0,4},{1,5},{2,6},{3,7},{4,0},{5,1},{6,2},{7,3},{8,12},{9,13},{10,... | collective-permute-start | bytes 104 | tf_op jit(solution)/shard_map/ppermute | solution.py:83
  23.6 3.5 %collective-permute-done.2 = s32[4,2]{0,1:T(2,128)S(1)} collective-permute-done((s32[4,2]{0,1:T(2,128)S(1)}, s32[4,2]{0,1:T(2,128)S(1)}, u32[]{:S(2)}, u32[]{:S(2)}) %collective-permute-start.2) | collective-permute-done | bytes 64 | tf_op jit(solution)/shard_map/ppermute | solution.py:83
  27.2 0.1 copy.9
  27.3 5.3 %all-to-all-done.held_ref = bf16[16,256,128]{2,1,0:T(8,128)(2,1)S(1)} async-done(((bf16[16,256,128]{2,1,0:T(8,128)(2,1)}), bf16[16,256,128]{2,1,0:T(8,128)(2,1)S(1)}, u32[]{:S(2)}, u32[]{:S(2)}) %all-to-all-start) | async-done | bytes 1048608 | tf_op jit(solution)/shard_map/all_to_all | solution.py:424
  32.6 0.7 %pick_pieces.1 = (bf16[2,256,128]{2,1,0:T(8,128)(2,1)S(1)}, bf16[2,256,128]{2,1,0:T(8,128)(2,1)S(1)}, bf16[2,256,128]{2,1,0:T(8,128)(2,1)S(1)}, bf16[2,256,128]{...) custom-call(s32[8,2]{1,0:T(8,128)S(1)} %broadcast_clamp_fusion.reque, ...), custom_call_target="tpu_custom_call" | custom-call | tf_op jit(solution)/shard_map/pick_pieces/pallas_call | solution.py:104
  33.4 3.2 %collective-permute-start.4 = (bf16[2,256,128]{2,1,0:T(8,128)(2,1)S(1)}, bf16[2,256,128]{2,1,0:T(8,128)(2,1)S(1)}, u32[]{:S(2)}, u32[]{:S(2)}) collective-permute-start(bf16[2,256,128]{2,1,0:T(8,128)(2,1)S(1)} %get-tuple-element.31), channel_id=1, source_target_pairs={{0,4},{1,5},{2,6},{3,7},{4,0},{5,1},{6,2},{7,3},{8,12},{9,13},{10,... | collective-permute-start | bytes 393224 | tf_op jit(solution)/shard_map/ppermute | solution.py:83
  36.6 1.4 %collective-permute-start.5 = (bf16[2,256,128]{2,1,0:T(8,128)(2,1)S(1)}, bf16[2,256,128]{2,1,0:T(8,128)(2,1)S(1)}, u32[]{:S(2)}, u32[]{:S(2)}) collective-permute-start(bf16[2,256,128]{2,1,0:T(8,128)(2,1)S(1)} %get-tuple-element.32), channel_id=1, source_target_pairs={{0,2},{1,3},{2,0},{3,1},{4,6},{5,7},{6,4},{7,5},{8,10},{9,11},{10,... | collective-permute-start | bytes 393224 | tf_op jit(solution)/shard_map/ppermute | solution.py:83
  37.9 0.5 collective-permute-start.6
  38.4 0.5 collective-permute-start.7
  38.9 1.9 %collective-permute-start.8 = (bf16[2,256,128]{2,1,0:T(8,128)(2,1)S(1)}, bf16[2,256,128]{2,1,0:T(8,128)(2,1)S(1)}, u32[]{:S(2)}, u32[]{:S(2)}) collective-permute-start(bf16[2,256,128]{2,1,0:T(8,128)(2,1)S(1)} %get-tuple-element.37), channel_id=1, source_target_pairs={{0,6},{1,7},{2,4},{3,5},{4,2},{5,3},{6,0},{7,1},{8,14},{9,15},{10,... | collective-permute-start | bytes 393224 | tf_op jit(solution)/shard_map/ppermute | solution.py:83
  40.8 3.3 %collective-permute-start.9 = (bf16[2,256,128]{2,1,0:T(8,128)(2,1)S(1)}, bf16[2,256,128]{2,1,0:T(8,128)(2,1)S(1)}, u32[]{:S(2)}, u32[]{:S(2)}) collective-permute-start(bf16[2,256,128]{2,1,0:T(8,128)(2,1)S(1)} %get-tuple-element.38), channel_id=1, source_target_pairs={{0,7},{1,6},{2,5},{3,4},{4,3},{5,2},{6,1},{7,0},{8,15},{9,14},{10,... | collective-permute-start | bytes 393224 | tf_op jit(solution)/shard_map/ppermute | solution.py:83
  44.1 12.1 %early_attention.1 = (f32[256,4096]{1,0:T(8,128)S(1)}, f32[256,4096]{1,0:T(8,128)S(1)}) custom-call(s32[1,2]{1,0:T(1,128)S(1)} %copy-done.4, bf16[256,4096]{1,0:T(8,128)(2,1)S(1)} %copy-done.1, f32[256,4096]{1,0:T(8,128)} %get-tuple-element.25.own_in, f32[256,512]{1,0:T(8,128)} %get-tuple-element.26.level_in, bf16[2,8,32,128]{3,2,1,0:T(8,128)(2,1)S(1)} %bitcast.16, ...), custom_call_target="tpu_custom_call" | custom-call | flops 1073741824 | bytes 10485760 | tf_op jit(solution)/shard_map/early_attention/pallas_call | solution.py:398
  56.3 4.0 %late_attention.1 = bf16[256,4096]{1,0:T(8,128)(2,1)} custom-call(s32[1,2]{1,0:T(1,128)S(1)} %copy-done.4, bf16[256,4096]{1,0:T(8,128)(2,1)S(1)} %copy-done.1, f32[256,4096]{1,0:T(8,128)S(1)} %get-tuple-element.33.own_in, f32[256,4096]{1,0:T(8,128)S(1)} %get-tuple-element.34.level_in, bf16[2,8,32,128]{3,2,1,0:T(8,128)(2,1)S(1)} %bitcast.12, ...), custom_call_target="tpu_custom_call" | custom-call | flops 1073741824 | bytes 10485760 | tf_op jit(solution)/shard_map/late_attention/pallas_call | solution.py:398
  (19 shorter events, 0.3 us)
Async XLA Ops:
  0.0 18.1 %copy-start.4 = (s32[1,2]{1,0:T(1,128)S(1)}, s32[1,2]{1,0:T(1,128)}, u32[]{:S(2)}) copy-start(s32[1,2]{1,0:T(1,128)} %selected_ref.3) | copy-start | bytes 28
  0.0 44.1 %copy-start.1 = (bf16[256,4096]{1,0:T(8,128)(2,1)S(1)}, bf16[256,4096]{1,0:T(8,128)(2,1)}, u32[]{:S(2)}) copy-start(bf16[256,4096]{1,0:T(8,128)(2,1)} %query_ref.2) | copy-start | bytes 6291460
  2.2 30.5 %all-to-all-start = ((bf16[16,256,128]{2,1,0:T(8,128)(2,1)}), bf16[16,256,128]{2,1,0:T(8,128)(2,1)S(1)}, u32[]{:S(2)}, u32[]{:S(2)}) async-start(bf16[16,256,128]{2,1,0:T(8,128)(2,1)} %pack.1), calls=%async_computation | async-start | bytes 2097152 | tf_op jit(solution)/shard_map/all_to_all | solution.py:424
  9.5 1.6 %copy-start = (bf16[256,4096]{1,0:T(8,128)(2,1)S(1)}, bf16[256,4096]{1,0:T(8,128)(2,1)}, u32[]{:S(2)}) copy-start(bf16[256,4096]{1,0:T(8,128)(2,1)} %query_ref.2) | copy-start | bytes 6291460
  11.1 0.9 %copy-start.2 = (bf16[256,512]{1,0:T(8,128)(2,1)S(1)}, bf16[256,512]{1,0:T(8,128)(2,1)}, u32[]{:S(2)}) copy-start(bf16[256,512]{1,0:T(8,128)(2,1)} %key_ref.1) | copy-start | bytes 786436
  12.0 0.9 %copy-start.3 = (bf16[256,512]{1,0:T(8,128)(2,1)S(1)}, bf16[256,512]{1,0:T(8,128)(2,1)}, u32[]{:S(2)}) copy-start(bf16[256,512]{1,0:T(8,128)(2,1)} %value_ref.1) | copy-start | bytes 786436
  18.2 1.1 %collective-permute-start = (s32[1,2]{0,1:T(2,128)S(1)}, s32[1,2]{0,1:T(2,128)S(1)}, u32[]{:S(2)}, u32[]{:S(2)}) collective-permute-start(s32[1,2]{0,1:T(2,128)S(1)} %copy.8), channel_id=1, source_target_pairs={{0,1},{1,0},{2,3},{3,2},{4,5},{5,4},{6,7},{7,6},{8,9},{9,8},{10,11... | collective-permute-start | bytes 32 | tf_op jit(solution)/shard_map/ppermute | solution.py:83
  19.4 2.7 %collective-permute-start.1 = (s32[2,2]{0,1:T(2,128)S(1)}, s32[2,2]{0,1:T(2,128)S(1)}, u32[]{:S(2)}, u32[]{:S(2)}) collective-permute-start(s32[2,2]{0,1:T(2,128)S(1)} %pad_add_fusion), channel_id=1, source_target_pairs={{0,2},{1,3},{2,0},{3,1},{4,6},{5,7},{6,4},{7,5},{8,10},{9,11},{10,... | collective-permute-start | bytes 56 | tf_op jit(solution)/shard_map/ppermute | solution.py:83
  22.2 4.9 %collective-permute-start.2 = (s32[4,2]{0,1:T(2,128)S(1)}, s32[4,2]{0,1:T(2,128)S(1)}, u32[]{:S(2)}, u32[]{:S(2)}) collective-permute-start(s32[4,2]{0,1:T(2,128)S(1)} %pad_add_fusion.1), channel_id=1, source_target_pairs={{0,4},{1,5},{2,6},{3,7},{4,0},{5,1},{6,2},{7,3},{8,12},{9,13},{10,... | collective-permute-start | bytes 104 | tf_op jit(solution)/shard_map/ppermute | solution.py:83
  33.3 5.6 %collective-permute-start.3 = (bf16[2,256,128]{2,1,0:T(8,128)(2,1)S(1)}, bf16[2,256,128]{2,1,0:T(8,128)(2,1)S(1)}, u32[]{:S(2)}, u32[]{:S(2)}) collective-permute-start(bf16[2,256,128]{2,1,0:T(8,128)(2,1)S(1)} %get-tuple-element.30), channel_id=1, source_target_pairs={{0,1},{1,0},{2,3},{3,2},{4,5},{5,4},{6,7},{7,6},{8,9},{9,8},{10,11... | collective-permute-start | bytes 393224 | tf_op jit(solution)/shard_map/ppermute | solution.py:83
  33.4 7.4 %collective-permute-start.4 = (bf16[2,256,128]{2,1,0:T(8,128)(2,1)S(1)}, bf16[2,256,128]{2,1,0:T(8,128)(2,1)S(1)}, u32[]{:S(2)}, u32[]{:S(2)}) collective-permute-start(bf16[2,256,128]{2,1,0:T(8,128)(2,1)S(1)} %get-tuple-element.31), channel_id=1, source_target_pairs={{0,4},{1,5},{2,6},{3,7},{4,0},{5,1},{6,2},{7,3},{8,12},{9,13},{10,... | collective-permute-start | bytes 393224 | tf_op jit(solution)/shard_map/ppermute | solution.py:83
  36.6 7.6 %collective-permute-start.5 = (bf16[2,256,128]{2,1,0:T(8,128)(2,1)S(1)}, bf16[2,256,128]{2,1,0:T(8,128)(2,1)S(1)}, u32[]{:S(2)}, u32[]{:S(2)}) collective-permute-start(bf16[2,256,128]{2,1,0:T(8,128)(2,1)S(1)} %get-tuple-element.32), channel_id=1, source_target_pairs={{0,2},{1,3},{2,0},{3,1},{4,6},{5,7},{6,4},{7,5},{8,10},{9,11},{10,... | collective-permute-start | bytes 393224 | tf_op jit(solution)/shard_map/ppermute | solution.py:83
  37.9 18.3 %collective-permute-start.6 = (bf16[2,256,128]{2,1,0:T(8,128)(2,1)S(1)}, bf16[2,256,128]{2,1,0:T(8,128)(2,1)S(1)}, u32[]{:S(2)}, u32[]{:S(2)}) collective-permute-start(bf16[2,256,128]{2,1,0:T(8,128)(2,1)S(1)} %get-tuple-element.35), channel_id=1, source_target_pairs={{0,5},{1,4},{2,7},{3,6},{4,1},{5,0},{6,3},{7,2},{8,13},{9,12},{10,... | collective-permute-start | bytes 393224 | tf_op jit(solution)/shard_map/ppermute | solution.py:83
  38.4 17.9 %collective-permute-start.7 = (bf16[2,256,128]{2,1,0:T(8,128)(2,1)S(1)}, bf16[2,256,128]{2,1,0:T(8,128)(2,1)S(1)}, u32[]{:S(2)}, u32[]{:S(2)}) collective-permute-start(bf16[2,256,128]{2,1,0:T(8,128)(2,1)S(1)} %get-tuple-element.36), channel_id=1, source_target_pairs={{0,3},{1,2},{2,1},{3,0},{4,7},{5,6},{6,5},{7,4},{8,11},{9,10},{10,... | collective-permute-start | bytes 393224 | tf_op jit(solution)/shard_map/ppermute | solution.py:83
  38.9 17.3 %collective-permute-start.8 = (bf16[2,256,128]{2,1,0:T(8,128)(2,1)S(1)}, bf16[2,256,128]{2,1,0:T(8,128)(2,1)S(1)}, u32[]{:S(2)}, u32[]{:S(2)}) collective-permute-start(bf16[2,256,128]{2,1,0:T(8,128)(2,1)S(1)} %get-tuple-element.37), channel_id=1, source_target_pairs={{0,6},{1,7},{2,4},{3,5},{4,2},{5,3},{6,0},{7,1},{8,14},{9,15},{10,... | collective-permute-start | bytes 393224 | tf_op jit(solution)/shard_map/ppermute | solution.py:83
  40.8 15.4 %collective-permute-start.9 = (bf16[2,256,128]{2,1,0:T(8,128)(2,1)S(1)}, bf16[2,256,128]{2,1,0:T(8,128)(2,1)S(1)}, u32[]{:S(2)}, u32[]{:S(2)}) collective-permute-start(bf16[2,256,128]{2,1,0:T(8,128)(2,1)S(1)} %get-tuple-element.38), channel_id=1, source_target_pairs={{0,7},{1,6},{2,5},{3,4},{4,3},{5,2},{6,1},{7,0},{8,15},{9,14},{10,... | collective-permute-start | bytes 393224 | tf_op jit(solution)/shard_map/ppermute | solution.py:83

commit v8 on v7

--- a/solution.py
+++ b/solution.py
@@ -215,12 +215,14 @@
     )(queries, keys, values)
 
 
-def far_kernel(selected_ref, query_ref, own_in, level_in, *refs, last):
+def far_kernel(selected_ref, query_ref, own_in, level_in, *refs, first_call, last):
+    own_ref, level_ref = own_in, level_in
     if last:
         *far_refs, out_ref, staged, sems = refs
-        own_ref, level_ref = own_in, level_in
+    elif first_call:
+        *far_refs, out_ref, new_level_ref, own_ref, level_ref, sems = refs
     else:
-        *far_refs, out_ref, new_level_ref, own_ref, level_ref, sems = refs
+        *far_refs, out_ref, new_level_ref = refs
     rows = query_ref.shape[0]
     width = GROUP * HEAD_SIZE
 
@@ -234,7 +236,7 @@
         return pl.ds(start if fixed else pl.multiple_of(start, HEAD_SIZE), HEAD_SIZE)
 
     def level_of(group, head):
-        if last:
+        if not first_call:
             return level_ref[:, head_of(group, head)]
         one = level_ref[:, narrow(group)][:, head : head + 1]
         return jnp.broadcast_to(one, (rows, HEAD_SIZE))
@@ -250,7 +252,7 @@
         lanes = wide(group)
         return pltpu.make_async_copy(staged.at[:, lanes], out_ref.at[:, lanes], sems.at[group])
 
-    if not last:
+    if first_call:
         for group in range(KEY_VALUE_HEADS):
             fetch(group, 1).start()
             fetch(group, 0).start()
@@ -278,7 +280,8 @@
             return block(group).T, with_ones(block(group + KEY_VALUE_HEADS))
 
         def repeat(narrow):
-            return jnp.concatenate([narrow] * (count // HEAD_SIZE), axis=1)
+            whole = jnp.concatenate([narrow] * pl.cdiv(count, HEAD_SIZE), axis=1)
+            return whole[:, :count]
 
         def quick(group, head, scores, value, largest):
             lanes = head_of(group, head)
@@ -315,7 +318,7 @@
                 if later[0] not in held:
                     held[later[0]] = keys_and_values(later[0])
                 following = score(*later, held[later[0]][0])
-            if head == 0 and not last:
+            if head == 0 and first_call:
                 fetch(group, 1).wait()
                 fetch(group, 0).wait()
             largest = quick(group, head, scores, held[group][1], largest)
@@ -358,8 +361,9 @@
                 staged[:, lanes] = own_ref[:, lanes].astype(staged.dtype)
                 send(group).start()
             else:
-                fetch(group, 1).wait()
-                fetch(group, 0).wait()
+                if first_call:
+                    fetch(group, 1).wait()
+                    fetch(group, 0).wait()
                 out_ref[:, lanes] = own_ref[:, lanes]
                 for head in range(GROUP):
                     new_level_ref[:, head_of(group, head)] = level_of(group, head)
@@ -371,32 +375,31 @@
             send(group).wait()
 
 
-def far_attention(selected, queries, own, level, far, last):
+def far_attention(selected, queries, own, level, far, first_call=False, last=False):
     rows = queries.shape[0]
     scores = QUERY_HEADS * rows * 2 * sum(piece.shape[2] for piece in far)
     in_vmem = pl.BlockSpec(memory_space=pltpu.VMEM)
     anywhere = pl.BlockSpec(memory_space=pl.ANY)
+    earlier, scratch = in_vmem, []
+    out_shape, out_specs = [jax.ShapeDtypeStruct(queries.shape, jnp.float32)] * 2, [in_vmem] * 2
+    if first_call:
+        earlier = anywhere
+        own = pltpu.with_memory_space_constraint(own, pltpu.HBM)
+        level = pltpu.with_memory_space_constraint(level, pltpu.HBM)
+        scratch = [
+            pltpu.VMEM(own.shape, jnp.float32),
+            pltpu.VMEM(level.shape, jnp.float32),
+            pltpu.SemaphoreType.DMA((2, KEY_VALUE_HEADS)),
+        ]
     if last:
-        earlier = in_vmem
         out_shape = jax.ShapeDtypeStruct(queries.shape, jnp.bfloat16)
         out_specs = anywhere
         scratch = [
             pltpu.VMEM(queries.shape, jnp.bfloat16),
             pltpu.SemaphoreType.DMA((KEY_VALUE_HEADS,)),
         ]
-    else:
-        earlier = anywhere
-        own = pltpu.with_memory_space_constraint(own, pltpu.HBM)
-        level = pltpu.with_memory_space_constraint(level, pltpu.HBM)
-        out_shape = [jax.ShapeDtypeStruct(queries.shape, jnp.float32)] * 2
-        out_specs = [in_vmem] * 2
-        scratch = [
-            pltpu.VMEM(queries.shape, jnp.float32),
-            pltpu.VMEM(level.shape, jnp.float32),
-            pltpu.SemaphoreType.DMA((2, KEY_VALUE_HEADS)),
-        ]
     return pl.pallas_call(
-        functools.partial(far_kernel, last=last),
+        functools.partial(far_kernel, first_call=first_call, last=last),
         out_shape=out_shape,
         in_specs=[
             pl.BlockSpec(memory_space=pltpu.SMEM),
@@ -411,7 +414,7 @@
         cost_estimate=pl.CostEstimate(
             flops=4 * scores * HEAD_SIZE, bytes_accessed=10 * MIB, transcendentals=scores
         ),
-        name="late_attention" if last else "early_attention",
+        name="early_attention" if first_call else "late_attention" if last else "middle_attention",
     )(selected, queries, own, level, *far)
 
 
@@ -428,11 +431,13 @@
     requests = jnp.clip(requests, 0, devices - 1)
     moved = deliver(pick_pieces(requests, held), devices)
     far = [m.reshape(2, SLOTS, piece_rows, HEAD_SIZE) for m in moved]
-    early, late = far[: len(far) // 2], far[len(far) // 2 :]
+    half, quarter = len(far) // 2, len(far) // 4
+    parts = [far[:half], far[half:-quarter], far[-quarter:]]
     if piece_rows % 16 != 0:
-        early, late = [jnp.concatenate(early, axis=2)], [jnp.concatenate(late, axis=2)]
-    own, level = far_attention(selected, queries, own, level, early, last=False)
-    return far_attention(selected, queries, own, level, late, last=True)
+        parts = [[jnp.concatenate(part, axis=2)] for part in parts]
+    own, level = far_attention(selected, queries, own, level, parts[0], first_call=True)
+    own, level = far_attention(selected, queries, own, level, parts[1])
+    return far_attention(selected, queries, own, level, parts[2], last=True)
 
 
 def solution(mesh):

time: 60.7 us -> 63.8 us (1.051)
  Pallas kernels: 24 us -> 27.1 us
    pallas_call x2 -> x3, Pallas kernels: 16.1 us -> 19.1 us  [far_attention(): pl.pallas_call(functools.partial(far_kernel, first_call=first_call, last=...]
  transfers between devices with their start and end apart: 11 -> 11, of which waited for: 4 -> 4; matrix products, arithmetic and copies ran while one was open for 1% -> 1% of each run, Pallas kernels for 28% -> 32%
where the time goes in v8:
time: 63.8 us; the launch traced here: 63.5 us
  Pallas kernels  27.1 us (42%)
  starting transfers between devices  21.1 us (33%)
  waiting for transfers between devices  11.2 us (18%)
  local copies, waits for them, and re-layouts  3.67 us (6%)
    pallas_call x3, Pallas kernels, far_attention(): pl.pallas_call(functools.partial(far_kernel, first_call=first_call, last=...  19.1 us
    ppermute x10, starting transfers between devices, swap(): lax.ppermute(array, 'ctx', [(i, partner(i, step)) for i in range(devices)])  13.7 us
    all_to_all x1, starting transfers between devices, local(): lax.all_to_all(packed, 'ctx', split_axis=0, concat_axis=0, tiled=True)  7.33 us
    ppermute x10, waiting for transfers between devices, swap(): lax.ppermute(array, 'ctx', [(i, partner(i, step)) for i in range(devices)])  5.86 us
    all_to_all x1, waiting for transfers between devices, local(): lax.all_to_all(packed, 'ctx', split_axis=0, concat_axis=0, tiled=True)  5.31 us
    pallas_call x1, Pallas kernels, own_attention(): pl.pallas_call(own_kernel, out_shape=[pltpu.HBM(queries.shape, jnp.float3...  5.15 us
    unnamed x10, local copies, waits for them, and re-layouts  3.49 us
    pallas_call x1, Pallas kernels, pack(): pl.pallas_call(pack_kernel, out_shape=jax.ShapeDtypeStruct((devices, SLOT...  2.16 us
  transfers between devices with their start and end apart: 11, of which 4 were waited for; matrix products, arithmetic and copies ran while one was open for 1% of the time, Pallas kernels for 32%

profile of v8, /device:TPU:1, one launch (start us, length us, event | category | flops | bytes accessed | tf_op | source)
XLA Modules:
  0.0 63.5 jit_solution(17650860535680919774)
XLA Ops:
  0.0 2.2 %pack.1 = bf16[16,256,128]{2,1,0:T(8,128)(2,1)} custom-call(bf16[8,32,512]{2,1,0:T(8,128)(2,1)} %bitcast.10, bf16[8,32,512]{2,1,0:T(8,128)(2,1)} %bitcast.11), custom_call_target="tpu_custom_call" | custom-call | tf_op jit(solution)/shard_map/pack/pallas_call | solution.py:58
  2.2 7.3 %all-to-all-start = ((bf16[16,256,128]{2,1,0:T(8,128)(2,1)}), bf16[16,256,128]{2,1,0:T(8,128)(2,1)S(1)}, u32[]{:S(2)}, u32[]{:S(2)}) async-start(bf16[16,256,128]{2,1,0:T(8,128)(2,1)} %pack.1), calls=%async_computation | async-start | bytes 2097152 | tf_op jit(solution)/shard_map/all_to_all | solution.py:427
  9.5 1.6 %copy-done = bf16[256,4096]{1,0:T(8,128)(2,1)S(1)} copy-done((bf16[256,4096]{1,0:T(8,128)(2,1)S(1)}, bf16[256,4096]{1,0:T(8,128)(2,1)}, u32[]{:S(2)}) %copy-start) | copy-done | bytes 2097176
  11.1 0.9 %copy-done.2 = bf16[256,512]{1,0:T(8,128)(2,1)S(1)} copy-done((bf16[256,512]{1,0:T(8,128)(2,1)S(1)}, bf16[256,512]{1,0:T(8,128)(2,1)}, u32[]{:S(2)}) %copy-start.2) | copy-done | bytes 262168
  12.0 0.9 %copy-done.3 = bf16[256,512]{1,0:T(8,128)(2,1)S(1)} copy-done((bf16[256,512]{1,0:T(8,128)(2,1)S(1)}, bf16[256,512]{1,0:T(8,128)(2,1)}, u32[]{:S(2)}) %copy-start.3) | copy-done | bytes 262168
  13.0 5.2 %own_attention.1 = (f32[256,4096]{1,0:T(8,128)}, f32[256,512]{1,0:T(8,128)}) custom-call(bf16[256,4096]{1,0:T(8,128)(2,1)S(1)} %copy-done, bf16[256,512]{1,0:T(8,128)(2,1)S(1)} %copy-done.2, bf16[256,512]{1,0:T(8,128)(2,1)S(1)} %copy-done.3), custom_call_target="tpu_custom_call" | custom-call | flops 1073741824 | bytes 7340032 | tf_op jit(solution)/shard_map/own_attention/pallas_call | solution.py:194
  18.2 0.1 copy.8
  18.2 0.1 collective-permute-start
  18.3 1.0 %collective-permute-done = s32[1,2]{0,1:T(2,128)S(1)} collective-permute-done((s32[1,2]{0,1:T(2,128)S(1)}, s32[1,2]{0,1:T(2,128)S(1)}, u32[]{:S(2)}, u32[]{:S(2)}) %collective-permute-start) | collective-permute-done | bytes 40 | tf_op jit(solution)/shard_map/ppermute | solution.py:83
  19.5 1.4 %collective-permute-start.1 = (s32[2,2]{0,1:T(2,128)S(1)}, s32[2,2]{0,1:T(2,128)S(1)}, u32[]{:S(2)}, u32[]{:S(2)}) collective-permute-start(s32[2,2]{0,1:T(2,128)S(1)} %pad_add_fusion), channel_id=1, source_target_pairs={{0,2},{1,3},{2,0},{3,1},{4,6},{5,7},{6,4},{7,5},{8,10},{9,11},{10,... | collective-permute-start | bytes 56 | tf_op jit(solution)/shard_map/ppermute | solution.py:83
  20.9 1.3 %collective-permute-done.1 = s32[2,2]{0,1:T(2,128)S(1)} collective-permute-done((s32[2,2]{0,1:T(2,128)S(1)}, s32[2,2]{0,1:T(2,128)S(1)}, u32[]{:S(2)}, u32[]{:S(2)}) %collective-permute-start.1) | collective-permute-done | bytes 48 | tf_op jit(solution)/shard_map/ppermute | solution.py:83
  22.3 1.4 %collective-permute-start.2 = (s32[4,2]{0,1:T(2,128)S(1)}, s32[4,2]{0,1:T(2,128)S(1)}, u32[]{:S(2)}, u32[]{:S(2)}) collective-permute-start(s32[4,2]{0,1:T(2,128)S(1)} %pad_add_fusion.1), channel_id=1, source_target_pairs={{0,4},{1,5},{2,6},{3,7},{4,0},{5,1},{6,2},{7,3},{8,12},{9,13},{10,... | collective-permute-start | bytes 104 | tf_op jit(solution)/shard_map/ppermute | solution.py:83
  23.7 3.5 %collective-permute-done.2 = s32[4,2]{0,1:T(2,128)S(1)} collective-permute-done((s32[4,2]{0,1:T(2,128)S(1)}, s32[4,2]{0,1:T(2,128)S(1)}, u32[]{:S(2)}, u32[]{:S(2)}) %collective-permute-start.2) | collective-permute-done | bytes 64 | tf_op jit(solution)/shard_map/ppermute | solution.py:83
  27.3 5.3 %all-to-all-done.held_ref = bf16[16,256,128]{2,1,0:T(8,128)(2,1)S(1)} async-done(((bf16[16,256,128]{2,1,0:T(8,128)(2,1)}), bf16[16,256,128]{2,1,0:T(8,128)(2,1)S(1)}, u32[]{:S(2)}, u32[]{:S(2)}) %all-to-all-start) | async-done | bytes 1048608 | tf_op jit(solution)/shard_map/all_to_all | solution.py:427
  32.6 0.7 %pick_pieces.1 = (bf16[2,256,128]{2,1,0:T(8,128)(2,1)S(1)}, bf16[2,256,128]{2,1,0:T(8,128)(2,1)S(1)}, bf16[2,256,128]{2,1,0:T(8,128)(2,1)S(1)}, bf16[2,256,128]{...) custom-call(s32[8,2]{1,0:T(8,128)S(1)} %broadcast_clamp_fusion.reque, ...), custom_call_target="tpu_custom_call" | custom-call | tf_op jit(solution)/shard_map/pick_pieces/pallas_call | solution.py:104
  33.4 3.2 %collective-permute-start.4 = (bf16[2,256,128]{2,1,0:T(8,128)(2,1)S(1)}, bf16[2,256,128]{2,1,0:T(8,128)(2,1)S(1)}, u32[]{:S(2)}, u32[]{:S(2)}) collective-permute-start(bf16[2,256,128]{2,1,0:T(8,128)(2,1)S(1)} %get-tuple-element.33), channel_id=1, source_target_pairs={{0,4},{1,5},{2,6},{3,7},{4,0},{5,1},{6,2},{7,3},{8,12},{9,13},{10,... | collective-permute-start | bytes 393224 | tf_op jit(solution)/shard_map/ppermute | solution.py:83
  36.6 1.4 %collective-permute-start.5 = (bf16[2,256,128]{2,1,0:T(8,128)(2,1)S(1)}, bf16[2,256,128]{2,1,0:T(8,128)(2,1)S(1)}, u32[]{:S(2)}, u32[]{:S(2)}) collective-permute-start(bf16[2,256,128]{2,1,0:T(8,128)(2,1)S(1)} %get-tuple-element.34), channel_id=1, source_target_pairs={{0,2},{1,3},{2,0},{3,1},{4,6},{5,7},{6,4},{7,5},{8,10},{9,11},{10,... | collective-permute-start | bytes 393224 | tf_op jit(solution)/shard_map/ppermute | solution.py:83
  37.9 0.5 collective-permute-start.6
  38.4 0.5 collective-permute-start.7
  38.9 1.9 %collective-permute-start.8 = (bf16[2,256,128]{2,1,0:T(8,128)(2,1)S(1)}, bf16[2,256,128]{2,1,0:T(8,128)(2,1)S(1)}, u32[]{:S(2)}, u32[]{:S(2)}) collective-permute-start(bf16[2,256,128]{2,1,0:T(8,128)(2,1)S(1)} %get-tuple-element.41), channel_id=1, source_target_pairs={{0,6},{1,7},{2,4},{3,5},{4,2},{5,3},{6,0},{7,1},{8,14},{9,15},{10,... | collective-permute-start | bytes 393224 | tf_op jit(solution)/shard_map/ppermute | solution.py:83
  40.8 3.3 %collective-permute-start.9 = (bf16[2,256,128]{2,1,0:T(8,128)(2,1)S(1)}, bf16[2,256,128]{2,1,0:T(8,128)(2,1)S(1)}, u32[]{:S(2)}, u32[]{:S(2)}) collective-permute-start(bf16[2,256,128]{2,1,0:T(8,128)(2,1)S(1)} %get-tuple-element.42), channel_id=1, source_target_pairs={{0,7},{1,6},{2,5},{3,4},{4,3},{5,2},{6,1},{7,0},{8,15},{9,14},{10,... | collective-permute-start | bytes 393224 | tf_op jit(solution)/shard_map/ppermute | solution.py:83
  44.1 12.1 %early_attention.1 = (f32[256,4096]{1,0:T(8,128)S(1)}, f32[256,4096]{1,0:T(8,128)S(1)}) custom-call(s32[1,2]{1,0:T(1,128)S(1)} %copy-done.4, bf16[256,4096]{1,0:T(8,128)(2,1)S(1)} %copy-done.1, f32[256,4096]{1,0:T(8,128)} %get-tuple-element.27.own_in, f32[256,512]{1,0:T(8,128)} %get-tuple-element.28.level_in, bf16[2,8,32,128]{3,2,1,0:T(8,128)(2,1)S(1)} %bitcast.16, ...), custom_call_target="tpu_custom_call" | custom-call | flops 1073741824 | bytes 10485760 | tf_op jit(solution)/shard_map/early_attention/pallas_call | solution.py:401
  56.3 3.3 %middle_attention.1 = (f32[256,4096]{1,0:T(8,128)S(1)}, f32[256,4096]{1,0:T(8,128)S(1)}) custom-call(s32[1,2]{1,0:T(1,128)S(1)} %copy-done.4, bf16[256,4096]{1,0:T(8,128)(2,1)S(1)} %copy-done.1, f32[256,4096]{1,0:T(8,128)S(1)} %get-tuple-element.35.own_in, f32[256,4096]{1,0:T(8,128)S(1)} %get-tuple-element.36.level_in, bf16[2,8,32,128]{3,2,1,0:T(8,128)(2,1)S(1)} %bitcast.13, ...), custom_call_target="tpu_custom_call" | custom-call | flops 536870912 | bytes 10485760 | tf_op jit(solution)/shard_map/middle_attention/pallas_call | solution.py:401
  59.6 3.7 %late_attention.1 = bf16[256,4096]{1,0:T(8,128)(2,1)} custom-call(s32[1,2]{1,0:T(1,128)S(1)} %copy-done.4, bf16[256,4096]{1,0:T(8,128)(2,1)S(1)} %copy-done.1, f32[256,4096]{1,0:T(8,128)S(1)} %get-tuple-element.39.own_in, f32[256,4096]{1,0:T(8,128)S(1)} %get-tuple-element.40.level_in, bf16[2,8,32,128]{3,2,1,0:T(8,128)(2,1)S(1)} %bitcast.12, ...), custom_call_target="tpu_custom_call" | custom-call | flops 536870912 | bytes 10485760 | tf_op jit(solution)/shard_map/late_attention/pallas_call | solution.py:401
  (20 shorter events, 0.4 us)
Async XLA Ops:
  0.0 18.2 %copy-start.4 = (s32[1,2]{1,0:T(1,128)S(1)}, s32[1,2]{1,0:T(1,128)}, u32[]{:S(2)}) copy-start(s32[1,2]{1,0:T(1,128)} %selected_ref.5) | copy-start | bytes 28
  0.0 44.1 %copy-start.1 = (bf16[256,4096]{1,0:T(8,128)(2,1)S(1)}, bf16[256,4096]{1,0:T(8,128)(2,1)}, u32[]{:S(2)}) copy-start(bf16[256,4096]{1,0:T(8,128)(2,1)} %query_ref.3) | copy-start | bytes 6291460
  2.2 30.5 %all-to-all-start = ((bf16[16,256,128]{2,1,0:T(8,128)(2,1)}), bf16[16,256,128]{2,1,0:T(8,128)(2,1)S(1)}, u32[]{:S(2)}, u32[]{:S(2)}) async-start(bf16[16,256,128]{2,1,0:T(8,128)(2,1)} %pack.1), calls=%async_computation | async-start | bytes 2097152 | tf_op jit(solution)/shard_map/all_to_all | solution.py:427
  9.5 1.6 %copy-start = (bf16[256,4096]{1,0:T(8,128)(2,1)S(1)}, bf16[256,4096]{1,0:T(8,128)(2,1)}, u32[]{:S(2)}) copy-start(bf16[256,4096]{1,0:T(8,128)(2,1)} %query_ref.3) | copy-start | bytes 6291460
  11.1 0.9 %copy-start.2 = (bf16[256,512]{1,0:T(8,128)(2,1)S(1)}, bf16[256,512]{1,0:T(8,128)(2,1)}, u32[]{:S(2)}) copy-start(bf16[256,512]{1,0:T(8,128)(2,1)} %key_ref.1) | copy-start | bytes 786436
  12.0 0.9 %copy-start.3 = (bf16[256,512]{1,0:T(8,128)(2,1)S(1)}, bf16[256,512]{1,0:T(8,128)(2,1)}, u32[]{:S(2)}) copy-start(bf16[256,512]{1,0:T(8,128)(2,1)} %value_ref.1) | copy-start | bytes 786436
  18.2 1.1 %collective-permute-start = (s32[1,2]{0,1:T(2,128)S(1)}, s32[1,2]{0,1:T(2,128)S(1)}, u32[]{:S(2)}, u32[]{:S(2)}) collective-permute-start(s32[1,2]{0,1:T(2,128)S(1)} %copy.8), channel_id=1, source_target_pairs={{0,1},{1,0},{2,3},{3,2},{4,5},{5,4},{6,7},{7,6},{8,9},{9,8},{10,11... | collective-permute-start | bytes 32 | tf_op jit(solution)/shard_map/ppermute | solution.py:83
  19.5 2.7 %collective-permute-start.1 = (s32[2,2]{0,1:T(2,128)S(1)}, s32[2,2]{0,1:T(2,128)S(1)}, u32[]{:S(2)}, u32[]{:S(2)}) collective-permute-start(s32[2,2]{0,1:T(2,128)S(1)} %pad_add_fusion), channel_id=1, source_target_pairs={{0,2},{1,3},{2,0},{3,1},{4,6},{5,7},{6,4},{7,5},{8,10},{9,11},{10,... | collective-permute-start | bytes 56 | tf_op jit(solution)/shard_map/ppermute | solution.py:83
  22.3 4.9 %collective-permute-start.2 = (s32[4,2]{0,1:T(2,128)S(1)}, s32[4,2]{0,1:T(2,128)S(1)}, u32[]{:S(2)}, u32[]{:S(2)}) collective-permute-start(s32[4,2]{0,1:T(2,128)S(1)} %pad_add_fusion.1), channel_id=1, source_target_pairs={{0,4},{1,5},{2,6},{3,7},{4,0},{5,1},{6,2},{7,3},{8,12},{9,13},{10,... | collective-permute-start | bytes 104 | tf_op jit(solution)/shard_map/ppermute | solution.py:83
  33.3 5.6 %collective-permute-start.3 = (bf16[2,256,128]{2,1,0:T(8,128)(2,1)S(1)}, bf16[2,256,128]{2,1,0:T(8,128)(2,1)S(1)}, u32[]{:S(2)}, u32[]{:S(2)}) collective-permute-start(bf16[2,256,128]{2,1,0:T(8,128)(2,1)S(1)} %get-tuple-element.32), channel_id=1, source_target_pairs={{0,1},{1,0},{2,3},{3,2},{4,5},{5,4},{6,7},{7,6},{8,9},{9,8},{10,11... | collective-permute-start | bytes 393224 | tf_op jit(solution)/shard_map/ppermute | solution.py:83
  33.4 7.4 %collective-permute-start.4 = (bf16[2,256,128]{2,1,0:T(8,128)(2,1)S(1)}, bf16[2,256,128]{2,1,0:T(8,128)(2,1)S(1)}, u32[]{:S(2)}, u32[]{:S(2)}) collective-permute-start(bf16[2,256,128]{2,1,0:T(8,128)(2,1)S(1)} %get-tuple-element.33), channel_id=1, source_target_pairs={{0,4},{1,5},{2,6},{3,7},{4,0},{5,1},{6,2},{7,3},{8,12},{9,13},{10,... | collective-permute-start | bytes 393224 | tf_op jit(solution)/shard_map/ppermute | solution.py:83
  36.6 7.6 %collective-permute-start.5 = (bf16[2,256,128]{2,1,0:T(8,128)(2,1)S(1)}, bf16[2,256,128]{2,1,0:T(8,128)(2,1)S(1)}, u32[]{:S(2)}, u32[]{:S(2)}) collective-permute-start(bf16[2,256,128]{2,1,0:T(8,128)(2,1)S(1)} %get-tuple-element.34), channel_id=1, source_target_pairs={{0,2},{1,3},{2,0},{3,1},{4,6},{5,7},{6,4},{7,5},{8,10},{9,11},{10,... | collective-permute-start | bytes 393224 | tf_op jit(solution)/shard_map/ppermute | solution.py:83
  37.9 18.3 %collective-permute-start.6 = (bf16[2,256,128]{2,1,0:T(8,128)(2,1)S(1)}, bf16[2,256,128]{2,1,0:T(8,128)(2,1)S(1)}, u32[]{:S(2)}, u32[]{:S(2)}) collective-permute-start(bf16[2,256,128]{2,1,0:T(8,128)(2,1)S(1)} %get-tuple-element.37), channel_id=1, source_target_pairs={{0,5},{1,4},{2,7},{3,6},{4,1},{5,0},{6,3},{7,2},{8,13},{9,12},{10,... | collective-permute-start | bytes 393224 | tf_op jit(solution)/shard_map/ppermute | solution.py:83
  38.4 17.9 %collective-permute-start.7 = (bf16[2,256,128]{2,1,0:T(8,128)(2,1)S(1)}, bf16[2,256,128]{2,1,0:T(8,128)(2,1)S(1)}, u32[]{:S(2)}, u32[]{:S(2)}) collective-permute-start(bf16[2,256,128]{2,1,0:T(8,128)(2,1)S(1)} %get-tuple-element.38), channel_id=1, source_target_pairs={{0,3},{1,2},{2,1},{3,0},{4,7},{5,6},{6,5},{7,4},{8,11},{9,10},{10,... | collective-permute-start | bytes 393224 | tf_op jit(solution)/shard_map/ppermute | solution.py:83
  38.9 20.7 %collective-permute-start.8 = (bf16[2,256,128]{2,1,0:T(8,128)(2,1)S(1)}, bf16[2,256,128]{2,1,0:T(8,128)(2,1)S(1)}, u32[]{:S(2)}, u32[]{:S(2)}) collective-permute-start(bf16[2,256,128]{2,1,0:T(8,128)(2,1)S(1)} %get-tuple-element.41), channel_id=1, source_target_pairs={{0,6},{1,7},{2,4},{3,5},{4,2},{5,3},{6,0},{7,1},{8,14},{9,15},{10,... | collective-permute-start | bytes 393224 | tf_op jit(solution)/shard_map/ppermute | solution.py:83
  40.8 18.8 %collective-permute-start.9 = (bf16[2,256,128]{2,1,0:T(8,128)(2,1)S(1)}, bf16[2,256,128]{2,1,0:T(8,128)(2,1)S(1)}, u32[]{:S(2)}, u32[]{:S(2)}) collective-permute-start(bf16[2,256,128]{2,1,0:T(8,128)(2,1)S(1)} %get-tuple-element.42), channel_id=1, source_target_pairs={{0,7},{1,6},{2,5},{3,4},{4,3},{5,2},{6,1},{7,0},{8,15},{9,14},{10,... | collective-permute-start | bytes 393224 | tf_op jit(solution)/shard_map/ppermute | solution.py:83

commit v9 on v7

--- a/solution.py
+++ b/solution.py
@@ -12,67 +12,7 @@
 KEY_VALUE_HEADS = 4
 HEAD_SIZE = 128
 GROUP = QUERY_HEADS // KEY_VALUE_HEADS
-SLOTS = 2 * KEY_VALUE_HEADS
-COPIES = 2
 MIB = 1024 * 1024
-
-
-def pack_kernel(key_ref, value_ref, out_ref, staged, arrived, left):
-    shares, piece_rows, _ = key_ref.shape
-    half = KEY_VALUE_HEADS * piece_rows
-
-    def take(slot):
-        ref = key_ref if slot < KEY_VALUE_HEADS else value_ref
-        head = slot % KEY_VALUE_HEADS
-        lanes = pl.ds(head * HEAD_SIZE, HEAD_SIZE)
-        rows = pl.ds(slot * piece_rows, piece_rows)
-        return pltpu.make_async_copy(
-            ref.at[:, :, lanes], staged.at[:, rows, :], arrived.at[slot]
-        )
-
-    def give(which, copy):
-        rows = pl.ds(which * half, half)
-        return pltpu.make_async_copy(
-            staged.at[:, rows, :],
-            out_ref.at[pl.ds(copy * shares, shares), rows, :],
-            left.at[which, copy],
-        )
-
-    for slot in range(SLOTS):
-        take(slot).start()
-    for which in range(2):
-        for head in range(KEY_VALUE_HEADS):
-            take(which * KEY_VALUE_HEADS + head).wait()
-        for copy in range(COPIES):
-            give(which, copy).start()
-    for which in range(2):
-        for copy in range(COPIES):
-            give(which, copy).wait()
-
-
-def pack(keys, values, devices):
-    shares = devices // COPIES
-    piece_rows = keys.shape[0] // shares
-    if piece_rows % 16 == 0:
-        split = (shares, piece_rows, keys.shape[1])
-        return pl.pallas_call(
-            pack_kernel,
-            out_shape=jax.ShapeDtypeStruct(
-                (devices, SLOTS * piece_rows, HEAD_SIZE), jnp.bfloat16
-            ),
-            in_specs=[pl.BlockSpec(memory_space=pl.ANY)] * 2,
-            out_specs=pl.BlockSpec(memory_space=pl.ANY),
-            scratch_shapes=[
-                pltpu.VMEM((shares, SLOTS * piece_rows, HEAD_SIZE), jnp.bfloat16),
-                pltpu.SemaphoreType.DMA((SLOTS,)),
-                pltpu.SemaphoreType.DMA((2, COPIES)),
-            ],
-            name="pack",
-        )(keys.reshape(split), values.reshape(split))
-    both = jnp.concatenate([keys, values], axis=1)
-    both = both.reshape(shares, piece_rows, SLOTS, HEAD_SIZE).transpose(0, 2, 1, 3)
-    both = both.reshape(shares, SLOTS * piece_rows, HEAD_SIZE)
-    return jnp.concatenate([both] * COPIES, axis=0)
 
 
 def partner(position, step):
@@ -92,26 +32,68 @@
     return requests
 
 
-def pick_kernel(requests_ref, held_ref, *out_refs):
+def cut_kernel(*refs, run):
+    in_refs, out_refs = refs[:-run], refs[-run:]
+    rows = in_refs[0].shape[0] // run
+    me = lax.rem(lax.axis_index("ctx"), run)
+    for step, out_ref in enumerate(out_refs):
+        share = pl.ds(pl.multiple_of(partner(me, step) * rows, rows), rows)
+        parts = [
+            ref[share, head * HEAD_SIZE : (head + 1) * HEAD_SIZE]
+            for ref in in_refs
+            for head in range(KEY_VALUE_HEADS)
+        ]
+        out_ref[...] = jnp.concatenate(parts, axis=0)
+
+
+def cut(arrays, run):
+    rows = arrays[0].shape[0] // run
+    heads = len(arrays) * KEY_VALUE_HEADS
+    if rows % 16 == 0:
+        in_vmem = pl.BlockSpec(memory_space=pltpu.VMEM)
+        return pl.pallas_call(
+            functools.partial(cut_kernel, run=run),
+            out_shape=[jax.ShapeDtypeStruct((heads * rows, HEAD_SIZE), jnp.bfloat16)] * run,
+            in_specs=[in_vmem] * len(arrays),
+            out_specs=[in_vmem] * run,
+            compiler_params=pltpu.CompilerParams(vmem_limit_bytes=16 * MIB),
+            name="cut",
+        )(*arrays)
+    whole = jnp.concatenate(arrays, axis=1).reshape(run, rows, heads, HEAD_SIZE)
+    whole = whole.transpose(0, 2, 1, 3).reshape(run, heads * rows, HEAD_SIZE)
+    me = lax.rem(lax.axis_index("ctx"), run)
+    whole = jnp.take(whole, partner(jnp.arange(run), me), axis=0)
+    return [whole[step] for step in range(run)]
+
+
+def pick_kernel(requests_ref, *refs, run, start):
+    near_refs, over_refs = refs[:run], refs[run : 2 * run]
+    out_refs, held_ref = refs[2 * run : -1], refs[-1]
+    rows = held_ref.shape[1]
+    for step in range(run):
+        held_ref[step] = near_refs[step][start : start + rows]
+        held_ref[run + step] = over_refs[step][...]
+    me = lax.axis_index("ctx")
     for step, out_ref in enumerate(out_refs):
         for pick in range(2):
-            out_ref[pick] = held_ref[requests_ref[step, pick]]
-
-
-def pick_pieces(requests, held):
-    devices, rows, _ = held.shape
-    shares = devices // COPIES
+            block = requests_ref[step, pick]
+            place = partner(lax.rem(block, run), lax.rem(me, run))
+            other_run = (lax.div(block, run) != lax.div(me, run)).astype(jnp.int32)
+            out_ref[pick] = held_ref[place + run * other_run]
+
+
+def pick_pieces(requests, near, over, start):
+    run, rows = len(near), over[0].shape[0]
+    in_vmem = pl.BlockSpec(memory_space=pltpu.VMEM)
     return pl.pallas_call(
-        pick_kernel,
-        out_shape=[jax.ShapeDtypeStruct((2, rows, HEAD_SIZE), jnp.bfloat16)] * shares,
-        in_specs=[
-            pl.BlockSpec(memory_space=pltpu.SMEM),
-            pl.BlockSpec(memory_space=pltpu.VMEM),
-        ],
-        out_specs=[pl.BlockSpec(memory_space=pltpu.VMEM)] * shares,
+        functools.partial(pick_kernel, run=run, start=start),
+        out_shape=[jax.ShapeDtypeStruct((2, rows, HEAD_SIZE), jnp.bfloat16)] * run,
+        in_specs=[pl.BlockSpec(memory_space=pltpu.SMEM), *[in_vmem] * (2 * run)],
+        out_specs=[in_vmem] * run,
+        scratch_shapes=[pltpu.VMEM((2 * run, rows, HEAD_SIZE), jnp.bfloat16)],
         compiler_params=pltpu.CompilerParams(vmem_limit_bytes=16 * MIB),
         name="pick_pieces",
-    )(requests, held)
+    )(requests, *near, *over)
 
 
 def delivery_order(shares):
@@ -120,9 +102,11 @@
     return [*range(1, quarter), *[s for pair in apart for s in pair], *range(half + quarter, shares)]
 
 
-def deliver(pieces, devices):
-    order = delivery_order(len(pieces))
-    return [pieces[0]] + [swap(pieces[step], step, devices) for step in order]
+def trade(pieces, devices):
+    moved = {0: pieces[0]}
+    for step in delivery_order(len(pieces)):
+        moved[step] = swap(pieces[step], step, devices)
+    return [moved[step] for step in range(len(pieces))]
 
 
 FACTOR = math.log2(math.e) / math.sqrt(HEAD_SIZE)
@@ -269,13 +253,15 @@
             new_level_ref[:, lanes] = level + jnp.log2(row_sum)
 
     def attend(picks):
-        count = len(picks) * sum(ref.shape[2] for ref in far_refs)
-
-        def block(slot):
-            return jnp.concatenate([ref[p, slot] for p in picks for ref in far_refs], axis=0)
+        far_key_refs = far_refs[: len(far_refs) // 2]
+        far_value_refs = far_refs[len(far_refs) // 2 :]
+        count = len(picks) * sum(ref.shape[2] for ref in far_key_refs)
+
+        def block(pieces, group):
+            return jnp.concatenate([ref[p, group] for p in picks for ref in pieces], axis=0)
 
         def keys_and_values(group):
-            return block(group).T, with_ones(block(group + KEY_VALUE_HEADS))
+            return block(far_key_refs, group).T, with_ones(block(far_value_refs, group))
 
         def repeat(narrow):
             return jnp.concatenate([narrow] * (count // HEAD_SIZE), axis=1)
@@ -373,7 +359,7 @@
 
 def far_attention(selected, queries, own, level, far, last):
     rows = queries.shape[0]
-    scores = QUERY_HEADS * rows * 2 * sum(piece.shape[2] for piece in far)
+    scores = QUERY_HEADS * rows * sum(piece.shape[2] for piece in far)
     in_vmem = pl.BlockSpec(memory_space=pltpu.VMEM)
     anywhere = pl.BlockSpec(memory_space=pl.ANY)
     if last:
@@ -417,22 +403,40 @@
 
 def local(queries, all_key_states, all_value_states, selected):
     devices = lax.axis_size("ctx")
+    run = devices // 2
     rows = all_key_states.shape[0]
-    piece_rows = rows * COPIES // devices
-    packed = pack(all_key_states, all_value_states, devices)
-    packed, queries = lax.optimization_barrier((packed, queries))
-    held = lax.all_to_all(packed, "ctx", split_axis=0, concat_axis=0, tiled=True)
+    piece_rows = rows // run
+    upward = [(i, i + run) for i in range(run)]
+
+    keys_over = lax.ppermute(all_key_states, "ctx", upward)
+    values_next, keys_over = lax.optimization_barrier((all_value_states, keys_over))
+    values_over = lax.ppermute(values_next, "ctx", upward)
+
+    near = cut([all_key_states, all_value_states], run)
+    queries, mine, near = lax.optimization_barrier((queries, selected, near))
+    near = trade(near, devices)
     own, level = own_attention(queries, all_key_states, all_value_states)
-    mine, own, level = lax.optimization_barrier((selected, own, level))
-    requests = exchange_requests(mine, devices // COPIES, devices)
-    requests = jnp.clip(requests, 0, devices - 1)
-    moved = deliver(pick_pieces(requests, held), devices)
-    far = [m.reshape(2, SLOTS, piece_rows, HEAD_SIZE) for m in moved]
-    early, late = far[: len(far) // 2], far[len(far) // 2 :]
-    if piece_rows % 16 != 0:
-        early, late = [jnp.concatenate(early, axis=2)], [jnp.concatenate(late, axis=2)]
-    own, level = far_attention(selected, queries, own, level, early, last=False)
-    return far_attention(selected, queries, own, level, late, last=True)
+    requests = jnp.clip(exchange_requests(mine, run, devices), 0, devices - 1)
+
+    keys_over, own, level = lax.optimization_barrier((keys_over, own, level))
+    keys_over = trade(cut([keys_over], run), devices)
+    half = KEY_VALUE_HEADS * piece_rows
+    far_keys = trade(pick_pieces(requests, near, keys_over, 0), devices)
+
+    values_over = trade(cut([values_over], run), devices)
+    far_values = trade(pick_pieces(requests, near, values_over, half), devices)
+
+    shape = (2, KEY_VALUE_HEADS, piece_rows, HEAD_SIZE)
+    order = [0, *delivery_order(run)]
+    parts = []
+    for steps in (order[: run // 2], order[run // 2 :]):
+        both = []
+        for pieces in (far_keys, far_values):
+            pieces = [pieces[step].reshape(shape) for step in steps]
+            both += [jnp.concatenate(pieces, axis=2)] if piece_rows % 16 != 0 else pieces
+        parts.append(both)
+    own, level = far_attention(selected, queries, own, level, parts[0], last=False)
+    return far_attention(selected, queries, own, level, parts[1], last=True)
 
 
 def solution(mesh):

time: 60.7 us -> 97.7 us (1.61)
  the two profiles are of different devices: /device:TPU:1 before, /device:TPU:5 now
where the time goes in v9:
time: 97.7 us; the launch traced here: 96.9 us
  starting transfers between devices  61.8 us (63%)
  Pallas kernels  24.5 us (25%)
  waiting for transfers between devices  5.67 us (6%)
  local copies, waits for them, and re-layouts  4.36 us (4%)
    ppermute x38, starting transfers between devices, swap(): lax.ppermute(array, 'ctx', [(i, partner(i, step)) for i in range(devices)])  53.2 us
    pallas_call x2, Pallas kernels, far_attention(): pl.pallas_call(functools.partial(far_kernel, last=last), out_shape=out_sh...  16 us
    pallas_call x1, Pallas kernels, own_attention(): pl.pallas_call(own_kernel, out_shape=[pltpu.HBM(queries.shape, jnp.float3...  5.94 us
    ppermute x38, waiting for transfers between devices, swap(): lax.ppermute(array, 'ctx', [(i, partner(i, step)) for i in range(devices)])  5.66 us
    ppermute x1, starting transfers between devices, local(): values_over = lax.ppermute(values_next, 'ctx', upward)  4.3 us
    ppermute x1, starting transfers between devices, local(): keys_over = lax.ppermute(all_key_states, 'ctx', upward)  4.22 us
    unnamed x10, local copies, waits for them, and re-layouts  3.53 us
  transfers between devices with their start and end apart: 40, of which 4 were waited for; matrix products, arithmetic and copies ran while one was open for 1% of the time, Pallas kernels for 21%

profile of v9, /device:TPU:5, one launch (start us, length us, event | category | flops | bytes accessed | tf_op | source)
XLA Modules:
  0.0 96.9 jit_solution(4411443645472973666)
XLA Ops:
  0.0 4.2 %collective-permute-start = (bf16[256,512]{1,0:T(8,128)(2,1)}, bf16[256,512]{1,0:T(8,128)(2,1)S(1)}, u32[]{:S(2)}, u32[]{:S(2)}) collective-permute-start(bf16[256,512]{1,0:T(8,128)(2,1)} %key_ref.1), channel_id=1, source_target_pairs={{0,8},{1,9},{2,10},{3,11},{4,12},{5,13},{6,14},{7,15},{16,24},{17,... | collective-permute-start | bytes 786440 | tf_op jit(solution)/shard_map/ppermute | solution.py:411
  8.0 1.2 %collective-permute-start.5 = (bf16[256,128]{1,0:T(8,128)(2,1)S(1)}, bf16[256,128]{1,0:T(8,128)(2,1)S(1)}, u32[]{:S(2)}, u32[]{:S(2)}) collective-permute-start(bf16[256,128]{1,0:T(8,128)(2,1)S(1)} %get-tuple-element.81), channel_id=1, source_target_pairs={{0,2},{1,3},{2,0},{3,1},{4,6},{5,7},{6,4},{7,5},{8,10},{9,11},{10,... | collective-permute-start | bytes 196616 | tf_op jit(solution)/shard_map/ppermute | solution.py:23
  10.1 4.3 %collective-permute-start.21 = (bf16[256,512]{1,0:T(8,128)(2,1)}, bf16[256,512]{1,0:T(8,128)(2,1)S(1)}, u32[]{:S(2)}, u32[]{:S(2)}) collective-permute-start(bf16[256,512]{1,0:T(8,128)(2,1)} %value_ref.1), channel_id=1, source_target_pairs={{0,8},{1,9},{2,10},{3,11},{4,12},{5,13},{6,14},{7,15},{16,24},{17,... | collective-permute-start | bytes 786440 | tf_op jit(solution)/shard_map/ppermute | solution.py:413
  14.5 1.2 %collective-permute-start.2 = (s32[2,2]{0,1:T(2,128)S(1)}, s32[2,2]{0,1:T(2,128)S(1)}, u32[]{:S(2)}, u32[]{:S(2)}) collective-permute-start(s32[2,2]{0,1:T(2,128)S(1)} %pad_add_fusion), channel_id=1, source_target_pairs={{0,2},{1,3},{2,0},{3,1},{4,6},{5,7},{6,4},{7,5},{8,10},{9,11},{10,... | collective-permute-start | bytes 56 | tf_op jit(solution)/shard_map/ppermute | solution.py:23
  15.7 1.2 %collective-permute-done.2 = s32[2,2]{0,1:T(2,128)S(1)} collective-permute-done((s32[2,2]{0,1:T(2,128)S(1)}, s32[2,2]{0,1:T(2,128)S(1)}, u32[]{:S(2)}, u32[]{:S(2)}) %collective-permute-start.2) | collective-permute-done | bytes 48 | tf_op jit(solution)/shard_map/ppermute | solution.py:23
  17.0 13.4 %collective-permute-start.3 = (s32[4,2]{0,1:T(2,128)S(1)}, s32[4,2]{0,1:T(2,128)S(1)}, u32[]{:S(2)}, u32[]{:S(2)}) collective-permute-start(s32[4,2]{0,1:T(2,128)S(1)} %pad_add_fusion.1), channel_id=1, source_target_pairs={{0,4},{1,5},{2,6},{3,7},{4,0},{5,1},{6,2},{7,3},{8,12},{9,13},{10,... | collective-permute-start | bytes 104 | tf_op jit(solution)/shard_map/ppermute | solution.py:23
  31.4 1.5 %collective-permute-start.7 = (bf16[256,128]{1,0:T(8,128)(2,1)S(1)}, bf16[256,128]{1,0:T(8,128)(2,1)S(1)}, u32[]{:S(2)}, u32[]{:S(2)}) collective-permute-start(bf16[256,128]{1,0:T(8,128)(2,1)S(1)} %get-tuple-element.83), channel_id=1, source_target_pairs={{0,4},{1,5},{2,6},{3,7},{4,0},{5,1},{6,2},{7,3},{8,12},{9,13},{10,... | collective-permute-start | bytes 196616 | tf_op jit(solution)/shard_map/ppermute | solution.py:23
  32.9 3.0 %collective-permute-start.8 = (bf16[256,128]{1,0:T(8,128)(2,1)S(1)}, bf16[256,128]{1,0:T(8,128)(2,1)S(1)}, u32[]{:S(2)}, u32[]{:S(2)}) collective-permute-start(bf16[256,128]{1,0:T(8,128)(2,1)S(1)} %get-tuple-element.84), channel_id=1, source_target_pairs={{0,5},{1,4},{2,7},{3,6},{4,1},{5,0},{6,3},{7,2},{8,13},{9,12},{10,... | collective-permute-start | bytes 196616 | tf_op jit(solution)/shard_map/ppermute | solution.py:23
  35.9 2.6 %collective-permute-start.9 = (bf16[256,128]{1,0:T(8,128)(2,1)S(1)}, bf16[256,128]{1,0:T(8,128)(2,1)S(1)}, u32[]{:S(2)}, u32[]{:S(2)}) collective-permute-start(bf16[256,128]{1,0:T(8,128)(2,1)S(1)} %get-tuple-element.85), channel_id=1, source_target_pairs={{0,6},{1,7},{2,4},{3,5},{4,2},{5,3},{6,0},{7,1},{8,14},{9,15},{10,... | collective-permute-start | bytes 196616 | tf_op jit(solution)/shard_map/ppermute | solution.py:23
  38.8 1.6 %copy-done = bf16[256,4096]{1,0:T(8,128)(2,1)S(1)} copy-done((bf16[256,4096]{1,0:T(8,128)(2,1)S(1)}, bf16[256,4096]{1,0:T(8,128)(2,1)}, u32[]{:S(2)}) %copy-start) | copy-done | bytes 2097176
  41.4 5.9 %own_attention.1 = (f32[256,4096]{1,0:T(8,128)}, f32[256,512]{1,0:T(8,128)}) custom-call(bf16[256,4096]{1,0:T(8,128)(2,1)S(1)} %copy-done, bf16[256,512]{1,0:T(8,128)(2,1)S(1)} %copy-done.3, bf16[256,512]{1,0:T(8,128)(2,1)} %value_ref.1), custom_call_target="tpu_custom_call" | custom-call | flops 1073741824 | bytes 7340032 | tf_op jit(solution)/shard_map/own_attention/pallas_call | solution.py:178
  47.6 1.2 %collective-permute-start.12 = (bf16[128,128]{1,0:T(8,128)(2,1)S(1)}, bf16[128,128]{1,0:T(8,128)(2,1)S(1)}, u32[]{:S(2)}, u32[]{:S(2)}) collective-permute-start(bf16[128,128]{1,0:T(8,128)(2,1)S(1)} %get-tuple-element.90), channel_id=1, source_target_pairs={{0,2},{1,3},{2,0},{3,1},{4,6},{5,7},{6,4},{7,5},{8,10},{9,11},{10,... | collective-permute-start | bytes 98312 | tf_op jit(solution)/shard_map/ppermute | solution.py:23
  49.7 1.2 %collective-permute-start.14 = (bf16[128,128]{1,0:T(8,128)(2,1)S(1)}, bf16[128,128]{1,0:T(8,128)(2,1)S(1)}, u32[]{:S(2)}, u32[]{:S(2)}) collective-permute-start(bf16[128,128]{1,0:T(8,128)(2,1)S(1)} %get-tuple-element.92), channel_id=1, source_target_pairs={{0,4},{1,5},{2,6},{3,7},{4,0},{5,1},{6,2},{7,3},{8,12},{9,13},{10,... | collective-permute-start | bytes 98312 | tf_op jit(solution)/shard_map/ppermute | solution.py:23
  51.3 2.3 %collective-permute-start.16 = (bf16[128,128]{1,0:T(8,128)(2,1)S(1)}, bf16[128,128]{1,0:T(8,128)(2,1)S(1)}, u32[]{:S(2)}, u32[]{:S(2)}) collective-permute-start(bf16[128,128]{1,0:T(8,128)(2,1)S(1)} %get-tuple-element.94), channel_id=1, source_target_pairs={{0,6},{1,7},{2,4},{3,5},{4,2},{5,3},{6,0},{7,1},{8,14},{9,15},{10,... | collective-permute-start | bytes 98312 | tf_op jit(solution)/shard_map/ppermute | solution.py:23
  54.3 1.2 %collective-permute-start.23 = (bf16[128,128]{1,0:T(8,128)(2,1)S(1)}, bf16[128,128]{1,0:T(8,128)(2,1)S(1)}, u32[]{:S(2)}, u32[]{:S(2)}) collective-permute-start(bf16[128,128]{1,0:T(8,128)(2,1)S(1)} %get-tuple-element.103), channel_id=1, source_target_pairs={{0,2},{1,3},{2,0},{3,1},{4,6},{5,7},{6,4},{7,5},{8,10},{9,11},{10,... | collective-permute-start | bytes 98312 | tf_op jit(solution)/shard_map/ppermute | solution.py:23
  58.8 1.6 %collective-permute-start.27 = (bf16[128,128]{1,0:T(8,128)(2,1)S(1)}, bf16[128,128]{1,0:T(8,128)(2,1)S(1)}, u32[]{:S(2)}, u32[]{:S(2)}) collective-permute-start(bf16[128,128]{1,0:T(8,128)(2,1)S(1)} %get-tuple-element.107), channel_id=1, source_target_pairs={{0,6},{1,7},{2,4},{3,5},{4,2},{5,3},{6,0},{7,1},{8,14},{9,15},{10,... | collective-permute-start | bytes 98312 | tf_op jit(solution)/shard_map/ppermute | solution.py:23
  62.6 1.4 %collective-permute-start.32 = (bf16[2,128,128]{2,1,0:T(8,128)(2,1)S(1)}, bf16[2,128,128]{2,1,0:T(8,128)(2,1)S(1)}, u32[]{:S(2)}, u32[]{:S(2)}) collective-permute-start(bf16[2,128,128]{2,1,0:T(8,128)(2,1)S(1)} %get-tuple-element.115), channel_id=1, source_target_pairs={{0,5},{1,4},{2,7},{3,6},{4,1},{5,0},{6,3},{7,2},{8,13},{9,12},{10,... | collective-permute-start | bytes 196616 | tf_op jit(solution)/shard_map/ppermute | solution.py:23
  65.1 3.1 %collective-permute-done.28.refs_15_ = bf16[128,128]{1,0:T(8,128)(2,1)S(1)} collective-permute-done((bf16[128,128]{1,0:T(8,128)(2,1)S(1)}, bf16[128,128]{1,0:T(8,128)(2,1)S(1)}, u32[]{:S(2)}, u32[]{:S(2)}) %collective-permute-start.28) | collective-permute-done | bytes 32800 | tf_op jit(solution)/shard_map/ppermute | solution.py:23
  69.8 1.9 %collective-permute-start.34 = (bf16[2,128,128]{2,1,0:T(8,128)(2,1)S(1)}, bf16[2,128,128]{2,1,0:T(8,128)(2,1)S(1)}, u32[]{:S(2)}, u32[]{:S(2)}) collective-permute-start(bf16[2,128,128]{2,1,0:T(8,128)(2,1)S(1)} %get-tuple-element.117), channel_id=1, source_target_pairs={{0,6},{1,7},{2,4},{3,5},{4,2},{5,3},{6,0},{7,1},{8,14},{9,15},{10,... | collective-permute-start | bytes 196616 | tf_op jit(solution)/shard_map/ppermute | solution.py:23
  73.4 1.8 %collective-permute-start.35 = (bf16[2,128,128]{2,1,0:T(8,128)(2,1)S(1)}, bf16[2,128,128]{2,1,0:T(8,128)(2,1)S(1)}, u32[]{:S(2)}, u32[]{:S(2)}) collective-permute-start(bf16[2,128,128]{2,1,0:T(8,128)(2,1)S(1)} %get-tuple-element.118), channel_id=1, source_target_pairs={{0,7},{1,6},{2,5},{3,4},{4,3},{5,2},{6,1},{7,0},{8,15},{9,14},{10,... | collective-permute-start | bytes 196616 | tf_op jit(solution)/shard_map/ppermute | solution.py:23
  76.9 1.3 %collective-permute-start.38 = (bf16[2,128,128]{2,1,0:T(8,128)(2,1)S(1)}, bf16[2,128,128]{2,1,0:T(8,128)(2,1)S(1)}, u32[]{:S(2)}, u32[]{:S(2)}) collective-permute-start(bf16[2,128,128]{2,1,0:T(8,128)(2,1)S(1)} %get-tuple-element.121), channel_id=1, source_target_pairs={{0,6},{1,7},{2,4},{3,5},{4,2},{5,3},{6,0},{7,1},{8,14},{9,15},{10,... | collective-permute-start | bytes 196616 | tf_op jit(solution)/shard_map/ppermute | solution.py:23
  78.2 2.4 %collective-permute-start.39 = (bf16[2,128,128]{2,1,0:T(8,128)(2,1)S(1)}, bf16[2,128,128]{2,1,0:T(8,128)(2,1)S(1)}, u32[]{:S(2)}, u32[]{:S(2)}) collective-permute-start(bf16[2,128,128]{2,1,0:T(8,128)(2,1)S(1)} %get-tuple-element.122), channel_id=1, source_target_pairs={{0,7},{1,6},{2,5},{3,4},{4,3},{5,2},{6,1},{7,0},{8,15},{9,14},{10,... | collective-permute-start | bytes 196616 | tf_op jit(solution)/shard_map/ppermute | solution.py:23
  80.6 12.2 %early_attention.1 = (f32[256,4096]{1,0:T(8,128)S(1)}, f32[256,4096]{1,0:T(8,128)S(1)}) custom-call(s32[1,2]{1,0:T(1,128)S(1)} %copy-done.4, bf16[256,4096]{1,0:T(8,128)(2,1)S(1)} %copy-done.1, f32[256,4096]{1,0:T(8,128)} %get-tuple-element.76.own_in, f32[256,512]{1,0:T(8,128)} %get-tuple-element.77.level_in, bf16[2,4,32,128]{3,2,1,0:T(8,128)(2,1)S(1)} %bitcast.24, ...), custom_call_target="tpu_custom_call" | custom-call | flops 1073741824 | bytes 10485760 | tf_op jit(solution)/shard_map/early_attention/pallas_call | solution.py:384
  92.9 3.8 %late_attention.1 = bf16[256,4096]{1,0:T(8,128)(2,1)} custom-call(s32[1,2]{1,0:T(1,128)S(1)} %copy-done.4, bf16[256,4096]{1,0:T(8,128)(2,1)S(1)} %copy-done.1, f32[256,4096]{1,0:T(8,128)S(1)} %get-tuple-element.113.own_in, f32[256,4096]{1,0:T(8,128)S(1)} %get-tuple-element.114.level_in, bf16[2,4,32,128]{3,2,1,0:T(8,128)(2,1)S(1)} %bitcast.16, ...), custom_call_target="tpu_custom_call" | custom-call | flops 1073741824 | bytes 10485760 | tf_op jit(solution)/shard_map/late_attention/pallas_call | solution.py:384
  (80 shorter events, 20.9 us)
Async XLA Ops:
  0.0 10.1 %collective-permute-start = (bf16[256,512]{1,0:T(8,128)(2,1)}, bf16[256,512]{1,0:T(8,128)(2,1)S(1)}, u32[]{:S(2)}, u32[]{:S(2)}) collective-permute-start(bf16[256,512]{1,0:T(8,128)(2,1)} %key_ref.1), channel_id=1, source_target_pairs={{0,8},{1,9},{2,10},{3,11},{4,12},{5,13},{6,14},{7,15},{16,24},{17,... | collective-permute-start | bytes 786440 | tf_op jit(solution)/shard_map/ppermute | solution.py:411
  7.0 7.4 %collective-permute-start.1 = (s32[1,2]{0,1:T(2,128)S(1)}, s32[1,2]{0,1:T(2,128)S(1)}, u32[]{:S(2)}, u32[]{:S(2)}) collective-permute-start(s32[1,2]{0,1:T(2,128)S(1)} %copy.8), channel_id=1, source_target_pairs={{0,1},{1,0},{2,3},{3,2},{4,5},{5,4},{6,7},{7,6},{8,9},{9,8},{10,11... | collective-permute-start | bytes 32 | tf_op jit(solution)/shard_map/ppermute | solution.py:23
  8.0 24.9 %collective-permute-start.4 = (bf16[256,128]{1,0:T(8,128)(2,1)S(1)}, bf16[256,128]{1,0:T(8,128)(2,1)S(1)}, u32[]{:S(2)}, u32[]{:S(2)}) collective-permute-start(bf16[256,128]{1,0:T(8,128)(2,1)S(1)} %get-tuple-element.80), channel_id=1, source_target_pairs={{0,1},{1,0},{2,3},{3,2},{4,5},{5,4},{6,7},{7,6},{8,9},{9,8},{10,11... | collective-permute-start | bytes 196616 | tf_op jit(solution)/shard_map/ppermute | solution.py:23
  8.0 27.9 %collective-permute-start.5 = (bf16[256,128]{1,0:T(8,128)(2,1)S(1)}, bf16[256,128]{1,0:T(8,128)(2,1)S(1)}, u32[]{:S(2)}, u32[]{:S(2)}) collective-permute-start(bf16[256,128]{1,0:T(8,128)(2,1)S(1)} %get-tuple-element.81), channel_id=1, source_target_pairs={{0,2},{1,3},{2,0},{3,1},{4,6},{5,7},{6,4},{7,5},{8,10},{9,11},{10,... | collective-permute-start | bytes 196616 | tf_op jit(solution)/shard_map/ppermute | solution.py:23
  9.2 29.3 %collective-permute-start.6 = (bf16[256,128]{1,0:T(8,128)(2,1)S(1)}, bf16[256,128]{1,0:T(8,128)(2,1)S(1)}, u32[]{:S(2)}, u32[]{:S(2)}) collective-permute-start(bf16[256,128]{1,0:T(8,128)(2,1)S(1)} %get-tuple-element.82), channel_id=1, source_target_pairs={{0,3},{1,2},{2,1},{3,0},{4,7},{5,6},{6,5},{7,4},{8,11},{9,10},{10,... | collective-permute-start | bytes 196616 | tf_op jit(solution)/shard_map/ppermute | solution.py:23
  10.1 38.6 %collective-permute-start.21 = (bf16[256,512]{1,0:T(8,128)(2,1)}, bf16[256,512]{1,0:T(8,128)(2,1)S(1)}, u32[]{:S(2)}, u32[]{:S(2)}) collective-permute-start(bf16[256,512]{1,0:T(8,128)(2,1)} %value_ref.1), channel_id=1, source_target_pairs={{0,8},{1,9},{2,10},{3,11},{4,12},{5,13},{6,14},{7,15},{16,24},{17,... | collective-permute-start | bytes 786440 | tf_op jit(solution)/shard_map/ppermute | solution.py:413
  17.0 14.4 %collective-permute-start.3 = (s32[4,2]{0,1:T(2,128)S(1)}, s32[4,2]{0,1:T(2,128)S(1)}, u32[]{:S(2)}, u32[]{:S(2)}) collective-permute-start(s32[4,2]{0,1:T(2,128)S(1)} %pad_add_fusion.1), channel_id=1, source_target_pairs={{0,4},{1,5},{2,6},{3,7},{4,0},{5,1},{6,2},{7,3},{8,12},{9,13},{10,... | collective-permute-start | bytes 104 | tf_op jit(solution)/shard_map/ppermute | solution.py:23
  31.4 16.0 %collective-permute-start.7 = (bf16[256,128]{1,0:T(8,128)(2,1)S(1)}, bf16[256,128]{1,0:T(8,128)(2,1)S(1)}, u32[]{:S(2)}, u32[]{:S(2)}) collective-permute-start(bf16[256,128]{1,0:T(8,128)(2,1)S(1)} %get-tuple-element.83), channel_id=1, source_target_pairs={{0,4},{1,5},{2,6},{3,7},{4,0},{5,1},{6,2},{7,3},{8,12},{9,13},{10,... | collective-permute-start | bytes 196616 | tf_op jit(solution)/shard_map/ppermute | solution.py:23
  32.9 14.7 %collective-permute-start.8 = (bf16[256,128]{1,0:T(8,128)(2,1)S(1)}, bf16[256,128]{1,0:T(8,128)(2,1)S(1)}, u32[]{:S(2)}, u32[]{:S(2)}) collective-permute-start(bf16[256,128]{1,0:T(8,128)(2,1)S(1)} %get-tuple-element.84), channel_id=1, source_target_pairs={{0,5},{1,4},{2,7},{3,6},{4,1},{5,0},{6,3},{7,2},{8,13},{9,12},{10,... | collective-permute-start | bytes 196616 | tf_op jit(solution)/shard_map/ppermute | solution.py:23
  35.9 13.8 %collective-permute-start.9 = (bf16[256,128]{1,0:T(8,128)(2,1)S(1)}, bf16[256,128]{1,0:T(8,128)(2,1)S(1)}, u32[]{:S(2)}, u32[]{:S(2)}) collective-permute-start(bf16[256,128]{1,0:T(8,128)(2,1)S(1)} %get-tuple-element.85), channel_id=1, source_target_pairs={{0,6},{1,7},{2,4},{3,5},{4,2},{5,3},{6,0},{7,1},{8,14},{9,15},{10,... | collective-permute-start | bytes 196616 | tf_op jit(solution)/shard_map/ppermute | solution.py:23
  38.5 12.3 %collective-permute-start.10 = (bf16[256,128]{1,0:T(8,128)(2,1)S(1)}, bf16[256,128]{1,0:T(8,128)(2,1)S(1)}, u32[]{:S(2)}, u32[]{:S(2)}) collective-permute-start(bf16[256,128]{1,0:T(8,128)(2,1)S(1)} %get-tuple-element.86), channel_id=1, source_target_pairs={{0,7},{1,6},{2,5},{3,4},{4,3},{5,2},{6,1},{7,0},{8,15},{9,14},{10,... | collective-permute-start | bytes 196616 | tf_op jit(solution)/shard_map/ppermute | solution.py:23
  47.6 6.0 %collective-permute-start.12 = (bf16[128,128]{1,0:T(8,128)(2,1)S(1)}, bf16[128,128]{1,0:T(8,128)(2,1)S(1)}, u32[]{:S(2)}, u32[]{:S(2)}) collective-permute-start(bf16[128,128]{1,0:T(8,128)(2,1)S(1)} %get-tuple-element.90), channel_id=1, source_target_pairs={{0,2},{1,3},{2,0},{3,1},{4,6},{5,7},{6,4},{7,5},{8,10},{9,11},{10,... | collective-permute-start | bytes 98312 | tf_op jit(solution)/shard_map/ppermute | solution.py:23
  54.3 6.8 %collective-permute-start.23 = (bf16[128,128]{1,0:T(8,128)(2,1)S(1)}, bf16[128,128]{1,0:T(8,128)(2,1)S(1)}, u32[]{:S(2)}, u32[]{:S(2)}) collective-permute-start(bf16[128,128]{1,0:T(8,128)(2,1)S(1)} %get-tuple-element.103), channel_id=1, source_target_pairs={{0,2},{1,3},{2,0},{3,1},{4,6},{5,7},{6,4},{7,5},{8,10},{9,11},{10,... | collective-permute-start | bytes 98312 | tf_op jit(solution)/shard_map/ppermute | solution.py:23
  55.6 5.9 %collective-permute-start.24 = (bf16[128,128]{1,0:T(8,128)(2,1)S(1)}, bf16[128,128]{1,0:T(8,128)(2,1)S(1)}, u32[]{:S(2)}, u32[]{:S(2)}) collective-permute-start(bf16[128,128]{1,0:T(8,128)(2,1)S(1)} %get-tuple-element.104), channel_id=1, source_target_pairs={{0,3},{1,2},{2,1},{3,0},{4,7},{5,6},{6,5},{7,4},{8,11},{9,10},{10,... | collective-permute-start | bytes 98312 | tf_op jit(solution)/shard_map/ppermute | solution.py:23
  61.1 8.7 %collective-permute-start.18 = (bf16[2,128,128]{2,1,0:T(8,128)(2,1)S(1)}, bf16[2,128,128]{2,1,0:T(8,128)(2,1)S(1)}, u32[]{:S(2)}, u32[]{:S(2)}) collective-permute-start(bf16[2,128,128]{2,1,0:T(8,128)(2,1)S(1)} %get-tuple-element.97), channel_id=1, source_target_pairs={{0,1},{1,0},{2,3},{3,2},{4,5},{5,4},{6,7},{7,6},{8,9},{9,8},{10,11... | collective-permute-start | bytes 196616 | tf_op jit(solution)/shard_map/ppermute | solution.py:23
  61.4 10.2 %collective-permute-start.19 = (bf16[2,128,128]{2,1,0:T(8,128)(2,1)S(1)}, bf16[2,128,128]{2,1,0:T(8,128)(2,1)S(1)}, u32[]{:S(2)}, u32[]{:S(2)}) collective-permute-start(bf16[2,128,128]{2,1,0:T(8,128)(2,1)S(1)} %get-tuple-element.98), channel_id=1, source_target_pairs={{0,4},{1,5},{2,6},{3,7},{4,0},{5,1},{6,2},{7,3},{8,12},{9,13},{10,... | collective-permute-start | bytes 196616 | tf_op jit(solution)/shard_map/ppermute | solution.py:23
  61.8 10.2 %collective-permute-start.20 = (bf16[2,128,128]{2,1,0:T(8,128)(2,1)S(1)}, bf16[2,128,128]{2,1,0:T(8,128)(2,1)S(1)}, u32[]{:S(2)}, u32[]{:S(2)}) collective-permute-start(bf16[2,128,128]{2,1,0:T(8,128)(2,1)S(1)} %get-tuple-element.99), channel_id=1, source_target_pairs={{0,2},{1,3},{2,0},{3,1},{4,6},{5,7},{6,4},{7,5},{8,10},{9,11},{10,... | collective-permute-start | bytes 196616 | tf_op jit(solution)/shard_map/ppermute | solution.py:23
  62.6 9.7 %collective-permute-start.32 = (bf16[2,128,128]{2,1,0:T(8,128)(2,1)S(1)}, bf16[2,128,128]{2,1,0:T(8,128)(2,1)S(1)}, u32[]{:S(2)}, u32[]{:S(2)}) collective-permute-start(bf16[2,128,128]{2,1,0:T(8,128)(2,1)S(1)} %get-tuple-element.115), channel_id=1, source_target_pairs={{0,5},{1,4},{2,7},{3,6},{4,1},{5,0},{6,3},{7,2},{8,13},{9,12},{10,... | collective-permute-start | bytes 196616 | tf_op jit(solution)/shard_map/ppermute | solution.py:23
  72.3 5.9 %collective-permute-start.31 = (bf16[2,128,128]{2,1,0:T(8,128)(2,1)S(1)}, bf16[2,128,128]{2,1,0:T(8,128)(2,1)S(1)}, u32[]{:S(2)}, u32[]{:S(2)}) collective-permute-start(bf16[2,128,128]{2,1,0:T(8,128)(2,1)S(1)} %get-tuple-element.112), channel_id=1, source_target_pairs={{0,2},{1,3},{2,0},{3,1},{4,6},{5,7},{6,4},{7,5},{8,10},{9,11},{10,... | collective-permute-start | bytes 196616 | tf_op jit(solution)/shard_map/ppermute | solution.py:23
  73.4 19.5 %collective-permute-start.35 = (bf16[2,128,128]{2,1,0:T(8,128)(2,1)S(1)}, bf16[2,128,128]{2,1,0:T(8,128)(2,1)S(1)}, u32[]{:S(2)}, u32[]{:S(2)}) collective-permute-start(bf16[2,128,128]{2,1,0:T(8,128)(2,1)S(1)} %get-tuple-element.118), channel_id=1, source_target_pairs={{0,7},{1,6},{2,5},{3,4},{4,3},{5,2},{6,1},{7,0},{8,15},{9,14},{10,... | collective-permute-start | bytes 196616 | tf_op jit(solution)/shard_map/ppermute | solution.py:23
  75.3 17.6 %collective-permute-start.36 = (bf16[2,128,128]{2,1,0:T(8,128)(2,1)S(1)}, bf16[2,128,128]{2,1,0:T(8,128)(2,1)S(1)}, u32[]{:S(2)}, u32[]{:S(2)}) collective-permute-start(bf16[2,128,128]{2,1,0:T(8,128)(2,1)S(1)} %get-tuple-element.119), channel_id=1, source_target_pairs={{0,5},{1,4},{2,7},{3,6},{4,1},{5,0},{6,3},{7,2},{8,13},{9,12},{10,... | collective-permute-start | bytes 196616 | tf_op jit(solution)/shard_map/ppermute | solution.py:23
  76.0 16.9 %collective-permute-start.37 = (bf16[2,128,128]{2,1,0:T(8,128)(2,1)S(1)}, bf16[2,128,128]{2,1,0:T(8,128)(2,1)S(1)}, u32[]{:S(2)}, u32[]{:S(2)}) collective-permute-start(bf16[2,128,128]{2,1,0:T(8,128)(2,1)S(1)} %get-tuple-element.120), channel_id=1, source_target_pairs={{0,3},{1,2},{2,1},{3,0},{4,7},{5,6},{6,5},{7,4},{8,11},{9,10},{10,... | collective-permute-start | bytes 196616 | tf_op jit(solution)/shard_map/ppermute | solution.py:23
  76.9 16.0 %collective-permute-start.38 = (bf16[2,128,128]{2,1,0:T(8,128)(2,1)S(1)}, bf16[2,128,128]{2,1,0:T(8,128)(2,1)S(1)}, u32[]{:S(2)}, u32[]{:S(2)}) collective-permute-start(bf16[2,128,128]{2,1,0:T(8,128)(2,1)S(1)} %get-tuple-element.121), channel_id=1, source_target_pairs={{0,6},{1,7},{2,4},{3,5},{4,2},{5,3},{6,0},{7,1},{8,14},{9,15},{10,... | collective-permute-start | bytes 196616 | tf_op jit(solution)/shard_map/ppermute | solution.py:23
  78.2 14.7 %collective-permute-start.39 = (bf16[2,128,128]{2,1,0:T(8,128)(2,1)S(1)}, bf16[2,128,128]{2,1,0:T(8,128)(2,1)S(1)}, u32[]{:S(2)}, u32[]{:S(2)}) collective-permute-start(bf16[2,128,128]{2,1,0:T(8,128)(2,1)S(1)} %get-tuple-element.122), channel_id=1, source_target_pairs={{0,7},{1,6},{2,5},{3,4},{4,3},{5,2},{6,1},{7,0},{8,15},{9,14},{10,... | collective-permute-start | bytes 196616 | tf_op jit(solution)/shard_map/ppermute | solution.py:23
  (21 other events, 192.8 us)

commit v10 on v7

--- a/solution.py
+++ b/solution.py
@@ -92,23 +92,22 @@
     return requests
 
 
-def pick_kernel(requests_ref, held_ref, *out_refs):
-    for step, out_ref in enumerate(out_refs):
+def pick_kernel(requests_ref, held_ref, *out_refs, steps):
+    for step, out_ref in zip(steps, out_refs):
         for pick in range(2):
             out_ref[pick] = held_ref[requests_ref[step, pick]]
 
 
-def pick_pieces(requests, held):
-    devices, rows, _ = held.shape
-    shares = devices // COPIES
+def pick_pieces(requests, held, steps):
+    rows = held.shape[1]
     return pl.pallas_call(
-        pick_kernel,
-        out_shape=[jax.ShapeDtypeStruct((2, rows, HEAD_SIZE), jnp.bfloat16)] * shares,
+        functools.partial(pick_kernel, steps=steps),
+        out_shape=[jax.ShapeDtypeStruct((2, rows, HEAD_SIZE), jnp.bfloat16)] * len(steps),
         in_specs=[
             pl.BlockSpec(memory_space=pltpu.SMEM),
             pl.BlockSpec(memory_space=pltpu.VMEM),
         ],
-        out_specs=[pl.BlockSpec(memory_space=pltpu.VMEM)] * shares,
+        out_specs=[pl.BlockSpec(memory_space=pltpu.VMEM)] * len(steps),
         compiler_params=pltpu.CompilerParams(vmem_limit_bytes=16 * MIB),
         name="pick_pieces",
     )(requests, held)
@@ -116,17 +115,28 @@
 
 def delivery_order(shares):
     half, quarter = shares // 2, shares // 4
-    apart = zip(range(half, half + quarter), range(quarter, half))
-    return [*range(1, quarter), *[s for pair in apart for s in pair], *range(half + quarter, shares)]
-
-
-def deliver(pieces, devices):
-    order = delivery_order(len(pieces))
-    return [pieces[0]] + [swap(pieces[step], step, devices) for step in order]
+    return [
+        *range(1, quarter),
+        *range(half, half + quarter),
+        *range(quarter, half),
+        *range(half + quarter, shares),
+    ]
+
+
+def deliver(requests, held):
+    devices = held.shape[0]
+    order = delivery_order(devices // COPIES)
+    early, late = order[: len(order) // 2], [*order[len(order) // 2 :], 0]
+    moved = []
+    for steps in (early, late):
+        pieces = pick_pieces(requests, held, steps)
+        moved += [p if s == 0 else swap(p, s, devices) for s, p in zip(steps, pieces)]
+    return [moved[-1], *moved[:-1]]
 
 
 FACTOR = math.log2(math.e) / math.sqrt(HEAD_SIZE)
 PAIR = 2
+SENT = 4
 LARGE_SUM = 2.0**100
 
 
@@ -246,9 +256,13 @@
             source.at[:, lanes], target.at[:, lanes], sems.at[which, group]
         )
 
-    def send(group):
-        lanes = wide(group)
-        return pltpu.make_async_copy(staged.at[:, lanes], out_ref.at[:, lanes], sems.at[group])
+    def send(part):
+        start = part * SENT * HEAD_SIZE
+        fixed = isinstance(part, int)
+        lanes = pl.ds(
+            start if fixed else pl.multiple_of(start, SENT * HEAD_SIZE), SENT * HEAD_SIZE
+        )
+        return pltpu.make_async_copy(staged.at[:, lanes], out_ref.at[:, lanes], sems.at[part])
 
     if not last:
         for group in range(KEY_VALUE_HEADS):
@@ -319,21 +333,24 @@
                 fetch(group, 1).wait()
                 fetch(group, 0).wait()
             largest = quick(group, head, scores, held[group][1], largest)
-            if head == GROUP - 1 and last:
-                send(group).start()
+            if (head + 1) % SENT == 0 and last:
+                send((group * GROUP + head) // SENT).start()
             scores = following
 
         @pl.when(jnp.max(largest) > LARGE_SUM)
         def _():
             @pl.loop(0, KEY_VALUE_HEADS)
             def _(group):
+                parts = [group * (GROUP // SENT) + part for part in range(GROUP // SENT)]
                 if last:
-                    send(group).wait()
+                    for part in parts:
+                        send(part).wait()
                 keys_across, value = keys_and_values(group)
                 for head in range(GROUP):
                     careful(group, head, score(group, head, keys_across), value)
                 if last:
-                    send(group).start()
+                    for part in parts:
+                        send(part).start()
 
     my_block = lax.axis_index("ctx")
     chosen = selected_ref[0, 0], selected_ref[0, 1]
@@ -356,7 +373,8 @@
             lanes = wide(group)
             if last:
                 staged[:, lanes] = own_ref[:, lanes].astype(staged.dtype)
-                send(group).start()
+                for part in range(GROUP // SENT):
+                    send(group * (GROUP // SENT) + part).start()
             else:
                 fetch(group, 1).wait()
                 fetch(group, 0).wait()
@@ -366,9 +384,9 @@
 
     if last:
 
-        @pl.loop(0, KEY_VALUE_HEADS)
-        def _(group):
-            send(group).wait()
+        @pl.loop(0, QUERY_HEADS // SENT)
+        def _(part):
+            send(part).wait()
 
 
 def far_attention(selected, queries, own, level, far, last):
@@ -382,7 +400,7 @@
         out_specs = anywhere
         scratch = [
             pltpu.VMEM(queries.shape, jnp.bfloat16),
-            pltpu.SemaphoreType.DMA((KEY_VALUE_HEADS,)),
+            pltpu.SemaphoreType.DMA((QUERY_HEADS // SENT,)),
         ]
     else:
         earlier = anywhere
@@ -426,7 +444,7 @@
     mine, own, level = lax.optimization_barrier((selected, own, level))
     requests = exchange_requests(mine, devices // COPIES, devices)
     requests = jnp.clip(requests, 0, devices - 1)
-    moved = deliver(pick_pieces(requests, held), devices)
+    moved = deliver(requests, held)
     far = [m.reshape(2, SLOTS, piece_rows, HEAD_SIZE) for m in moved]
     early, late = far[: len(far) // 2], far[len(far) // 2 :]
     if piece_rows % 16 != 0:

time: 60.7 us -> 60.7 us (level)
  the two profiles are of different devices: /device:TPU:1 before, /device:TPU:5 now
where the time goes in v10:
time: 60.7 us; the launch traced here: 59.5 us
  Pallas kernels  24.4 us (40%)
  starting transfers between devices  19.7 us (32%)
  waiting for transfers between devices  11.2 us (18%)
  local copies, waits for them, and re-layouts  3.67 us (6%)
    pallas_call x2, Pallas kernels, far_attention(): pl.pallas_call(functools.partial(far_kernel, last=last), out_shape=out_sh...  16 us
    ppermute x10, starting transfers between devices, swap(): lax.ppermute(array, 'ctx', [(i, partner(i, step)) for i in range(devices)])  13.1 us
    all_to_all x1, starting transfers between devices, local(): lax.all_to_all(packed, 'ctx', split_axis=0, concat_axis=0, tiled=True)  6.64 us
    ppermute x10, waiting for transfers between devices, swap(): lax.ppermute(array, 'ctx', [(i, partner(i, step)) for i in range(devices)])  5.85 us
    all_to_all x1, waiting for transfers between devices, local(): lax.all_to_all(packed, 'ctx', split_axis=0, concat_axis=0, tiled=True)  5.31 us
    pallas_call x1, Pallas kernels, own_attention(): pl.pallas_call(own_kernel, out_shape=[pltpu.HBM(queries.shape, jnp.float3...  5.14 us
    unnamed x10, local copies, waits for them, and re-layouts  3.49 us
    pallas_call x1, Pallas kernels, pack(): pl.pallas_call(pack_kernel, out_shape=jax.ShapeDtypeStruct((devices, SLOT...  2.02 us
  transfers between devices with their start and end apart: 11, of which 4 were waited for; matrix products, arithmetic and copies ran while one was open for 1% of the time, Pallas kernels for 30%

profile of v10, /device:TPU:5, one launch (start us, length us, event | category | flops | bytes accessed | tf_op | source)
XLA Modules:
  0.0 59.5 jit_solution(17555162262657989375)
XLA Ops:
  0.0 2.0 %pack.1 = bf16[16,256,128]{2,1,0:T(8,128)(2,1)} custom-call(bf16[8,32,512]{2,1,0:T(8,128)(2,1)} %bitcast.10, bf16[8,32,512]{2,1,0:T(8,128)(2,1)} %bitcast.11), custom_call_target="tpu_custom_call" | custom-call | tf_op jit(solution)/shard_map/pack/pallas_call | solution.py:58
  2.0 6.6 %all-to-all-start = ((bf16[16,256,128]{2,1,0:T(8,128)(2,1)}), bf16[16,256,128]{2,1,0:T(8,128)(2,1)S(1)}, u32[]{:S(2)}, u32[]{:S(2)}) async-start(bf16[16,256,128]{2,1,0:T(8,128)(2,1)} %pack.1), calls=%async_computation | async-start | bytes 2097152 | tf_op jit(solution)/shard_map/all_to_all | solution.py:442
  8.7 1.6 %copy-done = bf16[256,4096]{1,0:T(8,128)(2,1)S(1)} copy-done((bf16[256,4096]{1,0:T(8,128)(2,1)S(1)}, bf16[256,4096]{1,0:T(8,128)(2,1)}, u32[]{:S(2)}) %copy-start) | copy-done | bytes 2097176
  10.3 0.9 %copy-done.2 = bf16[256,512]{1,0:T(8,128)(2,1)S(1)} copy-done((bf16[256,512]{1,0:T(8,128)(2,1)S(1)}, bf16[256,512]{1,0:T(8,128)(2,1)}, u32[]{:S(2)}) %copy-start.2) | copy-done | bytes 262168
  11.2 0.9 %copy-done.3 = bf16[256,512]{1,0:T(8,128)(2,1)S(1)} copy-done((bf16[256,512]{1,0:T(8,128)(2,1)S(1)}, bf16[256,512]{1,0:T(8,128)(2,1)}, u32[]{:S(2)}) %copy-start.3) | copy-done | bytes 262168
  12.2 5.1 %own_attention.1 = (f32[256,4096]{1,0:T(8,128)}, f32[256,512]{1,0:T(8,128)}) custom-call(bf16[256,4096]{1,0:T(8,128)(2,1)S(1)} %copy-done, bf16[256,512]{1,0:T(8,128)(2,1)S(1)} %copy-done.2, bf16[256,512]{1,0:T(8,128)(2,1)S(1)} %copy-done.3), custom_call_target="tpu_custom_call" | custom-call | flops 1073741824 | bytes 7340032 | tf_op jit(solution)/shard_map/own_attention/pallas_call | solution.py:204
  17.3 0.1 copy.8
  17.4 0.1 collective-permute-start
  17.5 1.0 %collective-permute-done = s32[1,2]{0,1:T(2,128)S(1)} collective-permute-done((s32[1,2]{0,1:T(2,128)S(1)}, s32[1,2]{0,1:T(2,128)S(1)}, u32[]{:S(2)}, u32[]{:S(2)}) %collective-permute-start) | collective-permute-done | bytes 40 | tf_op jit(solution)/shard_map/ppermute | solution.py:83
  18.6 1.4 %collective-permute-start.1 = (s32[2,2]{0,1:T(2,128)S(1)}, s32[2,2]{0,1:T(2,128)S(1)}, u32[]{:S(2)}, u32[]{:S(2)}) collective-permute-start(s32[2,2]{0,1:T(2,128)S(1)} %pad_add_fusion), channel_id=1, source_target_pairs={{0,2},{1,3},{2,0},{3,1},{4,6},{5,7},{6,4},{7,5},{8,10},{9,11},{10,... | collective-permute-start | bytes 56 | tf_op jit(solution)/shard_map/ppermute | solution.py:83
  20.1 1.3 %collective-permute-done.1 = s32[2,2]{0,1:T(2,128)S(1)} collective-permute-done((s32[2,2]{0,1:T(2,128)S(1)}, s32[2,2]{0,1:T(2,128)S(1)}, u32[]{:S(2)}, u32[]{:S(2)}) %collective-permute-start.1) | collective-permute-done | bytes 48 | tf_op jit(solution)/shard_map/ppermute | solution.py:83
  21.4 1.4 %collective-permute-start.2 = (s32[4,2]{0,1:T(2,128)S(1)}, s32[4,2]{0,1:T(2,128)S(1)}, u32[]{:S(2)}, u32[]{:S(2)}) collective-permute-start(s32[4,2]{0,1:T(2,128)S(1)} %pad_add_fusion.1), channel_id=1, source_target_pairs={{0,4},{1,5},{2,6},{3,7},{4,0},{5,1},{6,2},{7,3},{8,12},{9,13},{10,... | collective-permute-start | bytes 104 | tf_op jit(solution)/shard_map/ppermute | solution.py:83
  22.9 3.5 %collective-permute-done.2 = s32[4,2]{0,1:T(2,128)S(1)} collective-permute-done((s32[4,2]{0,1:T(2,128)S(1)}, s32[4,2]{0,1:T(2,128)S(1)}, u32[]{:S(2)}, u32[]{:S(2)}) %collective-permute-start.2) | collective-permute-done | bytes 64 | tf_op jit(solution)/shard_map/ppermute | solution.py:83
  26.5 5.3 %all-to-all-done.held_ref = bf16[16,256,128]{2,1,0:T(8,128)(2,1)S(1)} async-done(((bf16[16,256,128]{2,1,0:T(8,128)(2,1)}), bf16[16,256,128]{2,1,0:T(8,128)(2,1)S(1)}, u32[]{:S(2)}, u32[]{:S(2)}) %all-to-all-start) | async-done | bytes 1048608 | tf_op jit(solution)/shard_map/all_to_all | solution.py:442
  31.8 0.6 %pick_pieces.3 = (bf16[2,256,128]{2,1,0:T(8,128)(2,1)S(1)}, bf16[2,256,128]{2,1,0:T(8,128)(2,1)S(1)}, bf16[2,256,128]{2,1,0:T(8,128)(2,1)S(1)}) custom-call(s32[8,2]{1,0:T(8,128)S(1)} %broadcast_clamp_fusion.requests_ref, bf16[16,256,128]{2,1,0:T(8,128)(2,1)S(1)} %all-to-all-done.held_ref), custom_call_target="tpu_custom_call" | custom-call | tf_op jit(solution)/shard_map/pick_pieces/pallas_call | solution.py:103
  32.5 3.2 %collective-permute-start.4 = (bf16[2,256,128]{2,1,0:T(8,128)(2,1)S(1)}, bf16[2,256,128]{2,1,0:T(8,128)(2,1)S(1)}, u32[]{:S(2)}, u32[]{:S(2)}) collective-permute-start(bf16[2,256,128]{2,1,0:T(8,128)(2,1)S(1)} %get-tuple-element.31), channel_id=1, source_target_pairs={{0,4},{1,5},{2,6},{3,7},{4,0},{5,1},{6,2},{7,3},{8,12},{9,13},{10,... | collective-permute-start | bytes 393224 | tf_op jit(solution)/shard_map/ppermute | solution.py:83
  35.7 0.3 collective-permute-start.5
  36.0 0.6 %pick_pieces.2 = (bf16[2,256,128]{2,1,0:T(8,128)(2,1)S(1)}, bf16[2,256,128]{2,1,0:T(8,128)(2,1)S(1)}, bf16[2,256,128]{2,1,0:T(8,128)(2,1)S(1)}, bf16[2,256,128]{2,1,0:T(8,128)(2,1)S(1)}, bf16[2,256,128]{2,1,0:T(8,128)(2,1)S(1)}) custom-call(s32[8,2]{1,0:T(8,128)S(1)} %broadcast_clamp_fusion.requests_ref, bf16[16,256,128]{2,1,0:T(8,128)(2,1)S(1)} %all-to-all-done.held_ref), custom_call_target="tpu_custom_call" | custom-call | tf_op jit(solution)/shard_map/pick_pieces/pallas_call | solution.py:103
  36.7 1.3 %collective-permute-start.6 = (bf16[2,256,128]{2,1,0:T(8,128)(2,1)S(1)}, bf16[2,256,128]{2,1,0:T(8,128)(2,1)S(1)}, u32[]{:S(2)}, u32[]{:S(2)}) collective-permute-start(bf16[2,256,128]{2,1,0:T(8,128)(2,1)S(1)} %get-tuple-element.35), channel_id=1, source_target_pairs={{0,2},{1,3},{2,0},{3,1},{4,6},{5,7},{6,4},{7,5},{8,10},{9,11},{10,... | collective-permute-start | bytes 393224 | tf_op jit(solution)/shard_map/ppermute | solution.py:83
  38.0 0.8 %collective-permute-start.7 = (bf16[2,256,128]{2,1,0:T(8,128)(2,1)S(1)}, bf16[2,256,128]{2,1,0:T(8,128)(2,1)S(1)}, u32[]{:S(2)}, u32[]{:S(2)}) collective-permute-start(bf16[2,256,128]{2,1,0:T(8,128)(2,1)S(1)} %get-tuple-element.36), channel_id=1, source_target_pairs={{0,3},{1,2},{2,1},{3,0},{4,7},{5,6},{6,5},{7,4},{8,11},{9,10},{10,... | collective-permute-start | bytes 393224 | tf_op jit(solution)/shard_map/ppermute | solution.py:83
  38.8 2.2 %collective-permute-start.8 = (bf16[2,256,128]{2,1,0:T(8,128)(2,1)S(1)}, bf16[2,256,128]{2,1,0:T(8,128)(2,1)S(1)}, u32[]{:S(2)}, u32[]{:S(2)}) collective-permute-start(bf16[2,256,128]{2,1,0:T(8,128)(2,1)S(1)} %get-tuple-element.37), channel_id=1, source_target_pairs={{0,6},{1,7},{2,4},{3,5},{4,2},{5,3},{6,0},{7,1},{8,14},{9,15},{10,... | collective-permute-start | bytes 393224 | tf_op jit(solution)/shard_map/ppermute | solution.py:83
  41.0 2.3 %collective-permute-start.9 = (bf16[2,256,128]{2,1,0:T(8,128)(2,1)S(1)}, bf16[2,256,128]{2,1,0:T(8,128)(2,1)S(1)}, u32[]{:S(2)}, u32[]{:S(2)}) collective-permute-start(bf16[2,256,128]{2,1,0:T(8,128)(2,1)S(1)} %get-tuple-element.38), channel_id=1, source_target_pairs={{0,7},{1,6},{2,5},{3,4},{4,3},{5,2},{6,1},{7,0},{8,15},{9,14},{10,... | collective-permute-start | bytes 393224 | tf_op jit(solution)/shard_map/ppermute | solution.py:83
  43.3 12.1 %early_attention.1 = (f32[256,4096]{1,0:T(8,128)S(1)}, f32[256,4096]{1,0:T(8,128)S(1)}) custom-call(s32[1,2]{1,0:T(1,128)S(1)} %copy-done.4, bf16[256,4096]{1,0:T(8,128)(2,1)S(1)} %copy-done.1, f32[256,4096]{1,0:T(8,128)} %get-tuple-element.25.own_in, f32[256,512]{1,0:T(8,128)} %get-tuple-element.26.level_in, bf16[2,8,32,128]{3,2,1,0:T(8,128)(2,1)S(1)} %bitcast.19, ...), custom_call_target="tpu_custom_call" | custom-call | flops 1073741824 | bytes 10485760 | tf_op jit(solution)/shard_map/early_attention/pallas_call | solution.py:416
  55.4 3.9 %late_attention.1 = bf16[256,4096]{1,0:T(8,128)(2,1)} custom-call(s32[1,2]{1,0:T(1,128)S(1)} %copy-done.4, bf16[256,4096]{1,0:T(8,128)(2,1)S(1)} %copy-done.1, f32[256,4096]{1,0:T(8,128)S(1)} %get-tuple-element.33.own_in, f32[256,4096]{1,0:T(8,128)S(1)} %get-tuple-element.34.level_in, bf16[2,8,32,128]{3,2,1,0:T(8,128)(2,1)S(1)} %bitcast.12, ...), custom_call_target="tpu_custom_call" | custom-call | flops 1073741824 | bytes 10485760 | tf_op jit(solution)/shard_map/late_attention/pallas_call | solution.py:416
  (20 shorter events, 0.4 us)
Async XLA Ops:
  0.0 17.3 %copy-start.4 = (s32[1,2]{1,0:T(1,128)S(1)}, s32[1,2]{1,0:T(1,128)}, u32[]{:S(2)}) copy-start(s32[1,2]{1,0:T(1,128)} %selected_ref.3) | copy-start | bytes 28
  2.0 41.2 %copy-start.1 = (bf16[256,4096]{1,0:T(8,128)(2,1)S(1)}, bf16[256,4096]{1,0:T(8,128)(2,1)}, u32[]{:S(2)}) copy-start(bf16[256,4096]{1,0:T(8,128)(2,1)} %query_ref.2) | copy-start | bytes 6291460
  2.0 29.8 %all-to-all-start = ((bf16[16,256,128]{2,1,0:T(8,128)(2,1)}), bf16[16,256,128]{2,1,0:T(8,128)(2,1)S(1)}, u32[]{:S(2)}, u32[]{:S(2)}) async-start(bf16[16,256,128]{2,1,0:T(8,128)(2,1)} %pack.1), calls=%async_computation | async-start | bytes 2097152 | tf_op jit(solution)/shard_map/all_to_all | solution.py:442
  8.7 1.6 %copy-start = (bf16[256,4096]{1,0:T(8,128)(2,1)S(1)}, bf16[256,4096]{1,0:T(8,128)(2,1)}, u32[]{:S(2)}) copy-start(bf16[256,4096]{1,0:T(8,128)(2,1)} %query_ref.2) | copy-start | bytes 6291460
  10.3 0.9 %copy-start.2 = (bf16[256,512]{1,0:T(8,128)(2,1)S(1)}, bf16[256,512]{1,0:T(8,128)(2,1)}, u32[]{:S(2)}) copy-start(bf16[256,512]{1,0:T(8,128)(2,1)} %key_ref.1) | copy-start | bytes 786436
  11.2 0.9 %copy-start.3 = (bf16[256,512]{1,0:T(8,128)(2,1)S(1)}, bf16[256,512]{1,0:T(8,128)(2,1)}, u32[]{:S(2)}) copy-start(bf16[256,512]{1,0:T(8,128)(2,1)} %value_ref.1) | copy-start | bytes 786436
  17.4 1.1 %collective-permute-start = (s32[1,2]{0,1:T(2,128)S(1)}, s32[1,2]{0,1:T(2,128)S(1)}, u32[]{:S(2)}, u32[]{:S(2)}) collective-permute-start(s32[1,2]{0,1:T(2,128)S(1)} %copy.8), channel_id=1, source_target_pairs={{0,1},{1,0},{2,3},{3,2},{4,5},{5,4},{6,7},{7,6},{8,9},{9,8},{10,11... | collective-permute-start | bytes 32 | tf_op jit(solution)/shard_map/ppermute | solution.py:83
  18.6 2.7 %collective-permute-start.1 = (s32[2,2]{0,1:T(2,128)S(1)}, s32[2,2]{0,1:T(2,128)S(1)}, u32[]{:S(2)}, u32[]{:S(2)}) collective-permute-start(s32[2,2]{0,1:T(2,128)S(1)} %pad_add_fusion), channel_id=1, source_target_pairs={{0,2},{1,3},{2,0},{3,1},{4,6},{5,7},{6,4},{7,5},{8,10},{9,11},{10,... | collective-permute-start | bytes 56 | tf_op jit(solution)/shard_map/ppermute | solution.py:83
  21.4 4.9 %collective-permute-start.2 = (s32[4,2]{0,1:T(2,128)S(1)}, s32[4,2]{0,1:T(2,128)S(1)}, u32[]{:S(2)}, u32[]{:S(2)}) collective-permute-start(s32[4,2]{0,1:T(2,128)S(1)} %pad_add_fusion.1), channel_id=1, source_target_pairs={{0,4},{1,5},{2,6},{3,7},{4,0},{5,1},{6,2},{7,3},{8,12},{9,13},{10,... | collective-permute-start | bytes 104 | tf_op jit(solution)/shard_map/ppermute | solution.py:83
  32.5 6.3 %collective-permute-start.3 = (bf16[2,256,128]{2,1,0:T(8,128)(2,1)S(1)}, bf16[2,256,128]{2,1,0:T(8,128)(2,1)S(1)}, u32[]{:S(2)}, u32[]{:S(2)}) collective-permute-start(bf16[2,256,128]{2,1,0:T(8,128)(2,1)S(1)} %get-tuple-element.30), channel_id=1, source_target_pairs={{0,1},{1,0},{2,3},{3,2},{4,5},{5,4},{6,7},{7,6},{8,9},{9,8},{10,11... | collective-permute-start | bytes 393224 | tf_op jit(solution)/shard_map/ppermute | solution.py:83
  32.5 8.4 %collective-permute-start.4 = (bf16[2,256,128]{2,1,0:T(8,128)(2,1)S(1)}, bf16[2,256,128]{2,1,0:T(8,128)(2,1)S(1)}, u32[]{:S(2)}, u32[]{:S(2)}) collective-permute-start(bf16[2,256,128]{2,1,0:T(8,128)(2,1)S(1)} %get-tuple-element.31), channel_id=1, source_target_pairs={{0,4},{1,5},{2,6},{3,7},{4,0},{5,1},{6,2},{7,3},{8,12},{9,13},{10,... | collective-permute-start | bytes 393224 | tf_op jit(solution)/shard_map/ppermute | solution.py:83
  35.7 7.6 %collective-permute-start.5 = (bf16[2,256,128]{2,1,0:T(8,128)(2,1)S(1)}, bf16[2,256,128]{2,1,0:T(8,128)(2,1)S(1)}, u32[]{:S(2)}, u32[]{:S(2)}) collective-permute-start(bf16[2,256,128]{2,1,0:T(8,128)(2,1)S(1)} %get-tuple-element.32), channel_id=1, source_target_pairs={{0,5},{1,4},{2,7},{3,6},{4,1},{5,0},{6,3},{7,2},{8,13},{9,12},{10,... | collective-permute-start | bytes 393224 | tf_op jit(solution)/shard_map/ppermute | solution.py:83
  36.7 18.7 %collective-permute-start.6 = (bf16[2,256,128]{2,1,0:T(8,128)(2,1)S(1)}, bf16[2,256,128]{2,1,0:T(8,128)(2,1)S(1)}, u32[]{:S(2)}, u32[]{:S(2)}) collective-permute-start(bf16[2,256,128]{2,1,0:T(8,128)(2,1)S(1)} %get-tuple-element.35), channel_id=1, source_target_pairs={{0,2},{1,3},{2,0},{3,1},{4,6},{5,7},{6,4},{7,5},{8,10},{9,11},{10,... | collective-permute-start | bytes 393224 | tf_op jit(solution)/shard_map/ppermute | solution.py:83
  38.0 17.4 %collective-permute-start.7 = (bf16[2,256,128]{2,1,0:T(8,128)(2,1)S(1)}, bf16[2,256,128]{2,1,0:T(8,128)(2,1)S(1)}, u32[]{:S(2)}, u32[]{:S(2)}) collective-permute-start(bf16[2,256,128]{2,1,0:T(8,128)(2,1)S(1)} %get-tuple-element.36), channel_id=1, source_target_pairs={{0,3},{1,2},{2,1},{3,0},{4,7},{5,6},{6,5},{7,4},{8,11},{9,10},{10,... | collective-permute-start | bytes 393224 | tf_op jit(solution)/shard_map/ppermute | solution.py:83
  38.8 16.6 %collective-permute-start.8 = (bf16[2,256,128]{2,1,0:T(8,128)(2,1)S(1)}, bf16[2,256,128]{2,1,0:T(8,128)(2,1)S(1)}, u32[]{:S(2)}, u32[]{:S(2)}) collective-permute-start(bf16[2,256,128]{2,1,0:T(8,128)(2,1)S(1)} %get-tuple-element.37), channel_id=1, source_target_pairs={{0,6},{1,7},{2,4},{3,5},{4,2},{5,3},{6,0},{7,1},{8,14},{9,15},{10,... | collective-permute-start | bytes 393224 | tf_op jit(solution)/shard_map/ppermute | solution.py:83
  41.0 14.4 %collective-permute-start.9 = (bf16[2,256,128]{2,1,0:T(8,128)(2,1)S(1)}, bf16[2,256,128]{2,1,0:T(8,128)(2,1)S(1)}, u32[]{:S(2)}, u32[]{:S(2)}) collective-permute-start(bf16[2,256,128]{2,1,0:T(8,128)(2,1)S(1)} %get-tuple-element.38), channel_id=1, source_target_pairs={{0,7},{1,6},{2,5},{3,4},{4,3},{5,2},{6,1},{7,0},{8,15},{9,14},{10,... | collective-permute-start | bytes 393224 | tf_op jit(solution)/shard_map/ppermute | solution.py:83

commit v11 on v10

--- a/solution.py
+++ b/solution.py
@@ -17,62 +17,16 @@
 MIB = 1024 * 1024
 
 
-def pack_kernel(key_ref, value_ref, out_ref, staged, arrived, left):
-    shares, piece_rows, _ = key_ref.shape
-    half = KEY_VALUE_HEADS * piece_rows
-
-    def take(slot):
-        ref = key_ref if slot < KEY_VALUE_HEADS else value_ref
-        head = slot % KEY_VALUE_HEADS
-        lanes = pl.ds(head * HEAD_SIZE, HEAD_SIZE)
-        rows = pl.ds(slot * piece_rows, piece_rows)
-        return pltpu.make_async_copy(
-            ref.at[:, :, lanes], staged.at[:, rows, :], arrived.at[slot]
-        )
-
-    def give(which, copy):
-        rows = pl.ds(which * half, half)
-        return pltpu.make_async_copy(
-            staged.at[:, rows, :],
-            out_ref.at[pl.ds(copy * shares, shares), rows, :],
-            left.at[which, copy],
-        )
-
-    for slot in range(SLOTS):
-        take(slot).start()
-    for which in range(2):
-        for head in range(KEY_VALUE_HEADS):
-            take(which * KEY_VALUE_HEADS + head).wait()
-        for copy in range(COPIES):
-            give(which, copy).start()
-    for which in range(2):
-        for copy in range(COPIES):
-            give(which, copy).wait()
-
-
 def pack(keys, values, devices):
     shares = devices // COPIES
     piece_rows = keys.shape[0] // shares
-    if piece_rows % 16 == 0:
-        split = (shares, piece_rows, keys.shape[1])
-        return pl.pallas_call(
-            pack_kernel,
-            out_shape=jax.ShapeDtypeStruct(
-                (devices, SLOTS * piece_rows, HEAD_SIZE), jnp.bfloat16
-            ),
-            in_specs=[pl.BlockSpec(memory_space=pl.ANY)] * 2,
-            out_specs=pl.BlockSpec(memory_space=pl.ANY),
-            scratch_shapes=[
-                pltpu.VMEM((shares, SLOTS * piece_rows, HEAD_SIZE), jnp.bfloat16),
-                pltpu.SemaphoreType.DMA((SLOTS,)),
-                pltpu.SemaphoreType.DMA((2, COPIES)),
-            ],
-            name="pack",
-        )(keys.reshape(split), values.reshape(split))
     both = jnp.concatenate([keys, values], axis=1)
-    both = both.reshape(shares, piece_rows, SLOTS, HEAD_SIZE).transpose(0, 2, 1, 3)
-    both = both.reshape(shares, SLOTS * piece_rows, HEAD_SIZE)
-    return jnp.concatenate([both] * COPIES, axis=0)
+    if piece_rows % 16 != 0:
+        both = both.reshape(shares, piece_rows, SLOTS, HEAD_SIZE).transpose(0, 2, 1, 3)
+        both = both.reshape(shares, SLOTS * piece_rows, HEAD_SIZE)
+    else:
+        both = both.reshape(shares, piece_rows, SLOTS * HEAD_SIZE)
+    return jnp.broadcast_to(both[None], (COPIES, *both.shape)).reshape(devices, *both.shape[1:])
 
 
 def partner(position, step):
@@ -92,22 +46,23 @@
     return requests
 
 
-def pick_kernel(requests_ref, held_ref, *out_refs, steps):
-    for step, out_ref in zip(steps, out_refs):
+def pick_kernel(requests_ref, held_ref, *out_refs):
+    for step, out_ref in enumerate(out_refs):
         for pick in range(2):
             out_ref[pick] = held_ref[requests_ref[step, pick]]
 
 
-def pick_pieces(requests, held, steps):
-    rows = held.shape[1]
+def pick_pieces(requests, held):
+    devices, rows, width = held.shape
+    shares = devices // COPIES
     return pl.pallas_call(
-        functools.partial(pick_kernel, steps=steps),
-        out_shape=[jax.ShapeDtypeStruct((2, rows, HEAD_SIZE), jnp.bfloat16)] * len(steps),
+        pick_kernel,
+        out_shape=[jax.ShapeDtypeStruct((2, rows, width), jnp.bfloat16)] * shares,
         in_specs=[
             pl.BlockSpec(memory_space=pltpu.SMEM),
             pl.BlockSpec(memory_space=pltpu.VMEM),
         ],
-        out_specs=[pl.BlockSpec(memory_space=pltpu.VMEM)] * len(steps),
+        out_specs=[pl.BlockSpec(memory_space=pltpu.VMEM)] * shares,
         compiler_params=pltpu.CompilerParams(vmem_limit_bytes=16 * MIB),
         name="pick_pieces",
     )(requests, held)
@@ -115,23 +70,13 @@
 
 def delivery_order(shares):
     half, quarter = shares // 2, shares // 4
-    return [
-        *range(1, quarter),
-        *range(half, half + quarter),
-        *range(quarter, half),
-        *range(half + quarter, shares),
-    ]
-
-
-def deliver(requests, held):
-    devices = held.shape[0]
-    order = delivery_order(devices // COPIES)
-    early, late = order[: len(order) // 2], [*order[len(order) // 2 :], 0]
-    moved = []
-    for steps in (early, late):
-        pieces = pick_pieces(requests, held, steps)
-        moved += [p if s == 0 else swap(p, s, devices) for s, p in zip(steps, pieces)]
-    return [moved[-1], *moved[:-1]]
+    apart = zip(range(half, half + quarter), range(quarter, half))
+    return [*range(1, quarter), *range(half + quarter, shares), *[s for pair in apart for s in pair]]
+
+
+def deliver(pieces, devices):
+    order = delivery_order(len(pieces))
+    return [pieces[0]] + [swap(pieces[step], step, devices) for step in order]
 
 
 FACTOR = math.log2(math.e) / math.sqrt(HEAD_SIZE)
@@ -283,10 +228,11 @@
             new_level_ref[:, lanes] = level + jnp.log2(row_sum)
 
     def attend(picks):
-        count = len(picks) * sum(ref.shape[2] for ref in far_refs)
+        count = len(picks) * sum(ref.shape[1] for ref in far_refs)
 
         def block(slot):
-            return jnp.concatenate([ref[p, slot] for p in picks for ref in far_refs], axis=0)
+            lanes = narrow(slot)
+            return jnp.concatenate([ref[p, :, lanes] for p in picks for ref in far_refs], axis=0)
 
         def keys_and_values(group):
             return block(group).T, with_ones(block(group + KEY_VALUE_HEADS))
@@ -391,7 +337,7 @@
 
 def far_attention(selected, queries, own, level, far, last):
     rows = queries.shape[0]
-    scores = QUERY_HEADS * rows * 2 * sum(piece.shape[2] for piece in far)
+    scores = QUERY_HEADS * rows * 2 * sum(piece.shape[1] for piece in far)
     in_vmem = pl.BlockSpec(memory_space=pltpu.VMEM)
     anywhere = pl.BlockSpec(memory_space=pl.ANY)
     if last:
@@ -433,6 +379,11 @@
     )(selected, queries, own, level, *far)
 
 
+def join(pieces, piece_rows):
+    pieces = [p.reshape(2, SLOTS, piece_rows, HEAD_SIZE).transpose(0, 2, 1, 3) for p in pieces]
+    return jnp.concatenate(pieces, axis=1).reshape(2, -1, SLOTS * HEAD_SIZE)
+
+
 def local(queries, all_key_states, all_value_states, selected):
     devices = lax.axis_size("ctx")
     rows = all_key_states.shape[0]
@@ -444,11 +395,10 @@
     mine, own, level = lax.optimization_barrier((selected, own, level))
     requests = exchange_requests(mine, devices // COPIES, devices)
     requests = jnp.clip(requests, 0, devices - 1)
-    moved = deliver(requests, held)
-    far = [m.reshape(2, SLOTS, piece_rows, HEAD_SIZE) for m in moved]
-    early, late = far[: len(far) // 2], far[len(far) // 2 :]
+    moved = deliver(pick_pieces(requests, held), devices)
+    early, late = moved[: len(moved) // 2], moved[len(moved) // 2 :]
     if piece_rows % 16 != 0:
-        early, late = [jnp.concatenate(early, axis=2)], [jnp.concatenate(late, axis=2)]
+        early, late = [join(early, piece_rows)], [join(late, piece_rows)]
     own, level = far_attention(selected, queries, own, level, early, last=False)
     return far_attention(selected, queries, own, level, late, last=True)
 

time: 60.7 us -> 60.8 us (level)
  the two profiles are of different devices: /device:TPU:5 before, /device:TPU:21 now
where the time goes in v11:
time: 60.8 us; the launch traced here: 59.9 us
  Pallas kernels  21 us (35%)
  waiting for transfers between devices  19.6 us (32%)
  starting transfers between devices  15.3 us (25%)
  local copies, waits for them, and re-layouts  2.24 us (4%)
  other arithmetic  1.46 us (2%)
    pallas_call x2, Pallas kernels, far_attention(): pl.pallas_call(functools.partial(far_kernel, last=last), out_shape=out_sh...  15.1 us
    ppermute x10, waiting for transfers between devices, swap(): lax.ppermute(array, 'ctx', [(i, partner(i, step)) for i in range(devices)])  14.3 us
    ppermute x10, starting transfers between devices, swap(): lax.ppermute(array, 'ctx', [(i, partner(i, step)) for i in range(devices)])  8.8 us
    all_to_all x1, starting transfers between devices, local(): lax.all_to_all(packed, 'ctx', split_axis=0, concat_axis=0, tiled=True)  6.47 us
    all_to_all x1, waiting for transfers between devices, local(): lax.all_to_all(packed, 'ctx', split_axis=0, concat_axis=0, tiled=True)  5.33 us
    pallas_call x1, Pallas kernels, own_attention(): pl.pallas_call(own_kernel, out_shape=[pltpu.HBM(queries.shape, jnp.float3...  5.24 us
    concatenate x1, other arithmetic, pack(): both = jnp.concatenate([keys, values], axis=1)  1.23 us
  transfers between devices with their start and end apart: 11, of which 6 were waited for; matrix products, arithmetic and copies ran while one was open for 1% of the time, Pallas kernels for 27%

profile of v11, /device:TPU:21, one launch (start us, length us, event | category | flops | bytes accessed | tf_op | source)
XLA Modules:
  0.0 59.9 jit_solution(11735692664034332547)
XLA Ops:
  0.0 1.2 %pad_maximum_fusion = bf16[256,1024]{1,0:T(8,128)(2,1)S(1)} fusion(bf16[256,512]{1,0:T(8,128)(2,1)} %value_ref.1, bf16[256,512]{1,0:T(8,128)(2,1)} %key_ref.1), kind=kLoop, calls=%fused_computation | loop fusion | flops 1048576 | bytes 1048576 | tf_op jit(solution)/shard_map/concatenate | solution.py:23
  1.2 1.1 %broadcast_in_dim.8 = bf16[2,8,32,1024]{3,2,1,0:T(8,128)(2,1)} broadcast(bf16[8,32,1024]{2,1,0:T(8,128)(2,1)S(1)} %bitcast.3), dimensions={1,2,3} | broadcast | bytes 1572864 | tf_op jit(solution)/shard_map/broadcast_in_dim | solution.py:29
  2.4 6.5 %all-to-all-start = ((bf16[16,32,1024]{2,1,0:T(8,128)(2,1)}), bf16[16,32,1024]{2,1,0:T(8,128)(2,1)S(1)}, u32[]{:S(2)}, u32[]{:S(2)}) async-start(bf16[16,32,1024]{2,1,0:T(8,128)(2,1)} %bitcast.2), calls=%async_computation | async-start | bytes 2097152 | tf_op jit(solution)/shard_map/all_to_all | solution.py:393
  8.9 0.9 %copy-done.2 = bf16[256,512]{1,0:T(8,128)(2,1)S(1)} copy-done((bf16[256,512]{1,0:T(8,128)(2,1)S(1)}, bf16[256,512]{1,0:T(8,128)(2,1)}, u32[]{:S(2)}) %copy-start.2) | copy-done | bytes 262168
  9.8 5.2 %own_attention.1 = (f32[256,4096]{1,0:T(8,128)}, f32[256,512]{1,0:T(8,128)}) custom-call(bf16[256,4096]{1,0:T(8,128)(2,1)S(1)} %copy-done, bf16[256,512]{1,0:T(8,128)(2,1)S(1)} %copy-done.1, bf16[256,512]{1,0:T(8,128)(2,1)S(1)} %copy-done.2), custom_call_target="tpu_custom_call" | custom-call | flops 1073741824 | bytes 7340032 | tf_op jit(solution)/shard_map/own_attention/pallas_call | solution.py:149
  15.0 0.1 copy.8
  15.1 0.4 collective-permute-start
  15.5 0.8 %collective-permute-done = s32[1,2]{0,1:T(2,128)S(1)} collective-permute-done((s32[1,2]{0,1:T(2,128)S(1)}, s32[1,2]{0,1:T(2,128)S(1)}, u32[]{:S(2)}, u32[]{:S(2)}) %collective-permute-start) | collective-permute-done | bytes 40 | tf_op jit(solution)/shard_map/ppermute | solution.py:37
  16.4 1.2 %collective-permute-start.1 = (s32[2,2]{0,1:T(2,128)S(1)}, s32[2,2]{0,1:T(2,128)S(1)}, u32[]{:S(2)}, u32[]{:S(2)}) collective-permute-start(s32[2,2]{0,1:T(2,128)S(1)} %pad_add_fusion), channel_id=1, source_target_pairs={{0,2},{1,3},{2,0},{3,1},{4,6},{5,7},{6,4},{7,5},{8,10},{9,11},{10,... | collective-permute-start | bytes 56 | tf_op jit(solution)/shard_map/ppermute | solution.py:37
  17.6 1.5 %collective-permute-done.1 = s32[2,2]{0,1:T(2,128)S(1)} collective-permute-done((s32[2,2]{0,1:T(2,128)S(1)}, s32[2,2]{0,1:T(2,128)S(1)}, u32[]{:S(2)}, u32[]{:S(2)}) %collective-permute-start.1) | collective-permute-done | bytes 48 | tf_op jit(solution)/shard_map/ppermute | solution.py:37
  19.1 1.3 %collective-permute-start.2 = (s32[4,2]{0,1:T(2,128)S(1)}, s32[4,2]{0,1:T(2,128)S(1)}, u32[]{:S(2)}, u32[]{:S(2)}) collective-permute-start(s32[4,2]{0,1:T(2,128)S(1)} %pad_add_fusion.1), channel_id=1, source_target_pairs={{0,4},{1,5},{2,6},{3,7},{4,0},{5,1},{6,2},{7,3},{8,12},{9,13},{10,... | collective-permute-start | bytes 104 | tf_op jit(solution)/shard_map/ppermute | solution.py:37
  20.5 7.5 %collective-permute-done.2 = s32[4,2]{0,1:T(2,128)S(1)} collective-permute-done((s32[4,2]{0,1:T(2,128)S(1)}, s32[4,2]{0,1:T(2,128)S(1)}, u32[]{:S(2)}, u32[]{:S(2)}) %collective-permute-start.2) | collective-permute-done | bytes 64 | tf_op jit(solution)/shard_map/ppermute | solution.py:37
  28.2 5.3 %all-to-all-done.held_ref = bf16[16,32,1024]{2,1,0:T(8,128)(2,1)S(1)} async-done(((bf16[16,32,1024]{2,1,0:T(8,128)(2,1)}), bf16[16,32,1024]{2,1,0:T(8,128)(2,1)S(1)}, u32[]{:S(2)}, u32[]{:S(2)}) %all-to-all-start) | async-done | bytes 1048608 | tf_op jit(solution)/shard_map/all_to_all | solution.py:393
  33.5 0.7 %pick_pieces.1 = (bf16[2,32,1024]{2,1,0:T(8,128)(2,1)S(1)}, bf16[2,32,1024]{2,1,0:T(8,128)(2,1)S(1)}, bf16[2,32,1024]{2,1,0:T(8,128)(2,1)S(1)}, bf16[2,32,1024]{...) custom-call(s32[8,2]{1,0:T(8,128)S(1)} %broadcast_clamp_fusion.reque, ...), custom_call_target="tpu_custom_call" | custom-call | tf_op jit(solution)/shard_map/pick_pieces/pallas_call | solution.py:58
  34.2 0.9 %collective-permute-start.3 = (bf16[2,32,1024]{2,1,0:T(8,128)(2,1)S(1)}, bf16[2,32,1024]{2,1,0:T(8,128)(2,1)S(1)}, u32[]{:S(2)}, u32[]{:S(2)}) collective-permute-start(bf16[2,32,1024]{2,1,0:T(8,128)(2,1)S(1)} %get-tuple-element.30), channel_id=1, source_target_pairs={{0,1},{1,0},{2,3},{3,2},{4,5},{5,4},{6,7},{7,6},{8,9},{9,8},{10,11... | collective-permute-start | bytes 393224 | tf_op jit(solution)/shard_map/ppermute | solution.py:37
  35.1 0.7 %collective-permute-start.4 = (bf16[2,32,1024]{2,1,0:T(8,128)(2,1)S(1)}, bf16[2,32,1024]{2,1,0:T(8,128)(2,1)S(1)}, u32[]{:S(2)}, u32[]{:S(2)}) collective-permute-start(bf16[2,32,1024]{2,1,0:T(8,128)(2,1)S(1)} %get-tuple-element.31), channel_id=1, source_target_pairs={{0,6},{1,7},{2,4},{3,5},{4,2},{5,3},{6,0},{7,1},{8,14},{9,15},{10,... | collective-permute-start | bytes 393224 | tf_op jit(solution)/shard_map/ppermute | solution.py:37
  35.8 1.9 %collective-permute-start.5 = (bf16[2,32,1024]{2,1,0:T(8,128)(2,1)S(1)}, bf16[2,32,1024]{2,1,0:T(8,128)(2,1)S(1)}, u32[]{:S(2)}, u32[]{:S(2)}) collective-permute-start(bf16[2,32,1024]{2,1,0:T(8,128)(2,1)S(1)} %get-tuple-element.32), channel_id=1, source_target_pairs={{0,7},{1,6},{2,5},{3,4},{4,3},{5,2},{6,1},{7,0},{8,15},{9,14},{10,... | collective-permute-start | bytes 393224 | tf_op jit(solution)/shard_map/ppermute | solution.py:37
  37.7 1.2 %collective-permute-start.7 = (bf16[2,32,1024]{2,1,0:T(8,128)(2,1)S(1)}, bf16[2,32,1024]{2,1,0:T(8,128)(2,1)S(1)}, u32[]{:S(2)}, u32[]{:S(2)}) collective-permute-start(bf16[2,32,1024]{2,1,0:T(8,128)(2,1)S(1)} %get-tuple-element.36), channel_id=1, source_target_pairs={{0,2},{1,3},{2,0},{3,1},{4,6},{5,7},{6,4},{7,5},{8,10},{9,11},{10,... | collective-permute-start | bytes 393224 | tf_op jit(solution)/shard_map/ppermute | solution.py:37
  38.9 0.6 collective-permute-start.8
  39.5 1.6 %collective-permute-done.4.refs_2_ = bf16[2,32,1024]{2,1,0:T(8,128)(2,1)S(1)} collective-permute-done((bf16[2,32,1024]{2,1,0:T(8,128)(2,1)S(1)}, bf16[2,32,1024]{2,1,0:T(8,128)(2,1)S(1)}, u32[]{:S(2)}, u32[]{:S(2)}) %collective-permute-start.4) | collective-permute-done | bytes 131104 | tf_op jit(solution)/shard_map/ppermute | solution.py:37
  41.1 0.6 collective-permute-start.9
  41.7 2.9 %collective-permute-done.5.refs_3_ = bf16[2,32,1024]{2,1,0:T(8,128)(2,1)S(1)} collective-permute-done((bf16[2,32,1024]{2,1,0:T(8,128)(2,1)S(1)}, bf16[2,32,1024]{2,1,0:T(8,128)(2,1)S(1)}, u32[]{:S(2)}, u32[]{:S(2)}) %collective-permute-start.5) | collective-permute-done | bytes 131104 | tf_op jit(solution)/shard_map/ppermute | solution.py:37
  44.5 11.0 %early_attention.1 = (f32[256,4096]{1,0:T(8,128)S(1)}, f32[256,4096]{1,0:T(8,128)S(1)}) custom-call(s32[1,2]{1,0:T(1,128)S(1)} %copy-done.3, bf16[256,4096]{1,0:T(8,128)(2,1)S(1)} %copy-done, f32[256,4096]{1,0:T(8,128)} %get-tuple-element.25.own_in, f32[256,512]{1,0:T(8,128)} %get-tuple-element.26.level_in, ...), custom_call_target="tpu_custom_call" | custom-call | flops 1073741824 | bytes 10485760 | tf_op jit(solution)/shard_map/early_attention/pallas_call | solution.py:362
  55.6 4.1 %late_attention.1 = bf16[256,4096]{1,0:T(8,128)(2,1)} custom-call(s32[1,2]{1,0:T(1,128)S(1)} %copy-done.3, bf16[256,4096]{1,0:T(8,128)(2,1)S(1)} %copy-done, f32[256,4096]{1,0:T(8,128)S(1)} %get-tuple-element.33.own_in, f32[256,4096]{1,0:T(8,128)S(1)} %get-tuple-element.34.level_in, bf16[2,32,1024]{2,1,0:T(8,128)(2,1)S(1)} %collective-permute-done.6.refs_0_, ...), custom_call_target="tpu_custom_call" | custom-call | flops 1073741824 | bytes 10485760 | tf_op jit(solution)/shard_map/late_attention/pallas_call | solution.py:362
  (18 shorter events, 0.3 us)
Async XLA Ops:
  0.0 8.8 %copy-start.1 = (bf16[256,512]{1,0:T(8,128)(2,1)S(1)}, bf16[256,512]{1,0:T(8,128)(2,1)}, u32[]{:S(2)}) copy-start(bf16[256,512]{1,0:T(8,128)(2,1)} %key_ref.1) | copy-start | bytes 786436
  0.0 8.8 %copy-start = (bf16[256,4096]{1,0:T(8,128)(2,1)S(1)}, bf16[256,4096]{1,0:T(8,128)(2,1)}, u32[]{:S(2)}) copy-start(bf16[256,4096]{1,0:T(8,128)(2,1)} %query_ref.2) | copy-start | bytes 6291460
  0.0 15.0 %copy-start.3 = (s32[1,2]{1,0:T(1,128)S(1)}, s32[1,2]{1,0:T(1,128)}, u32[]{:S(2)}) copy-start(s32[1,2]{1,0:T(1,128)} %selected_ref.3) | copy-start | bytes 28
  2.4 31.1 %all-to-all-start = ((bf16[16,32,1024]{2,1,0:T(8,128)(2,1)}), bf16[16,32,1024]{2,1,0:T(8,128)(2,1)S(1)}, u32[]{:S(2)}, u32[]{:S(2)}) async-start(bf16[16,32,1024]{2,1,0:T(8,128)(2,1)} %bitcast.2), calls=%async_computation | async-start | bytes 2097152 | tf_op jit(solution)/shard_map/all_to_all | solution.py:393
  8.8 1.0 %copy-start.2 = (bf16[256,512]{1,0:T(8,128)(2,1)S(1)}, bf16[256,512]{1,0:T(8,128)(2,1)}, u32[]{:S(2)}) copy-start(bf16[256,512]{1,0:T(8,128)(2,1)} %value_ref.1) | copy-start | bytes 786436
  15.1 1.2 %collective-permute-start = (s32[1,2]{0,1:T(2,128)S(1)}, s32[1,2]{0,1:T(2,128)S(1)}, u32[]{:S(2)}, u32[]{:S(2)}) collective-permute-start(s32[1,2]{0,1:T(2,128)S(1)} %copy.8), channel_id=1, source_target_pairs={{0,1},{1,0},{2,3},{3,2},{4,5},{5,4},{6,7},{7,6},{8,9},{9,8},{10,11... | collective-permute-start | bytes 32 | tf_op jit(solution)/shard_map/ppermute | solution.py:37
  16.4 2.7 %collective-permute-start.1 = (s32[2,2]{0,1:T(2,128)S(1)}, s32[2,2]{0,1:T(2,128)S(1)}, u32[]{:S(2)}, u32[]{:S(2)}) collective-permute-start(s32[2,2]{0,1:T(2,128)S(1)} %pad_add_fusion), channel_id=1, source_target_pairs={{0,2},{1,3},{2,0},{3,1},{4,6},{5,7},{6,4},{7,5},{8,10},{9,11},{10,... | collective-permute-start | bytes 56 | tf_op jit(solution)/shard_map/ppermute | solution.py:37
  19.1 8.9 %collective-permute-start.2 = (s32[4,2]{0,1:T(2,128)S(1)}, s32[4,2]{0,1:T(2,128)S(1)}, u32[]{:S(2)}, u32[]{:S(2)}) collective-permute-start(s32[4,2]{0,1:T(2,128)S(1)} %pad_add_fusion.1), channel_id=1, source_target_pairs={{0,4},{1,5},{2,6},{3,7},{4,0},{5,1},{6,2},{7,3},{8,12},{9,13},{10,... | collective-permute-start | bytes 104 | tf_op jit(solution)/shard_map/ppermute | solution.py:37
  34.2 4.8 %collective-permute-start.3 = (bf16[2,32,1024]{2,1,0:T(8,128)(2,1)S(1)}, bf16[2,32,1024]{2,1,0:T(8,128)(2,1)S(1)}, u32[]{:S(2)}, u32[]{:S(2)}) collective-permute-start(bf16[2,32,1024]{2,1,0:T(8,128)(2,1)S(1)} %get-tuple-element.30), channel_id=1, source_target_pairs={{0,1},{1,0},{2,3},{3,2},{4,5},{5,4},{6,7},{7,6},{8,9},{9,8},{10,11... | collective-permute-start | bytes 393224 | tf_op jit(solution)/shard_map/ppermute | solution.py:37
  35.1 6.0 %collective-permute-start.4 = (bf16[2,32,1024]{2,1,0:T(8,128)(2,1)S(1)}, bf16[2,32,1024]{2,1,0:T(8,128)(2,1)S(1)}, u32[]{:S(2)}, u32[]{:S(2)}) collective-permute-start(bf16[2,32,1024]{2,1,0:T(8,128)(2,1)S(1)} %get-tuple-element.31), channel_id=1, source_target_pairs={{0,6},{1,7},{2,4},{3,5},{4,2},{5,3},{6,0},{7,1},{8,14},{9,15},{10,... | collective-permute-start | bytes 393224 | tf_op jit(solution)/shard_map/ppermute | solution.py:37
  35.8 8.7 %collective-permute-start.5 = (bf16[2,32,1024]{2,1,0:T(8,128)(2,1)S(1)}, bf16[2,32,1024]{2,1,0:T(8,128)(2,1)S(1)}, u32[]{:S(2)}, u32[]{:S(2)}) collective-permute-start(bf16[2,32,1024]{2,1,0:T(8,128)(2,1)S(1)} %get-tuple-element.32), channel_id=1, source_target_pairs={{0,7},{1,6},{2,5},{3,4},{4,3},{5,2},{6,1},{7,0},{8,15},{9,14},{10,... | collective-permute-start | bytes 393224 | tf_op jit(solution)/shard_map/ppermute | solution.py:37
  37.7 17.9 %collective-permute-start.6 = (bf16[2,32,1024]{2,1,0:T(8,128)(2,1)S(1)}, bf16[2,32,1024]{2,1,0:T(8,128)(2,1)S(1)}, u32[]{:S(2)}, u32[]{:S(2)}) collective-permute-start(bf16[2,32,1024]{2,1,0:T(8,128)(2,1)S(1)} %get-tuple-element.35), channel_id=1, source_target_pairs={{0,4},{1,5},{2,6},{3,7},{4,0},{5,1},{6,2},{7,3},{8,12},{9,13},{10,... | collective-permute-start | bytes 393224 | tf_op jit(solution)/shard_map/ppermute | solution.py:37
  37.7 17.9 %collective-permute-start.7 = (bf16[2,32,1024]{2,1,0:T(8,128)(2,1)S(1)}, bf16[2,32,1024]{2,1,0:T(8,128)(2,1)S(1)}, u32[]{:S(2)}, u32[]{:S(2)}) collective-permute-start(bf16[2,32,1024]{2,1,0:T(8,128)(2,1)S(1)} %get-tuple-element.36), channel_id=1, source_target_pairs={{0,2},{1,3},{2,0},{3,1},{4,6},{5,7},{6,4},{7,5},{8,10},{9,11},{10,... | collective-permute-start | bytes 393224 | tf_op jit(solution)/shard_map/ppermute | solution.py:37
  38.9 16.7 %collective-permute-start.8 = (bf16[2,32,1024]{2,1,0:T(8,128)(2,1)S(1)}, bf16[2,32,1024]{2,1,0:T(8,128)(2,1)S(1)}, u32[]{:S(2)}, u32[]{:S(2)}) collective-permute-start(bf16[2,32,1024]{2,1,0:T(8,128)(2,1)S(1)} %get-tuple-element.37), channel_id=1, source_target_pairs={{0,5},{1,4},{2,7},{3,6},{4,1},{5,0},{6,3},{7,2},{8,13},{9,12},{10,... | collective-permute-start | bytes 393224 | tf_op jit(solution)/shard_map/ppermute | solution.py:37
  41.1 14.5 %collective-permute-start.9 = (bf16[2,32,1024]{2,1,0:T(8,128)(2,1)S(1)}, bf16[2,32,1024]{2,1,0:T(8,128)(2,1)S(1)}, u32[]{:S(2)}, u32[]{:S(2)}) collective-permute-start(bf16[2,32,1024]{2,1,0:T(8,128)(2,1)S(1)} %get-tuple-element.38), channel_id=1, source_target_pairs={{0,3},{1,2},{2,1},{3,0},{4,7},{5,6},{6,5},{7,4},{8,11},{9,10},{10,... | collective-permute-start | bytes 393224 | tf_op jit(solution)/shard_map/ppermute | solution.py:37

commit v12 on v7

--- a/solution.py
+++ b/solution.py
@@ -92,10 +92,18 @@
     return requests
 
 
+def scalar_of(values, row, column):
+    rows = lax.broadcasted_iota(jnp.int32, values.shape, 0)
+    columns = lax.broadcasted_iota(jnp.int32, values.shape, 1)
+    here = jnp.logical_and(rows == row, columns == column)
+    return jnp.max(jnp.where(here, values.astype(jnp.float32), 0.0)).astype(jnp.int32)
+
+
 def pick_kernel(requests_ref, held_ref, *out_refs):
+    requests = requests_ref[...]
     for step, out_ref in enumerate(out_refs):
         for pick in range(2):
-            out_ref[pick] = held_ref[requests_ref[step, pick]]
+            out_ref[pick] = held_ref[scalar_of(requests, step, pick)]
 
 
 def pick_pieces(requests, held):
@@ -104,10 +112,7 @@
     return pl.pallas_call(
         pick_kernel,
         out_shape=[jax.ShapeDtypeStruct((2, rows, HEAD_SIZE), jnp.bfloat16)] * shares,
-        in_specs=[
-            pl.BlockSpec(memory_space=pltpu.SMEM),
-            pl.BlockSpec(memory_space=pltpu.VMEM),
-        ],
+        in_specs=[pl.BlockSpec(memory_space=pltpu.VMEM)] * 2,
         out_specs=[pl.BlockSpec(memory_space=pltpu.VMEM)] * shares,
         compiler_params=pltpu.CompilerParams(vmem_limit_bytes=16 * MIB),
         name="pick_pieces",
@@ -127,6 +132,7 @@
 
 FACTOR = math.log2(math.e) / math.sqrt(HEAD_SIZE)
 PAIR = 2
+SENT = 4
 LARGE_SUM = 2.0**100
 
 
@@ -246,9 +252,13 @@
             source.at[:, lanes], target.at[:, lanes], sems.at[which, group]
         )
 
-    def send(group):
-        lanes = wide(group)
-        return pltpu.make_async_copy(staged.at[:, lanes], out_ref.at[:, lanes], sems.at[group])
+    def send(part):
+        start = part * SENT * HEAD_SIZE
+        fixed = isinstance(part, int)
+        lanes = pl.ds(
+            start if fixed else pl.multiple_of(start, SENT * HEAD_SIZE), SENT * HEAD_SIZE
+        )
+        return pltpu.make_async_copy(staged.at[:, lanes], out_ref.at[:, lanes], sems.at[part])
 
     if not last:
         for group in range(KEY_VALUE_HEADS):
@@ -319,24 +329,28 @@
                 fetch(group, 1).wait()
                 fetch(group, 0).wait()
             largest = quick(group, head, scores, held[group][1], largest)
-            if head == GROUP - 1 and last:
-                send(group).start()
+            if (head + 1) % SENT == 0 and last:
+                send((group * GROUP + head) // SENT).start()
             scores = following
 
         @pl.when(jnp.max(largest) > LARGE_SUM)
         def _():
             @pl.loop(0, KEY_VALUE_HEADS)
             def _(group):
+                parts = [group * (GROUP // SENT) + part for part in range(GROUP // SENT)]
                 if last:
-                    send(group).wait()
+                    for part in parts:
+                        send(part).wait()
                 keys_across, value = keys_and_values(group)
                 for head in range(GROUP):
                     careful(group, head, score(group, head, keys_across), value)
                 if last:
-                    send(group).start()
+                    for part in parts:
+                        send(part).start()
 
     my_block = lax.axis_index("ctx")
-    chosen = selected_ref[0, 0], selected_ref[0, 1]
+    selected = selected_ref[...]
+    chosen = scalar_of(selected, 0, 0), scalar_of(selected, 0, 1)
     first = chosen[0] < my_block
     second = jnp.logical_and(chosen[1] < my_block, chosen[1] != chosen[0])
     valid = first.astype(jnp.int32) + second.astype(jnp.int32)
@@ -356,7 +370,8 @@
             lanes = wide(group)
             if last:
                 staged[:, lanes] = own_ref[:, lanes].astype(staged.dtype)
-                send(group).start()
+                for part in range(GROUP // SENT):
+                    send(group * (GROUP // SENT) + part).start()
             else:
                 fetch(group, 1).wait()
                 fetch(group, 0).wait()
@@ -366,9 +381,9 @@
 
     if last:
 
-        @pl.loop(0, KEY_VALUE_HEADS)
-        def _(group):
-            send(group).wait()
+        @pl.loop(0, QUERY_HEADS // SENT)
+        def _(part):
+            send(part).wait()
 
 
 def far_attention(selected, queries, own, level, far, last):
@@ -382,7 +397,7 @@
         out_specs = anywhere
         scratch = [
             pltpu.VMEM(queries.shape, jnp.bfloat16),
-            pltpu.SemaphoreType.DMA((KEY_VALUE_HEADS,)),
+            pltpu.SemaphoreType.DMA((QUERY_HEADS // SENT,)),
         ]
     else:
         earlier = anywhere
@@ -399,7 +414,7 @@
         functools.partial(far_kernel, last=last),
         out_shape=out_shape,
         in_specs=[
-            pl.BlockSpec(memory_space=pltpu.SMEM),
+            in_vmem,
             in_vmem,
             earlier,
             earlier,

time: 60.7 us -> 58.8 us (0.969)
  the two profiles are of different devices: /device:TPU:1 before, /device:TPU:5 now
where the time goes in v12:
time: 58.8 us; the launch traced here: 58.1 us
  Pallas kernels  22.5 us (38%)
  starting transfers between devices  20.2 us (34%)
  waiting for transfers between devices  11.2 us (19%)
  local copies, waits for them, and re-layouts  3.67 us (6%)
    pallas_call x2, Pallas kernels, far_attention(): pl.pallas_call(functools.partial(far_kernel, last=last), out_shape=out_sh...  15 us
    ppermute x10, starting transfers between devices, swap(): lax.ppermute(array, 'ctx', [(i, partner(i, step)) for i in range(devices)])  13.7 us
    all_to_all x1, starting transfers between devices, local(): lax.all_to_all(packed, 'ctx', split_axis=0, concat_axis=0, tiled=True)  6.5 us
    ppermute x10, waiting for transfers between devices, swap(): lax.ppermute(array, 'ctx', [(i, partner(i, step)) for i in range(devices)])  5.89 us
    all_to_all x1, waiting for transfers between devices, local(): lax.all_to_all(packed, 'ctx', split_axis=0, concat_axis=0, tiled=True)  5.31 us
    pallas_call x1, Pallas kernels, own_attention(): pl.pallas_call(own_kernel, out_shape=[pltpu.HBM(queries.shape, jnp.float3...  5.13 us
    unnamed x10, local copies, waits for them, and re-layouts  3.49 us
    pallas_call x1, Pallas kernels, pack(): pl.pallas_call(pack_kernel, out_shape=jax.ShapeDtypeStruct((devices, SLOT...  2.16 us
  transfers between devices with their start and end apart: 11, of which 4 were waited for; matrix products, arithmetic and copies ran while one was open for 1% of the time, Pallas kernels for 29%

profile of v12, /device:TPU:5, one launch (start us, length us, event | category | flops | bytes accessed | tf_op | source)
XLA Modules:
  0.0 58.1 jit_solution(3104631180286914811)
XLA Ops:
  0.0 2.2 %pack.1 = bf16[16,256,128]{2,1,0:T(8,128)(2,1)} custom-call(bf16[8,32,512]{2,1,0:T(8,128)(2,1)} %bitcast.10, bf16[8,32,512]{2,1,0:T(8,128)(2,1)} %bitcast.11), custom_call_target="tpu_custom_call" | custom-call | tf_op jit(solution)/shard_map/pack/pallas_call | solution.py:58
  2.2 6.5 %all-to-all-start = ((bf16[16,256,128]{2,1,0:T(8,128)(2,1)}), bf16[16,256,128]{2,1,0:T(8,128)(2,1)S(1)}, u32[]{:S(2)}, u32[]{:S(2)}) async-start(bf16[16,256,128]{2,1,0:T(8,128)(2,1)} %pack.1), calls=%async_computation | async-start | bytes 2097152 | tf_op jit(solution)/shard_map/all_to_all | solution.py:439
  8.7 1.6 %copy-done = bf16[256,4096]{1,0:T(8,128)(2,1)S(1)} copy-done((bf16[256,4096]{1,0:T(8,128)(2,1)S(1)}, bf16[256,4096]{1,0:T(8,128)(2,1)}, u32[]{:S(2)}) %copy-start) | copy-done | bytes 2097176
  10.3 0.9 %copy-done.2 = bf16[256,512]{1,0:T(8,128)(2,1)S(1)} copy-done((bf16[256,512]{1,0:T(8,128)(2,1)S(1)}, bf16[256,512]{1,0:T(8,128)(2,1)}, u32[]{:S(2)}) %copy-start.2) | copy-done | bytes 262168
  11.2 0.9 %copy-done.3 = bf16[256,512]{1,0:T(8,128)(2,1)S(1)} copy-done((bf16[256,512]{1,0:T(8,128)(2,1)S(1)}, bf16[256,512]{1,0:T(8,128)(2,1)}, u32[]{:S(2)}) %copy-start.3) | copy-done | bytes 262168
  12.2 5.1 %own_attention.1 = (f32[256,4096]{1,0:T(8,128)}, f32[256,512]{1,0:T(8,128)}) custom-call(bf16[256,4096]{1,0:T(8,128)(2,1)S(1)} %copy-done, bf16[256,512]{1,0:T(8,128)(2,1)S(1)} %copy-done.2, bf16[256,512]{1,0:T(8,128)(2,1)S(1)} %copy-done.3), custom_call_target="tpu_custom_call" | custom-call | flops 1073741824 | bytes 7340032 | tf_op jit(solution)/shard_map/own_attention/pallas_call | solution.py:200
  17.3 0.1 copy.8
  17.4 0.1 collective-permute-start
  17.5 1.0 %collective-permute-done = s32[1,2]{0,1:T(2,128)S(1)} collective-permute-done((s32[1,2]{0,1:T(2,128)S(1)}, s32[1,2]{0,1:T(2,128)S(1)}, u32[]{:S(2)}, u32[]{:S(2)}) %collective-permute-start) | collective-permute-done | bytes 40 | tf_op jit(solution)/shard_map/ppermute | solution.py:83
  18.6 1.4 %collective-permute-start.1 = (s32[2,2]{0,1:T(2,128)S(1)}, s32[2,2]{0,1:T(2,128)S(1)}, u32[]{:S(2)}, u32[]{:S(2)}) collective-permute-start(s32[2,2]{0,1:T(2,128)S(1)} %pad_add_fusion), channel_id=1, source_target_pairs={{0,2},{1,3},{2,0},{3,1},{4,6},{5,7},{6,4},{7,5},{8,10},{9,11},{10,... | collective-permute-start | bytes 56 | tf_op jit(solution)/shard_map/ppermute | solution.py:83
  20.0 1.3 %collective-permute-done.1 = s32[2,2]{0,1:T(2,128)S(1)} collective-permute-done((s32[2,2]{0,1:T(2,128)S(1)}, s32[2,2]{0,1:T(2,128)S(1)}, u32[]{:S(2)}, u32[]{:S(2)}) %collective-permute-start.1) | collective-permute-done | bytes 48 | tf_op jit(solution)/shard_map/ppermute | solution.py:83
  21.4 1.4 %collective-permute-start.2 = (s32[4,2]{0,1:T(2,128)S(1)}, s32[4,2]{0,1:T(2,128)S(1)}, u32[]{:S(2)}, u32[]{:S(2)}) collective-permute-start(s32[4,2]{0,1:T(2,128)S(1)} %pad_add_fusion.1), channel_id=1, source_target_pairs={{0,4},{1,5},{2,6},{3,7},{4,0},{5,1},{6,2},{7,3},{8,12},{9,13},{10,... | collective-permute-start | bytes 104 | tf_op jit(solution)/shard_map/ppermute | solution.py:83
  22.8 3.5 %collective-permute-done.2 = s32[4,2]{0,1:T(2,128)S(1)} collective-permute-done((s32[4,2]{0,1:T(2,128)S(1)}, s32[4,2]{0,1:T(2,128)S(1)}, u32[]{:S(2)}, u32[]{:S(2)}) %collective-permute-start.2) | collective-permute-done | bytes 64 | tf_op jit(solution)/shard_map/ppermute | solution.py:83
  26.4 0.1 copy.9
  26.5 5.3 %all-to-all-done.held_ref = bf16[16,256,128]{2,1,0:T(8,128)(2,1)S(1)} async-done(((bf16[16,256,128]{2,1,0:T(8,128)(2,1)}), bf16[16,256,128]{2,1,0:T(8,128)(2,1)S(1)}, u32[]{:S(2)}, u32[]{:S(2)}) %all-to-all-start) | async-done | bytes 1048608 | tf_op jit(solution)/shard_map/all_to_all | solution.py:439
  31.8 0.2 pick_pieces.1
  32.1 3.2 %collective-permute-start.4 = (bf16[2,256,128]{2,1,0:T(8,128)(2,1)S(1)}, bf16[2,256,128]{2,1,0:T(8,128)(2,1)S(1)}, u32[]{:S(2)}, u32[]{:S(2)}) collective-permute-start(bf16[2,256,128]{2,1,0:T(8,128)(2,1)S(1)} %get-tuple-element.31), channel_id=1, source_target_pairs={{0,4},{1,5},{2,6},{3,7},{4,0},{5,1},{6,2},{7,3},{8,12},{9,13},{10,... | collective-permute-start | bytes 393224 | tf_op jit(solution)/shard_map/ppermute | solution.py:83
  35.2 1.4 %collective-permute-start.5 = (bf16[2,256,128]{2,1,0:T(8,128)(2,1)S(1)}, bf16[2,256,128]{2,1,0:T(8,128)(2,1)S(1)}, u32[]{:S(2)}, u32[]{:S(2)}) collective-permute-start(bf16[2,256,128]{2,1,0:T(8,128)(2,1)S(1)} %get-tuple-element.32), channel_id=1, source_target_pairs={{0,2},{1,3},{2,0},{3,1},{4,6},{5,7},{6,4},{7,5},{8,10},{9,11},{10,... | collective-permute-start | bytes 393224 | tf_op jit(solution)/shard_map/ppermute | solution.py:83
  36.6 0.5 collective-permute-start.6
  37.1 0.5 collective-permute-start.7
  37.6 1.9 %collective-permute-start.8 = (bf16[2,256,128]{2,1,0:T(8,128)(2,1)S(1)}, bf16[2,256,128]{2,1,0:T(8,128)(2,1)S(1)}, u32[]{:S(2)}, u32[]{:S(2)}) collective-permute-start(bf16[2,256,128]{2,1,0:T(8,128)(2,1)S(1)} %get-tuple-element.37), channel_id=1, source_target_pairs={{0,6},{1,7},{2,4},{3,5},{4,2},{5,3},{6,0},{7,1},{8,14},{9,15},{10,... | collective-permute-start | bytes 393224 | tf_op jit(solution)/shard_map/ppermute | solution.py:83
  39.5 3.3 %collective-permute-start.9 = (bf16[2,256,128]{2,1,0:T(8,128)(2,1)S(1)}, bf16[2,256,128]{2,1,0:T(8,128)(2,1)S(1)}, u32[]{:S(2)}, u32[]{:S(2)}) collective-permute-start(bf16[2,256,128]{2,1,0:T(8,128)(2,1)S(1)} %get-tuple-element.38), channel_id=1, source_target_pairs={{0,7},{1,6},{2,5},{3,4},{4,3},{5,2},{6,1},{7,0},{8,15},{9,14},{10,... | collective-permute-start | bytes 393224 | tf_op jit(solution)/shard_map/ppermute | solution.py:83
  42.8 11.5 %early_attention.1 = (f32[256,4096]{1,0:T(8,128)S(1)}, f32[256,4096]{1,0:T(8,128)S(1)}) custom-call(s32[1,2]{1,0:T(1,128)S(1)} %copy-done.4, bf16[256,4096]{1,0:T(8,128)(2,1)S(1)} %copy-done.1, f32[256,4096]{1,0:T(8,128)} %get-tuple-element.25.own_in, f32[256,512]{1,0:T(8,128)} %get-tuple-element.26.level_in, bf16[2,8,32,128]{3,2,1,0:T(8,128)(2,1)S(1)} %bitcast.16, ...), custom_call_target="tpu_custom_call" | custom-call | flops 1073741824 | bytes 10485760 | tf_op jit(solution)/shard_map/early_attention/pallas_call | solution.py:413
  54.4 3.5 %late_attention.1 = bf16[256,4096]{1,0:T(8,128)(2,1)} custom-call(s32[1,2]{1,0:T(1,128)S(1)} %copy-done.4, bf16[256,4096]{1,0:T(8,128)(2,1)S(1)} %copy-done.1, f32[256,4096]{1,0:T(8,128)S(1)} %get-tuple-element.33.own_in, f32[256,4096]{1,0:T(8,128)S(1)} %get-tuple-element.34.level_in, bf16[2,8,32,128]{3,2,1,0:T(8,128)(2,1)S(1)} %bitcast.12, ...), custom_call_target="tpu_custom_call" | custom-call | flops 1073741824 | bytes 10485760 | tf_op jit(solution)/shard_map/late_attention/pallas_call | solution.py:413
  (19 shorter events, 0.3 us)
Async XLA Ops:
  0.0 17.3 %copy-start.4 = (s32[1,2]{1,0:T(1,128)S(1)}, s32[1,2]{1,0:T(1,128)}, u32[]{:S(2)}) copy-start(s32[1,2]{1,0:T(1,128)} %selected_ref.3) | copy-start | bytes 28
  0.0 42.8 %copy-start.1 = (bf16[256,4096]{1,0:T(8,128)(2,1)S(1)}, bf16[256,4096]{1,0:T(8,128)(2,1)}, u32[]{:S(2)}) copy-start(bf16[256,4096]{1,0:T(8,128)(2,1)} %query_ref.2) | copy-start | bytes 6291460
  2.2 29.6 %all-to-all-start = ((bf16[16,256,128]{2,1,0:T(8,128)(2,1)}), bf16[16,256,128]{2,1,0:T(8,128)(2,1)S(1)}, u32[]{:S(2)}, u32[]{:S(2)}) async-start(bf16[16,256,128]{2,1,0:T(8,128)(2,1)} %pack.1), calls=%async_computation | async-start | bytes 2097152 | tf_op jit(solution)/shard_map/all_to_all | solution.py:439
  8.7 1.6 %copy-start = (bf16[256,4096]{1,0:T(8,128)(2,1)S(1)}, bf16[256,4096]{1,0:T(8,128)(2,1)}, u32[]{:S(2)}) copy-start(bf16[256,4096]{1,0:T(8,128)(2,1)} %query_ref.2) | copy-start | bytes 6291460
  10.3 0.9 %copy-start.2 = (bf16[256,512]{1,0:T(8,128)(2,1)S(1)}, bf16[256,512]{1,0:T(8,128)(2,1)}, u32[]{:S(2)}) copy-start(bf16[256,512]{1,0:T(8,128)(2,1)} %key_ref.1) | copy-start | bytes 786436
  11.2 0.9 %copy-start.3 = (bf16[256,512]{1,0:T(8,128)(2,1)S(1)}, bf16[256,512]{1,0:T(8,128)(2,1)}, u32[]{:S(2)}) copy-start(bf16[256,512]{1,0:T(8,128)(2,1)} %value_ref.1) | copy-start | bytes 786436
  17.4 1.1 %collective-permute-start = (s32[1,2]{0,1:T(2,128)S(1)}, s32[1,2]{0,1:T(2,128)S(1)}, u32[]{:S(2)}, u32[]{:S(2)}) collective-permute-start(s32[1,2]{0,1:T(2,128)S(1)} %copy.8), channel_id=1, source_target_pairs={{0,1},{1,0},{2,3},{3,2},{4,5},{5,4},{6,7},{7,6},{8,9},{9,8},{10,11... | collective-permute-start | bytes 32 | tf_op jit(solution)/shard_map/ppermute | solution.py:83
  18.6 2.7 %collective-permute-start.1 = (s32[2,2]{0,1:T(2,128)S(1)}, s32[2,2]{0,1:T(2,128)S(1)}, u32[]{:S(2)}, u32[]{:S(2)}) collective-permute-start(s32[2,2]{0,1:T(2,128)S(1)} %pad_add_fusion), channel_id=1, source_target_pairs={{0,2},{1,3},{2,0},{3,1},{4,6},{5,7},{6,4},{7,5},{8,10},{9,11},{10,... | collective-permute-start | bytes 56 | tf_op jit(solution)/shard_map/ppermute | solution.py:83
  21.4 4.9 %collective-permute-start.2 = (s32[4,2]{0,1:T(2,128)S(1)}, s32[4,2]{0,1:T(2,128)S(1)}, u32[]{:S(2)}, u32[]{:S(2)}) collective-permute-start(s32[4,2]{0,1:T(2,128)S(1)} %pad_add_fusion.1), channel_id=1, source_target_pairs={{0,4},{1,5},{2,6},{3,7},{4,0},{5,1},{6,2},{7,3},{8,12},{9,13},{10,... | collective-permute-start | bytes 104 | tf_op jit(solution)/shard_map/ppermute | solution.py:83
  32.0 5.6 %collective-permute-start.3 = (bf16[2,256,128]{2,1,0:T(8,128)(2,1)S(1)}, bf16[2,256,128]{2,1,0:T(8,128)(2,1)S(1)}, u32[]{:S(2)}, u32[]{:S(2)}) collective-permute-start(bf16[2,256,128]{2,1,0:T(8,128)(2,1)S(1)} %get-tuple-element.30), channel_id=1, source_target_pairs={{0,1},{1,0},{2,3},{3,2},{4,5},{5,4},{6,7},{7,6},{8,9},{9,8},{10,11... | collective-permute-start | bytes 393224 | tf_op jit(solution)/shard_map/ppermute | solution.py:83
  32.1 7.4 %collective-permute-start.4 = (bf16[2,256,128]{2,1,0:T(8,128)(2,1)S(1)}, bf16[2,256,128]{2,1,0:T(8,128)(2,1)S(1)}, u32[]{:S(2)}, u32[]{:S(2)}) collective-permute-start(bf16[2,256,128]{2,1,0:T(8,128)(2,1)S(1)} %get-tuple-element.31), channel_id=1, source_target_pairs={{0,4},{1,5},{2,6},{3,7},{4,0},{5,1},{6,2},{7,3},{8,12},{9,13},{10,... | collective-permute-start | bytes 393224 | tf_op jit(solution)/shard_map/ppermute | solution.py:83
  35.2 7.6 %collective-permute-start.5 = (bf16[2,256,128]{2,1,0:T(8,128)(2,1)S(1)}, bf16[2,256,128]{2,1,0:T(8,128)(2,1)S(1)}, u32[]{:S(2)}, u32[]{:S(2)}) collective-permute-start(bf16[2,256,128]{2,1,0:T(8,128)(2,1)S(1)} %get-tuple-element.32), channel_id=1, source_target_pairs={{0,2},{1,3},{2,0},{3,1},{4,6},{5,7},{6,4},{7,5},{8,10},{9,11},{10,... | collective-permute-start | bytes 393224 | tf_op jit(solution)/shard_map/ppermute | solution.py:83
  36.6 17.8 %collective-permute-start.6 = (bf16[2,256,128]{2,1,0:T(8,128)(2,1)S(1)}, bf16[2,256,128]{2,1,0:T(8,128)(2,1)S(1)}, u32[]{:S(2)}, u32[]{:S(2)}) collective-permute-start(bf16[2,256,128]{2,1,0:T(8,128)(2,1)S(1)} %get-tuple-element.35), channel_id=1, source_target_pairs={{0,5},{1,4},{2,7},{3,6},{4,1},{5,0},{6,3},{7,2},{8,13},{9,12},{10,... | collective-permute-start | bytes 393224 | tf_op jit(solution)/shard_map/ppermute | solution.py:83
  37.1 17.3 %collective-permute-start.7 = (bf16[2,256,128]{2,1,0:T(8,128)(2,1)S(1)}, bf16[2,256,128]{2,1,0:T(8,128)(2,1)S(1)}, u32[]{:S(2)}, u32[]{:S(2)}) collective-permute-start(bf16[2,256,128]{2,1,0:T(8,128)(2,1)S(1)} %get-tuple-element.36), channel_id=1, source_target_pairs={{0,3},{1,2},{2,1},{3,0},{4,7},{5,6},{6,5},{7,4},{8,11},{9,10},{10,... | collective-permute-start | bytes 393224 | tf_op jit(solution)/shard_map/ppermute | solution.py:83
  37.6 16.8 %collective-permute-start.8 = (bf16[2,256,128]{2,1,0:T(8,128)(2,1)S(1)}, bf16[2,256,128]{2,1,0:T(8,128)(2,1)S(1)}, u32[]{:S(2)}, u32[]{:S(2)}) collective-permute-start(bf16[2,256,128]{2,1,0:T(8,128)(2,1)S(1)} %get-tuple-element.37), channel_id=1, source_target_pairs={{0,6},{1,7},{2,4},{3,5},{4,2},{5,3},{6,0},{7,1},{8,14},{9,15},{10,... | collective-permute-start | bytes 393224 | tf_op jit(solution)/shard_map/ppermute | solution.py:83
  39.5 14.9 %collective-permute-start.9 = (bf16[2,256,128]{2,1,0:T(8,128)(2,1)S(1)}, bf16[2,256,128]{2,1,0:T(8,128)(2,1)S(1)}, u32[]{:S(2)}, u32[]{:S(2)}) collective-permute-start(bf16[2,256,128]{2,1,0:T(8,128)(2,1)S(1)} %get-tuple-element.38), channel_id=1, source_target_pairs={{0,7},{1,6},{2,5},{3,4},{4,3},{5,2},{6,1},{7,0},{8,15},{9,14},{10,... | collective-permute-start | bytes 393224 | tf_op jit(solution)/shard_map/ppermute | solution.py:83

commit v13 on v12

--- a/solution.py
+++ b/solution.py
@@ -291,15 +291,21 @@
             return jnp.concatenate([narrow] * (count // HEAD_SIZE), axis=1)
 
         def quick(group, head, scores, value, largest):
-            lanes = head_of(group, head)
-            level = level_of(group, head)
-            weights = jnp.exp2(scores * FACTOR - repeat(level)).astype(jnp.bfloat16)
-            both = dot(weights, value)
-            row_sum = 1.0 + both[:, HEAD_SIZE:]
-            store(lanes, own_ref[:, lanes] + both[:, :HEAD_SIZE], row_sum, level)
-            return jnp.maximum(
-                largest, jnp.max(row_sum.reshape(rows // 8, 8, HEAD_SIZE), axis=0)
-            )
+            lanes = [head_of(group, head + h) for h in range(PAIR)]
+            levels = [level_of(group, head + h) for h in range(PAIR)]
+            weights = [
+                jnp.exp2(scores[h * rows : (h + 1) * rows] * FACTOR - repeat(levels[h]))
+                for h in range(PAIR)
+            ]
+            both = dot(jnp.concatenate(weights, axis=0).astype(jnp.bfloat16), value)
+            for h in range(PAIR):
+                part = both[h * rows : (h + 1) * rows]
+                row_sum = 1.0 + part[:, HEAD_SIZE:]
+                store(lanes[h], own_ref[:, lanes[h]] + part[:, :HEAD_SIZE], row_sum, levels[h])
+                largest = jnp.maximum(
+                    largest, jnp.max(row_sum.reshape(rows // 8, 8, HEAD_SIZE), axis=0)
+                )
+            return largest
 
         def careful(group, head, scores, value):
             lanes = head_of(group, head)
@@ -312,24 +318,25 @@
             mixture = own_ref[:, lanes] * share + both[:, :HEAD_SIZE]
             store(lanes, mixture, share + both[:, HEAD_SIZE:], shift)
 
-        def score(group, head, keys_across):
-            return dot(query_ref[:, head_of(group, head)], keys_across)
+        def score(group, head, keys_across, heads=1):
+            query = [query_ref[:, head_of(group, head + h)] for h in range(heads)]
+            return dot(jnp.concatenate(query, axis=0), keys_across)
 
         largest = jnp.zeros((8, HEAD_SIZE), jnp.float32)
-        order = [(g, h) for g in range(KEY_VALUE_HEADS) for h in range(GROUP)]
+        order = [(g, h) for g in range(KEY_VALUE_HEADS) for h in range(0, GROUP, PAIR)]
         held = {0: keys_and_values(0)}
-        scores = score(0, 0, held[0][0])
+        scores = score(0, 0, held[0][0], PAIR)
         for (group, head), later in zip(order, order[1:] + [None]):
             following = None
             if later is not None:
                 if later[0] not in held:
                     held[later[0]] = keys_and_values(later[0])
-                following = score(*later, held[later[0]][0])
+                following = score(*later, held[later[0]][0], PAIR)
             if head == 0 and not last:
                 fetch(group, 1).wait()
                 fetch(group, 0).wait()
             largest = quick(group, head, scores, held[group][1], largest)
-            if (head + 1) % SENT == 0 and last:
+            if (head + PAIR) % SENT == 0 and last:
                 send((group * GROUP + head) // SENT).start()
             scores = following
 

time: 58.8 us -> 58.6 us (level)
  Pallas kernels: 22.5 us -> 21.8 us
    pallas_call x2, Pallas kernels: 15 us -> 14.4 us  [far_attention(): pl.pallas_call(functools.partial(far_kernel, last=last), out_shape=out_sh...]
where the time goes in v13:
time: 58.6 us; the launch traced here: 57.4 us
  Pallas kernels  21.8 us (37%)
  starting transfers between devices  20.2 us (34%)
  waiting for transfers between devices  11.2 us (19%)
  local copies, waits for them, and re-layouts  3.67 us (6%)
    pallas_call x2, Pallas kernels, far_attention(): pl.pallas_call(functools.partial(far_kernel, last=last), out_shape=out_sh...  14.4 us
    ppermute x10, starting transfers between devices, swap(): lax.ppermute(array, 'ctx', [(i, partner(i, step)) for i in range(devices)])  13.7 us
    all_to_all x1, starting transfers between devices, local(): lax.all_to_all(packed, 'ctx', split_axis=0, concat_axis=0, tiled=True)  6.5 us
    ppermute x10, waiting for transfers between devices, swap(): lax.ppermute(array, 'ctx', [(i, partner(i, step)) for i in range(devices)])  5.89 us
    all_to_all x1, waiting for transfers between devices, local(): lax.all_to_all(packed, 'ctx', split_axis=0, concat_axis=0, tiled=True)  5.31 us
    pallas_call x1, Pallas kernels, own_attention(): pl.pallas_call(own_kernel, out_shape=[pltpu.HBM(queries.shape, jnp.float3...  5.13 us
    unnamed x10, local copies, waits for them, and re-layouts  3.49 us
    pallas_call x1, Pallas kernels, pack(): pl.pallas_call(pack_kernel, out_shape=jax.ShapeDtypeStruct((devices, SLOT...  2.16 us
  transfers between devices with their start and end apart: 11, of which 4 were waited for; matrix products, arithmetic and copies ran while one was open for 1% of the time, Pallas kernels for 29%

profile of v13, /device:TPU:5, one launch (start us, length us, event | category | flops | bytes accessed | tf_op | source)
XLA Modules:
  0.0 57.4 jit_solution(17532947789745006057)
XLA Ops:
  0.0 2.2 %pack.1 = bf16[16,256,128]{2,1,0:T(8,128)(2,1)} custom-call(bf16[8,32,512]{2,1,0:T(8,128)(2,1)} %bitcast.10, bf16[8,32,512]{2,1,0:T(8,128)(2,1)} %bitcast.11), custom_call_target="tpu_custom_call" | custom-call | tf_op jit(solution)/shard_map/pack/pallas_call | solution.py:58
  2.2 6.5 %all-to-all-start = ((bf16[16,256,128]{2,1,0:T(8,128)(2,1)}), bf16[16,256,128]{2,1,0:T(8,128)(2,1)S(1)}, u32[]{:S(2)}, u32[]{:S(2)}) async-start(bf16[16,256,128]{2,1,0:T(8,128)(2,1)} %pack.1), calls=%async_computation | async-start | bytes 2097152 | tf_op jit(solution)/shard_map/all_to_all | solution.py:446
  8.7 1.6 %copy-done = bf16[256,4096]{1,0:T(8,128)(2,1)S(1)} copy-done((bf16[256,4096]{1,0:T(8,128)(2,1)S(1)}, bf16[256,4096]{1,0:T(8,128)(2,1)}, u32[]{:S(2)}) %copy-start) | copy-done | bytes 2097176
  10.3 0.9 %copy-done.2 = bf16[256,512]{1,0:T(8,128)(2,1)S(1)} copy-done((bf16[256,512]{1,0:T(8,128)(2,1)S(1)}, bf16[256,512]{1,0:T(8,128)(2,1)}, u32[]{:S(2)}) %copy-start.2) | copy-done | bytes 262168
  11.2 0.9 %copy-done.3 = bf16[256,512]{1,0:T(8,128)(2,1)S(1)} copy-done((bf16[256,512]{1,0:T(8,128)(2,1)S(1)}, bf16[256,512]{1,0:T(8,128)(2,1)}, u32[]{:S(2)}) %copy-start.3) | copy-done | bytes 262168
  12.2 5.1 %own_attention.1 = (f32[256,4096]{1,0:T(8,128)}, f32[256,512]{1,0:T(8,128)}) custom-call(bf16[256,4096]{1,0:T(8,128)(2,1)S(1)} %copy-done, bf16[256,512]{1,0:T(8,128)(2,1)S(1)} %copy-done.2, bf16[256,512]{1,0:T(8,128)(2,1)S(1)} %copy-done.3), custom_call_target="tpu_custom_call" | custom-call | flops 1073741824 | bytes 7340032 | tf_op jit(solution)/shard_map/own_attention/pallas_call | solution.py:200
  17.3 0.1 copy.8
  17.4 0.1 collective-permute-start
  17.5 1.0 %collective-permute-done = s32[1,2]{0,1:T(2,128)S(1)} collective-permute-done((s32[1,2]{0,1:T(2,128)S(1)}, s32[1,2]{0,1:T(2,128)S(1)}, u32[]{:S(2)}, u32[]{:S(2)}) %collective-permute-start) | collective-permute-done | bytes 40 | tf_op jit(solution)/shard_map/ppermute | solution.py:83
  18.6 1.4 %collective-permute-start.1 = (s32[2,2]{0,1:T(2,128)S(1)}, s32[2,2]{0,1:T(2,128)S(1)}, u32[]{:S(2)}, u32[]{:S(2)}) collective-permute-start(s32[2,2]{0,1:T(2,128)S(1)} %pad_add_fusion), channel_id=1, source_target_pairs={{0,2},{1,3},{2,0},{3,1},{4,6},{5,7},{6,4},{7,5},{8,10},{9,11},{10,... | collective-permute-start | bytes 56 | tf_op jit(solution)/shard_map/ppermute | solution.py:83
  20.0 1.3 %collective-permute-done.1 = s32[2,2]{0,1:T(2,128)S(1)} collective-permute-done((s32[2,2]{0,1:T(2,128)S(1)}, s32[2,2]{0,1:T(2,128)S(1)}, u32[]{:S(2)}, u32[]{:S(2)}) %collective-permute-start.1) | collective-permute-done | bytes 48 | tf_op jit(solution)/shard_map/ppermute | solution.py:83
  21.4 1.4 %collective-permute-start.2 = (s32[4,2]{0,1:T(2,128)S(1)}, s32[4,2]{0,1:T(2,128)S(1)}, u32[]{:S(2)}, u32[]{:S(2)}) collective-permute-start(s32[4,2]{0,1:T(2,128)S(1)} %pad_add_fusion.1), channel_id=1, source_target_pairs={{0,4},{1,5},{2,6},{3,7},{4,0},{5,1},{6,2},{7,3},{8,12},{9,13},{10,... | collective-permute-start | bytes 104 | tf_op jit(solution)/shard_map/ppermute | solution.py:83
  22.8 3.5 %collective-permute-done.2 = s32[4,2]{0,1:T(2,128)S(1)} collective-permute-done((s32[4,2]{0,1:T(2,128)S(1)}, s32[4,2]{0,1:T(2,128)S(1)}, u32[]{:S(2)}, u32[]{:S(2)}) %collective-permute-start.2) | collective-permute-done | bytes 64 | tf_op jit(solution)/shard_map/ppermute | solution.py:83
  26.4 0.1 copy.9
  26.5 5.3 %all-to-all-done.held_ref = bf16[16,256,128]{2,1,0:T(8,128)(2,1)S(1)} async-done(((bf16[16,256,128]{2,1,0:T(8,128)(2,1)}), bf16[16,256,128]{2,1,0:T(8,128)(2,1)S(1)}, u32[]{:S(2)}, u32[]{:S(2)}) %all-to-all-start) | async-done | bytes 1048608 | tf_op jit(solution)/shard_map/all_to_all | solution.py:446
  31.8 0.2 pick_pieces.1
  32.1 3.2 %collective-permute-start.4 = (bf16[2,256,128]{2,1,0:T(8,128)(2,1)S(1)}, bf16[2,256,128]{2,1,0:T(8,128)(2,1)S(1)}, u32[]{:S(2)}, u32[]{:S(2)}) collective-permute-start(bf16[2,256,128]{2,1,0:T(8,128)(2,1)S(1)} %get-tuple-element.31), channel_id=1, source_target_pairs={{0,4},{1,5},{2,6},{3,7},{4,0},{5,1},{6,2},{7,3},{8,12},{9,13},{10,... | collective-permute-start | bytes 393224 | tf_op jit(solution)/shard_map/ppermute | solution.py:83
  35.2 1.4 %collective-permute-start.5 = (bf16[2,256,128]{2,1,0:T(8,128)(2,1)S(1)}, bf16[2,256,128]{2,1,0:T(8,128)(2,1)S(1)}, u32[]{:S(2)}, u32[]{:S(2)}) collective-permute-start(bf16[2,256,128]{2,1,0:T(8,128)(2,1)S(1)} %get-tuple-element.32), channel_id=1, source_target_pairs={{0,2},{1,3},{2,0},{3,1},{4,6},{5,7},{6,4},{7,5},{8,10},{9,11},{10,... | collective-permute-start | bytes 393224 | tf_op jit(solution)/shard_map/ppermute | solution.py:83
  36.6 0.5 collective-permute-start.6
  37.1 0.5 collective-permute-start.7
  37.6 1.9 %collective-permute-start.8 = (bf16[2,256,128]{2,1,0:T(8,128)(2,1)S(1)}, bf16[2,256,128]{2,1,0:T(8,128)(2,1)S(1)}, u32[]{:S(2)}, u32[]{:S(2)}) collective-permute-start(bf16[2,256,128]{2,1,0:T(8,128)(2,1)S(1)} %get-tuple-element.37), channel_id=1, source_target_pairs={{0,6},{1,7},{2,4},{3,5},{4,2},{5,3},{6,0},{7,1},{8,14},{9,15},{10,... | collective-permute-start | bytes 393224 | tf_op jit(solution)/shard_map/ppermute | solution.py:83
  39.5 3.3 %collective-permute-start.9 = (bf16[2,256,128]{2,1,0:T(8,128)(2,1)S(1)}, bf16[2,256,128]{2,1,0:T(8,128)(2,1)S(1)}, u32[]{:S(2)}, u32[]{:S(2)}) collective-permute-start(bf16[2,256,128]{2,1,0:T(8,128)(2,1)S(1)} %get-tuple-element.38), channel_id=1, source_target_pairs={{0,7},{1,6},{2,5},{3,4},{4,3},{5,2},{6,1},{7,0},{8,15},{9,14},{10,... | collective-permute-start | bytes 393224 | tf_op jit(solution)/shard_map/ppermute | solution.py:83
  42.8 11.3 %early_attention.1 = (f32[256,4096]{1,0:T(8,128)S(1)}, f32[256,4096]{1,0:T(8,128)S(1)}) custom-call(s32[1,2]{1,0:T(1,128)S(1)} %copy-done.4, bf16[256,4096]{1,0:T(8,128)(2,1)S(1)} %copy-done.1, f32[256,4096]{1,0:T(8,128)} %get-tuple-element.25.own_in, f32[256,512]{1,0:T(8,128)} %get-tuple-element.26.level_in, bf16[2,8,32,128]{3,2,1,0:T(8,128)(2,1)S(1)} %bitcast.16, ...), custom_call_target="tpu_custom_call" | custom-call | flops 1073741824 | bytes 10485760 | tf_op jit(solution)/shard_map/early_attention/pallas_call | solution.py:420
  54.2 3.1 %late_attention.1 = bf16[256,4096]{1,0:T(8,128)(2,1)} custom-call(s32[1,2]{1,0:T(1,128)S(1)} %copy-done.4, bf16[256,4096]{1,0:T(8,128)(2,1)S(1)} %copy-done.1, f32[256,4096]{1,0:T(8,128)S(1)} %get-tuple-element.33.own_in, f32[256,4096]{1,0:T(8,128)S(1)} %get-tuple-element.34.level_in, bf16[2,8,32,128]{3,2,1,0:T(8,128)(2,1)S(1)} %bitcast.12, ...), custom_call_target="tpu_custom_call" | custom-call | flops 1073741824 | bytes 10485760 | tf_op jit(solution)/shard_map/late_attention/pallas_call | solution.py:420
  (19 shorter events, 0.3 us)
Async XLA Ops:
  0.0 17.3 %copy-start.4 = (s32[1,2]{1,0:T(1,128)S(1)}, s32[1,2]{1,0:T(1,128)}, u32[]{:S(2)}) copy-start(s32[1,2]{1,0:T(1,128)} %selected_ref.3) | copy-start | bytes 28
  0.0 42.8 %copy-start.1 = (bf16[256,4096]{1,0:T(8,128)(2,1)S(1)}, bf16[256,4096]{1,0:T(8,128)(2,1)}, u32[]{:S(2)}) copy-start(bf16[256,4096]{1,0:T(8,128)(2,1)} %query_ref.2) | copy-start | bytes 6291460
  2.2 29.6 %all-to-all-start = ((bf16[16,256,128]{2,1,0:T(8,128)(2,1)}), bf16[16,256,128]{2,1,0:T(8,128)(2,1)S(1)}, u32[]{:S(2)}, u32[]{:S(2)}) async-start(bf16[16,256,128]{2,1,0:T(8,128)(2,1)} %pack.1), calls=%async_computation | async-start | bytes 2097152 | tf_op jit(solution)/shard_map/all_to_all | solution.py:446
  8.7 1.6 %copy-start = (bf16[256,4096]{1,0:T(8,128)(2,1)S(1)}, bf16[256,4096]{1,0:T(8,128)(2,1)}, u32[]{:S(2)}) copy-start(bf16[256,4096]{1,0:T(8,128)(2,1)} %query_ref.2) | copy-start | bytes 6291460
  10.3 0.9 %copy-start.2 = (bf16[256,512]{1,0:T(8,128)(2,1)S(1)}, bf16[256,512]{1,0:T(8,128)(2,1)}, u32[]{:S(2)}) copy-start(bf16[256,512]{1,0:T(8,128)(2,1)} %key_ref.1) | copy-start | bytes 786436
  11.2 0.9 %copy-start.3 = (bf16[256,512]{1,0:T(8,128)(2,1)S(1)}, bf16[256,512]{1,0:T(8,128)(2,1)}, u32[]{:S(2)}) copy-start(bf16[256,512]{1,0:T(8,128)(2,1)} %value_ref.1) | copy-start | bytes 786436
  17.4 1.1 %collective-permute-start = (s32[1,2]{0,1:T(2,128)S(1)}, s32[1,2]{0,1:T(2,128)S(1)}, u32[]{:S(2)}, u32[]{:S(2)}) collective-permute-start(s32[1,2]{0,1:T(2,128)S(1)} %copy.8), channel_id=1, source_target_pairs={{0,1},{1,0},{2,3},{3,2},{4,5},{5,4},{6,7},{7,6},{8,9},{9,8},{10,11... | collective-permute-start | bytes 32 | tf_op jit(solution)/shard_map/ppermute | solution.py:83
  18.6 2.7 %collective-permute-start.1 = (s32[2,2]{0,1:T(2,128)S(1)}, s32[2,2]{0,1:T(2,128)S(1)}, u32[]{:S(2)}, u32[]{:S(2)}) collective-permute-start(s32[2,2]{0,1:T(2,128)S(1)} %pad_add_fusion), channel_id=1, source_target_pairs={{0,2},{1,3},{2,0},{3,1},{4,6},{5,7},{6,4},{7,5},{8,10},{9,11},{10,... | collective-permute-start | bytes 56 | tf_op jit(solution)/shard_map/ppermute | solution.py:83
  21.4 4.9 %collective-permute-start.2 = (s32[4,2]{0,1:T(2,128)S(1)}, s32[4,2]{0,1:T(2,128)S(1)}, u32[]{:S(2)}, u32[]{:S(2)}) collective-permute-start(s32[4,2]{0,1:T(2,128)S(1)} %pad_add_fusion.1), channel_id=1, source_target_pairs={{0,4},{1,5},{2,6},{3,7},{4,0},{5,1},{6,2},{7,3},{8,12},{9,13},{10,... | collective-permute-start | bytes 104 | tf_op jit(solution)/shard_map/ppermute | solution.py:83
  32.0 5.6 %collective-permute-start.3 = (bf16[2,256,128]{2,1,0:T(8,128)(2,1)S(1)}, bf16[2,256,128]{2,1,0:T(8,128)(2,1)S(1)}, u32[]{:S(2)}, u32[]{:S(2)}) collective-permute-start(bf16[2,256,128]{2,1,0:T(8,128)(2,1)S(1)} %get-tuple-element.30), channel_id=1, source_target_pairs={{0,1},{1,0},{2,3},{3,2},{4,5},{5,4},{6,7},{7,6},{8,9},{9,8},{10,11... | collective-permute-start | bytes 393224 | tf_op jit(solution)/shard_map/ppermute | solution.py:83
  32.1 7.4 %collective-permute-start.4 = (bf16[2,256,128]{2,1,0:T(8,128)(2,1)S(1)}, bf16[2,256,128]{2,1,0:T(8,128)(2,1)S(1)}, u32[]{:S(2)}, u32[]{:S(2)}) collective-permute-start(bf16[2,256,128]{2,1,0:T(8,128)(2,1)S(1)} %get-tuple-element.31), channel_id=1, source_target_pairs={{0,4},{1,5},{2,6},{3,7},{4,0},{5,1},{6,2},{7,3},{8,12},{9,13},{10,... | collective-permute-start | bytes 393224 | tf_op jit(solution)/shard_map/ppermute | solution.py:83
  35.2 7.6 %collective-permute-start.5 = (bf16[2,256,128]{2,1,0:T(8,128)(2,1)S(1)}, bf16[2,256,128]{2,1,0:T(8,128)(2,1)S(1)}, u32[]{:S(2)}, u32[]{:S(2)}) collective-permute-start(bf16[2,256,128]{2,1,0:T(8,128)(2,1)S(1)} %get-tuple-element.32), channel_id=1, source_target_pairs={{0,2},{1,3},{2,0},{3,1},{4,6},{5,7},{6,4},{7,5},{8,10},{9,11},{10,... | collective-permute-start | bytes 393224 | tf_op jit(solution)/shard_map/ppermute | solution.py:83
  36.6 17.5 %collective-permute-start.6 = (bf16[2,256,128]{2,1,0:T(8,128)(2,1)S(1)}, bf16[2,256,128]{2,1,0:T(8,128)(2,1)S(1)}, u32[]{:S(2)}, u32[]{:S(2)}) collective-permute-start(bf16[2,256,128]{2,1,0:T(8,128)(2,1)S(1)} %get-tuple-element.35), channel_id=1, source_target_pairs={{0,5},{1,4},{2,7},{3,6},{4,1},{5,0},{6,3},{7,2},{8,13},{9,12},{10,... | collective-permute-start | bytes 393224 | tf_op jit(solution)/shard_map/ppermute | solution.py:83
  37.1 17.1 %collective-permute-start.7 = (bf16[2,256,128]{2,1,0:T(8,128)(2,1)S(1)}, bf16[2,256,128]{2,1,0:T(8,128)(2,1)S(1)}, u32[]{:S(2)}, u32[]{:S(2)}) collective-permute-start(bf16[2,256,128]{2,1,0:T(8,128)(2,1)S(1)} %get-tuple-element.36), channel_id=1, source_target_pairs={{0,3},{1,2},{2,1},{3,0},{4,7},{5,6},{6,5},{7,4},{8,11},{9,10},{10,... | collective-permute-start | bytes 393224 | tf_op jit(solution)/shard_map/ppermute | solution.py:83
  37.6 16.5 %collective-permute-start.8 = (bf16[2,256,128]{2,1,0:T(8,128)(2,1)S(1)}, bf16[2,256,128]{2,1,0:T(8,128)(2,1)S(1)}, u32[]{:S(2)}, u32[]{:S(2)}) collective-permute-start(bf16[2,256,128]{2,1,0:T(8,128)(2,1)S(1)} %get-tuple-element.37), channel_id=1, source_target_pairs={{0,6},{1,7},{2,4},{3,5},{4,2},{5,3},{6,0},{7,1},{8,14},{9,15},{10,... | collective-permute-start | bytes 393224 | tf_op jit(solution)/shard_map/ppermute | solution.py:83
  39.5 14.6 %collective-permute-start.9 = (bf16[2,256,128]{2,1,0:T(8,128)(2,1)S(1)}, bf16[2,256,128]{2,1,0:T(8,128)(2,1)S(1)}, u32[]{:S(2)}, u32[]{:S(2)}) collective-permute-start(bf16[2,256,128]{2,1,0:T(8,128)(2,1)S(1)} %get-tuple-element.38), channel_id=1, source_target_pairs={{0,7},{1,6},{2,5},{3,4},{4,3},{5,2},{6,1},{7,0},{8,15},{9,14},{10,... | collective-permute-start | bytes 393224 | tf_op jit(solution)/shard_map/ppermute | solution.py:83

commit v14 on v12

--- a/solution.py
+++ b/solution.py
@@ -15,6 +15,16 @@
 SLOTS = 2 * KEY_VALUE_HEADS
 COPIES = 2
 MIB = 1024 * 1024
+
+
+def mixed_order(devices):
+    shares = devices // COPIES
+    return [copy * shares + share for share in range(shares) for copy in range(COPIES)]
+
+
+def place_of(block, devices):
+    shares = devices // COPIES
+    return block % shares * COPIES + block // shares
 
 
 def pack_kernel(key_ref, value_ref, out_ref, staged, arrived, left):
@@ -33,9 +43,7 @@
     def give(which, copy):
         rows = pl.ds(which * half, half)
         return pltpu.make_async_copy(
-            staged.at[:, rows, :],
-            out_ref.at[pl.ds(copy * shares, shares), rows, :],
-            left.at[which, copy],
+            staged.at[:, rows, :], out_ref.at[:, copy, rows, :], left.at[which, copy]
         )
 
     for slot in range(SLOTS):
@@ -58,7 +66,7 @@
         return pl.pallas_call(
             pack_kernel,
             out_shape=jax.ShapeDtypeStruct(
-                (devices, SLOTS * piece_rows, HEAD_SIZE), jnp.bfloat16
+                (shares, COPIES, SLOTS * piece_rows, HEAD_SIZE), jnp.bfloat16
             ),
             in_specs=[pl.BlockSpec(memory_space=pl.ANY)] * 2,
             out_specs=pl.BlockSpec(memory_space=pl.ANY),
@@ -68,11 +76,13 @@
                 pltpu.SemaphoreType.DMA((2, COPIES)),
             ],
             name="pack",
-        )(keys.reshape(split), values.reshape(split))
+        )(keys.reshape(split), values.reshape(split)).reshape(
+            devices, SLOTS * piece_rows, HEAD_SIZE
+        )
     both = jnp.concatenate([keys, values], axis=1)
     both = both.reshape(shares, piece_rows, SLOTS, HEAD_SIZE).transpose(0, 2, 1, 3)
     both = both.reshape(shares, SLOTS * piece_rows, HEAD_SIZE)
-    return jnp.concatenate([both] * COPIES, axis=0)
+    return jnp.repeat(both, COPIES, axis=0)
 
 
 def partner(position, step):
@@ -436,11 +446,18 @@
     piece_rows = rows * COPIES // devices
     packed = pack(all_key_states, all_value_states, devices)
     packed, queries = lax.optimization_barrier((packed, queries))
-    held = lax.all_to_all(packed, "ctx", split_axis=0, concat_axis=0, tiled=True)
+    held = lax.all_to_all(
+        packed,
+        "ctx",
+        split_axis=0,
+        concat_axis=0,
+        axis_index_groups=[mixed_order(devices)],
+        tiled=True,
+    )
     own, level = own_attention(queries, all_key_states, all_value_states)
     mine, own, level = lax.optimization_barrier((selected, own, level))
     requests = exchange_requests(mine, devices // COPIES, devices)
-    requests = jnp.clip(requests, 0, devices - 1)
+    requests = place_of(jnp.clip(requests, 0, devices - 1), devices)
     moved = deliver(pick_pieces(requests, held), devices)
     far = [m.reshape(2, SLOTS, piece_rows, HEAD_SIZE) for m in moved]
     early, late = far[: len(far) // 2], far[len(far) // 2 :]

time: 58.8 us -> 58.9 us (level)
  starting transfers between devices: 20.2 us -> 16.1 us
  waiting for transfers between devices: 11.2 us -> 14.9 us
    ppermute x10, starting transfers between devices: 13.7 us -> 9.64 us  [swap(): lax.ppermute(array, 'ctx', [(i, partner(i, step)) for i in range(devices)])]
    all_to_all x1, waiting for transfers between devices: 5.31 us -> 8.13 us  [local(): lax.all_to_all(packed, 'ctx', split_axis=0, concat_axis=0, axis_index_gro...]
    ppermute x10, waiting for transfers between devices: 5.89 us -> 6.82 us  [swap(): lax.ppermute(array, 'ctx', [(i, partner(i, step)) for i in range(devices)])]
  transfers between devices with their start and end apart: 11 -> 11, of which waited for: 4 -> 5; matrix products, arithmetic and copies ran while one was open for 1% -> 1% of each run, Pallas kernels for 29% -> 29%
where the time goes in v14:
time: 58.9 us; the launch traced here: 57.8 us
  Pallas kernels  22.5 us (38%)
  starting transfers between devices  16.1 us (27%)
  waiting for transfers between devices  14.9 us (25%)
  local copies, waits for them, and re-layouts  3.67 us (6%)
    pallas_call x2, Pallas kernels, far_attention(): pl.pallas_call(functools.partial(far_kernel, last=last), out_shape=out_sh...  15 us
    ppermute x10, starting transfers between devices, swap(): lax.ppermute(array, 'ctx', [(i, partner(i, step)) for i in range(devices)])  9.64 us
    all_to_all x1, waiting for transfers between devices, local(): lax.all_to_all(packed, 'ctx', split_axis=0, concat_axis=0, axis_index_gro...  8.13 us
    ppermute x10, waiting for transfers between devices, swap(): lax.ppermute(array, 'ctx', [(i, partner(i, step)) for i in range(devices)])  6.82 us
    all_to_all x1, starting transfers between devices, local(): lax.all_to_all(packed, 'ctx', split_axis=0, concat_axis=0, axis_index_gro...  6.5 us
    pallas_call x1, Pallas kernels, own_attention(): pl.pallas_call(own_kernel, out_shape=[pltpu.HBM(queries.shape, jnp.float3...  5.13 us
    unnamed x10, local copies, waits for them, and re-layouts  3.49 us
    pallas_call x1, Pallas kernels, pack(): pl.pallas_call(pack_kernel, out_shape=jax.ShapeDtypeStruct((shares, COPIE...  2.16 us
  transfers between devices with their start and end apart: 11, of which 5 were waited for; matrix products, arithmetic and copies ran while one was open for 1% of the time, Pallas kernels for 29%

profile of v14, /device:TPU:5, one launch (start us, length us, event | category | flops | bytes accessed | tf_op | source)
XLA Modules:
  0.0 57.8 jit_solution(10815689114599874344)
XLA Ops:
  0.0 2.2 %pack.1 = bf16[8,2,256,128]{3,2,1,0:T(8,128)(2,1)} custom-call(bf16[8,32,512]{2,1,0:T(8,128)(2,1)} %bitcast.11, bf16[8,32,512]{2,1,0:T(8,128)(2,1)} %bitcast.12), custom_call_target="tpu_custom_call" | custom-call | tf_op jit(solution)/shard_map/pack/pallas_call | solution.py:66
  2.2 6.5 %all-to-all-start = ((bf16[16,256,128]{2,1,0:T(8,128)(2,1)}), bf16[16,256,128]{2,1,0:T(8,128)(2,1)S(1)}, u32[]{:S(2)}, u32[]{:S(2)}) async-start(bf16[16,256,128]{2,1,0:T(8,128)(2,1)} %bitcast.21), calls=%async_computation | async-start | bytes 2097152 | tf_op jit(solution)/shard_map/all_to_all | solution.py:449
  8.7 1.6 %copy-done = bf16[256,4096]{1,0:T(8,128)(2,1)S(1)} copy-done((bf16[256,4096]{1,0:T(8,128)(2,1)S(1)}, bf16[256,4096]{1,0:T(8,128)(2,1)}, u32[]{:S(2)}) %copy-start) | copy-done | bytes 2097176
  10.3 0.9 %copy-done.2 = bf16[256,512]{1,0:T(8,128)(2,1)S(1)} copy-done((bf16[256,512]{1,0:T(8,128)(2,1)S(1)}, bf16[256,512]{1,0:T(8,128)(2,1)}, u32[]{:S(2)}) %copy-start.2) | copy-done | bytes 262168
  11.2 0.9 %copy-done.3 = bf16[256,512]{1,0:T(8,128)(2,1)S(1)} copy-done((bf16[256,512]{1,0:T(8,128)(2,1)S(1)}, bf16[256,512]{1,0:T(8,128)(2,1)}, u32[]{:S(2)}) %copy-start.3) | copy-done | bytes 262168
  12.2 5.1 %own_attention.1 = (f32[256,4096]{1,0:T(8,128)}, f32[256,512]{1,0:T(8,128)}) custom-call(bf16[256,4096]{1,0:T(8,128)(2,1)S(1)} %copy-done, bf16[256,512]{1,0:T(8,128)(2,1)S(1)} %copy-done.2, bf16[256,512]{1,0:T(8,128)(2,1)S(1)} %copy-done.3), custom_call_target="tpu_custom_call" | custom-call | flops 1073741824 | bytes 7340032 | tf_op jit(solution)/shard_map/own_attention/pallas_call | solution.py:210
  17.3 0.1 copy.8
  17.4 0.1 collective-permute-start
  17.5 1.0 %collective-permute-done = s32[1,2]{0,1:T(2,128)S(1)} collective-permute-done((s32[1,2]{0,1:T(2,128)S(1)}, s32[1,2]{0,1:T(2,128)S(1)}, u32[]{:S(2)}, u32[]{:S(2)}) %collective-permute-start) | collective-permute-done | bytes 40 | tf_op jit(solution)/shard_map/ppermute | solution.py:93
  18.6 1.4 %collective-permute-start.1 = (s32[2,2]{0,1:T(2,128)S(1)}, s32[2,2]{0,1:T(2,128)S(1)}, u32[]{:S(2)}, u32[]{:S(2)}) collective-permute-start(s32[2,2]{0,1:T(2,128)S(1)} %pad_add_fusion), channel_id=1, source_target_pairs={{0,2},{1,3},{2,0},{3,1},{4,6},{5,7},{6,4},{7,5},{8,10},{9,11},{10,... | collective-permute-start | bytes 56 | tf_op jit(solution)/shard_map/ppermute | solution.py:93
  20.0 1.3 %collective-permute-done.1 = s32[2,2]{0,1:T(2,128)S(1)} collective-permute-done((s32[2,2]{0,1:T(2,128)S(1)}, s32[2,2]{0,1:T(2,128)S(1)}, u32[]{:S(2)}, u32[]{:S(2)}) %collective-permute-start.1) | collective-permute-done | bytes 48 | tf_op jit(solution)/shard_map/ppermute | solution.py:93
  21.4 1.1 %collective-permute-start.2 = (s32[4,2]{0,1:T(2,128)S(1)}, s32[4,2]{0,1:T(2,128)S(1)}, u32[]{:S(2)}, u32[]{:S(2)}) collective-permute-start(s32[4,2]{0,1:T(2,128)S(1)} %pad_add_fusion.1), channel_id=1, source_target_pairs={{0,4},{1,5},{2,6},{3,7},{4,0},{5,1},{6,2},{7,3},{8,12},{9,13},{10,... | collective-permute-start | bytes 104 | tf_op jit(solution)/shard_map/ppermute | solution.py:93
  22.5 3.7 %collective-permute-done.2 = s32[4,2]{0,1:T(2,128)S(1)} collective-permute-done((s32[4,2]{0,1:T(2,128)S(1)}, s32[4,2]{0,1:T(2,128)S(1)}, u32[]{:S(2)}, u32[]{:S(2)}) %collective-permute-start.2) | collective-permute-done | bytes 64 | tf_op jit(solution)/shard_map/ppermute | solution.py:93
  26.4 8.1 %all-to-all-done.held_ref = bf16[16,256,128]{2,1,0:T(8,128)(2,1)S(1)} async-done(((bf16[16,256,128]{2,1,0:T(8,128)(2,1)}), bf16[16,256,128]{2,1,0:T(8,128)(2,1)S(1)}, u32[]{:S(2)}, u32[]{:S(2)}) %all-to-all-start) | async-done | bytes 1048608 | tf_op jit(solution)/shard_map/all_to_all | solution.py:449
  34.6 0.2 pick_pieces.1
  34.8 0.8 %collective-permute-start.3 = (bf16[2,256,128]{2,1,0:T(8,128)(2,1)S(1)}, bf16[2,256,128]{2,1,0:T(8,128)(2,1)S(1)}, u32[]{:S(2)}, u32[]{:S(2)}) collective-permute-start(bf16[2,256,128]{2,1,0:T(8,128)(2,1)S(1)} %get-tuple-element.30), channel_id=1, source_target_pairs={{0,1},{1,0},{2,3},{3,2},{4,5},{5,4},{6,7},{7,6},{8,9},{9,8},{10,11... | collective-permute-start | bytes 393224 | tf_op jit(solution)/shard_map/ppermute | solution.py:93
  35.6 1.1 %collective-permute-start.5 = (bf16[2,256,128]{2,1,0:T(8,128)(2,1)S(1)}, bf16[2,256,128]{2,1,0:T(8,128)(2,1)S(1)}, u32[]{:S(2)}, u32[]{:S(2)}) collective-permute-start(bf16[2,256,128]{2,1,0:T(8,128)(2,1)S(1)} %get-tuple-element.32), channel_id=1, source_target_pairs={{0,2},{1,3},{2,0},{3,1},{4,6},{5,7},{6,4},{7,5},{8,10},{9,11},{10,... | collective-permute-start | bytes 393224 | tf_op jit(solution)/shard_map/ppermute | solution.py:93
  36.7 2.0 %collective-permute-start.6 = (bf16[2,256,128]{2,1,0:T(8,128)(2,1)S(1)}, bf16[2,256,128]{2,1,0:T(8,128)(2,1)S(1)}, u32[]{:S(2)}, u32[]{:S(2)}) collective-permute-start(bf16[2,256,128]{2,1,0:T(8,128)(2,1)S(1)} %get-tuple-element.35), channel_id=1, source_target_pairs={{0,5},{1,4},{2,7},{3,6},{4,1},{5,0},{6,3},{7,2},{8,13},{9,12},{10,... | collective-permute-start | bytes 393224 | tf_op jit(solution)/shard_map/ppermute | solution.py:93
  38.7 0.1 collective-permute-start.7
  38.8 1.1 %collective-permute-start.8 = (bf16[2,256,128]{2,1,0:T(8,128)(2,1)S(1)}, bf16[2,256,128]{2,1,0:T(8,128)(2,1)S(1)}, u32[]{:S(2)}, u32[]{:S(2)}) collective-permute-start(bf16[2,256,128]{2,1,0:T(8,128)(2,1)S(1)} %get-tuple-element.37), channel_id=1, source_target_pairs={{0,6},{1,7},{2,4},{3,5},{4,2},{5,3},{6,0},{7,1},{8,14},{9,15},{10,... | collective-permute-start | bytes 393224 | tf_op jit(solution)/shard_map/ppermute | solution.py:93
  39.9 0.8 %collective-permute-done.4 = bf16[2,256,128]{2,1,0:T(8,128)(2,1)S(1)} collective-permute-done((bf16[2,256,128]{2,1,0:T(8,128)(2,1)S(1)}, bf16[2,256,128]{2,1,0:T(8,128)(2,1)S(1)}, u32[]{:S(2)}, u32[]{:S(2)}) %collective-permute-start.4) | collective-permute-done | bytes 131104 | tf_op jit(solution)/shard_map/ppermute | solution.py:93
  40.7 1.8 %collective-permute-start.9 = (bf16[2,256,128]{2,1,0:T(8,128)(2,1)S(1)}, bf16[2,256,128]{2,1,0:T(8,128)(2,1)S(1)}, u32[]{:S(2)}, u32[]{:S(2)}) collective-permute-start(bf16[2,256,128]{2,1,0:T(8,128)(2,1)S(1)} %get-tuple-element.38), channel_id=1, source_target_pairs={{0,7},{1,6},{2,5},{3,4},{4,3},{5,2},{6,1},{7,0},{8,15},{9,14},{10,... | collective-permute-start | bytes 393224 | tf_op jit(solution)/shard_map/ppermute | solution.py:93
  42.5 11.5 %early_attention.1 = (f32[256,4096]{1,0:T(8,128)S(1)}, f32[256,4096]{1,0:T(8,128)S(1)}) custom-call(s32[1,2]{1,0:T(1,128)S(1)} %copy-done.4, bf16[256,4096]{1,0:T(8,128)(2,1)S(1)} %copy-done.1, f32[256,4096]{1,0:T(8,128)} %get-tuple-element.25.own_in, f32[256,512]{1,0:T(8,128)} %get-tuple-element.26.level_in, bf16[2,8,32,128]{3,2,1,0:T(8,128)(2,1)S(1)} %bitcast.17, ...), custom_call_target="tpu_custom_call" | custom-call | flops 1073741824 | bytes 10485760 | tf_op jit(solution)/shard_map/early_attention/pallas_call | solution.py:423
  54.1 3.5 %late_attention.1 = bf16[256,4096]{1,0:T(8,128)(2,1)} custom-call(s32[1,2]{1,0:T(1,128)S(1)} %copy-done.4, bf16[256,4096]{1,0:T(8,128)(2,1)S(1)} %copy-done.1, f32[256,4096]{1,0:T(8,128)S(1)} %get-tuple-element.33.own_in, f32[256,4096]{1,0:T(8,128)S(1)} %get-tuple-element.34.level_in, bf16[2,8,32,128]{3,2,1,0:T(8,128)(2,1)S(1)} %bitcast.13, ...), custom_call_target="tpu_custom_call" | custom-call | flops 1073741824 | bytes 10485760 | tf_op jit(solution)/shard_map/late_attention/pallas_call | solution.py:423
  (19 shorter events, 0.4 us)
Async XLA Ops:
  0.0 17.3 %copy-start.4 = (s32[1,2]{1,0:T(1,128)S(1)}, s32[1,2]{1,0:T(1,128)}, u32[]{:S(2)}) copy-start(s32[1,2]{1,0:T(1,128)} %selected_ref.3) | copy-start | bytes 28
  0.0 42.5 %copy-start.1 = (bf16[256,4096]{1,0:T(8,128)(2,1)S(1)}, bf16[256,4096]{1,0:T(8,128)(2,1)}, u32[]{:S(2)}) copy-start(bf16[256,4096]{1,0:T(8,128)(2,1)} %query_ref.2) | copy-start | bytes 6291460
  2.2 32.4 %all-to-all-start = ((bf16[16,256,128]{2,1,0:T(8,128)(2,1)}), bf16[16,256,128]{2,1,0:T(8,128)(2,1)S(1)}, u32[]{:S(2)}, u32[]{:S(2)}) async-start(bf16[16,256,128]{2,1,0:T(8,128)(2,1)} %bitcast.21), calls=%async_computation | async-start | bytes 2097152 | tf_op jit(solution)/shard_map/all_to_all | solution.py:449
  8.7 1.6 %copy-start = (bf16[256,4096]{1,0:T(8,128)(2,1)S(1)}, bf16[256,4096]{1,0:T(8,128)(2,1)}, u32[]{:S(2)}) copy-start(bf16[256,4096]{1,0:T(8,128)(2,1)} %query_ref.2) | copy-start | bytes 6291460
  10.3 0.9 %copy-start.2 = (bf16[256,512]{1,0:T(8,128)(2,1)S(1)}, bf16[256,512]{1,0:T(8,128)(2,1)}, u32[]{:S(2)}) copy-start(bf16[256,512]{1,0:T(8,128)(2,1)} %key_ref.1) | copy-start | bytes 786436
  11.2 0.9 %copy-start.3 = (bf16[256,512]{1,0:T(8,128)(2,1)S(1)}, bf16[256,512]{1,0:T(8,128)(2,1)}, u32[]{:S(2)}) copy-start(bf16[256,512]{1,0:T(8,128)(2,1)} %value_ref.1) | copy-start | bytes 786436
  17.4 1.1 %collective-permute-start = (s32[1,2]{0,1:T(2,128)S(1)}, s32[1,2]{0,1:T(2,128)S(1)}, u32[]{:S(2)}, u32[]{:S(2)}) collective-permute-start(s32[1,2]{0,1:T(2,128)S(1)} %copy.8), channel_id=1, source_target_pairs={{0,1},{1,0},{2,3},{3,2},{4,5},{5,4},{6,7},{7,6},{8,9},{9,8},{10,11... | collective-permute-start | bytes 32 | tf_op jit(solution)/shard_map/ppermute | solution.py:93
  18.6 2.7 %collective-permute-start.1 = (s32[2,2]{0,1:T(2,128)S(1)}, s32[2,2]{0,1:T(2,128)S(1)}, u32[]{:S(2)}, u32[]{:S(2)}) collective-permute-start(s32[2,2]{0,1:T(2,128)S(1)} %pad_add_fusion), channel_id=1, source_target_pairs={{0,2},{1,3},{2,0},{3,1},{4,6},{5,7},{6,4},{7,5},{8,10},{9,11},{10,... | collective-permute-start | bytes 56 | tf_op jit(solution)/shard_map/ppermute | solution.py:93
  21.4 4.8 %collective-permute-start.2 = (s32[4,2]{0,1:T(2,128)S(1)}, s32[4,2]{0,1:T(2,128)S(1)}, u32[]{:S(2)}, u32[]{:S(2)}) collective-permute-start(s32[4,2]{0,1:T(2,128)S(1)} %pad_add_fusion.1), channel_id=1, source_target_pairs={{0,4},{1,5},{2,6},{3,7},{4,0},{5,1},{6,2},{7,3},{8,12},{9,13},{10,... | collective-permute-start | bytes 104 | tf_op jit(solution)/shard_map/ppermute | solution.py:93
  34.8 4.1 %collective-permute-start.3 = (bf16[2,256,128]{2,1,0:T(8,128)(2,1)S(1)}, bf16[2,256,128]{2,1,0:T(8,128)(2,1)S(1)}, u32[]{:S(2)}, u32[]{:S(2)}) collective-permute-start(bf16[2,256,128]{2,1,0:T(8,128)(2,1)S(1)} %get-tuple-element.30), channel_id=1, source_target_pairs={{0,1},{1,0},{2,3},{3,2},{4,5},{5,4},{6,7},{7,6},{8,9},{9,8},{10,11... | collective-permute-start | bytes 393224 | tf_op jit(solution)/shard_map/ppermute | solution.py:93
  35.6 5.1 %collective-permute-start.4 = (bf16[2,256,128]{2,1,0:T(8,128)(2,1)S(1)}, bf16[2,256,128]{2,1,0:T(8,128)(2,1)S(1)}, u32[]{:S(2)}, u32[]{:S(2)}) collective-permute-start(bf16[2,256,128]{2,1,0:T(8,128)(2,1)S(1)} %get-tuple-element.31), channel_id=1, source_target_pairs={{0,4},{1,5},{2,6},{3,7},{4,0},{5,1},{6,2},{7,3},{8,12},{9,13},{10,... | collective-permute-start | bytes 393224 | tf_op jit(solution)/shard_map/ppermute | solution.py:93
  35.6 6.9 %collective-permute-start.5 = (bf16[2,256,128]{2,1,0:T(8,128)(2,1)S(1)}, bf16[2,256,128]{2,1,0:T(8,128)(2,1)S(1)}, u32[]{:S(2)}, u32[]{:S(2)}) collective-permute-start(bf16[2,256,128]{2,1,0:T(8,128)(2,1)S(1)} %get-tuple-element.32), channel_id=1, source_target_pairs={{0,2},{1,3},{2,0},{3,1},{4,6},{5,7},{6,4},{7,5},{8,10},{9,11},{10,... | collective-permute-start | bytes 393224 | tf_op jit(solution)/shard_map/ppermute | solution.py:93
  36.7 17.3 %collective-permute-start.6 = (bf16[2,256,128]{2,1,0:T(8,128)(2,1)S(1)}, bf16[2,256,128]{2,1,0:T(8,128)(2,1)S(1)}, u32[]{:S(2)}, u32[]{:S(2)}) collective-permute-start(bf16[2,256,128]{2,1,0:T(8,128)(2,1)S(1)} %get-tuple-element.35), channel_id=1, source_target_pairs={{0,5},{1,4},{2,7},{3,6},{4,1},{5,0},{6,3},{7,2},{8,13},{9,12},{10,... | collective-permute-start | bytes 393224 | tf_op jit(solution)/shard_map/ppermute | solution.py:93
  38.7 15.3 %collective-permute-start.7 = (bf16[2,256,128]{2,1,0:T(8,128)(2,1)S(1)}, bf16[2,256,128]{2,1,0:T(8,128)(2,1)S(1)}, u32[]{:S(2)}, u32[]{:S(2)}) collective-permute-start(bf16[2,256,128]{2,1,0:T(8,128)(2,1)S(1)} %get-tuple-element.36), channel_id=1, source_target_pairs={{0,3},{1,2},{2,1},{3,0},{4,7},{5,6},{6,5},{7,4},{8,11},{9,10},{10,... | collective-permute-start | bytes 393224 | tf_op jit(solution)/shard_map/ppermute | solution.py:93
  38.8 15.3 %collective-permute-start.8 = (bf16[2,256,128]{2,1,0:T(8,128)(2,1)S(1)}, bf16[2,256,128]{2,1,0:T(8,128)(2,1)S(1)}, u32[]{:S(2)}, u32[]{:S(2)}) collective-permute-start(bf16[2,256,128]{2,1,0:T(8,128)(2,1)S(1)} %get-tuple-element.37), channel_id=1, source_target_pairs={{0,6},{1,7},{2,4},{3,5},{4,2},{5,3},{6,0},{7,1},{8,14},{9,15},{10,... | collective-permute-start | bytes 393224 | tf_op jit(solution)/shard_map/ppermute | solution.py:93
  40.7 13.4 %collective-permute-start.9 = (bf16[2,256,128]{2,1,0:T(8,128)(2,1)S(1)}, bf16[2,256,128]{2,1,0:T(8,128)(2,1)S(1)}, u32[]{:S(2)}, u32[]{:S(2)}) collective-permute-start(bf16[2,256,128]{2,1,0:T(8,128)(2,1)S(1)} %get-tuple-element.38), channel_id=1, source_target_pairs={{0,7},{1,6},{2,5},{3,4},{4,3},{5,2},{6,1},{7,0},{8,15},{9,14},{10,... | collective-permute-start | bytes 393224 | tf_op jit(solution)/shard_map/ppermute | solution.py:93

commit v15 on v14

--- a/solution.py
+++ b/solution.py
@@ -19,16 +19,22 @@
 
 def mixed_order(devices):
     shares = devices // COPIES
-    return [copy * shares + share for share in range(shares) for copy in range(COPIES)]
+    return [
+        copy * shares + share + core
+        for share in range(0, shares, 2)
+        for copy in range(COPIES)
+        for core in range(2)
+    ]
 
 
 def place_of(block, devices):
     shares = devices // COPIES
-    return block % shares * COPIES + block // shares
+    share, copy = block % shares, block // shares
+    return share // 2 * (2 * COPIES) + copy * 2 + share % 2
 
 
 def pack_kernel(key_ref, value_ref, out_ref, staged, arrived, left):
-    shares, piece_rows, _ = key_ref.shape
+    piece_rows = key_ref.shape[2]
     half = KEY_VALUE_HEADS * piece_rows
 
     def take(slot):
@@ -37,13 +43,13 @@
         lanes = pl.ds(head * HEAD_SIZE, HEAD_SIZE)
         rows = pl.ds(slot * piece_rows, piece_rows)
         return pltpu.make_async_copy(
-            ref.at[:, :, lanes], staged.at[:, rows, :], arrived.at[slot]
+            ref.at[:, :, :, lanes], staged.at[:, :, rows, :], arrived.at[slot]
         )
 
     def give(which, copy):
         rows = pl.ds(which * half, half)
         return pltpu.make_async_copy(
-            staged.at[:, rows, :], out_ref.at[:, copy, rows, :], left.at[which, copy]
+            staged.at[:, :, rows, :], out_ref.at[:, copy, :, rows, :], left.at[which, copy]
         )
 
     for slot in range(SLOTS):
@@ -62,16 +68,16 @@
     shares = devices // COPIES
     piece_rows = keys.shape[0] // shares
     if piece_rows % 16 == 0:
-        split = (shares, piece_rows, keys.shape[1])
+        split = (shares // 2, 2, piece_rows, keys.shape[1])
         return pl.pallas_call(
             pack_kernel,
             out_shape=jax.ShapeDtypeStruct(
-                (shares, COPIES, SLOTS * piece_rows, HEAD_SIZE), jnp.bfloat16
+                (shares // 2, COPIES, 2, SLOTS * piece_rows, HEAD_SIZE), jnp.bfloat16
             ),
             in_specs=[pl.BlockSpec(memory_space=pl.ANY)] * 2,
             out_specs=pl.BlockSpec(memory_space=pl.ANY),
             scratch_shapes=[
-                pltpu.VMEM((shares, SLOTS * piece_rows, HEAD_SIZE), jnp.bfloat16),
+                pltpu.VMEM((shares // 2, 2, SLOTS * piece_rows, HEAD_SIZE), jnp.bfloat16),
                 pltpu.SemaphoreType.DMA((SLOTS,)),
                 pltpu.SemaphoreType.DMA((2, COPIES)),
             ],
@@ -81,8 +87,8 @@
         )
     both = jnp.concatenate([keys, values], axis=1)
     both = both.reshape(shares, piece_rows, SLOTS, HEAD_SIZE).transpose(0, 2, 1, 3)
-    both = both.reshape(shares, SLOTS * piece_rows, HEAD_SIZE)
-    return jnp.repeat(both, COPIES, axis=0)
+    both = both.reshape(shares // 2, 2, SLOTS * piece_rows, HEAD_SIZE)
+    return jnp.repeat(both, COPIES, axis=0).reshape(devices, SLOTS * piece_rows, HEAD_SIZE)
 
 
 def partner(position, step):

time: 58.9 us -> 58.9 us (level)
  starting transfers between devices: 16.1 us -> 17.5 us
  waiting for transfers between devices: 14.9 us -> 13.6 us
    ppermute x10, starting transfers between devices: 9.64 us -> 11 us  [swap(): lax.ppermute(array, 'ctx', [(i, partner(i, step)) for i in range(devices)])]
    all_to_all x1, waiting for transfers between devices: 8.13 us -> 7.13 us  [local(): lax.all_to_all(packed, 'ctx', split_axis=0, concat_axis=0, axis_index_gro...]
where the time goes in v15:
time: 58.9 us; the launch traced here: 57.8 us
  Pallas kernels  22.5 us (38%)
  starting transfers between devices  17.5 us (30%)
  waiting for transfers between devices  13.6 us (23%)
  local copies, waits for them, and re-layouts  3.67 us (6%)
    pallas_call x2, Pallas kernels, far_attention(): pl.pallas_call(functools.partial(far_kernel, last=last), out_shape=out_sh...  15 us
    ppermute x10, starting transfers between devices, swap(): lax.ppermute(array, 'ctx', [(i, partner(i, step)) for i in range(devices)])  11 us
    all_to_all x1, waiting for transfers between devices, local(): lax.all_to_all(packed, 'ctx', split_axis=0, concat_axis=0, axis_index_gro...  7.13 us
    all_to_all x1, starting transfers between devices, local(): lax.all_to_all(packed, 'ctx', split_axis=0, concat_axis=0, axis_index_gro...  6.5 us
    ppermute x10, waiting for transfers between devices, swap(): lax.ppermute(array, 'ctx', [(i, partner(i, step)) for i in range(devices)])  6.46 us
    pallas_call x1, Pallas kernels, own_attention(): pl.pallas_call(own_kernel, out_shape=[pltpu.HBM(queries.shape, jnp.float3...  5.13 us
    unnamed x10, local copies, waits for them, and re-layouts  3.49 us
    pallas_call x1, Pallas kernels, pack(): pl.pallas_call(pack_kernel, out_shape=jax.ShapeDtypeStruct((shares // 2,...  2.16 us
  transfers between devices with their start and end apart: 11, of which 5 were waited for; matrix products, arithmetic and copies ran while one was open for 1% of the time, Pallas kernels for 29%

profile of v15, /device:TPU:5, one launch (start us, length us, event | category | flops | bytes accessed | tf_op | source)
XLA Modules:
  0.0 57.8 jit_solution(16515275190964969124)
XLA Ops:
  0.0 2.2 %pack.1 = bf16[4,2,2,256,128]{4,3,2,1,0:T(8,128)(2,1)} custom-call(bf16[4,2,32,512]{3,2,1,0:T(8,128)(2,1)} %bitcast.11, bf16[4,2,32,512]{3,2,1,0:T(8,128)(2,1)} %bitcast.12), custom_call_target="tpu_custom_call" | custom-call | tf_op jit(solution)/shard_map/pack/pallas_call | solution.py:72
  2.2 6.5 %all-to-all-start = ((bf16[16,256,128]{2,1,0:T(8,128)(2,1)}), bf16[16,256,128]{2,1,0:T(8,128)(2,1)S(1)}, u32[]{:S(2)}, u32[]{:S(2)}) async-start(bf16[16,256,128]{2,1,0:T(8,128)(2,1)} %bitcast.21), calls=%async_computation | async-start | bytes 2097152 | tf_op jit(solution)/shard_map/all_to_all | solution.py:455
  8.7 1.6 %copy-done = bf16[256,4096]{1,0:T(8,128)(2,1)S(1)} copy-done((bf16[256,4096]{1,0:T(8,128)(2,1)S(1)}, bf16[256,4096]{1,0:T(8,128)(2,1)}, u32[]{:S(2)}) %copy-start) | copy-done | bytes 2097176
  10.3 0.9 %copy-done.2 = bf16[256,512]{1,0:T(8,128)(2,1)S(1)} copy-done((bf16[256,512]{1,0:T(8,128)(2,1)S(1)}, bf16[256,512]{1,0:T(8,128)(2,1)}, u32[]{:S(2)}) %copy-start.2) | copy-done | bytes 262168
  11.2 0.9 %copy-done.3 = bf16[256,512]{1,0:T(8,128)(2,1)S(1)} copy-done((bf16[256,512]{1,0:T(8,128)(2,1)S(1)}, bf16[256,512]{1,0:T(8,128)(2,1)}, u32[]{:S(2)}) %copy-start.3) | copy-done | bytes 262168
  12.2 5.1 %own_attention.1 = (f32[256,4096]{1,0:T(8,128)}, f32[256,512]{1,0:T(8,128)}) custom-call(bf16[256,4096]{1,0:T(8,128)(2,1)S(1)} %copy-done, bf16[256,512]{1,0:T(8,128)(2,1)S(1)} %copy-done.2, bf16[256,512]{1,0:T(8,128)(2,1)S(1)} %copy-done.3), custom_call_target="tpu_custom_call" | custom-call | flops 1073741824 | bytes 7340032 | tf_op jit(solution)/shard_map/own_attention/pallas_call | solution.py:216
  17.3 0.1 copy.8
  17.4 0.1 collective-permute-start
  17.5 1.0 %collective-permute-done = s32[1,2]{0,1:T(2,128)S(1)} collective-permute-done((s32[1,2]{0,1:T(2,128)S(1)}, s32[1,2]{0,1:T(2,128)S(1)}, u32[]{:S(2)}, u32[]{:S(2)}) %collective-permute-start) | collective-permute-done | bytes 40 | tf_op jit(solution)/shard_map/ppermute | solution.py:99
  18.6 1.4 %collective-permute-start.1 = (s32[2,2]{0,1:T(2,128)S(1)}, s32[2,2]{0,1:T(2,128)S(1)}, u32[]{:S(2)}, u32[]{:S(2)}) collective-permute-start(s32[2,2]{0,1:T(2,128)S(1)} %pad_add_fusion), channel_id=1, source_target_pairs={{0,2},{1,3},{2,0},{3,1},{4,6},{5,7},{6,4},{7,5},{8,10},{9,11},{10,... | collective-permute-start | bytes 56 | tf_op jit(solution)/shard_map/ppermute | solution.py:99
  20.0 1.3 %collective-permute-done.1 = s32[2,2]{0,1:T(2,128)S(1)} collective-permute-done((s32[2,2]{0,1:T(2,128)S(1)}, s32[2,2]{0,1:T(2,128)S(1)}, u32[]{:S(2)}, u32[]{:S(2)}) %collective-permute-start.1) | collective-permute-done | bytes 48 | tf_op jit(solution)/shard_map/ppermute | solution.py:99
  21.4 1.4 %collective-permute-start.2 = (s32[4,2]{0,1:T(2,128)S(1)}, s32[4,2]{0,1:T(2,128)S(1)}, u32[]{:S(2)}, u32[]{:S(2)}) collective-permute-start(s32[4,2]{0,1:T(2,128)S(1)} %pad_add_fusion.1), channel_id=1, source_target_pairs={{0,4},{1,5},{2,6},{3,7},{4,0},{5,1},{6,2},{7,3},{8,12},{9,13},{10,... | collective-permute-start | bytes 104 | tf_op jit(solution)/shard_map/ppermute | solution.py:99
  22.8 3.5 %collective-permute-done.2 = s32[4,2]{0,1:T(2,128)S(1)} collective-permute-done((s32[4,2]{0,1:T(2,128)S(1)}, s32[4,2]{0,1:T(2,128)S(1)}, u32[]{:S(2)}, u32[]{:S(2)}) %collective-permute-start.2) | collective-permute-done | bytes 64 | tf_op jit(solution)/shard_map/ppermute | solution.py:99
  26.3 0.1 pad_add_fusion.2
  26.4 0.1 copy.9
  26.5 7.1 %all-to-all-done.held_ref = bf16[16,256,128]{2,1,0:T(8,128)(2,1)S(1)} async-done(((bf16[16,256,128]{2,1,0:T(8,128)(2,1)}), bf16[16,256,128]{2,1,0:T(8,128)(2,1)S(1)}, u32[]{:S(2)}, u32[]{:S(2)}) %all-to-all-start) | async-done | bytes 1048608 | tf_op jit(solution)/shard_map/all_to_all | solution.py:455
  33.6 0.2 pick_pieces.1
  33.9 2.8 %collective-permute-start.4 = (bf16[2,256,128]{2,1,0:T(8,128)(2,1)S(1)}, bf16[2,256,128]{2,1,0:T(8,128)(2,1)S(1)}, u32[]{:S(2)}, u32[]{:S(2)}) collective-permute-start(bf16[2,256,128]{2,1,0:T(8,128)(2,1)S(1)} %get-tuple-element.31), channel_id=1, source_target_pairs={{0,4},{1,5},{2,6},{3,7},{4,0},{5,1},{6,2},{7,3},{8,12},{9,13},{10,... | collective-permute-start | bytes 393224 | tf_op jit(solution)/shard_map/ppermute | solution.py:99
  36.8 1.9 %collective-permute-start.6 = (bf16[2,256,128]{2,1,0:T(8,128)(2,1)S(1)}, bf16[2,256,128]{2,1,0:T(8,128)(2,1)S(1)}, u32[]{:S(2)}, u32[]{:S(2)}) collective-permute-start(bf16[2,256,128]{2,1,0:T(8,128)(2,1)S(1)} %get-tuple-element.35), channel_id=1, source_target_pairs={{0,5},{1,4},{2,7},{3,6},{4,1},{5,0},{6,3},{7,2},{8,13},{9,12},{10,... | collective-permute-start | bytes 393224 | tf_op jit(solution)/shard_map/ppermute | solution.py:99
  38.7 1.2 %collective-permute-start.8 = (bf16[2,256,128]{2,1,0:T(8,128)(2,1)S(1)}, bf16[2,256,128]{2,1,0:T(8,128)(2,1)S(1)}, u32[]{:S(2)}, u32[]{:S(2)}) collective-permute-start(bf16[2,256,128]{2,1,0:T(8,128)(2,1)S(1)} %get-tuple-element.37), channel_id=1, source_target_pairs={{0,6},{1,7},{2,4},{3,5},{4,2},{5,3},{6,0},{7,1},{8,14},{9,15},{10,... | collective-permute-start | bytes 393224 | tf_op jit(solution)/shard_map/ppermute | solution.py:99
  39.9 0.6 %collective-permute-done.4 = bf16[2,256,128]{2,1,0:T(8,128)(2,1)S(1)} collective-permute-done((bf16[2,256,128]{2,1,0:T(8,128)(2,1)S(1)}, bf16[2,256,128]{2,1,0:T(8,128)(2,1)S(1)}, u32[]{:S(2)}, u32[]{:S(2)}) %collective-permute-start.4) | collective-permute-done | bytes 131104 | tf_op jit(solution)/shard_map/ppermute | solution.py:99
  40.5 2.0 %collective-permute-start.9 = (bf16[2,256,128]{2,1,0:T(8,128)(2,1)S(1)}, bf16[2,256,128]{2,1,0:T(8,128)(2,1)S(1)}, u32[]{:S(2)}, u32[]{:S(2)}) collective-permute-start(bf16[2,256,128]{2,1,0:T(8,128)(2,1)S(1)} %get-tuple-element.38), channel_id=1, source_target_pairs={{0,7},{1,6},{2,5},{3,4},{4,3},{5,2},{6,1},{7,0},{8,15},{9,14},{10,... | collective-permute-start | bytes 393224 | tf_op jit(solution)/shard_map/ppermute | solution.py:99
  42.5 11.5 %early_attention.1 = (f32[256,4096]{1,0:T(8,128)S(1)}, f32[256,4096]{1,0:T(8,128)S(1)}) custom-call(s32[1,2]{1,0:T(1,128)S(1)} %copy-done.4, bf16[256,4096]{1,0:T(8,128)(2,1)S(1)} %copy-done.1, f32[256,4096]{1,0:T(8,128)} %get-tuple-element.25.own_in, f32[256,512]{1,0:T(8,128)} %get-tuple-element.26.level_in, bf16[2,8,32,128]{3,2,1,0:T(8,128)(2,1)S(1)} %bitcast.17, ...), custom_call_target="tpu_custom_call" | custom-call | flops 1073741824 | bytes 10485760 | tf_op jit(solution)/shard_map/early_attention/pallas_call | solution.py:429
  54.1 3.5 %late_attention.1 = bf16[256,4096]{1,0:T(8,128)(2,1)} custom-call(s32[1,2]{1,0:T(1,128)S(1)} %copy-done.4, bf16[256,4096]{1,0:T(8,128)(2,1)S(1)} %copy-done.1, f32[256,4096]{1,0:T(8,128)S(1)} %get-tuple-element.33.own_in, f32[256,4096]{1,0:T(8,128)S(1)} %get-tuple-element.34.level_in, bf16[2,8,32,128]{3,2,1,0:T(8,128)(2,1)S(1)} %bitcast.13, ...), custom_call_target="tpu_custom_call" | custom-call | flops 1073741824 | bytes 10485760 | tf_op jit(solution)/shard_map/late_attention/pallas_call | solution.py:429
  (19 shorter events, 0.3 us)
Async XLA Ops:
  0.0 17.3 %copy-start.4 = (s32[1,2]{1,0:T(1,128)S(1)}, s32[1,2]{1,0:T(1,128)}, u32[]{:S(2)}) copy-start(s32[1,2]{1,0:T(1,128)} %selected_ref.3) | copy-start | bytes 28
  0.0 42.5 %copy-start.1 = (bf16[256,4096]{1,0:T(8,128)(2,1)S(1)}, bf16[256,4096]{1,0:T(8,128)(2,1)}, u32[]{:S(2)}) copy-start(bf16[256,4096]{1,0:T(8,128)(2,1)} %query_ref.2) | copy-start | bytes 6291460
  2.2 31.5 %all-to-all-start = ((bf16[16,256,128]{2,1,0:T(8,128)(2,1)}), bf16[16,256,128]{2,1,0:T(8,128)(2,1)S(1)}, u32[]{:S(2)}, u32[]{:S(2)}) async-start(bf16[16,256,128]{2,1,0:T(8,128)(2,1)} %bitcast.21), calls=%async_computation | async-start | bytes 2097152 | tf_op jit(solution)/shard_map/all_to_all | solution.py:455
  8.7 1.6 %copy-start = (bf16[256,4096]{1,0:T(8,128)(2,1)S(1)}, bf16[256,4096]{1,0:T(8,128)(2,1)}, u32[]{:S(2)}) copy-start(bf16[256,4096]{1,0:T(8,128)(2,1)} %query_ref.2) | copy-start | bytes 6291460
  10.3 0.9 %copy-start.2 = (bf16[256,512]{1,0:T(8,128)(2,1)S(1)}, bf16[256,512]{1,0:T(8,128)(2,1)}, u32[]{:S(2)}) copy-start(bf16[256,512]{1,0:T(8,128)(2,1)} %key_ref.1) | copy-start | bytes 786436
  11.2 0.9 %copy-start.3 = (bf16[256,512]{1,0:T(8,128)(2,1)S(1)}, bf16[256,512]{1,0:T(8,128)(2,1)}, u32[]{:S(2)}) copy-start(bf16[256,512]{1,0:T(8,128)(2,1)} %value_ref.1) | copy-start | bytes 786436
  17.4 1.1 %collective-permute-start = (s32[1,2]{0,1:T(2,128)S(1)}, s32[1,2]{0,1:T(2,128)S(1)}, u32[]{:S(2)}, u32[]{:S(2)}) collective-permute-start(s32[1,2]{0,1:T(2,128)S(1)} %copy.8), channel_id=1, source_target_pairs={{0,1},{1,0},{2,3},{3,2},{4,5},{5,4},{6,7},{7,6},{8,9},{9,8},{10,11... | collective-permute-start | bytes 32 | tf_op jit(solution)/shard_map/ppermute | solution.py:99
  18.6 2.7 %collective-permute-start.1 = (s32[2,2]{0,1:T(2,128)S(1)}, s32[2,2]{0,1:T(2,128)S(1)}, u32[]{:S(2)}, u32[]{:S(2)}) collective-permute-start(s32[2,2]{0,1:T(2,128)S(1)} %pad_add_fusion), channel_id=1, source_target_pairs={{0,2},{1,3},{2,0},{3,1},{4,6},{5,7},{6,4},{7,5},{8,10},{9,11},{10,... | collective-permute-start | bytes 56 | tf_op jit(solution)/shard_map/ppermute | solution.py:99
  21.4 4.9 %collective-permute-start.2 = (s32[4,2]{0,1:T(2,128)S(1)}, s32[4,2]{0,1:T(2,128)S(1)}, u32[]{:S(2)}, u32[]{:S(2)}) collective-permute-start(s32[4,2]{0,1:T(2,128)S(1)} %pad_add_fusion.1), channel_id=1, source_target_pairs={{0,4},{1,5},{2,6},{3,7},{4,0},{5,1},{6,2},{7,3},{8,12},{9,13},{10,... | collective-permute-start | bytes 104 | tf_op jit(solution)/shard_map/ppermute | solution.py:99
  33.8 4.9 %collective-permute-start.3 = (bf16[2,256,128]{2,1,0:T(8,128)(2,1)S(1)}, bf16[2,256,128]{2,1,0:T(8,128)(2,1)S(1)}, u32[]{:S(2)}, u32[]{:S(2)}) collective-permute-start(bf16[2,256,128]{2,1,0:T(8,128)(2,1)S(1)} %get-tuple-element.30), channel_id=1, source_target_pairs={{0,1},{1,0},{2,3},{3,2},{4,5},{5,4},{6,7},{7,6},{8,9},{9,8},{10,11... | collective-permute-start | bytes 393224 | tf_op jit(solution)/shard_map/ppermute | solution.py:99
  33.9 6.6 %collective-permute-start.4 = (bf16[2,256,128]{2,1,0:T(8,128)(2,1)S(1)}, bf16[2,256,128]{2,1,0:T(8,128)(2,1)S(1)}, u32[]{:S(2)}, u32[]{:S(2)}) collective-permute-start(bf16[2,256,128]{2,1,0:T(8,128)(2,1)S(1)} %get-tuple-element.31), channel_id=1, source_target_pairs={{0,4},{1,5},{2,6},{3,7},{4,0},{5,1},{6,2},{7,3},{8,12},{9,13},{10,... | collective-permute-start | bytes 393224 | tf_op jit(solution)/shard_map/ppermute | solution.py:99
  36.8 5.7 %collective-permute-start.5 = (bf16[2,256,128]{2,1,0:T(8,128)(2,1)S(1)}, bf16[2,256,128]{2,1,0:T(8,128)(2,1)S(1)}, u32[]{:S(2)}, u32[]{:S(2)}) collective-permute-start(bf16[2,256,128]{2,1,0:T(8,128)(2,1)S(1)} %get-tuple-element.32), channel_id=1, source_target_pairs={{0,2},{1,3},{2,0},{3,1},{4,6},{5,7},{6,4},{7,5},{8,10},{9,11},{10,... | collective-permute-start | bytes 393224 | tf_op jit(solution)/shard_map/ppermute | solution.py:99
  36.8 17.3 %collective-permute-start.6 = (bf16[2,256,128]{2,1,0:T(8,128)(2,1)S(1)}, bf16[2,256,128]{2,1,0:T(8,128)(2,1)S(1)}, u32[]{:S(2)}, u32[]{:S(2)}) collective-permute-start(bf16[2,256,128]{2,1,0:T(8,128)(2,1)S(1)} %get-tuple-element.35), channel_id=1, source_target_pairs={{0,5},{1,4},{2,7},{3,6},{4,1},{5,0},{6,3},{7,2},{8,13},{9,12},{10,... | collective-permute-start | bytes 393224 | tf_op jit(solution)/shard_map/ppermute | solution.py:99
  38.7 15.3 %collective-permute-start.7 = (bf16[2,256,128]{2,1,0:T(8,128)(2,1)S(1)}, bf16[2,256,128]{2,1,0:T(8,128)(2,1)S(1)}, u32[]{:S(2)}, u32[]{:S(2)}) collective-permute-start(bf16[2,256,128]{2,1,0:T(8,128)(2,1)S(1)} %get-tuple-element.36), channel_id=1, source_target_pairs={{0,3},{1,2},{2,1},{3,0},{4,7},{5,6},{6,5},{7,4},{8,11},{9,10},{10,... | collective-permute-start | bytes 393224 | tf_op jit(solution)/shard_map/ppermute | solution.py:99
  38.7 15.3 %collective-permute-start.8 = (bf16[2,256,128]{2,1,0:T(8,128)(2,1)S(1)}, bf16[2,256,128]{2,1,0:T(8,128)(2,1)S(1)}, u32[]{:S(2)}, u32[]{:S(2)}) collective-permute-start(bf16[2,256,128]{2,1,0:T(8,128)(2,1)S(1)} %get-tuple-element.37), channel_id=1, source_target_pairs={{0,6},{1,7},{2,4},{3,5},{4,2},{5,3},{6,0},{7,1},{8,14},{9,15},{10,... | collective-permute-start | bytes 393224 | tf_op jit(solution)/shard_map/ppermute | solution.py:99
  40.5 13.5 %collective-permute-start.9 = (bf16[2,256,128]{2,1,0:T(8,128)(2,1)S(1)}, bf16[2,256,128]{2,1,0:T(8,128)(2,1)S(1)}, u32[]{:S(2)}, u32[]{:S(2)}) collective-permute-start(bf16[2,256,128]{2,1,0:T(8,128)(2,1)S(1)} %get-tuple-element.38), channel_id=1, source_target_pairs={{0,7},{1,6},{2,5},{3,4},{4,3},{5,2},{6,1},{7,0},{8,15},{9,14},{10,... | collective-permute-start | bytes 393224 | tf_op jit(solution)/shard_map/ppermute | solution.py:99

commit v16 on v12

--- a/solution.py
+++ b/solution.py
@@ -290,13 +290,16 @@
         def repeat(narrow):
             return jnp.concatenate([narrow] * (count // HEAD_SIZE), axis=1)
 
-        def quick(group, head, scores, value, largest):
+        def weigh(group, head, scores):
+            level = level_of(group, head)
+            return jnp.exp2(scores * FACTOR - repeat(level)).astype(jnp.bfloat16)
+
+        def mix(group, head, weights, value, largest):
             lanes = head_of(group, head)
-            level = level_of(group, head)
-            weights = jnp.exp2(scores * FACTOR - repeat(level)).astype(jnp.bfloat16)
             both = dot(weights, value)
             row_sum = 1.0 + both[:, HEAD_SIZE:]
-            store(lanes, own_ref[:, lanes] + both[:, :HEAD_SIZE], row_sum, level)
+            mixture = own_ref[:, lanes] + both[:, :HEAD_SIZE]
+            store(lanes, mixture, row_sum, level_of(group, head))
             return jnp.maximum(
                 largest, jnp.max(row_sum.reshape(rows // 8, 8, HEAD_SIZE), axis=0)
             )
@@ -317,21 +320,24 @@
 
         largest = jnp.zeros((8, HEAD_SIZE), jnp.float32)
         order = [(g, h) for g in range(KEY_VALUE_HEADS) for h in range(GROUP)]
-        held = {0: keys_and_values(0)}
-        scores = score(0, 0, held[0][0])
-        for (group, head), later in zip(order, order[1:] + [None]):
-            following = None
-            if later is not None:
-                if later[0] not in held:
-                    held[later[0]] = keys_and_values(later[0])
-                following = score(*later, held[later[0]][0])
-            if head == 0 and not last:
-                fetch(group, 1).wait()
-                fetch(group, 0).wait()
-            largest = quick(group, head, scores, held[group][1], largest)
-            if (head + 1) % SENT == 0 and last:
-                send((group * GROUP + head) // SENT).start()
-            scores = following
+        held, scores, weights = {}, {}, {}
+        for turn in range(len(order) + 2):
+            if turn < len(order):
+                group, head = order[turn]
+                if group not in held:
+                    held[group] = keys_and_values(group)
+                scores[turn] = score(group, head, held[group][0])
+            if 1 <= turn <= len(order):
+                group, head = order[turn - 1]
+                if head == 0 and not last:
+                    fetch(group, 1).wait()
+                    fetch(group, 0).wait()
+                weights[turn - 1] = weigh(group, head, scores.pop(turn - 1))
+            if turn >= 2:
+                group, head = order[turn - 2]
+                largest = mix(group, head, weights.pop(turn - 2), held[group][1], largest)
+                if (head + 1) % SENT == 0 and last:
+                    send((group * GROUP + head) // SENT).start()
 
         @pl.when(jnp.max(largest) > LARGE_SUM)
         def _():

time: 58.8 us -> 58.8 us (level)
  the two profiles are of different devices: /device:TPU:5 before, /device:TPU:1 now
where the time goes in v16:
time: 58.8 us; the launch traced here: 58.5 us
  Pallas kernels  22.1 us (38%)
  starting transfers between devices  21.1 us (36%)
  waiting for transfers between devices  11.2 us (19%)
  local copies, waits for them, and re-layouts  3.67 us (6%)
    pallas_call x2, Pallas kernels, far_attention(): pl.pallas_call(functools.partial(far_kernel, last=last), out_shape=out_sh...  14.7 us
    ppermute x10, starting transfers between devices, swap(): lax.ppermute(array, 'ctx', [(i, partner(i, step)) for i in range(devices)])  13.7 us
    all_to_all x1, starting transfers between devices, local(): lax.all_to_all(packed, 'ctx', split_axis=0, concat_axis=0, tiled=True)  7.33 us
    ppermute x10, waiting for transfers between devices, swap(): lax.ppermute(array, 'ctx', [(i, partner(i, step)) for i in range(devices)])  5.88 us
    all_to_all x1, waiting for transfers between devices, local(): lax.all_to_all(packed, 'ctx', split_axis=0, concat_axis=0, tiled=True)  5.31 us
    pallas_call x1, Pallas kernels, own_attention(): pl.pallas_call(own_kernel, out_shape=[pltpu.HBM(queries.shape, jnp.float3...  5.13 us
    unnamed x10, local copies, waits for them, and re-layouts  3.49 us
    pallas_call x1, Pallas kernels, pack(): pl.pallas_call(pack_kernel, out_shape=jax.ShapeDtypeStruct((devices, SLOT...  2.16 us
  transfers between devices with their start and end apart: 11, of which 4 were waited for; matrix products, arithmetic and copies ran while one was open for 1% of the time, Pallas kernels for 29%

profile of v16, /device:TPU:1, one launch (start us, length us, event | category | flops | bytes accessed | tf_op | source)
XLA Modules:
  0.0 58.5 jit_solution(14164731032770868335)
XLA Ops:
  0.0 2.2 %pack.1 = bf16[16,256,128]{2,1,0:T(8,128)(2,1)} custom-call(bf16[8,32,512]{2,1,0:T(8,128)(2,1)} %bitcast.10, bf16[8,32,512]{2,1,0:T(8,128)(2,1)} %bitcast.11), custom_call_target="tpu_custom_call" | custom-call | tf_op jit(solution)/shard_map/pack/pallas_call | solution.py:58
  2.2 7.3 %all-to-all-start = ((bf16[16,256,128]{2,1,0:T(8,128)(2,1)}), bf16[16,256,128]{2,1,0:T(8,128)(2,1)S(1)}, u32[]{:S(2)}, u32[]{:S(2)}) async-start(bf16[16,256,128]{2,1,0:T(8,128)(2,1)} %pack.1), calls=%async_computation | async-start | bytes 2097152 | tf_op jit(solution)/shard_map/all_to_all | solution.py:445
  9.5 1.6 %copy-done = bf16[256,4096]{1,0:T(8,128)(2,1)S(1)} copy-done((bf16[256,4096]{1,0:T(8,128)(2,1)S(1)}, bf16[256,4096]{1,0:T(8,128)(2,1)}, u32[]{:S(2)}) %copy-start) | copy-done | bytes 2097176
  11.1 0.9 %copy-done.2 = bf16[256,512]{1,0:T(8,128)(2,1)S(1)} copy-done((bf16[256,512]{1,0:T(8,128)(2,1)S(1)}, bf16[256,512]{1,0:T(8,128)(2,1)}, u32[]{:S(2)}) %copy-start.2) | copy-done | bytes 262168
  12.0 0.9 %copy-done.3 = bf16[256,512]{1,0:T(8,128)(2,1)S(1)} copy-done((bf16[256,512]{1,0:T(8,128)(2,1)S(1)}, bf16[256,512]{1,0:T(8,128)(2,1)}, u32[]{:S(2)}) %copy-start.3) | copy-done | bytes 262168
  13.0 5.1 %own_attention.1 = (f32[256,4096]{1,0:T(8,128)}, f32[256,512]{1,0:T(8,128)}) custom-call(bf16[256,4096]{1,0:T(8,128)(2,1)S(1)} %copy-done, bf16[256,512]{1,0:T(8,128)(2,1)S(1)} %copy-done.2, bf16[256,512]{1,0:T(8,128)(2,1)S(1)} %copy-done.3), custom_call_target="tpu_custom_call" | custom-call | flops 1073741824 | bytes 7340032 | tf_op jit(solution)/shard_map/own_attention/pallas_call | solution.py:200
  18.1 0.1 copy.8
  18.2 0.1 collective-permute-start
  18.3 1.0 %collective-permute-done = s32[1,2]{0,1:T(2,128)S(1)} collective-permute-done((s32[1,2]{0,1:T(2,128)S(1)}, s32[1,2]{0,1:T(2,128)S(1)}, u32[]{:S(2)}, u32[]{:S(2)}) %collective-permute-start) | collective-permute-done | bytes 40 | tf_op jit(solution)/shard_map/ppermute | solution.py:83
  19.4 1.4 %collective-permute-start.1 = (s32[2,2]{0,1:T(2,128)S(1)}, s32[2,2]{0,1:T(2,128)S(1)}, u32[]{:S(2)}, u32[]{:S(2)}) collective-permute-start(s32[2,2]{0,1:T(2,128)S(1)} %pad_add_fusion), channel_id=1, source_target_pairs={{0,2},{1,3},{2,0},{3,1},{4,6},{5,7},{6,4},{7,5},{8,10},{9,11},{10,... | collective-permute-start | bytes 56 | tf_op jit(solution)/shard_map/ppermute | solution.py:83
  20.9 1.3 %collective-permute-done.1 = s32[2,2]{0,1:T(2,128)S(1)} collective-permute-done((s32[2,2]{0,1:T(2,128)S(1)}, s32[2,2]{0,1:T(2,128)S(1)}, u32[]{:S(2)}, u32[]{:S(2)}) %collective-permute-start.1) | collective-permute-done | bytes 48 | tf_op jit(solution)/shard_map/ppermute | solution.py:83
  22.2 1.4 %collective-permute-start.2 = (s32[4,2]{0,1:T(2,128)S(1)}, s32[4,2]{0,1:T(2,128)S(1)}, u32[]{:S(2)}, u32[]{:S(2)}) collective-permute-start(s32[4,2]{0,1:T(2,128)S(1)} %pad_add_fusion.1), channel_id=1, source_target_pairs={{0,4},{1,5},{2,6},{3,7},{4,0},{5,1},{6,2},{7,3},{8,12},{9,13},{10,... | collective-permute-start | bytes 104 | tf_op jit(solution)/shard_map/ppermute | solution.py:83
  23.6 3.5 %collective-permute-done.2 = s32[4,2]{0,1:T(2,128)S(1)} collective-permute-done((s32[4,2]{0,1:T(2,128)S(1)}, s32[4,2]{0,1:T(2,128)S(1)}, u32[]{:S(2)}, u32[]{:S(2)}) %collective-permute-start.2) | collective-permute-done | bytes 64 | tf_op jit(solution)/shard_map/ppermute | solution.py:83
  27.2 0.1 copy.9
  27.3 5.3 %all-to-all-done.held_ref = bf16[16,256,128]{2,1,0:T(8,128)(2,1)S(1)} async-done(((bf16[16,256,128]{2,1,0:T(8,128)(2,1)}), bf16[16,256,128]{2,1,0:T(8,128)(2,1)S(1)}, u32[]{:S(2)}, u32[]{:S(2)}) %all-to-all-start) | async-done | bytes 1048608 | tf_op jit(solution)/shard_map/all_to_all | solution.py:445
  32.6 0.2 pick_pieces.1
  32.9 3.2 %collective-permute-start.4 = (bf16[2,256,128]{2,1,0:T(8,128)(2,1)S(1)}, bf16[2,256,128]{2,1,0:T(8,128)(2,1)S(1)}, u32[]{:S(2)}, u32[]{:S(2)}) collective-permute-start(bf16[2,256,128]{2,1,0:T(8,128)(2,1)S(1)} %get-tuple-element.31), channel_id=1, source_target_pairs={{0,4},{1,5},{2,6},{3,7},{4,0},{5,1},{6,2},{7,3},{8,12},{9,13},{10,... | collective-permute-start | bytes 393224 | tf_op jit(solution)/shard_map/ppermute | solution.py:83
  36.1 1.4 %collective-permute-start.5 = (bf16[2,256,128]{2,1,0:T(8,128)(2,1)S(1)}, bf16[2,256,128]{2,1,0:T(8,128)(2,1)S(1)}, u32[]{:S(2)}, u32[]{:S(2)}) collective-permute-start(bf16[2,256,128]{2,1,0:T(8,128)(2,1)S(1)} %get-tuple-element.32), channel_id=1, source_target_pairs={{0,2},{1,3},{2,0},{3,1},{4,6},{5,7},{6,4},{7,5},{8,10},{9,11},{10,... | collective-permute-start | bytes 393224 | tf_op jit(solution)/shard_map/ppermute | solution.py:83
  37.4 0.5 collective-permute-start.6
  37.9 0.5 collective-permute-start.7
  38.4 1.9 %collective-permute-start.8 = (bf16[2,256,128]{2,1,0:T(8,128)(2,1)S(1)}, bf16[2,256,128]{2,1,0:T(8,128)(2,1)S(1)}, u32[]{:S(2)}, u32[]{:S(2)}) collective-permute-start(bf16[2,256,128]{2,1,0:T(8,128)(2,1)S(1)} %get-tuple-element.37), channel_id=1, source_target_pairs={{0,6},{1,7},{2,4},{3,5},{4,2},{5,3},{6,0},{7,1},{8,14},{9,15},{10,... | collective-permute-start | bytes 393224 | tf_op jit(solution)/shard_map/ppermute | solution.py:83
  40.4 3.3 %collective-permute-start.9 = (bf16[2,256,128]{2,1,0:T(8,128)(2,1)S(1)}, bf16[2,256,128]{2,1,0:T(8,128)(2,1)S(1)}, u32[]{:S(2)}, u32[]{:S(2)}) collective-permute-start(bf16[2,256,128]{2,1,0:T(8,128)(2,1)S(1)} %get-tuple-element.38), channel_id=1, source_target_pairs={{0,7},{1,6},{2,5},{3,4},{4,3},{5,2},{6,1},{7,0},{8,15},{9,14},{10,... | collective-permute-start | bytes 393224 | tf_op jit(solution)/shard_map/ppermute | solution.py:83
  43.7 11.8 %early_attention.1 = (f32[256,4096]{1,0:T(8,128)S(1)}, f32[256,4096]{1,0:T(8,128)S(1)}) custom-call(s32[1,2]{1,0:T(1,128)S(1)} %copy-done.4, bf16[256,4096]{1,0:T(8,128)(2,1)S(1)} %copy-done.1, f32[256,4096]{1,0:T(8,128)} %get-tuple-element.25.own_in, f32[256,512]{1,0:T(8,128)} %get-tuple-element.26.level_in, bf16[2,8,32,128]{3,2,1,0:T(8,128)(2,1)S(1)} %bitcast.16, ...), custom_call_target="tpu_custom_call" | custom-call | flops 1073741824 | bytes 10485760 | tf_op jit(solution)/shard_map/early_attention/pallas_call | solution.py:419
  55.5 2.9 %late_attention.1 = bf16[256,4096]{1,0:T(8,128)(2,1)} custom-call(s32[1,2]{1,0:T(1,128)S(1)} %copy-done.4, bf16[256,4096]{1,0:T(8,128)(2,1)S(1)} %copy-done.1, f32[256,4096]{1,0:T(8,128)S(1)} %get-tuple-element.33.own_in, f32[256,4096]{1,0:T(8,128)S(1)} %get-tuple-element.34.level_in, bf16[2,8,32,128]{3,2,1,0:T(8,128)(2,1)S(1)} %bitcast.12, ...), custom_call_target="tpu_custom_call" | custom-call | flops 1073741824 | bytes 10485760 | tf_op jit(solution)/shard_map/late_attention/pallas_call | solution.py:419
  (19 shorter events, 0.3 us)
Async XLA Ops:
  0.0 18.1 %copy-start.4 = (s32[1,2]{1,0:T(1,128)S(1)}, s32[1,2]{1,0:T(1,128)}, u32[]{:S(2)}) copy-start(s32[1,2]{1,0:T(1,128)} %selected_ref.3) | copy-start | bytes 28
  0.0 43.7 %copy-start.1 = (bf16[256,4096]{1,0:T(8,128)(2,1)S(1)}, bf16[256,4096]{1,0:T(8,128)(2,1)}, u32[]{:S(2)}) copy-start(bf16[256,4096]{1,0:T(8,128)(2,1)} %query_ref.2) | copy-start | bytes 6291460
  2.2 30.5 %all-to-all-start = ((bf16[16,256,128]{2,1,0:T(8,128)(2,1)}), bf16[16,256,128]{2,1,0:T(8,128)(2,1)S(1)}, u32[]{:S(2)}, u32[]{:S(2)}) async-start(bf16[16,256,128]{2,1,0:T(8,128)(2,1)} %pack.1), calls=%async_computation | async-start | bytes 2097152 | tf_op jit(solution)/shard_map/all_to_all | solution.py:445
  9.5 1.6 %copy-start = (bf16[256,4096]{1,0:T(8,128)(2,1)S(1)}, bf16[256,4096]{1,0:T(8,128)(2,1)}, u32[]{:S(2)}) copy-start(bf16[256,4096]{1,0:T(8,128)(2,1)} %query_ref.2) | copy-start | bytes 6291460
  11.1 0.9 %copy-start.2 = (bf16[256,512]{1,0:T(8,128)(2,1)S(1)}, bf16[256,512]{1,0:T(8,128)(2,1)}, u32[]{:S(2)}) copy-start(bf16[256,512]{1,0:T(8,128)(2,1)} %key_ref.1) | copy-start | bytes 786436
  12.0 0.9 %copy-start.3 = (bf16[256,512]{1,0:T(8,128)(2,1)S(1)}, bf16[256,512]{1,0:T(8,128)(2,1)}, u32[]{:S(2)}) copy-start(bf16[256,512]{1,0:T(8,128)(2,1)} %value_ref.1) | copy-start | bytes 786436
  18.2 1.1 %collective-permute-start = (s32[1,2]{0,1:T(2,128)S(1)}, s32[1,2]{0,1:T(2,128)S(1)}, u32[]{:S(2)}, u32[]{:S(2)}) collective-permute-start(s32[1,2]{0,1:T(2,128)S(1)} %copy.8), channel_id=1, source_target_pairs={{0,1},{1,0},{2,3},{3,2},{4,5},{5,4},{6,7},{7,6},{8,9},{9,8},{10,11... | collective-permute-start | bytes 32 | tf_op jit(solution)/shard_map/ppermute | solution.py:83
  19.4 2.7 %collective-permute-start.1 = (s32[2,2]{0,1:T(2,128)S(1)}, s32[2,2]{0,1:T(2,128)S(1)}, u32[]{:S(2)}, u32[]{:S(2)}) collective-permute-start(s32[2,2]{0,1:T(2,128)S(1)} %pad_add_fusion), channel_id=1, source_target_pairs={{0,2},{1,3},{2,0},{3,1},{4,6},{5,7},{6,4},{7,5},{8,10},{9,11},{10,... | collective-permute-start | bytes 56 | tf_op jit(solution)/shard_map/ppermute | solution.py:83
  22.2 4.9 %collective-permute-start.2 = (s32[4,2]{0,1:T(2,128)S(1)}, s32[4,2]{0,1:T(2,128)S(1)}, u32[]{:S(2)}, u32[]{:S(2)}) collective-permute-start(s32[4,2]{0,1:T(2,128)S(1)} %pad_add_fusion.1), channel_id=1, source_target_pairs={{0,4},{1,5},{2,6},{3,7},{4,0},{5,1},{6,2},{7,3},{8,12},{9,13},{10,... | collective-permute-start | bytes 104 | tf_op jit(solution)/shard_map/ppermute | solution.py:83
  32.8 5.6 %collective-permute-start.3 = (bf16[2,256,128]{2,1,0:T(8,128)(2,1)S(1)}, bf16[2,256,128]{2,1,0:T(8,128)(2,1)S(1)}, u32[]{:S(2)}, u32[]{:S(2)}) collective-permute-start(bf16[2,256,128]{2,1,0:T(8,128)(2,1)S(1)} %get-tuple-element.30), channel_id=1, source_target_pairs={{0,1},{1,0},{2,3},{3,2},{4,5},{5,4},{6,7},{7,6},{8,9},{9,8},{10,11... | collective-permute-start | bytes 393224 | tf_op jit(solution)/shard_map/ppermute | solution.py:83
  32.9 7.4 %collective-permute-start.4 = (bf16[2,256,128]{2,1,0:T(8,128)(2,1)S(1)}, bf16[2,256,128]{2,1,0:T(8,128)(2,1)S(1)}, u32[]{:S(2)}, u32[]{:S(2)}) collective-permute-start(bf16[2,256,128]{2,1,0:T(8,128)(2,1)S(1)} %get-tuple-element.31), channel_id=1, source_target_pairs={{0,4},{1,5},{2,6},{3,7},{4,0},{5,1},{6,2},{7,3},{8,12},{9,13},{10,... | collective-permute-start | bytes 393224 | tf_op jit(solution)/shard_map/ppermute | solution.py:83
  36.1 7.6 %collective-permute-start.5 = (bf16[2,256,128]{2,1,0:T(8,128)(2,1)S(1)}, bf16[2,256,128]{2,1,0:T(8,128)(2,1)S(1)}, u32[]{:S(2)}, u32[]{:S(2)}) collective-permute-start(bf16[2,256,128]{2,1,0:T(8,128)(2,1)S(1)} %get-tuple-element.32), channel_id=1, source_target_pairs={{0,2},{1,3},{2,0},{3,1},{4,6},{5,7},{6,4},{7,5},{8,10},{9,11},{10,... | collective-permute-start | bytes 393224 | tf_op jit(solution)/shard_map/ppermute | solution.py:83
  37.4 18.0 %collective-permute-start.6 = (bf16[2,256,128]{2,1,0:T(8,128)(2,1)S(1)}, bf16[2,256,128]{2,1,0:T(8,128)(2,1)S(1)}, u32[]{:S(2)}, u32[]{:S(2)}) collective-permute-start(bf16[2,256,128]{2,1,0:T(8,128)(2,1)S(1)} %get-tuple-element.35), channel_id=1, source_target_pairs={{0,5},{1,4},{2,7},{3,6},{4,1},{5,0},{6,3},{7,2},{8,13},{9,12},{10,... | collective-permute-start | bytes 393224 | tf_op jit(solution)/shard_map/ppermute | solution.py:83
  37.9 17.6 %collective-permute-start.7 = (bf16[2,256,128]{2,1,0:T(8,128)(2,1)S(1)}, bf16[2,256,128]{2,1,0:T(8,128)(2,1)S(1)}, u32[]{:S(2)}, u32[]{:S(2)}) collective-permute-start(bf16[2,256,128]{2,1,0:T(8,128)(2,1)S(1)} %get-tuple-element.36), channel_id=1, source_target_pairs={{0,3},{1,2},{2,1},{3,0},{4,7},{5,6},{6,5},{7,4},{8,11},{9,10},{10,... | collective-permute-start | bytes 393224 | tf_op jit(solution)/shard_map/ppermute | solution.py:83
  38.4 17.1 %collective-permute-start.8 = (bf16[2,256,128]{2,1,0:T(8,128)(2,1)S(1)}, bf16[2,256,128]{2,1,0:T(8,128)(2,1)S(1)}, u32[]{:S(2)}, u32[]{:S(2)}) collective-permute-start(bf16[2,256,128]{2,1,0:T(8,128)(2,1)S(1)} %get-tuple-element.37), channel_id=1, source_target_pairs={{0,6},{1,7},{2,4},{3,5},{4,2},{5,3},{6,0},{7,1},{8,14},{9,15},{10,... | collective-permute-start | bytes 393224 | tf_op jit(solution)/shard_map/ppermute | solution.py:83
  40.4 15.1 %collective-permute-start.9 = (bf16[2,256,128]{2,1,0:T(8,128)(2,1)S(1)}, bf16[2,256,128]{2,1,0:T(8,128)(2,1)S(1)}, u32[]{:S(2)}, u32[]{:S(2)}) collective-permute-start(bf16[2,256,128]{2,1,0:T(8,128)(2,1)S(1)} %get-tuple-element.38), channel_id=1, source_target_pairs={{0,7},{1,6},{2,5},{3,4},{4,3},{5,2},{6,1},{7,0},{8,15},{9,14},{10,... | collective-permute-start | bytes 393224 | tf_op jit(solution)/shard_map/ppermute | solution.py:83

commit v17 on v16

--- a/solution.py
+++ b/solution.py
@@ -132,7 +132,7 @@
 
 FACTOR = math.log2(math.e) / math.sqrt(HEAD_SIZE)
 PAIR = 2
-SENT = 4
+SENT = 2
 LARGE_SUM = 2.0**100
 
 
@@ -324,8 +324,10 @@
         for turn in range(len(order) + 2):
             if turn < len(order):
                 group, head = order[turn]
-                if group not in held:
-                    held[group] = keys_and_values(group)
+                soon = order[min(turn + GROUP // 2, len(order) - 1)][0]
+                for needed in (group, soon):
+                    if needed not in held:
+                        held[needed] = keys_and_values(needed)
                 scores[turn] = score(group, head, held[group][0])
             if 1 <= turn <= len(order):
                 group, head = order[turn - 1]

time: 58.8 us -> 58.5 us (level)
  the two profiles are of different devices: /device:TPU:1 before, /device:TPU:5 now
where the time goes in v17:
time: 58.5 us; the launch traced here: 57.7 us
  Pallas kernels  22.2 us (38%)
  starting transfers between devices  20.2 us (35%)
  waiting for transfers between devices  11.2 us (19%)
  local copies, waits for them, and re-layouts  3.67 us (6%)
    pallas_call x2, Pallas kernels, far_attention(): pl.pallas_call(functools.partial(far_kernel, last=last), out_shape=out_sh...  14.7 us
    ppermute x10, starting transfers between devices, swap(): lax.ppermute(array, 'ctx', [(i, partner(i, step)) for i in range(devices)])  13.7 us
    all_to_all x1, starting transfers between devices, local(): lax.all_to_all(packed, 'ctx', split_axis=0, concat_axis=0, tiled=True)  6.5 us
    ppermute x10, waiting for transfers between devices, swap(): lax.ppermute(array, 'ctx', [(i, partner(i, step)) for i in range(devices)])  5.89 us
    all_to_all x1, waiting for transfers between devices, local(): lax.all_to_all(packed, 'ctx', split_axis=0, concat_axis=0, tiled=True)  5.31 us
    pallas_call x1, Pallas kernels, own_attention(): pl.pallas_call(own_kernel, out_shape=[pltpu.HBM(queries.shape, jnp.float3...  5.13 us
    unnamed x10, local copies, waits for them, and re-layouts  3.49 us
    pallas_call x1, Pallas kernels, pack(): pl.pallas_call(pack_kernel, out_shape=jax.ShapeDtypeStruct((devices, SLOT...  2.16 us
  transfers between devices with their start and end apart: 11, of which 4 were waited for; matrix products, arithmetic and copies ran while one was open for 1% of the time, Pallas kernels for 29%

profile of v17, /device:TPU:5, one launch (start us, length us, event | category | flops | bytes accessed | tf_op | source)
XLA Modules:
  0.0 57.7 jit_solution(16758441501825135268)
XLA Ops:
  0.0 2.2 %pack.1 = bf16[16,256,128]{2,1,0:T(8,128)(2,1)} custom-call(bf16[8,32,512]{2,1,0:T(8,128)(2,1)} %bitcast.10, bf16[8,32,512]{2,1,0:T(8,128)(2,1)} %bitcast.11), custom_call_target="tpu_custom_call" | custom-call | tf_op jit(solution)/shard_map/pack/pallas_call | solution.py:58
  2.2 6.5 %all-to-all-start = ((bf16[16,256,128]{2,1,0:T(8,128)(2,1)}), bf16[16,256,128]{2,1,0:T(8,128)(2,1)S(1)}, u32[]{:S(2)}, u32[]{:S(2)}) async-start(bf16[16,256,128]{2,1,0:T(8,128)(2,1)} %pack.1), calls=%async_computation | async-start | bytes 2097152 | tf_op jit(solution)/shard_map/all_to_all | solution.py:447
  8.7 1.6 %copy-done = bf16[256,4096]{1,0:T(8,128)(2,1)S(1)} copy-done((bf16[256,4096]{1,0:T(8,128)(2,1)S(1)}, bf16[256,4096]{1,0:T(8,128)(2,1)}, u32[]{:S(2)}) %copy-start) | copy-done | bytes 2097176
  10.3 0.9 %copy-done.2 = bf16[256,512]{1,0:T(8,128)(2,1)S(1)} copy-done((bf16[256,512]{1,0:T(8,128)(2,1)S(1)}, bf16[256,512]{1,0:T(8,128)(2,1)}, u32[]{:S(2)}) %copy-start.2) | copy-done | bytes 262168
  11.2 0.9 %copy-done.3 = bf16[256,512]{1,0:T(8,128)(2,1)S(1)} copy-done((bf16[256,512]{1,0:T(8,128)(2,1)S(1)}, bf16[256,512]{1,0:T(8,128)(2,1)}, u32[]{:S(2)}) %copy-start.3) | copy-done | bytes 262168
  12.2 5.1 %own_attention.1 = (f32[256,4096]{1,0:T(8,128)}, f32[256,512]{1,0:T(8,128)}) custom-call(bf16[256,4096]{1,0:T(8,128)(2,1)S(1)} %copy-done, bf16[256,512]{1,0:T(8,128)(2,1)S(1)} %copy-done.2, bf16[256,512]{1,0:T(8,128)(2,1)S(1)} %copy-done.3), custom_call_target="tpu_custom_call" | custom-call | flops 1073741824 | bytes 7340032 | tf_op jit(solution)/shard_map/own_attention/pallas_call | solution.py:200
  17.3 0.1 copy.8
  17.4 0.1 collective-permute-start
  17.5 1.0 %collective-permute-done = s32[1,2]{0,1:T(2,128)S(1)} collective-permute-done((s32[1,2]{0,1:T(2,128)S(1)}, s32[1,2]{0,1:T(2,128)S(1)}, u32[]{:S(2)}, u32[]{:S(2)}) %collective-permute-start) | collective-permute-done | bytes 40 | tf_op jit(solution)/shard_map/ppermute | solution.py:83
  18.6 1.4 %collective-permute-start.1 = (s32[2,2]{0,1:T(2,128)S(1)}, s32[2,2]{0,1:T(2,128)S(1)}, u32[]{:S(2)}, u32[]{:S(2)}) collective-permute-start(s32[2,2]{0,1:T(2,128)S(1)} %pad_add_fusion), channel_id=1, source_target_pairs={{0,2},{1,3},{2,0},{3,1},{4,6},{5,7},{6,4},{7,5},{8,10},{9,11},{10,... | collective-permute-start | bytes 56 | tf_op jit(solution)/shard_map/ppermute | solution.py:83
  20.0 1.3 %collective-permute-done.1 = s32[2,2]{0,1:T(2,128)S(1)} collective-permute-done((s32[2,2]{0,1:T(2,128)S(1)}, s32[2,2]{0,1:T(2,128)S(1)}, u32[]{:S(2)}, u32[]{:S(2)}) %collective-permute-start.1) | collective-permute-done | bytes 48 | tf_op jit(solution)/shard_map/ppermute | solution.py:83
  21.4 1.4 %collective-permute-start.2 = (s32[4,2]{0,1:T(2,128)S(1)}, s32[4,2]{0,1:T(2,128)S(1)}, u32[]{:S(2)}, u32[]{:S(2)}) collective-permute-start(s32[4,2]{0,1:T(2,128)S(1)} %pad_add_fusion.1), channel_id=1, source_target_pairs={{0,4},{1,5},{2,6},{3,7},{4,0},{5,1},{6,2},{7,3},{8,12},{9,13},{10,... | collective-permute-start | bytes 104 | tf_op jit(solution)/shard_map/ppermute | solution.py:83
  22.8 3.5 %collective-permute-done.2 = s32[4,2]{0,1:T(2,128)S(1)} collective-permute-done((s32[4,2]{0,1:T(2,128)S(1)}, s32[4,2]{0,1:T(2,128)S(1)}, u32[]{:S(2)}, u32[]{:S(2)}) %collective-permute-start.2) | collective-permute-done | bytes 64 | tf_op jit(solution)/shard_map/ppermute | solution.py:83
  26.4 0.1 copy.9
  26.5 5.3 %all-to-all-done.held_ref = bf16[16,256,128]{2,1,0:T(8,128)(2,1)S(1)} async-done(((bf16[16,256,128]{2,1,0:T(8,128)(2,1)}), bf16[16,256,128]{2,1,0:T(8,128)(2,1)S(1)}, u32[]{:S(2)}, u32[]{:S(2)}) %all-to-all-start) | async-done | bytes 1048608 | tf_op jit(solution)/shard_map/all_to_all | solution.py:447
  31.8 0.2 pick_pieces.1
  32.1 3.2 %collective-permute-start.4 = (bf16[2,256,128]{2,1,0:T(8,128)(2,1)S(1)}, bf16[2,256,128]{2,1,0:T(8,128)(2,1)S(1)}, u32[]{:S(2)}, u32[]{:S(2)}) collective-permute-start(bf16[2,256,128]{2,1,0:T(8,128)(2,1)S(1)} %get-tuple-element.31), channel_id=1, source_target_pairs={{0,4},{1,5},{2,6},{3,7},{4,0},{5,1},{6,2},{7,3},{8,12},{9,13},{10,... | collective-permute-start | bytes 393224 | tf_op jit(solution)/shard_map/ppermute | solution.py:83
  35.2 1.4 %collective-permute-start.5 = (bf16[2,256,128]{2,1,0:T(8,128)(2,1)S(1)}, bf16[2,256,128]{2,1,0:T(8,128)(2,1)S(1)}, u32[]{:S(2)}, u32[]{:S(2)}) collective-permute-start(bf16[2,256,128]{2,1,0:T(8,128)(2,1)S(1)} %get-tuple-element.32), channel_id=1, source_target_pairs={{0,2},{1,3},{2,0},{3,1},{4,6},{5,7},{6,4},{7,5},{8,10},{9,11},{10,... | collective-permute-start | bytes 393224 | tf_op jit(solution)/shard_map/ppermute | solution.py:83
  36.6 0.5 collective-permute-start.6
  37.1 0.5 collective-permute-start.7
  37.6 1.9 %collective-permute-start.8 = (bf16[2,256,128]{2,1,0:T(8,128)(2,1)S(1)}, bf16[2,256,128]{2,1,0:T(8,128)(2,1)S(1)}, u32[]{:S(2)}, u32[]{:S(2)}) collective-permute-start(bf16[2,256,128]{2,1,0:T(8,128)(2,1)S(1)} %get-tuple-element.37), channel_id=1, source_target_pairs={{0,6},{1,7},{2,4},{3,5},{4,2},{5,3},{6,0},{7,1},{8,14},{9,15},{10,... | collective-permute-start | bytes 393224 | tf_op jit(solution)/shard_map/ppermute | solution.py:83
  39.5 3.3 %collective-permute-start.9 = (bf16[2,256,128]{2,1,0:T(8,128)(2,1)S(1)}, bf16[2,256,128]{2,1,0:T(8,128)(2,1)S(1)}, u32[]{:S(2)}, u32[]{:S(2)}) collective-permute-start(bf16[2,256,128]{2,1,0:T(8,128)(2,1)S(1)} %get-tuple-element.38), channel_id=1, source_target_pairs={{0,7},{1,6},{2,5},{3,4},{4,3},{5,2},{6,1},{7,0},{8,15},{9,14},{10,... | collective-permute-start | bytes 393224 | tf_op jit(solution)/shard_map/ppermute | solution.py:83
  42.8 11.8 %early_attention.1 = (f32[256,4096]{1,0:T(8,128)S(1)}, f32[256,4096]{1,0:T(8,128)S(1)}) custom-call(s32[1,2]{1,0:T(1,128)S(1)} %copy-done.4, bf16[256,4096]{1,0:T(8,128)(2,1)S(1)} %copy-done.1, f32[256,4096]{1,0:T(8,128)} %get-tuple-element.25.own_in, f32[256,512]{1,0:T(8,128)} %get-tuple-element.26.level_in, bf16[2,8,32,128]{3,2,1,0:T(8,128)(2,1)S(1)} %bitcast.16, ...), custom_call_target="tpu_custom_call" | custom-call | flops 1073741824 | bytes 10485760 | tf_op jit(solution)/shard_map/early_attention/pallas_call | solution.py:421
  54.7 2.9 %late_attention.1 = bf16[256,4096]{1,0:T(8,128)(2,1)} custom-call(s32[1,2]{1,0:T(1,128)S(1)} %copy-done.4, bf16[256,4096]{1,0:T(8,128)(2,1)S(1)} %copy-done.1, f32[256,4096]{1,0:T(8,128)S(1)} %get-tuple-element.33.own_in, f32[256,4096]{1,0:T(8,128)S(1)} %get-tuple-element.34.level_in, bf16[2,8,32,128]{3,2,1,0:T(8,128)(2,1)S(1)} %bitcast.12, ...), custom_call_target="tpu_custom_call" | custom-call | flops 1073741824 | bytes 10485760 | tf_op jit(solution)/shard_map/late_attention/pallas_call | solution.py:421
  (19 shorter events, 0.3 us)
Async XLA Ops:
  0.0 17.3 %copy-start.4 = (s32[1,2]{1,0:T(1,128)S(1)}, s32[1,2]{1,0:T(1,128)}, u32[]{:S(2)}) copy-start(s32[1,2]{1,0:T(1,128)} %selected_ref.3) | copy-start | bytes 28
  0.0 42.8 %copy-start.1 = (bf16[256,4096]{1,0:T(8,128)(2,1)S(1)}, bf16[256,4096]{1,0:T(8,128)(2,1)}, u32[]{:S(2)}) copy-start(bf16[256,4096]{1,0:T(8,128)(2,1)} %query_ref.2) | copy-start | bytes 6291460
  2.2 29.6 %all-to-all-start = ((bf16[16,256,128]{2,1,0:T(8,128)(2,1)}), bf16[16,256,128]{2,1,0:T(8,128)(2,1)S(1)}, u32[]{:S(2)}, u32[]{:S(2)}) async-start(bf16[16,256,128]{2,1,0:T(8,128)(2,1)} %pack.1), calls=%async_computation | async-start | bytes 2097152 | tf_op jit(solution)/shard_map/all_to_all | solution.py:447
  8.7 1.6 %copy-start = (bf16[256,4096]{1,0:T(8,128)(2,1)S(1)}, bf16[256,4096]{1,0:T(8,128)(2,1)}, u32[]{:S(2)}) copy-start(bf16[256,4096]{1,0:T(8,128)(2,1)} %query_ref.2) | copy-start | bytes 6291460
  10.3 0.9 %copy-start.2 = (bf16[256,512]{1,0:T(8,128)(2,1)S(1)}, bf16[256,512]{1,0:T(8,128)(2,1)}, u32[]{:S(2)}) copy-start(bf16[256,512]{1,0:T(8,128)(2,1)} %key_ref.1) | copy-start | bytes 786436
  11.2 0.9 %copy-start.3 = (bf16[256,512]{1,0:T(8,128)(2,1)S(1)}, bf16[256,512]{1,0:T(8,128)(2,1)}, u32[]{:S(2)}) copy-start(bf16[256,512]{1,0:T(8,128)(2,1)} %value_ref.1) | copy-start | bytes 786436
  17.4 1.1 %collective-permute-start = (s32[1,2]{0,1:T(2,128)S(1)}, s32[1,2]{0,1:T(2,128)S(1)}, u32[]{:S(2)}, u32[]{:S(2)}) collective-permute-start(s32[1,2]{0,1:T(2,128)S(1)} %copy.8), channel_id=1, source_target_pairs={{0,1},{1,0},{2,3},{3,2},{4,5},{5,4},{6,7},{7,6},{8,9},{9,8},{10,11... | collective-permute-start | bytes 32 | tf_op jit(solution)/shard_map/ppermute | solution.py:83
  18.6 2.7 %collective-permute-start.1 = (s32[2,2]{0,1:T(2,128)S(1)}, s32[2,2]{0,1:T(2,128)S(1)}, u32[]{:S(2)}, u32[]{:S(2)}) collective-permute-start(s32[2,2]{0,1:T(2,128)S(1)} %pad_add_fusion), channel_id=1, source_target_pairs={{0,2},{1,3},{2,0},{3,1},{4,6},{5,7},{6,4},{7,5},{8,10},{9,11},{10,... | collective-permute-start | bytes 56 | tf_op jit(solution)/shard_map/ppermute | solution.py:83
  21.4 4.9 %collective-permute-start.2 = (s32[4,2]{0,1:T(2,128)S(1)}, s32[4,2]{0,1:T(2,128)S(1)}, u32[]{:S(2)}, u32[]{:S(2)}) collective-permute-start(s32[4,2]{0,1:T(2,128)S(1)} %pad_add_fusion.1), channel_id=1, source_target_pairs={{0,4},{1,5},{2,6},{3,7},{4,0},{5,1},{6,2},{7,3},{8,12},{9,13},{10,... | collective-permute-start | bytes 104 | tf_op jit(solution)/shard_map/ppermute | solution.py:83
  32.0 5.6 %collective-permute-start.3 = (bf16[2,256,128]{2,1,0:T(8,128)(2,1)S(1)}, bf16[2,256,128]{2,1,0:T(8,128)(2,1)S(1)}, u32[]{:S(2)}, u32[]{:S(2)}) collective-permute-start(bf16[2,256,128]{2,1,0:T(8,128)(2,1)S(1)} %get-tuple-element.30), channel_id=1, source_target_pairs={{0,1},{1,0},{2,3},{3,2},{4,5},{5,4},{6,7},{7,6},{8,9},{9,8},{10,11... | collective-permute-start | bytes 393224 | tf_op jit(solution)/shard_map/ppermute | solution.py:83
  32.1 7.4 %collective-permute-start.4 = (bf16[2,256,128]{2,1,0:T(8,128)(2,1)S(1)}, bf16[2,256,128]{2,1,0:T(8,128)(2,1)S(1)}, u32[]{:S(2)}, u32[]{:S(2)}) collective-permute-start(bf16[2,256,128]{2,1,0:T(8,128)(2,1)S(1)} %get-tuple-element.31), channel_id=1, source_target_pairs={{0,4},{1,5},{2,6},{3,7},{4,0},{5,1},{6,2},{7,3},{8,12},{9,13},{10,... | collective-permute-start | bytes 393224 | tf_op jit(solution)/shard_map/ppermute | solution.py:83
  35.2 7.6 %collective-permute-start.5 = (bf16[2,256,128]{2,1,0:T(8,128)(2,1)S(1)}, bf16[2,256,128]{2,1,0:T(8,128)(2,1)S(1)}, u32[]{:S(2)}, u32[]{:S(2)}) collective-permute-start(bf16[2,256,128]{2,1,0:T(8,128)(2,1)S(1)} %get-tuple-element.32), channel_id=1, source_target_pairs={{0,2},{1,3},{2,0},{3,1},{4,6},{5,7},{6,4},{7,5},{8,10},{9,11},{10,... | collective-permute-start | bytes 393224 | tf_op jit(solution)/shard_map/ppermute | solution.py:83
  36.6 18.0 %collective-permute-start.6 = (bf16[2,256,128]{2,1,0:T(8,128)(2,1)S(1)}, bf16[2,256,128]{2,1,0:T(8,128)(2,1)S(1)}, u32[]{:S(2)}, u32[]{:S(2)}) collective-permute-start(bf16[2,256,128]{2,1,0:T(8,128)(2,1)S(1)} %get-tuple-element.35), channel_id=1, source_target_pairs={{0,5},{1,4},{2,7},{3,6},{4,1},{5,0},{6,3},{7,2},{8,13},{9,12},{10,... | collective-permute-start | bytes 393224 | tf_op jit(solution)/shard_map/ppermute | solution.py:83
  37.1 17.6 %collective-permute-start.7 = (bf16[2,256,128]{2,1,0:T(8,128)(2,1)S(1)}, bf16[2,256,128]{2,1,0:T(8,128)(2,1)S(1)}, u32[]{:S(2)}, u32[]{:S(2)}) collective-permute-start(bf16[2,256,128]{2,1,0:T(8,128)(2,1)S(1)} %get-tuple-element.36), channel_id=1, source_target_pairs={{0,3},{1,2},{2,1},{3,0},{4,7},{5,6},{6,5},{7,4},{8,11},{9,10},{10,... | collective-permute-start | bytes 393224 | tf_op jit(solution)/shard_map/ppermute | solution.py:83
  37.6 17.1 %collective-permute-start.8 = (bf16[2,256,128]{2,1,0:T(8,128)(2,1)S(1)}, bf16[2,256,128]{2,1,0:T(8,128)(2,1)S(1)}, u32[]{:S(2)}, u32[]{:S(2)}) collective-permute-start(bf16[2,256,128]{2,1,0:T(8,128)(2,1)S(1)} %get-tuple-element.37), channel_id=1, source_target_pairs={{0,6},{1,7},{2,4},{3,5},{4,2},{5,3},{6,0},{7,1},{8,14},{9,15},{10,... | collective-permute-start | bytes 393224 | tf_op jit(solution)/shard_map/ppermute | solution.py:83
  39.5 15.1 %collective-permute-start.9 = (bf16[2,256,128]{2,1,0:T(8,128)(2,1)S(1)}, bf16[2,256,128]{2,1,0:T(8,128)(2,1)S(1)}, u32[]{:S(2)}, u32[]{:S(2)}) collective-permute-start(bf16[2,256,128]{2,1,0:T(8,128)(2,1)S(1)} %get-tuple-element.38), channel_id=1, source_target_pairs={{0,7},{1,6},{2,5},{3,4},{4,3},{5,2},{6,1},{7,0},{8,15},{9,14},{10,... | collective-permute-start | bytes 393224 | tf_op jit(solution)/shard_map/ppermute | solution.py:83

commit v18 on v17

--- a/solution.py
+++ b/solution.py
@@ -19,7 +19,6 @@
 
 def pack_kernel(key_ref, value_ref, out_ref, staged, arrived, left):
     shares, piece_rows, _ = key_ref.shape
-    half = KEY_VALUE_HEADS * piece_rows
 
     def take(slot):
         ref = key_ref if slot < KEY_VALUE_HEADS else value_ref
@@ -31,7 +30,7 @@
         )
 
     def give(which, copy):
-        rows = pl.ds(which * half, half)
+        rows = pl.ds(which * piece_rows, piece_rows)
         return pltpu.make_async_copy(
             staged.at[:, rows, :],
             out_ref.at[pl.ds(copy * shares, shares), rows, :],
@@ -40,12 +39,11 @@
 
     for slot in range(SLOTS):
         take(slot).start()
-    for which in range(2):
-        for head in range(KEY_VALUE_HEADS):
-            take(which * KEY_VALUE_HEADS + head).wait()
+    for slot in range(SLOTS):
+        take(slot).wait()
         for copy in range(COPIES):
-            give(which, copy).start()
-    for which in range(2):
+            give(slot, copy).start()
+    for which in range(SLOTS):
         for copy in range(COPIES):
             give(which, copy).wait()
 
@@ -65,7 +63,7 @@
             scratch_shapes=[
                 pltpu.VMEM((shares, SLOTS * piece_rows, HEAD_SIZE), jnp.bfloat16),
                 pltpu.SemaphoreType.DMA((SLOTS,)),
-                pltpu.SemaphoreType.DMA((2, COPIES)),
+                pltpu.SemaphoreType.DMA((SLOTS, COPIES)),
             ],
             name="pack",
         )(keys.reshape(split), values.reshape(split))

time: 58.5 us -> 56.7 us (0.969)
  the two profiles are of different devices: /device:TPU:5 before, /device:TPU:17 now
where the time goes in v18:
time: 56.7 us; the launch traced here: 55.9 us
  Pallas kernels  21.9 us (39%)
  starting transfers between devices  15.8 us (28%)
  waiting for transfers between devices  14.1 us (25%)
  local copies, waits for them, and re-layouts  3.67 us (6%)
    pallas_call x2, Pallas kernels, far_attention(): pl.pallas_call(functools.partial(far_kernel, last=last), out_shape=out_sh...  14.4 us
    ppermute x10, starting transfers between devices, swap(): lax.ppermute(array, 'ctx', [(i, partner(i, step)) for i in range(devices)])  9.29 us
    ppermute x10, waiting for transfers between devices, swap(): lax.ppermute(array, 'ctx', [(i, partner(i, step)) for i in range(devices)])  8.73 us
    all_to_all x1, starting transfers between devices, local(): lax.all_to_all(packed, 'ctx', split_axis=0, concat_axis=0, tiled=True)  6.48 us
    all_to_all x1, waiting for transfers between devices, local(): lax.all_to_all(packed, 'ctx', split_axis=0, concat_axis=0, tiled=True)  5.33 us
    pallas_call x1, Pallas kernels, own_attention(): pl.pallas_call(own_kernel, out_shape=[pltpu.HBM(queries.shape, jnp.float3...  5.12 us
    unnamed x10, local copies, waits for them, and re-layouts  3.49 us
    pallas_call x1, Pallas kernels, pack(): pl.pallas_call(pack_kernel, out_shape=jax.ShapeDtypeStruct((devices, SLOT...  2.15 us
  transfers between devices with their start and end apart: 11, of which 5 were waited for; matrix products, arithmetic and copies ran while one was open for 1% of the time, Pallas kernels for 29%

profile of v18, /device:TPU:17, one launch (start us, length us, event | category | flops | bytes accessed | tf_op | source)
XLA Modules:
  0.0 55.9 jit_solution(11342489988153739076)
XLA Ops:
  0.0 2.1 %pack.1 = bf16[16,256,128]{2,1,0:T(8,128)(2,1)} custom-call(bf16[8,32,512]{2,1,0:T(8,128)(2,1)} %bitcast.10, bf16[8,32,512]{2,1,0:T(8,128)(2,1)} %bitcast.11), custom_call_target="tpu_custom_call" | custom-call | tf_op jit(solution)/shard_map/pack/pallas_call | solution.py:56
  2.2 6.5 %all-to-all-start = ((bf16[16,256,128]{2,1,0:T(8,128)(2,1)}), bf16[16,256,128]{2,1,0:T(8,128)(2,1)S(1)}, u32[]{:S(2)}, u32[]{:S(2)}) async-start(bf16[16,256,128]{2,1,0:T(8,128)(2,1)} %pack.1), calls=%async_computation | async-start | bytes 2097152 | tf_op jit(solution)/shard_map/all_to_all | solution.py:445
  8.7 1.6 %copy-done = bf16[256,4096]{1,0:T(8,128)(2,1)S(1)} copy-done((bf16[256,4096]{1,0:T(8,128)(2,1)S(1)}, bf16[256,4096]{1,0:T(8,128)(2,1)}, u32[]{:S(2)}) %copy-start) | copy-done | bytes 2097176
  10.2 0.9 %copy-done.2 = bf16[256,512]{1,0:T(8,128)(2,1)S(1)} copy-done((bf16[256,512]{1,0:T(8,128)(2,1)S(1)}, bf16[256,512]{1,0:T(8,128)(2,1)}, u32[]{:S(2)}) %copy-start.2) | copy-done | bytes 262168
  11.2 0.9 %copy-done.3 = bf16[256,512]{1,0:T(8,128)(2,1)S(1)} copy-done((bf16[256,512]{1,0:T(8,128)(2,1)S(1)}, bf16[256,512]{1,0:T(8,128)(2,1)}, u32[]{:S(2)}) %copy-start.3) | copy-done | bytes 262168
  12.1 5.1 %own_attention.1 = (f32[256,4096]{1,0:T(8,128)}, f32[256,512]{1,0:T(8,128)}) custom-call(bf16[256,4096]{1,0:T(8,128)(2,1)S(1)} %copy-done, bf16[256,512]{1,0:T(8,128)(2,1)S(1)} %copy-done.2, bf16[256,512]{1,0:T(8,128)(2,1)S(1)} %copy-done.3), custom_call_target="tpu_custom_call" | custom-call | flops 1073741824 | bytes 7340032 | tf_op jit(solution)/shard_map/own_attention/pallas_call | solution.py:198
  17.3 0.1 copy.8
  17.4 0.4 collective-permute-start
  17.7 0.8 %collective-permute-done = s32[1,2]{0,1:T(2,128)S(1)} collective-permute-done((s32[1,2]{0,1:T(2,128)S(1)}, s32[1,2]{0,1:T(2,128)S(1)}, u32[]{:S(2)}, u32[]{:S(2)}) %collective-permute-start) | collective-permute-done | bytes 40 | tf_op jit(solution)/shard_map/ppermute | solution.py:81
  18.6 1.2 %collective-permute-start.1 = (s32[2,2]{0,1:T(2,128)S(1)}, s32[2,2]{0,1:T(2,128)S(1)}, u32[]{:S(2)}, u32[]{:S(2)}) collective-permute-start(s32[2,2]{0,1:T(2,128)S(1)} %pad_add_fusion), channel_id=1, source_target_pairs={{0,2},{1,3},{2,0},{3,1},{4,6},{5,7},{6,4},{7,5},{8,10},{9,11},{10,... | collective-permute-start | bytes 56 | tf_op jit(solution)/shard_map/ppermute | solution.py:81
  19.8 1.5 %collective-permute-done.1 = s32[2,2]{0,1:T(2,128)S(1)} collective-permute-done((s32[2,2]{0,1:T(2,128)S(1)}, s32[2,2]{0,1:T(2,128)S(1)}, u32[]{:S(2)}, u32[]{:S(2)}) %collective-permute-start.1) | collective-permute-done | bytes 48 | tf_op jit(solution)/shard_map/ppermute | solution.py:81
  21.4 1.2 %collective-permute-start.2 = (s32[4,2]{0,1:T(2,128)S(1)}, s32[4,2]{0,1:T(2,128)S(1)}, u32[]{:S(2)}, u32[]{:S(2)}) collective-permute-start(s32[4,2]{0,1:T(2,128)S(1)} %pad_add_fusion.1), channel_id=1, source_target_pairs={{0,4},{1,5},{2,6},{3,7},{4,0},{5,1},{6,2},{7,3},{8,12},{9,13},{10,... | collective-permute-start | bytes 104 | tf_op jit(solution)/shard_map/ppermute | solution.py:81
  22.6 5.2 %collective-permute-done.2 = s32[4,2]{0,1:T(2,128)S(1)} collective-permute-done((s32[4,2]{0,1:T(2,128)S(1)}, s32[4,2]{0,1:T(2,128)S(1)}, u32[]{:S(2)}, u32[]{:S(2)}) %collective-permute-start.2) | collective-permute-done | bytes 64 | tf_op jit(solution)/shard_map/ppermute | solution.py:81
  28.0 5.3 %all-to-all-done.held_ref = bf16[16,256,128]{2,1,0:T(8,128)(2,1)S(1)} async-done(((bf16[16,256,128]{2,1,0:T(8,128)(2,1)}), bf16[16,256,128]{2,1,0:T(8,128)(2,1)S(1)}, u32[]{:S(2)}, u32[]{:S(2)}) %all-to-all-start) | async-done | bytes 1048608 | tf_op jit(solution)/shard_map/all_to_all | solution.py:445
  33.3 0.2 pick_pieces.1
  33.5 0.9 %collective-permute-start.3 = (bf16[2,256,128]{2,1,0:T(8,128)(2,1)S(1)}, bf16[2,256,128]{2,1,0:T(8,128)(2,1)S(1)}, u32[]{:S(2)}, u32[]{:S(2)}) collective-permute-start(bf16[2,256,128]{2,1,0:T(8,128)(2,1)S(1)} %get-tuple-element.30), channel_id=1, source_target_pairs={{0,1},{1,0},{2,3},{3,2},{4,5},{5,4},{6,7},{7,6},{8,9},{9,8},{10,11... | collective-permute-start | bytes 393224 | tf_op jit(solution)/shard_map/ppermute | solution.py:81
  34.5 1.0 %collective-permute-start.5 = (bf16[2,256,128]{2,1,0:T(8,128)(2,1)S(1)}, bf16[2,256,128]{2,1,0:T(8,128)(2,1)S(1)}, u32[]{:S(2)}, u32[]{:S(2)}) collective-permute-start(bf16[2,256,128]{2,1,0:T(8,128)(2,1)S(1)} %get-tuple-element.32), channel_id=1, source_target_pairs={{0,2},{1,3},{2,0},{3,1},{4,6},{5,7},{6,4},{7,5},{8,10},{9,11},{10,... | collective-permute-start | bytes 393224 | tf_op jit(solution)/shard_map/ppermute | solution.py:81
  35.4 0.7 %collective-permute-start.6 = (bf16[2,256,128]{2,1,0:T(8,128)(2,1)S(1)}, bf16[2,256,128]{2,1,0:T(8,128)(2,1)S(1)}, u32[]{:S(2)}, u32[]{:S(2)}) collective-permute-start(bf16[2,256,128]{2,1,0:T(8,128)(2,1)S(1)} %get-tuple-element.35), channel_id=1, source_target_pairs={{0,5},{1,4},{2,7},{3,6},{4,1},{5,0},{6,3},{7,2},{8,13},{9,12},{10,... | collective-permute-start | bytes 393224 | tf_op jit(solution)/shard_map/ppermute | solution.py:81
  36.2 1.5 %collective-permute-start.7 = (bf16[2,256,128]{2,1,0:T(8,128)(2,1)S(1)}, bf16[2,256,128]{2,1,0:T(8,128)(2,1)S(1)}, u32[]{:S(2)}, u32[]{:S(2)}) collective-permute-start(bf16[2,256,128]{2,1,0:T(8,128)(2,1)S(1)} %get-tuple-element.36), channel_id=1, source_target_pairs={{0,3},{1,2},{2,1},{3,0},{4,7},{5,6},{6,5},{7,4},{8,11},{9,10},{10,... | collective-permute-start | bytes 393224 | tf_op jit(solution)/shard_map/ppermute | solution.py:81
  37.7 0.7 %collective-permute-start.8 = (bf16[2,256,128]{2,1,0:T(8,128)(2,1)S(1)}, bf16[2,256,128]{2,1,0:T(8,128)(2,1)S(1)}, u32[]{:S(2)}, u32[]{:S(2)}) collective-permute-start(bf16[2,256,128]{2,1,0:T(8,128)(2,1)S(1)} %get-tuple-element.37), channel_id=1, source_target_pairs={{0,6},{1,7},{2,4},{3,5},{4,2},{5,3},{6,0},{7,1},{8,14},{9,15},{10,... | collective-permute-start | bytes 393224 | tf_op jit(solution)/shard_map/ppermute | solution.py:81
  38.4 1.2 %collective-permute-done.4 = bf16[2,256,128]{2,1,0:T(8,128)(2,1)S(1)} collective-permute-done((bf16[2,256,128]{2,1,0:T(8,128)(2,1)S(1)}, bf16[2,256,128]{2,1,0:T(8,128)(2,1)S(1)}, u32[]{:S(2)}, u32[]{:S(2)}) %collective-permute-start.4) | collective-permute-done | bytes 131104 | tf_op jit(solution)/shard_map/ppermute | solution.py:81
  39.5 1.7 %collective-permute-start.9 = (bf16[2,256,128]{2,1,0:T(8,128)(2,1)S(1)}, bf16[2,256,128]{2,1,0:T(8,128)(2,1)S(1)}, u32[]{:S(2)}, u32[]{:S(2)}) collective-permute-start(bf16[2,256,128]{2,1,0:T(8,128)(2,1)S(1)} %get-tuple-element.38), channel_id=1, source_target_pairs={{0,7},{1,6},{2,5},{3,4},{4,3},{5,2},{6,1},{7,0},{8,15},{9,14},{10,... | collective-permute-start | bytes 393224 | tf_op jit(solution)/shard_map/ppermute | solution.py:81
  41.2 11.0 %early_attention.1 = (f32[256,4096]{1,0:T(8,128)S(1)}, f32[256,4096]{1,0:T(8,128)S(1)}) custom-call(s32[1,2]{1,0:T(1,128)S(1)} %copy-done.4, bf16[256,4096]{1,0:T(8,128)(2,1)S(1)} %copy-done.1, f32[256,4096]{1,0:T(8,128)} %get-tuple-element.25.own_in, f32[256,512]{1,0:T(8,128)} %get-tuple-element.26.level_in, bf16[2,8,32,128]{3,2,1,0:T(8,128)(2,1)S(1)} %bitcast.16, ...), custom_call_target="tpu_custom_call" | custom-call | flops 1073741824 | bytes 10485760 | tf_op jit(solution)/shard_map/early_attention/pallas_call | solution.py:419
  52.3 3.5 %late_attention.1 = bf16[256,4096]{1,0:T(8,128)(2,1)} custom-call(s32[1,2]{1,0:T(1,128)S(1)} %copy-done.4, bf16[256,4096]{1,0:T(8,128)(2,1)S(1)} %copy-done.1, f32[256,4096]{1,0:T(8,128)S(1)} %get-tuple-element.33.own_in, f32[256,4096]{1,0:T(8,128)S(1)} %get-tuple-element.34.level_in, bf16[2,8,32,128]{3,2,1,0:T(8,128)(2,1)S(1)} %bitcast.12, ...), custom_call_target="tpu_custom_call" | custom-call | flops 1073741824 | bytes 10485760 | tf_op jit(solution)/shard_map/late_attention/pallas_call | solution.py:419
  (19 shorter events, 0.3 us)
Async XLA Ops:
  0.0 17.3 %copy-start.4 = (s32[1,2]{1,0:T(1,128)S(1)}, s32[1,2]{1,0:T(1,128)}, u32[]{:S(2)}) copy-start(s32[1,2]{1,0:T(1,128)} %selected_ref.3) | copy-start | bytes 28
  0.0 41.2 %copy-start.1 = (bf16[256,4096]{1,0:T(8,128)(2,1)S(1)}, bf16[256,4096]{1,0:T(8,128)(2,1)}, u32[]{:S(2)}) copy-start(bf16[256,4096]{1,0:T(8,128)(2,1)} %query_ref.2) | copy-start | bytes 6291460
  2.2 31.1 %all-to-all-start = ((bf16[16,256,128]{2,1,0:T(8,128)(2,1)}), bf16[16,256,128]{2,1,0:T(8,128)(2,1)S(1)}, u32[]{:S(2)}, u32[]{:S(2)}) async-start(bf16[16,256,128]{2,1,0:T(8,128)(2,1)} %pack.1), calls=%async_computation | async-start | bytes 2097152 | tf_op jit(solution)/shard_map/all_to_all | solution.py:445
  8.6 1.6 %copy-start = (bf16[256,4096]{1,0:T(8,128)(2,1)S(1)}, bf16[256,4096]{1,0:T(8,128)(2,1)}, u32[]{:S(2)}) copy-start(bf16[256,4096]{1,0:T(8,128)(2,1)} %query_ref.2) | copy-start | bytes 6291460
  10.2 0.9 %copy-start.2 = (bf16[256,512]{1,0:T(8,128)(2,1)S(1)}, bf16[256,512]{1,0:T(8,128)(2,1)}, u32[]{:S(2)}) copy-start(bf16[256,512]{1,0:T(8,128)(2,1)} %key_ref.1) | copy-start | bytes 786436
  11.2 0.9 %copy-start.3 = (bf16[256,512]{1,0:T(8,128)(2,1)S(1)}, bf16[256,512]{1,0:T(8,128)(2,1)}, u32[]{:S(2)}) copy-start(bf16[256,512]{1,0:T(8,128)(2,1)} %value_ref.1) | copy-start | bytes 786436
  17.4 1.2 %collective-permute-start = (s32[1,2]{0,1:T(2,128)S(1)}, s32[1,2]{0,1:T(2,128)S(1)}, u32[]{:S(2)}, u32[]{:S(2)}) collective-permute-start(s32[1,2]{0,1:T(2,128)S(1)} %copy.8), channel_id=1, source_target_pairs={{0,1},{1,0},{2,3},{3,2},{4,5},{5,4},{6,7},{7,6},{8,9},{9,8},{10,11... | collective-permute-start | bytes 32 | tf_op jit(solution)/shard_map/ppermute | solution.py:81
  18.6 2.7 %collective-permute-start.1 = (s32[2,2]{0,1:T(2,128)S(1)}, s32[2,2]{0,1:T(2,128)S(1)}, u32[]{:S(2)}, u32[]{:S(2)}) collective-permute-start(s32[2,2]{0,1:T(2,128)S(1)} %pad_add_fusion), channel_id=1, source_target_pairs={{0,2},{1,3},{2,0},{3,1},{4,6},{5,7},{6,4},{7,5},{8,10},{9,11},{10,... | collective-permute-start | bytes 56 | tf_op jit(solution)/shard_map/ppermute | solution.py:81
  21.4 6.4 %collective-permute-start.2 = (s32[4,2]{0,1:T(2,128)S(1)}, s32[4,2]{0,1:T(2,128)S(1)}, u32[]{:S(2)}, u32[]{:S(2)}) collective-permute-start(s32[4,2]{0,1:T(2,128)S(1)} %pad_add_fusion.1), channel_id=1, source_target_pairs={{0,4},{1,5},{2,6},{3,7},{4,0},{5,1},{6,2},{7,3},{8,12},{9,13},{10,... | collective-permute-start | bytes 104 | tf_op jit(solution)/shard_map/ppermute | solution.py:81
  33.5 4.2 %collective-permute-start.3 = (bf16[2,256,128]{2,1,0:T(8,128)(2,1)S(1)}, bf16[2,256,128]{2,1,0:T(8,128)(2,1)S(1)}, u32[]{:S(2)}, u32[]{:S(2)}) collective-permute-start(bf16[2,256,128]{2,1,0:T(8,128)(2,1)S(1)} %get-tuple-element.30), channel_id=1, source_target_pairs={{0,1},{1,0},{2,3},{3,2},{4,5},{5,4},{6,7},{7,6},{8,9},{9,8},{10,11... | collective-permute-start | bytes 393224 | tf_op jit(solution)/shard_map/ppermute | solution.py:81
  34.4 5.1 %collective-permute-start.4 = (bf16[2,256,128]{2,1,0:T(8,128)(2,1)S(1)}, bf16[2,256,128]{2,1,0:T(8,128)(2,1)S(1)}, u32[]{:S(2)}, u32[]{:S(2)}) collective-permute-start(bf16[2,256,128]{2,1,0:T(8,128)(2,1)S(1)} %get-tuple-element.31), channel_id=1, source_target_pairs={{0,4},{1,5},{2,6},{3,7},{4,0},{5,1},{6,2},{7,3},{8,12},{9,13},{10,... | collective-permute-start | bytes 393224 | tf_op jit(solution)/shard_map/ppermute | solution.py:81
  34.5 6.8 %collective-permute-start.5 = (bf16[2,256,128]{2,1,0:T(8,128)(2,1)S(1)}, bf16[2,256,128]{2,1,0:T(8,128)(2,1)S(1)}, u32[]{:S(2)}, u32[]{:S(2)}) collective-permute-start(bf16[2,256,128]{2,1,0:T(8,128)(2,1)S(1)} %get-tuple-element.32), channel_id=1, source_target_pairs={{0,2},{1,3},{2,0},{3,1},{4,6},{5,7},{6,4},{7,5},{8,10},{9,11},{10,... | collective-permute-start | bytes 393224 | tf_op jit(solution)/shard_map/ppermute | solution.py:81
  35.4 16.8 %collective-permute-start.6 = (bf16[2,256,128]{2,1,0:T(8,128)(2,1)S(1)}, bf16[2,256,128]{2,1,0:T(8,128)(2,1)S(1)}, u32[]{:S(2)}, u32[]{:S(2)}) collective-permute-start(bf16[2,256,128]{2,1,0:T(8,128)(2,1)S(1)} %get-tuple-element.35), channel_id=1, source_target_pairs={{0,5},{1,4},{2,7},{3,6},{4,1},{5,0},{6,3},{7,2},{8,13},{9,12},{10,... | collective-permute-start | bytes 393224 | tf_op jit(solution)/shard_map/ppermute | solution.py:81
  36.2 16.1 %collective-permute-start.7 = (bf16[2,256,128]{2,1,0:T(8,128)(2,1)S(1)}, bf16[2,256,128]{2,1,0:T(8,128)(2,1)S(1)}, u32[]{:S(2)}, u32[]{:S(2)}) collective-permute-start(bf16[2,256,128]{2,1,0:T(8,128)(2,1)S(1)} %get-tuple-element.36), channel_id=1, source_target_pairs={{0,3},{1,2},{2,1},{3,0},{4,7},{5,6},{6,5},{7,4},{8,11},{9,10},{10,... | collective-permute-start | bytes 393224 | tf_op jit(solution)/shard_map/ppermute | solution.py:81
  37.7 14.6 %collective-permute-start.8 = (bf16[2,256,128]{2,1,0:T(8,128)(2,1)S(1)}, bf16[2,256,128]{2,1,0:T(8,128)(2,1)S(1)}, u32[]{:S(2)}, u32[]{:S(2)}) collective-permute-start(bf16[2,256,128]{2,1,0:T(8,128)(2,1)S(1)} %get-tuple-element.37), channel_id=1, source_target_pairs={{0,6},{1,7},{2,4},{3,5},{4,2},{5,3},{6,0},{7,1},{8,14},{9,15},{10,... | collective-permute-start | bytes 393224 | tf_op jit(solution)/shard_map/ppermute | solution.py:81
  39.5 12.7 %collective-permute-start.9 = (bf16[2,256,128]{2,1,0:T(8,128)(2,1)S(1)}, bf16[2,256,128]{2,1,0:T(8,128)(2,1)S(1)}, u32[]{:S(2)}, u32[]{:S(2)}) collective-permute-start(bf16[2,256,128]{2,1,0:T(8,128)(2,1)S(1)} %get-tuple-element.38), channel_id=1, source_target_pairs={{0,7},{1,6},{2,5},{3,4},{4,3},{5,2},{6,1},{7,0},{8,15},{9,14},{10,... | collective-permute-start | bytes 393224 | tf_op jit(solution)/shard_map/ppermute | solution.py:81
